TPU v7x, 32 devices: a whole 2x2x4 slice. The times are simulated.
32 devices in a mesh: groups: 2 (over y), seq: 4 (over z), mp: 4 (over x, core).
Axes of the slice: x: 2, y: 2, z: 4, core: 2. Of those that a mesh axis runs over, the one named last changes fastest.
Arguments:
- queries: bfloat16 [2048, 4096], P(('groups', 'seq'), 'mp'), parts along dimension 0, may hold values from -170 to 170
- keys: bfloat16 [2048, 512], P(('groups', 'seq'), 'mp'), parts along dimension 0, may hold values from -4.5 to 4.5
- values: bfloat16 [2048, 512], P(('groups', 'seq'), 'mp'), parts along dimension 0, may hold values from -6 to 6
- lengths: int32 [6], P('groups'), parts along dimension 0, may hold values from 1 to 512, 1024 in all
- old_place: int32 [256], P('groups'), parts along dimension 0, may hold values from 0 to 127, as said below
Outputs:
- attended: bfloat16 [2048, 4096], P(('groups', 'seq'), 'mp'), parts along dimension 0
There are 2 independent parts, one for each index of `groups`. A program takes and returns all parts, laid end to end along the dimension named above; each array names one. Nothing has to cross between parts.
Inputs may be any that keep to these rules, and one draw needn't show every extreme that they name: Each of the 3 lengths is at least 1, they sum to 1024, and the largest is exactly 512. `old_place`: A permutation of the 128 block places; places p * 32 to p * 32 + 31 belong to old owner p, blocks p * 32 to p * 32 + 31 to new owner p (index p of seq). Between any old owner and any new owner either no block or exactly 8 blocks move.
All inputs are finite; a program needn't handle non-finite values.
Results may differ from a plain program's by a relative error of at most 0.0029.
Values may be sent and summed in bfloat16 or wider, within the bound.
No kernel may reach another device: no remote copies, remote signals or barrier semaphores. Data moves between devices by JAX's collectives and lax.ppermute only.
A program may use at most 64 MiB of HBM per device.

v0:
```python
import jax
import jax.numpy as jnp
from jax import lax
from jax.sharding import PartitionSpec as P

QUERY_HEAD_TOTAL = 32
SHARED_KV_HEADS = 4
HEAD_WIDTH = 128


NEG_FILL = -1e30


def passed_along(value, axis, by):
    devices = lax.axis_size(axis)
    pairs = [(i, i + by) for i in range(devices) if 0 <= i + by < devices]
    return lax.ppermute(value, axis, pairs)


def split_heads(matrix, heads):
    count_rows = matrix.shape[0]
    return matrix.reshape(count_rows, heads, -1).transpose(1, 0, 2)


def pack_blocks(matrix, index, slots, block_rows):
    width = matrix.shape[1]
    blocks = matrix.reshape(-1, block_rows, width)
    empty = jnp.zeros((slots, block_rows, width), matrix.dtype)
    return empty.at[index].set(blocks).reshape(slots * block_rows, width)


def unpack_blocks(matrix, index, block_rows):
    width = matrix.shape[1]
    return matrix.reshape(-1, block_rows, width)[index].reshape(-1, width)


def attend(carry, pairs, key_first, context):
    query_heads, query_pos, query_start, lowest, highest = context
    key_count = pairs.shape[0]
    heads = query_heads.shape[0]
    half_width = pairs.shape[1] // 2

    def compute(running):
        running_max, running_sum, summed = running
        key_heads = split_heads(pairs[:, :half_width], heads)
        value_heads = split_heads(pairs[:, half_width:], heads)
        key_pos = key_first + jnp.arange(key_count, dtype=jnp.int32)
        visible = (key_pos[None, :] >= query_start[:, None]) & (
            key_pos[None, :] <= query_pos[:, None]
        )
        scores = jnp.einsum(
            "cih,cjh->cij", query_heads, key_heads, preferred_element_type=jnp.float32
        ) * HEAD_WIDTH ** (-0.5)
        new_max = jnp.maximum(
            running_max, jnp.max(jnp.where(visible[None], scores, NEG_FILL), axis=2)
        )
        rescale = jnp.exp(running_max - new_max)
        weights = jnp.where(visible[None], jnp.exp(scores - new_max[:, :, None]), 0.0)
        new_sum = running_sum * rescale + jnp.sum(weights, axis=2)
        update = jnp.einsum(
            "cij,cjh->cih",
            weights.astype(jnp.bfloat16),
            value_heads,
            preferred_element_type=jnp.float32,
        )
        return (new_max, new_sum, summed * rescale[:, :, None] + update)

    needed = (key_first <= highest) & (key_first + key_count - 1 >= lowest)
    return lax.cond(needed, compute, lambda running: running, carry)


def cycle_pass(carry, pairs, own_index, cycle_size, row_count, turns, mover, context):

    def one_turn(turn_id, packed):
        running, current = packed
        current = mover(current)
        anchor = (own_index - turn_id - 1) % cycle_size
        return (attend(running, current, anchor * row_count, context), current)

    return lax.fori_loop(0, turns, one_turn, (carry, pairs))[0]


def body(queries, keys, values, lengths, old_place):
    row_count, query_cols = queries.shape
    cycle_size = lax.axis_size("seq")
    own_index = lax.axis_index("seq")
    block_total = old_place.shape[0]
    per_device = block_total // cycle_size
    block_rows = row_count // per_device
    capacity = max(1, per_device // cycle_size)
    slot_total = cycle_size * capacity
    slot_ids = jnp.arange(block_total, dtype=jnp.int32)
    local_ids = jnp.arange(per_device, dtype=jnp.int32)
    new_block = jnp.zeros((block_total,), jnp.int32).at[old_place].set(slot_ids)
    new_owner = new_block // per_device
    target = lax.dynamic_slice_in_dim(new_owner, own_index * per_device, per_device)
    earlier = local_ids[None, :] < local_ids[:, None]
    send_rank = jnp.sum(((target[None, :] == target[:, None]) & earlier).astype(jnp.int32), axis=1)
    send_index = target * capacity + send_rank
    source_slot = lax.dynamic_slice_in_dim(old_place, own_index * per_device, per_device)
    source_owner = source_slot // per_device
    same_source = slot_ids[None, :] // per_device == source_owner[:, None]
    before_slot = slot_ids[None, :] < source_slot[:, None]
    toward_me = (new_owner == own_index)[None, :]
    receive_rank = jnp.sum((same_source & before_slot & toward_me).astype(jnp.int32), axis=1)
    receive_index = source_owner * capacity + receive_rank
    sent_queries = pack_blocks(queries, send_index, slot_total, block_rows)
    sent_pairs = pack_blocks(
        jnp.concatenate([keys, values], axis=1), send_index, slot_total, block_rows
    )
    got_queries, got_pairs = (
        lax.all_to_all(sent_queries, "seq", split_axis=0, concat_axis=0, tiled=True),
        lax.all_to_all(sent_pairs, "seq", split_axis=0, concat_axis=0, tiled=True),
    )
    new_queries = unpack_blocks(got_queries, receive_index, block_rows)
    new_pairs = unpack_blocks(got_pairs, receive_index, block_rows)
    heads = keys.shape[1] // HEAD_WIDTH
    query_group_width = QUERY_HEAD_TOTAL // SHARED_KV_HEADS
    query_heads = new_queries.reshape(row_count, heads, query_group_width * HEAD_WIDTH).transpose(
        1, 0, 2
    )
    query_heads = query_heads.reshape(heads, row_count * query_group_width, HEAD_WIDTH)
    bounds = jnp.cumsum(lengths)
    positions = own_index * row_count + jnp.arange(row_count, dtype=jnp.int32)
    starts = jnp.max(jnp.where(bounds[None, :] <= positions[:, None], bounds[None, :], 0), axis=1)
    context = (
        query_heads,
        jnp.repeat(positions, query_group_width),
        jnp.repeat(starts, query_group_width),
        jnp.min(starts),
        own_index * row_count + row_count - 1,
    )
    initial = (
        jnp.full((heads, row_count * query_group_width), NEG_FILL, jnp.float32),
        jnp.zeros((heads, row_count * query_group_width), jnp.float32),
        jnp.zeros((heads, row_count * query_group_width, HEAD_WIDTH), jnp.float32),
    )
    own_tile = attend(initial, new_pairs, own_index * row_count, context)
    final = cycle_pass(
        own_tile,
        new_pairs,
        own_index,
        cycle_size,
        row_count,
        cycle_size - 1,
        lambda moving: passed_along(moving, "seq", 1),
        context,
    )
    running_max, running_sum, summed = final
    attended = (summed / running_sum[:, :, None]).reshape(
        heads, row_count, query_group_width * HEAD_WIDTH
    )
    attended = attended.transpose(1, 0, 2).reshape(row_count, query_cols).astype(jnp.bfloat16)
    sent_back = pack_blocks(attended, receive_index, slot_total, block_rows)
    got_back = lax.all_to_all(sent_back, "seq", split_axis=0, concat_axis=0, tiled=True)
    return unpack_blocks(got_back, send_index, block_rows)


def solution(mesh):
    in_specs = (
        P(("groups", "seq"), "mp"),
        P(("groups", "seq"), "mp"),
        P(("groups", "seq"), "mp"),
        P("groups"),
        P("groups"),
    )
    out_specs = P(("groups", "seq"), "mp")
    return jax.shard_map(body, mesh=mesh, in_specs=in_specs, out_specs=out_specs, check_vma=False)
```

profile of v0, /device:TPU:0, one launch (start us, length us, event | category | flops | bytes accessed | tf_op | source)
XLA Modules:
  0.0 90.8 jit_solution(13633009606156503341)
XLA Ops:
  0.0 0.7 compare_select_fusion.2
  0.7 1.0 %scatter_custom_fusion = s32[128]{0:T(128)S(1)} fusion(s32[128]{0:T(128)S(1)} %compare_select_fusion.2, s32[128]{0:T(128)S(1)} %iota.32, s32[]{:T(128)} %constant.157.clone.1), kind=kCustom, calls=%fused_computation.79 | custom fusion | bytes 516 | tf_op jit(solution)/shard_map/scatter | solution.py:94
  1.7 0.1 dynamic_slice.7
  1.7 0.2 convert_reduce_fusion
  1.9 0.1 compare_select_fusion
  2.0 0.0 copy-start
  2.0 0.9 maximum_bitcast_fusion
  2.9 0.6 broadcast_in_dim.96
  3.6 3.5 %scatter_fusion.1 = bf16[32,8,256]{2,1,0:T(8,128)(2,1)} fusion(bf16[32,8,256]{2,1,0:T(8,128)(2,1)} %broadcast_in_dim.96, s32[32]{0:T(128)S(1)} %compare_select_fusion, bf16[32,8,256]{2,1,0:T(8,128)(2,1)S(1)} %maximum_bitcast_fusion), kind=kCustom, calls=%fused_computation.5 | custom fusion | bytes 393344 | tf_op jit(solution)/shard_map/scatter | solution.py:29
  7.1 6.3 %all-to-all-start.1 = ((bf16[4,64,256]{2,1,0:T(8,128)(2,1)}), bf16[4,64,256]{2,1,0:T(8,128)(2,1)S(1)}, u32[]{:S(2)}, u32[]{:S(2)}) async-start(bf16[4,64,256]{2,1,0:T(8,128)(2,1)} %bitcast.16), calls=%async_computation.1 | async-start | bytes 262144 | tf_op jit(solution)/shard_map/all_to_all | solution.py:113
  13.4 0.8 reduce-window.8
  14.2 0.9 broadcast.146.clone
  15.1 4.8 %scatter_fusion = bf16[32,8,1024]{2,1,0:T(8,128)(2,1)} fusion(bf16[32,8,1024]{2,1,0:T(8,128)(2,1)} %broadcast.146.clone, s32[32]{0:T(128)S(1)} %compare_select_fusion, bf16[32,8,1024]{2,1,0:T(8,128)(2,1)} %bitcast.41), kind=kCustom, calls=%fused_computation.4 | custom fusion | bytes 1572992 | tf_op jit(solution)/shard_map/scatter | solution.py:29
  19.9 0.0 all-to-all-done.1
  19.9 5.1 %all-to-all-start = ((bf16[4,64,1024]{2,1,0:T(8,128)(2,1)}), bf16[4,64,1024]{2,1,0:T(8,128)(2,1)S(1)}, u32[]{:S(2)}, u32[]{:S(2)}) async-start(bf16[4,64,1024]{2,1,0:T(8,128)(2,1)} %bitcast.13), calls=%async_computation | async-start | bytes 1048576 | tf_op jit(solution)/shard_map/all_to_all | solution.py:112
  25.0 0.1 select_reduce_fusion.2
  25.1 0.7 reduce_min.9
  26.5 0.0 copy-done
  26.5 0.1 and_select_fusion.2
  26.6 0.2 convert_reduce_fusion.1
  26.8 0.6 gather_fusion.1
  27.4 11.5 %all-to-all-done = bf16[4,64,1024]{2,1,0:T(8,128)(2,1)S(1)} async-done(((bf16[4,64,1024]{2,1,0:T(8,128)(2,1)}), bf16[4,64,1024]{2,1,0:T(8,128)(2,1)S(1)}, u32[]{:S(2)}, u32[]{:S(2)}) %all-to-all-start) | async-done | bytes 524320 | tf_op jit(solution)/shard_map/all_to_all | solution.py:112
  38.9 0.6 gather_fusion
  39.5 0.2 reshape_transpose_reshape_reshape.3
  39.7 5.3 %conditional.2 = (f32[1,2048]{1,0:T(1,128)}, f32[1,2048]{1,0:T(1,128)S(1)}, f32[1,2048,128]{2,1,0:T(8,128)S(1)}) conditional(s32[]{:T(128)} %convert_element_type.39, () %tuple.53, (s32[]{:T(128)}, s32[256]{0:T(256)S(1)}, s32[256]{0:T(256)S(1)}, bf16[1,2048,128]{2,1,0:T(8,128)(2,1)S(1)}, bf16[256,256]{1,0:T(8,128)(2,1)S(1)}) %tuple.88), branch_computations={%region_8.9_spmd, %region_9.12_spmd} | conditional | flops 278143232 | bytes 8189980 | solution.py:69
  39.8 0.1 broadcast_in_dim.107
  39.9 0.1 ge.38
  40.0 0.1 broadcast_in_dim.108
  40.1 0.1 le.29
  40.2 0.6 select_reduce_fusion
  40.8 0.6 exponential_multiply_fusion
  41.4 1.6 %fusion.4 = f32[1,2048,128]{2,1,0:T(8,128)S(1)} fusion(f32[2048,256]{0,1:T(8,128)S(1)} %get-tuple-element.532, f32[2048]{0:T(1024)} %get-tuple-element.530, s32[2048]{0:T(1024)S(1)} %le.29, s32[2048]{0:T(1024)S(1)} %ge.38, s32[256]{0:T(256)S(1)} %iota_add_fusion, f32[2048]{0:T(1024)S(1)} %get-tuple-element.529, bf16[256,256]{1,0:T(8,128)(2,1)S(1)} %get-tuple-element.433), kind=kOutput, calls=%fused_computation.11 | convolution fusion | flops 137625600 | bytes 3245056 | tf_op jit(solution)/shard_map/cond/branch_1_fun/cij,cjh->cih/dot_general | solution.py:60
  43.0 1.3 %fusion.6 = f32[2048]{0:T(1024)S(1)} fusion(f32[2048,256]{0,1:T(8,128)S(1)} %get-tuple-element.532, f32[2048]{0:T(1024)} %get-tuple-element.530, s32[2048]{0:T(1024)S(1)} %le.29, s32[2048]{0:T(1024)S(1)} %ge.38, s32[256]{0:T(256)S(1)} %iota_add_fusion), kind=kLoop, calls=%fused_computation.16 | loop fusion | flops 3143680 | bytes 2130944 | tf_op jit(solution)/shard_map/cond/branch_1_fun/reduce_sum | solution.py:59
  44.3 0.7 multiply_add_fusion
  45.1 22.5 %while.25 = (s32[]{:T(128)}, f32[1,2048]{1,0:T(1,128)}, f32[1,2048]{1,0:T(1,128)S(1)}, f32[1,2048,128]{2,1,0:T(8,128)S(1)}, bf16[256,256]{1,0:T(8,128)(2,1)S(1)}...) while((s32[]{:T(128)}, f32[1,2048]{1,0:T(1,128)}, ...), condition=%wide.region_17.18_spmd.clone, body=%wide.region_12.17_spmd.clone.sunk | while | flops 278401312 | bytes 10066432 | solution.py:80
  45.1 1.3 %collective-permute-start = (bf16[256,256]{1,0:T(8,128)(2,1)S(1)}, bf16[256,256]{1,0:T(8,128)(2,1)S(1)}, u32[]{:S(2)}, u32[]{:S(2)}) collective-permute-start(bf16[256,256]{1,0:T(8,128)(2,1)S(1)} %get-tuple-element.642), channel_id=1, source_target_pairs={{0,4},{4,8},{8,12},{1,5},{5,9},{9,13},{2,6},{6,10},{10,14},{3,7},{... | collective-permute-start | bytes 393224 | tf_op jit(solution)/shard_map/while/body/eval_jaxpr/ppermute | solution.py:17
  47.1 1.8 %collective-permute-done = bf16[256,256]{1,0:T(8,128)(2,1)S(1)} collective-permute-done((bf16[256,256]{1,0:T(8,128)(2,1)S(1)}, bf16[256,256]{1,0:T(8,128)(2,1)S(1)}, u32[]{:S(2)}, u32[]{:S(2)}) %collective-permute-start) | collective-permute-done | bytes 131104 | tf_op jit(solution)/shard_map/while/body/eval_jaxpr/ppermute | solution.py:17
  48.9 9.2 %collective-permute-start = (bf16[256,256]{1,0:T(8,128)(2,1)S(1)}, bf16[256,256]{1,0:T(8,128)(2,1)S(1)}, u32[]{:S(2)}, u32[]{:S(2)}) collective-permute-start(bf16[256,256]{1,0:T(8,128)(2,1)S(1)} %get-tuple-element.642), channel_id=1, source_target_pairs={{0,4},{4,8},{8,12},{1,5},{5,9},{9,13},{2,6},{6,10},{10,14},{3,7},{... | collective-permute-start | bytes 393224 | tf_op jit(solution)/shard_map/while/body/eval_jaxpr/ppermute | solution.py:17
  58.8 1.8 %collective-permute-done = bf16[256,256]{1,0:T(8,128)(2,1)S(1)} collective-permute-done((bf16[256,256]{1,0:T(8,128)(2,1)S(1)}, bf16[256,256]{1,0:T(8,128)(2,1)S(1)}, u32[]{:S(2)}, u32[]{:S(2)}) %collective-permute-start) | collective-permute-done | bytes 131104 | tf_op jit(solution)/shard_map/while/body/eval_jaxpr/ppermute | solution.py:17
  60.7 4.4 %collective-permute-start = (bf16[256,256]{1,0:T(8,128)(2,1)S(1)}, bf16[256,256]{1,0:T(8,128)(2,1)S(1)}, u32[]{:S(2)}, u32[]{:S(2)}) collective-permute-start(bf16[256,256]{1,0:T(8,128)(2,1)S(1)} %get-tuple-element.642), channel_id=1, source_target_pairs={{0,4},{4,8},{8,12},{1,5},{5,9},{9,13},{2,6},{6,10},{10,14},{3,7},{... | collective-permute-start | bytes 393224 | tf_op jit(solution)/shard_map/while/body/eval_jaxpr/ppermute | solution.py:17
  65.7 1.8 %collective-permute-done = bf16[256,256]{1,0:T(8,128)(2,1)S(1)} collective-permute-done((bf16[256,256]{1,0:T(8,128)(2,1)S(1)}, bf16[256,256]{1,0:T(8,128)(2,1)S(1)}, u32[]{:S(2)}, u32[]{:S(2)}) %collective-permute-start) | collective-permute-done | bytes 131104 | tf_op jit(solution)/shard_map/while/body/eval_jaxpr/ppermute | solution.py:17
  67.5 0.3 divide_convert_fusion
  67.9 0.2 reshape.283
  68.1 0.9 broadcast.146
  69.0 4.4 %scatter_fusion.2 = bf16[32,8,1024]{2,1,0:T(8,128)(2,1)} fusion(bf16[32,8,1024]{2,1,0:T(8,128)(2,1)} %broadcast.146, s32[32]{0:T(128)S(1)} %compare_select_fusion.1, bf16[32,8,1024]{2,1,0:T(8,128)(2,1)S(1)} %reshape.283), kind=kCustom, calls=%fused_computation.6 | custom fusion | bytes 1572992 | tf_op jit(solution)/shard_map/scatter | solution.py:29
  73.3 5.8 %all-to-all-start.2 = ((bf16[4,64,1024]{2,1,0:T(8,128)(2,1)}), bf16[4,64,1024]{2,1,0:T(8,128)(2,1)S(1)}, u32[]{:S(2)}, u32[]{:S(2)}) async-start(bf16[4,64,1024]{2,1,0:T(8,128)(2,1)} %bitcast.20), calls=%async_computation.2 | async-start | bytes 1048576 | tf_op jit(solution)/shard_map/all_to_all | solution.py:155
  79.1 10.3 %all-to-all-done.2 = bf16[4,64,1024]{2,1,0:T(8,128)(2,1)S(1)} async-done(((bf16[4,64,1024]{2,1,0:T(8,128)(2,1)}), bf16[4,64,1024]{2,1,0:T(8,128)(2,1)S(1)}, u32[]{:S(2)}, u32[]{:S(2)}) %all-to-all-start.2) | async-done | bytes 524320 | tf_op jit(solution)/shard_map/all_to_all | solution.py:155
  89.4 1.4 %gather_fusion.2 = bf16[32,8,1024]{2,1,0:T(8,128)(2,1)} fusion(bf16[32,8,1024]{2,1,0:T(8,128)(2,1)S(1)} %bitcast.39, s32[1024]{0:T(1024)S(1)} %pad_clamp_fusion), kind=kCustom, calls=%fused_computation.2 | custom fusion | bytes 1048704 | tf_op jit(solution)/shard_map/gather | solution.py:34
  (14 shorter events, 0.1 us)
Async XLA Ops:
  2.0 24.5 %copy-start = (s32[128]{0:T(128)S(1)}, s32[128]{0:T(128)}, u32[]{:S(2)}) copy-start(s32[128]{0:T(128)} %param.15) | copy-start | bytes 1540
  7.1 12.8 %all-to-all-start.1 = ((bf16[4,64,256]{2,1,0:T(8,128)(2,1)}), bf16[4,64,256]{2,1,0:T(8,128)(2,1)S(1)}, u32[]{:S(2)}, u32[]{:S(2)}) async-start(bf16[4,64,256]{2,1,0:T(8,128)(2,1)} %bitcast.16), calls=%async_computation.1 | async-start | bytes 262144 | tf_op jit(solution)/shard_map/all_to_all | solution.py:113
  19.9 19.0 %all-to-all-start = ((bf16[4,64,1024]{2,1,0:T(8,128)(2,1)}), bf16[4,64,1024]{2,1,0:T(8,128)(2,1)S(1)}, u32[]{:S(2)}, u32[]{:S(2)}) async-start(bf16[4,64,1024]{2,1,0:T(8,128)(2,1)} %bitcast.13), calls=%async_computation | async-start | bytes 1048576 | tf_op jit(solution)/shard_map/all_to_all | solution.py:112
  45.1 3.8 %collective-permute-start = (bf16[256,256]{1,0:T(8,128)(2,1)S(1)}, bf16[256,256]{1,0:T(8,128)(2,1)S(1)}, u32[]{:S(2)}, u32[]{:S(2)}) collective-permute-start(bf16[256,256]{1,0:T(8,128)(2,1)S(1)} %get-tuple-element.642), channel_id=1, source_target_pairs={{0,4},{4,8},{8,12},{1,5},{5,9},{9,13},{2,6},{6,10},{10,14},{3,7},{... | collective-permute-start | bytes 393224 | tf_op jit(solution)/shard_map/while/body/eval_jaxpr/ppermute | solution.py:17
  48.9 11.7 %collective-permute-start = (bf16[256,256]{1,0:T(8,128)(2,1)S(1)}, bf16[256,256]{1,0:T(8,128)(2,1)S(1)}, u32[]{:S(2)}, u32[]{:S(2)}) collective-permute-start(bf16[256,256]{1,0:T(8,128)(2,1)S(1)} %get-tuple-element.642), channel_id=1, source_target_pairs={{0,4},{4,8},{8,12},{1,5},{5,9},{9,13},{2,6},{6,10},{10,14},{3,7},{... | collective-permute-start | bytes 393224 | tf_op jit(solution)/shard_map/while/body/eval_jaxpr/ppermute | solution.py:17
  60.7 6.9 %collective-permute-start = (bf16[256,256]{1,0:T(8,128)(2,1)S(1)}, bf16[256,256]{1,0:T(8,128)(2,1)S(1)}, u32[]{:S(2)}, u32[]{:S(2)}) collective-permute-start(bf16[256,256]{1,0:T(8,128)(2,1)S(1)} %get-tuple-element.642), channel_id=1, source_target_pairs={{0,4},{4,8},{8,12},{1,5},{5,9},{9,13},{2,6},{6,10},{10,14},{3,7},{... | collective-permute-start | bytes 393224 | tf_op jit(solution)/shard_map/while/body/eval_jaxpr/ppermute | solution.py:17
  73.3 16.1 %all-to-all-start.2 = ((bf16[4,64,1024]{2,1,0:T(8,128)(2,1)}), bf16[4,64,1024]{2,1,0:T(8,128)(2,1)S(1)}, u32[]{:S(2)}, u32[]{:S(2)}) async-start(bf16[4,64,1024]{2,1,0:T(8,128)(2,1)} %bitcast.20), calls=%async_computation.2 | async-start | bytes 1048576 | tf_op jit(solution)/shard_map/all_to_all | solution.py:155
where the time goes:
time: 91.7 us; the launch traced here: 90.8 us
  starting transfers between devices  32.1 us (35%)
  waiting for transfers between devices  27.2 us (30%)
  local copies, waits for them, and re-layouts  19.5 us (21%)
  other arithmetic  6.71 us (7%)
  loops' own time  2.32 us (3%)
  matrix products  2.23 us (2%)
    ppermute x3, starting transfers between devices, passed_along(): return lax.ppermute(value, axis, pairs)  14.9 us
    scatter x3, local copies, waits for them, and re-layouts, pack_blocks(): return empty.at[index].set(blocks).reshape(slots * block_rows, width)  12.7 us
    all_to_all x1, waiting for transfers between devices, body(): lax.all_to_all(sent_queries, 'seq', split_axis=0, concat_axis=0, tiled=True)  11.5 us
    all_to_all x1, waiting for transfers between devices, body(): lax.all_to_all(sent_back, 'seq', split_axis=0, concat_axis=0, tiled=True)  10.3 us
    all_to_all x1, starting transfers between devices, body(): lax.all_to_all(sent_pairs, 'seq', split_axis=0, concat_axis=0, tiled=True)  6.31 us
    all_to_all x1, starting transfers between devices, body(): lax.all_to_all(sent_back, 'seq', split_axis=0, concat_axis=0, tiled=True)  5.79 us
    ppermute x3, waiting for transfers between devices, passed_along(): return lax.ppermute(value, axis, pairs)  5.33 us
    all_to_all x1, starting transfers between devices, body(): lax.all_to_all(sent_queries, 'seq', split_axis=0, concat_axis=0, tiled=True)  5.09 us
  transfers between devices with their start and end apart: 6, of which 5 were waited for; matrix products, arithmetic and copies ran while one was open for 9% of the time, Pallas kernels for 0%

commit v1 on v0

v1 whole, which is shorter than its diff:
```python
import jax
import jax.numpy as jnp
from jax import lax
from jax.experimental import pallas as pl
from jax.experimental.pallas import tpu as pltpu
from jax.sharding import PartitionSpec as P

HEAD_WIDTH = 128
LOG2_E = 1.4426950408889634
NEG_FILL = -1e30


def block_places(lengths, old_place, own_index, row_count, key_count):
    block_total = old_place.shape[0]
    block_rows = key_count // block_total
    ids = jnp.arange(block_total, dtype=jnp.int32)
    hit = old_place[:, None] == ids[None, :]
    new_block = jnp.sum(jnp.where(hit, ids[:, None], 0), axis=0)
    key_pos = (new_block[:, None] * block_rows + jnp.arange(block_rows, dtype=jnp.int32)).reshape(-1)
    query_pos = lax.dynamic_slice_in_dim(key_pos, own_index * row_count, row_count)
    bounds = jnp.cumsum(lengths)
    starts = jnp.max(jnp.where(bounds[None, :] <= query_pos[:, None], bounds[None, :], 0), axis=1)
    return key_pos.reshape(1, -1), query_pos.reshape(-1, 1), starts.reshape(-1, 1)


def weights_kernel(heads, q_ref, k_ref, key_pos_ref, query_pos_ref, start_ref, p_ref):
    rows = q_ref.shape[0]
    key_pos = key_pos_ref[...]
    visible = (key_pos >= start_ref[...]) & (key_pos <= query_pos_ref[...])
    bias = jnp.where(visible, 0.0, NEG_FILL)
    keys = k_ref[...]
    for head in range(heads):
        q = q_ref[:, head * HEAD_WIDTH:(head + 1) * HEAD_WIDTH]
        scores = lax.dot_general(
            q, keys, (((1,), (1,)), ((), ())), preferred_element_type=jnp.float32
        )
        scaled = scores * (HEAD_WIDTH ** -0.5 * LOG2_E) + bias
        peak = jnp.max(scaled, axis=1, keepdims=True)
        p_ref[head] = jnp.exp2(scaled - peak).astype(jnp.bfloat16)


def mix_kernel(heads, p_ref, v_ref, out_ref):
    values = v_ref[...]
    ext = jnp.concatenate([values, jnp.ones_like(values)], axis=1)
    for head in range(heads):
        acc = jnp.dot(p_ref[head], ext, preferred_element_type=jnp.float32)
        out_ref[:, head * HEAD_WIDTH:(head + 1) * HEAD_WIDTH] = (
            acc[:, :HEAD_WIDTH] / acc[:, HEAD_WIDTH:]
        ).astype(jnp.bfloat16)


def tiled_attention(queries, keys, values, key_pos, query_pos, starts, tile):
    rows, cols = queries.shape
    heads = cols // HEAD_WIDTH
    key_count = keys.shape[0]
    weights = pl.pallas_call(
        lambda *refs: weights_kernel(heads, *refs),
        grid=(rows // tile,),
        in_specs=[
            pl.BlockSpec((tile, cols), lambda i: (i, 0)),
            pl.BlockSpec((key_count, HEAD_WIDTH), lambda i: (0, 0)),
            pl.BlockSpec((1, key_count), lambda i: (0, 0)),
            pl.BlockSpec((tile, 1), lambda i: (i, 0)),
            pl.BlockSpec((tile, 1), lambda i: (i, 0)),
        ],
        out_specs=pl.BlockSpec((heads, tile, key_count), lambda i: (0, i, 0)),
        out_shape=jax.ShapeDtypeStruct((heads, rows, key_count), jnp.bfloat16),
        compiler_params=pltpu.CompilerParams(vmem_limit_bytes=32 << 20),
        cost_estimate=pl.CostEstimate(
            flops=2 * heads * rows * key_count * HEAD_WIDTH,
            bytes_accessed=2 * heads * rows * key_count,
            transcendentals=heads * rows * key_count,
        ),
        name="weights",
    )(queries, keys, key_pos, query_pos, starts)
    return pl.pallas_call(
        lambda *refs: mix_kernel(heads, *refs),
        grid=(rows // tile,),
        in_specs=[
            pl.BlockSpec((heads, tile, key_count), lambda i: (0, i, 0)),
            pl.BlockSpec((key_count, HEAD_WIDTH), lambda i: (0, 0)),
        ],
        out_specs=pl.BlockSpec((tile, cols), lambda i: (i, 0)),
        out_shape=jax.ShapeDtypeStruct((rows, cols), jnp.bfloat16),
        compiler_params=pltpu.CompilerParams(vmem_limit_bytes=32 << 20),
        cost_estimate=pl.CostEstimate(
            flops=4 * heads * rows * key_count * HEAD_WIDTH,
            bytes_accessed=2 * heads * rows * key_count,
            transcendentals=0,
        ),
        name="mix",
    )(weights, values)


def online_kernel(heads, q_ref, k_ref, v_ref, key_pos_ref, query_pos_ref, start_ref, out_ref, peak_ref, acc_ref):
    step = pl.program_id(0)

    @pl.when(step == 0)
    def _():
        peak_ref[...] = jnp.full(peak_ref.shape, NEG_FILL, jnp.float32)
        acc_ref[...] = jnp.zeros(acc_ref.shape, jnp.float32)

    key_pos = key_pos_ref[...]
    visible = (key_pos >= start_ref[...]) & (key_pos <= query_pos_ref[...])
    values = v_ref[...]
    ext = jnp.concatenate([values, jnp.ones_like(values)], axis=1)
    for head in range(heads):
        q = q_ref[:, head * HEAD_WIDTH:(head + 1) * HEAD_WIDTH]
        scores = lax.dot_general(
            q, k_ref[...], (((1,), (1,)), ((), ())), preferred_element_type=jnp.float32
        )
        scaled = jnp.where(visible, scores * (HEAD_WIDTH ** -0.5 * LOG2_E), NEG_FILL)
        before = peak_ref[head]
        peak = jnp.maximum(before, jnp.max(scaled, axis=1, keepdims=True))
        weights = jnp.where(visible, jnp.exp2(scaled - peak), 0.0).astype(jnp.bfloat16)
        peak_ref[head] = peak
        acc_ref[head] = acc_ref[head] * jnp.exp2(before - peak) + jnp.dot(
            weights, ext, preferred_element_type=jnp.float32
        )

    @pl.when(step == pl.num_programs(0) - 1)
    def _():
        for head in range(heads):
            acc = acc_ref[head]
            out_ref[:, head * HEAD_WIDTH:(head + 1) * HEAD_WIDTH] = (
                acc[:, :HEAD_WIDTH] / acc[:, HEAD_WIDTH:]
            ).astype(jnp.bfloat16)


def online_attention(queries, keys, values, key_pos, query_pos, starts, chunk):
    rows, cols = queries.shape
    heads = cols // HEAD_WIDTH
    key_count = keys.shape[0]
    return pl.pallas_call(
        lambda *refs: online_kernel(heads, *refs),
        grid=(key_count // chunk,),
        in_specs=[
            pl.BlockSpec((rows, cols), lambda j: (0, 0)),
            pl.BlockSpec((chunk, HEAD_WIDTH), lambda j: (j, 0)),
            pl.BlockSpec((chunk, HEAD_WIDTH), lambda j: (j, 0)),
            pl.BlockSpec((1, chunk), lambda j: (0, j)),
            pl.BlockSpec((rows, 1), lambda j: (0, 0)),
            pl.BlockSpec((rows, 1), lambda j: (0, 0)),
        ],
        out_specs=pl.BlockSpec((rows, cols), lambda j: (0, 0)),
        out_shape=jax.ShapeDtypeStruct((rows, cols), jnp.bfloat16),
        scratch_shapes=[
            pltpu.VMEM((heads, rows, 1), jnp.float32),
            pltpu.VMEM((heads, rows, 2 * HEAD_WIDTH), jnp.float32),
        ],
        compiler_params=pltpu.CompilerParams(vmem_limit_bytes=32 << 20),
        name="online",
    )(queries, keys, values, key_pos, query_pos, starts)


def body(queries, keys, values, lengths, old_place):
    own_index = lax.axis_index("seq")
    row_count = queries.shape[0]
    key_count = row_count * lax.axis_size("seq")
    all_keys = lax.all_gather(keys, "seq", axis=0, tiled=True)
    all_values = lax.all_gather(values, "seq", axis=0, tiled=True)
    key_pos, query_pos, starts = block_places(lengths, old_place, own_index, row_count, key_count)
    if key_count <= 1024:
        return tiled_attention(queries, all_keys, all_values, key_pos, query_pos, starts, 64)
    return online_attention(queries, all_keys, all_values, key_pos, query_pos, starts, 512)


def solution(mesh):
    in_specs = (
        P(("groups", "seq"), "mp"),
        P(("groups", "seq"), "mp"),
        P(("groups", "seq"), "mp"),
        P("groups"),
        P("groups"),
    )
    out_specs = P(("groups", "seq"), "mp")
    return jax.shard_map(body, mesh=mesh, in_specs=in_specs, out_specs=out_specs, check_vma=False)
```

time: 91.7 us -> 42.4 us (0.46)
  starting transfers between devices: 32.1 us -> 0 us
  blocking collectives: 0 us -> 30.3 us
  waiting for transfers between devices: 27.2 us -> 0 us
  local copies, waits for them, and re-layouts: 19.5 us -> 1.59 us
  Pallas kernels: 0 us -> 8.53 us
  other arithmetic: 6.71 us -> 1.78 us
  loops' own time: 2.32 us -> 0 us
  matrix products: 2.23 us -> 0 us
    all_gather x0 -> x2, blocking collectives: none -> 30.3 us  [the longest x1 15.8 us: body(): all_keys = lax.all_gather(keys, 'seq', axis=0, tiled=True)]
    all_to_all x3 -> x0, waiting for transfers between devices: 21.8 us -> none  [the longest x1 11.5 us: body(): lax.all_to_all(sent_queries, 'seq', split_axis=0, concat_axis=0, tiled=True)]
    all_to_all x3 -> x0, starting transfers between devices: 17.2 us -> none  [the longest x1 6.31 us: body(): lax.all_to_all(sent_pairs, 'seq', split_axis=0, concat_axis=0, tiled=True)]
    ppermute x3 -> x0, starting transfers between devices: 14.9 us -> none  [passed_along(): return lax.ppermute(value, axis, pairs)]
    scatter x4 -> x0, local copies, waits for them, and re-layouts: 13.7 us -> none  [the longest x3 12.7 us: pack_blocks(): return empty.at[index].set(blocks).reshape(slots * block_rows, width)]
    pallas_call x0 -> x2, Pallas kernels: none -> 8.53 us  [the longest x1 4.36 us: tiled_attention(): pl.pallas_call(lambda *refs: mix_kernel(heads, *refs), grid=(rows // tile...]
    ppermute x3 -> x0, waiting for transfers between devices: 5.33 us -> none  [passed_along(): return lax.ppermute(value, axis, pairs)]
    gather x3 -> x0, local copies, waits for them, and re-layouts: 2.52 us -> none  [unpack_blocks(): return matrix.reshape(-1, block_rows, width)[index].reshape(-1, width)]
  transfers between devices with their start and end apart: 6 -> 0, of which waited for: 5 -> 0; matrix products, arithmetic and copies ran while one was open for 9% -> 0% of each run, Pallas kernels for 0% -> 0%
where the time goes in v1:
time: 42.4 us; the launch traced here: 42.2 us
  blocking collectives  30.3 us (71%)
  Pallas kernels  8.53 us (20%)
  other arithmetic  1.78 us (4%)
  local copies, waits for them, and re-layouts  1.59 us (4%)
    all_gather x1, blocking collectives, body(): all_keys = lax.all_gather(keys, 'seq', axis=0, tiled=True)  15.8 us
    all_gather x1, blocking collectives, body(): all_values = lax.all_gather(values, 'seq', axis=0, tiled=True)  14.4 us
    pallas_call x1, Pallas kernels, tiled_attention(): pl.pallas_call(lambda *refs: mix_kernel(heads, *refs), grid=(rows // tile...  4.36 us
    pallas_call x1, Pallas kernels, tiled_attention(): pl.pallas_call(lambda *refs: weights_kernel(heads, *refs), grid=(rows //...  4.17 us
    unnamed x4, local copies, waits for them, and re-layouts  1.05 us

profile of v1, /device:TPU:0, one launch (start us, length us, event | category | flops | bytes accessed | tf_op | source)
XLA Modules:
  0.0 42.2 jit_solution(7343515204599492310)
XLA Ops:
  0.0 0.0 copy-start.1
  0.0 0.8 %select_reduce_fusion = s32[128]{0:T(128)S(1)} fusion(s32[128]{0:T(128)} %param.9), kind=kLoop, calls=%fused_computation.1 | loop fusion | flops 49024 | bytes 1024 | tf_op jit(solution)/shard_map/reduce_sum | solution.py:18
  0.8 0.1 iota_add_fusion
  0.9 0.1 add.34
  1.0 0.1 dynamic_slice.3
  1.1 0.8 %reduce-window.8 = s32[3,1]{0,1:T(1,128)S(1)} reduce-window(s32[3,1]{0,1:T(1,128)} %bitcast.7, s32[]{:T(128)} %constant.4.clone.1), window={size=3x1 pad=2_0x0_0}, to_apply=%region_1.2 | reduce-window | flops 6 | bytes 28 | tf_op jit(solution)/shard_map/reduce-window.3
  1.9 0.1 select_reduce_fusion.1
  2.0 0.1 copy.9.refs_4_
  2.1 0.1 copy.8.refs_3_
  2.3 0.1 add.33.refs_2_
  2.4 15.8 %all_gather.6.refs_1_ = bf16[1024,128]{1,0:T(8,128)(2,1)S(1)} all-gather(bf16[256,128]{1,0:T(8,128)(2,1)} %param.6), channel_id=1, replica_groups=mesh['groups'=2,'seq'=4,'mp'=4] {'seq'}, dimensions={0}, use_global_device_ids=true | all-gather | bytes 327680 | tf_op jit(solution)/shard_map/all_gather | solution.py:160
  18.2 0.0 copy-start
  18.2 1.0 %copy-done = bf16[256,1024]{1,0:T(8,128)(2,1)S(1)} copy-done((bf16[256,1024]{1,0:T(8,128)(2,1)S(1)}, bf16[256,1024]{1,0:T(8,128)(2,1)}, u32[]{:S(2)}) %copy-start) | copy-done | bytes 524312
  19.2 4.2 %weights.1.refs_0_ = bf16[8,256,1024]{2,1,0:T(8,128)(2,1)S(1)} custom-call(bf16[256,1024]{1,0:T(8,128)(2,1)S(1)} %copy-done, bf16[1024,128]{1,0:T(8,128)(2,1)S(1)} %all_gather.6.refs_1_, s32[1,1024]{1,0:T(1,128)S(1)} %add.33.refs_2_, s32[256,1]{1,0:T(8,128)S(1)} %copy.8.refs_3_, s32[256,1]{1,0:T(8,128)S(1)} %copy.9.refs_4_), custom_call_target="tpu_custom_call" | custom-call | flops 536870912 | bytes 4194304 | tf_op jit(solution)/shard_map/weights/pallas_call | solution.py:56
  23.4 0.0 copy-done.1
  23.4 14.4 %all_gather.7.refs_1_ = bf16[1024,128]{1,0:T(8,128)(2,1)S(1)} all-gather(bf16[256,128]{1,0:T(8,128)(2,1)S(1)} %copy-done.1), channel_id=1, replica_groups=mesh['groups'=2,'seq'=4,'mp'=4] {'seq'}, dimensions={0}, use_global_device_ids=true | all-gather | bytes 327680 | tf_op jit(solution)/shard_map/all_gather | solution.py:161
  37.9 4.4 %mix.1 = bf16[256,1024]{1,0:T(8,128)(2,1)} custom-call(bf16[8,256,1024]{2,1,0:T(8,128)(2,1)S(1)} %weights.1.refs_0_, bf16[1024,128]{1,0:T(8,128)(2,1)S(1)} %all_gather.7.refs_1_), custom_call_target="tpu_custom_call" | custom-call | flops 1073741824 | bytes 4194304 | tf_op jit(solution)/shard_map/mix/pallas_call | solution.py:76
  (1 shorter events, 0.0 us)
Async XLA Ops:
  0.0 23.4 %copy-start.1 = (bf16[256,128]{1,0:T(8,128)(2,1)S(1)}, bf16[256,128]{1,0:T(8,128)(2,1)}, u32[]{:S(2)}) copy-start(bf16[256,128]{1,0:T(8,128)(2,1)} %param.7) | copy-start | bytes 196612
  18.2 1.0 %copy-start = (bf16[256,1024]{1,0:T(8,128)(2,1)S(1)}, bf16[256,1024]{1,0:T(8,128)(2,1)}, u32[]{:S(2)}) copy-start(bf16[256,1024]{1,0:T(8,128)(2,1)} %refs_0_.1) | copy-start | bytes 1572868

commit v2 on v1

--- a/solution.py
+++ b/solution.py
@@ -23,12 +23,12 @@
     return key_pos.reshape(1, -1), query_pos.reshape(-1, 1), starts.reshape(-1, 1)
 
 
-def weights_kernel(heads, q_ref, k_ref, key_pos_ref, query_pos_ref, start_ref, p_ref):
-    rows = q_ref.shape[0]
+def weights_kernel(heads, q_ref, key_pos_ref, query_pos_ref, start_ref, *refs):
+    k_refs, p_ref = refs[:-1], refs[-1]
     key_pos = key_pos_ref[...]
     visible = (key_pos >= start_ref[...]) & (key_pos <= query_pos_ref[...])
     bias = jnp.where(visible, 0.0, NEG_FILL)
-    keys = k_ref[...]
+    keys = jnp.concatenate([k_ref[...] for k_ref in k_refs], axis=0)
     for head in range(heads):
         q = q_ref[:, head * HEAD_WIDTH:(head + 1) * HEAD_WIDTH]
         scores = lax.dot_general(
@@ -39,8 +39,9 @@
         p_ref[head] = jnp.exp2(scaled - peak).astype(jnp.bfloat16)
 
 
-def mix_kernel(heads, p_ref, v_ref, out_ref):
-    values = v_ref[...]
+def mix_kernel(heads, p_ref, *refs):
+    v_refs, out_ref = refs[:-1], refs[-1]
+    values = jnp.concatenate([v_ref[...] for v_ref in v_refs], axis=0)
     ext = jnp.concatenate([values, jnp.ones_like(values)], axis=1)
     for head in range(heads):
         acc = jnp.dot(p_ref[head], ext, preferred_element_type=jnp.float32)
@@ -52,17 +53,16 @@
 def tiled_attention(queries, keys, values, key_pos, query_pos, starts, tile):
     rows, cols = queries.shape
     heads = cols // HEAD_WIDTH
-    key_count = keys.shape[0]
+    key_count = sum(shard.shape[0] for shard in keys)
     weights = pl.pallas_call(
         lambda *refs: weights_kernel(heads, *refs),
         grid=(rows // tile,),
         in_specs=[
             pl.BlockSpec((tile, cols), lambda i: (i, 0)),
-            pl.BlockSpec((key_count, HEAD_WIDTH), lambda i: (0, 0)),
             pl.BlockSpec((1, key_count), lambda i: (0, 0)),
             pl.BlockSpec((tile, 1), lambda i: (i, 0)),
             pl.BlockSpec((tile, 1), lambda i: (i, 0)),
-        ],
+        ] + [pl.BlockSpec(shard.shape, lambda i: (0, 0)) for shard in keys],
         out_specs=pl.BlockSpec((heads, tile, key_count), lambda i: (0, i, 0)),
         out_shape=jax.ShapeDtypeStruct((heads, rows, key_count), jnp.bfloat16),
         compiler_params=pltpu.CompilerParams(vmem_limit_bytes=32 << 20),
@@ -72,14 +72,13 @@
             transcendentals=heads * rows * key_count,
         ),
         name="weights",
-    )(queries, keys, key_pos, query_pos, starts)
+    )(queries, key_pos, query_pos, starts, *keys)
     return pl.pallas_call(
         lambda *refs: mix_kernel(heads, *refs),
         grid=(rows // tile,),
         in_specs=[
             pl.BlockSpec((heads, tile, key_count), lambda i: (0, i, 0)),
-            pl.BlockSpec((key_count, HEAD_WIDTH), lambda i: (0, 0)),
-        ],
+        ] + [pl.BlockSpec(shard.shape, lambda i: (0, 0)) for shard in values],
         out_specs=pl.BlockSpec((tile, cols), lambda i: (i, 0)),
         out_shape=jax.ShapeDtypeStruct((rows, cols), jnp.bfloat16),
         compiler_params=pltpu.CompilerParams(vmem_limit_bytes=32 << 20),
@@ -89,7 +88,7 @@
             transcendentals=0,
         ),
         name="mix",
-    )(weights, values)
+    )(weights, *values)
 
 
 def online_kernel(heads, q_ref, k_ref, v_ref, key_pos_ref, query_pos_ref, start_ref, out_ref, peak_ref, acc_ref):
@@ -153,15 +152,28 @@
     )(queries, keys, values, key_pos, query_pos, starts)
 
 
+def from_others(matrix):
+    devices = lax.axis_size("seq")
+    return [
+        lax.ppermute(matrix, "seq", [(i, (i + by) % devices) for i in range(devices)])
+        for by in range(1, devices)
+    ]
+
+
 def body(queries, keys, values, lengths, old_place):
     own_index = lax.axis_index("seq")
     row_count = queries.shape[0]
-    key_count = row_count * lax.axis_size("seq")
+    devices = lax.axis_size("seq")
+    key_count = row_count * devices
+    key_pos, query_pos, starts = block_places(lengths, old_place, own_index, row_count, key_count)
+    if key_count <= 1024:
+        all_keys = [keys] + from_others(keys)
+        all_values = [values] + from_others(values)
+        by_device = key_pos.reshape(devices, row_count)
+        key_pos = jnp.concatenate([by_device[(own_index - by) % devices] for by in range(devices)]).reshape(1, -1)
+        return tiled_attention(queries, all_keys, all_values, key_pos, query_pos, starts, 64)
     all_keys = lax.all_gather(keys, "seq", axis=0, tiled=True)
     all_values = lax.all_gather(values, "seq", axis=0, tiled=True)
-    key_pos, query_pos, starts = block_places(lengths, old_place, own_index, row_count, key_count)
-    if key_count <= 1024:
-        return tiled_attention(queries, all_keys, all_values, key_pos, query_pos, starts, 64)
     return online_attention(queries, all_keys, all_values, key_pos, query_pos, starts, 512)
 
 

time: 42.4 us -> 25.1 us (0.59)
  blocking collectives: 30.3 us -> 0 us
  starting transfers between devices: 0 us -> 11.7 us
  local copies, waits for them, and re-layouts: 1.59 us -> 2.69 us
    all_gather x2 -> x0, blocking collectives: 30.3 us -> none  [the longest x1 15.8 us: body(): all_keys = lax.all_gather(keys, 'seq', axis=0, tiled=True)]
    ppermute x0 -> x6, starting transfers between devices: none -> 11.7 us  [from_others(): lax.ppermute(matrix, 'seq', [(i, (i + by) % devices) for i in range(devic...]
    unnamed x4 -> x6, local copies, waits for them, and re-layouts: 1.05 us -> 1.88 us
  transfers between devices with their start and end apart: 0 -> 6, of which waited for: 0 -> 0; matrix products, arithmetic and copies ran while one was open for 0% -> 10% of each run, Pallas kernels for 0% -> 17%
where the time goes in v2:
time: 25.1 us; the launch traced here: 24.9 us
  starting transfers between devices  11.7 us (47%)
  Pallas kernels  8.57 us (34%)
  local copies, waits for them, and re-layouts  2.69 us (11%)
  other arithmetic  1.77 us (7%)
    ppermute x6, starting transfers between devices, from_others(): lax.ppermute(matrix, 'seq', [(i, (i + by) % devices) for i in range(devic...  11.7 us
    pallas_call x1, Pallas kernels, tiled_attention(): pl.pallas_call(lambda *refs: mix_kernel(heads, *refs), grid=(rows // tile...  4.37 us
    pallas_call x1, Pallas kernels, tiled_attention(): pl.pallas_call(lambda *refs: weights_kernel(heads, *refs), grid=(rows //...  4.19 us
    unnamed x6, local copies, waits for them, and re-layouts  1.88 us
    another operation x1, other arithmetic  0.83 us
    reduce_sum x1, other arithmetic, block_places(): new_block = jnp.sum(jnp.where(hit, ids[:, None], 0), axis=0)  0.75 us
  transfers between devices with their start and end apart: 6, of which 0 were waited for; matrix products, arithmetic and copies ran while one was open for 10% of the time, Pallas kernels for 17%

profile of v2, /device:TPU:0, one launch (start us, length us, event | category | flops | bytes accessed | tf_op | source)
XLA Modules:
  0.0 24.9 jit_solution(11914355918595015041)
XLA Ops:
  0.0 0.0 copy-start.2
  0.0 4.0 %collective-permute-start.1 = (bf16[256,128]{1,0:T(8,128)(2,1)}, bf16[256,128]{1,0:T(8,128)(2,1)S(1)}, u32[]{:S(2)}, u32[]{:S(2)}) collective-permute-start(bf16[256,128]{1,0:T(8,128)(2,1)} %refs_4_.1), channel_id=1, source_target_pairs={{0,8},{4,12},{8,0},{12,4},{1,9},{5,13},{9,1},{13,5},{2,10},{6,14},... | collective-permute-start | bytes 196616 | tf_op jit(solution)/shard_map/ppermute | solution.py:158
  4.0 1.6 %collective-permute-start = (bf16[256,128]{1,0:T(8,128)(2,1)}, bf16[256,128]{1,0:T(8,128)(2,1)S(1)}, u32[]{:S(2)}, u32[]{:S(2)}) collective-permute-start(bf16[256,128]{1,0:T(8,128)(2,1)} %refs_4_.1), channel_id=1, source_target_pairs={{0,4},{4,8},{8,12},{12,0},{1,5},{5,9},{9,13},{13,1},{2,6},{6,10},{... | collective-permute-start | bytes 196616 | tf_op jit(solution)/shard_map/ppermute | solution.py:158
  5.6 2.2 %collective-permute-start.2 = (bf16[256,128]{1,0:T(8,128)(2,1)}, bf16[256,128]{1,0:T(8,128)(2,1)S(1)}, u32[]{:S(2)}, u32[]{:S(2)}) collective-permute-start(bf16[256,128]{1,0:T(8,128)(2,1)} %refs_4_.1), channel_id=1, source_target_pairs={{0,12},{4,0},{8,4},{12,8},{1,13},{5,1},{9,5},{13,9},{2,14},{6,2},{... | collective-permute-start | bytes 196616 | tf_op jit(solution)/shard_map/ppermute | solution.py:158
  7.9 0.0 collective-permute-start.4
  7.9 0.6 %collective-permute-start.3 = (bf16[256,128]{1,0:T(8,128)(2,1)}, bf16[256,128]{1,0:T(8,128)(2,1)S(1)}, u32[]{:S(2)}, u32[]{:S(2)}) collective-permute-start(bf16[256,128]{1,0:T(8,128)(2,1)} %refs_1_.1), channel_id=1, source_target_pairs={{0,4},{4,8},{8,12},{12,0},{1,5},{5,9},{9,13},{13,1},{2,6},{6,10},{... | collective-permute-start | bytes 196616 | tf_op jit(solution)/shard_map/ppermute | solution.py:158
  8.4 0.8 %select_reduce_fusion = s32[128]{0:T(128)S(1)} fusion(s32[128]{0:T(128)} %param.9), kind=kLoop, calls=%fused_computation.1 | loop fusion | flops 49024 | bytes 1024 | tf_op jit(solution)/shard_map/reduce_sum | solution.py:18
  9.2 0.1 mul.20
  9.3 0.1 iota_add_fusion
  9.4 0.8 %reduce-window.8 = s32[3,1]{0,1:T(1,128)S(1)} reduce-window(s32[3,1]{0,1:T(1,128)} %bitcast.17, s32[]{:T(128)} %constant.39.clone.1), window={size=3x1 pad=2_0x0_0}, to_apply=%region_1.2 | reduce-window | flops 6 | bytes 28 | tf_op jit(solution)/shard_map/reduce-window.3
  10.2 0.1 add.64
  10.3 0.1 add.61
  10.4 0.1 add.62
  10.5 0.1 add.78
  10.6 0.1 dynamic_slice.19
  10.7 0.1 select_reduce_fusion.1
  10.8 0.0 collective-permute-done.1.refs_6_
  10.8 3.3 %collective-permute-start.5 = (bf16[256,128]{1,0:T(8,128)(2,1)}, bf16[256,128]{1,0:T(8,128)(2,1)S(1)}, u32[]{:S(2)}, u32[]{:S(2)}) collective-permute-start(bf16[256,128]{1,0:T(8,128)(2,1)} %refs_1_.1), channel_id=1, source_target_pairs={{0,12},{4,0},{8,4},{12,8},{1,13},{5,1},{9,5},{13,9},{2,14},{6,2},{... | collective-permute-start | bytes 196616 | tf_op jit(solution)/shard_map/ppermute | solution.py:158
  14.1 0.1 copy.9.refs_3_
  14.3 0.1 copy.8.refs_2_
  14.4 0.0 collective-permute-done.refs_5_
  14.4 0.0 collective-permute-done.2.refs_7_
  14.4 0.0 copy-start
  14.4 1.0 %copy-done = bf16[256,1024]{1,0:T(8,128)(2,1)S(1)} copy-done((bf16[256,1024]{1,0:T(8,128)(2,1)S(1)}, bf16[256,1024]{1,0:T(8,128)(2,1)}, u32[]{:S(2)}) %copy-start) | copy-done | bytes 524312
  15.5 0.0 copy-start.1
  15.5 0.8 %copy-done.1 = bf16[256,128]{1,0:T(8,128)(2,1)S(1)} copy-done((bf16[256,128]{1,0:T(8,128)(2,1)S(1)}, bf16[256,128]{1,0:T(8,128)(2,1)}, u32[]{:S(2)}) %copy-start.1) | copy-done | bytes 65560
  16.3 4.2 %weights.1.refs_0_ = bf16[8,256,1024]{2,1,0:T(8,128)(2,1)S(1)} custom-call(bf16[256,1024]{1,0:T(8,128)(2,1)S(1)} %copy-done, s32[1,1024]{1,0:T(1,128)S(1)} %bitcast.9, s32[256,1]{1,0:T(8,128)S(1)} %copy.8.refs_2_, s32[256,1]{1,0:T(8,128)S(1)} %copy.9.refs_3_, bf16[256,128]{1,0:T(8,128)(2,1)S(1)} %copy-done.1, ...), custom_call_target="tpu_custom_call" | custom-call | flops 536870912 | bytes 4194304 | tf_op jit(solution)/shard_map/weights/pallas_call | solution.py:57
  20.5 0.0 collective-permute-done.4.refs_3_
  20.5 0.0 collective-permute-done.3.refs_2_
  20.5 0.0 collective-permute-done.5.refs_4_
  20.5 0.0 copy-done.2
  20.6 4.4 %mix.1 = bf16[256,1024]{1,0:T(8,128)(2,1)} custom-call(bf16[8,256,1024]{2,1,0:T(8,128)(2,1)S(1)} %weights.1.refs_0_, bf16[256,128]{1,0:T(8,128)(2,1)S(1)} %copy-done.2, bf16[256,128]{1,0:T(8,128)(2,1)S(1)} %collective-permute-done.3.refs_2_, bf16[256,128]{1,0:T(8,128)(2,1)S(1)} %collective-permute-done.4.refs_3_, ...), custom_call_target="tpu_custom_call" | custom-call | flops 1073741824 | bytes 4194304 | tf_op jit(solution)/shard_map/mix/pallas_call | solution.py:76
  (5 shorter events, 0.0 us)
Async XLA Ops:
  0.0 20.5 %copy-start.2 = (bf16[256,128]{1,0:T(8,128)(2,1)S(1)}, bf16[256,128]{1,0:T(8,128)(2,1)}, u32[]{:S(2)}) copy-start(bf16[256,128]{1,0:T(8,128)(2,1)} %refs_1_.1) | copy-start | bytes 196612
  0.0 10.8 %collective-permute-start.1 = (bf16[256,128]{1,0:T(8,128)(2,1)}, bf16[256,128]{1,0:T(8,128)(2,1)S(1)}, u32[]{:S(2)}, u32[]{:S(2)}) collective-permute-start(bf16[256,128]{1,0:T(8,128)(2,1)} %refs_4_.1), channel_id=1, source_target_pairs={{0,8},{4,12},{8,0},{12,4},{1,9},{5,13},{9,1},{13,5},{2,10},{6,14},... | collective-permute-start | bytes 196616 | tf_op jit(solution)/shard_map/ppermute | solution.py:158
  4.0 10.4 %collective-permute-start = (bf16[256,128]{1,0:T(8,128)(2,1)}, bf16[256,128]{1,0:T(8,128)(2,1)S(1)}, u32[]{:S(2)}, u32[]{:S(2)}) collective-permute-start(bf16[256,128]{1,0:T(8,128)(2,1)} %refs_4_.1), channel_id=1, source_target_pairs={{0,4},{4,8},{8,12},{12,0},{1,5},{5,9},{9,13},{13,1},{2,6},{6,10},{... | collective-permute-start | bytes 196616 | tf_op jit(solution)/shard_map/ppermute | solution.py:158
  5.6 8.8 %collective-permute-start.2 = (bf16[256,128]{1,0:T(8,128)(2,1)}, bf16[256,128]{1,0:T(8,128)(2,1)S(1)}, u32[]{:S(2)}, u32[]{:S(2)}) collective-permute-start(bf16[256,128]{1,0:T(8,128)(2,1)} %refs_4_.1), channel_id=1, source_target_pairs={{0,12},{4,0},{8,4},{12,8},{1,13},{5,1},{9,5},{13,9},{2,14},{6,2},{... | collective-permute-start | bytes 196616 | tf_op jit(solution)/shard_map/ppermute | solution.py:158
  7.9 12.7 %collective-permute-start.4 = (bf16[256,128]{1,0:T(8,128)(2,1)}, bf16[256,128]{1,0:T(8,128)(2,1)S(1)}, u32[]{:S(2)}, u32[]{:S(2)}) collective-permute-start(bf16[256,128]{1,0:T(8,128)(2,1)} %refs_1_.1), channel_id=1, source_target_pairs={{0,8},{4,12},{8,0},{12,4},{1,9},{5,13},{9,1},{13,5},{2,10},{6,14},... | collective-permute-start | bytes 196616 | tf_op jit(solution)/shard_map/ppermute | solution.py:158
  7.9 12.7 %collective-permute-start.3 = (bf16[256,128]{1,0:T(8,128)(2,1)}, bf16[256,128]{1,0:T(8,128)(2,1)S(1)}, u32[]{:S(2)}, u32[]{:S(2)}) collective-permute-start(bf16[256,128]{1,0:T(8,128)(2,1)} %refs_1_.1), channel_id=1, source_target_pairs={{0,4},{4,8},{8,12},{12,0},{1,5},{5,9},{9,13},{13,1},{2,6},{6,10},{... | collective-permute-start | bytes 196616 | tf_op jit(solution)/shard_map/ppermute | solution.py:158
  10.8 9.7 %collective-permute-start.5 = (bf16[256,128]{1,0:T(8,128)(2,1)}, bf16[256,128]{1,0:T(8,128)(2,1)S(1)}, u32[]{:S(2)}, u32[]{:S(2)}) collective-permute-start(bf16[256,128]{1,0:T(8,128)(2,1)} %refs_1_.1), channel_id=1, source_target_pairs={{0,12},{4,0},{8,4},{12,8},{1,13},{5,1},{9,5},{13,9},{2,14},{6,2},{... | collective-permute-start | bytes 196616 | tf_op jit(solution)/shard_map/ppermute | solution.py:158
  14.4 1.0 %copy-start = (bf16[256,1024]{1,0:T(8,128)(2,1)S(1)}, bf16[256,1024]{1,0:T(8,128)(2,1)}, u32[]{:S(2)}) copy-start(bf16[256,1024]{1,0:T(8,128)(2,1)} %refs_0_.1) | copy-start | bytes 1572868
  15.5 0.8 %copy-start.1 = (bf16[256,128]{1,0:T(8,128)(2,1)S(1)}, bf16[256,128]{1,0:T(8,128)(2,1)}, u32[]{:S(2)}) copy-start(bf16[256,128]{1,0:T(8,128)(2,1)} %refs_4_.1) | copy-start | bytes 196612

commit v3 on v1

--- a/solution.py
+++ b/solution.py
@@ -23,73 +23,158 @@
     return key_pos.reshape(1, -1), query_pos.reshape(-1, 1), starts.reshape(-1, 1)
 
 
-def weights_kernel(heads, q_ref, k_ref, key_pos_ref, query_pos_ref, start_ref, p_ref):
-    rows = q_ref.shape[0]
-    key_pos = key_pos_ref[...]
-    visible = (key_pos >= start_ref[...]) & (key_pos <= query_pos_ref[...])
-    bias = jnp.where(visible, 0.0, NEG_FILL)
-    keys = k_ref[...]
-    for head in range(heads):
-        q = q_ref[:, head * HEAD_WIDTH:(head + 1) * HEAD_WIDTH]
-        scores = lax.dot_general(
-            q, keys, (((1,), (1,)), ((), ())), preferred_element_type=jnp.float32
-        )
-        scaled = scores * (HEAD_WIDTH ** -0.5 * LOG2_E) + bias
-        peak = jnp.max(scaled, axis=1, keepdims=True)
-        p_ref[head] = jnp.exp2(scaled - peak).astype(jnp.bfloat16)
-
-
-def mix_kernel(heads, p_ref, v_ref, out_ref):
-    values = v_ref[...]
-    ext = jnp.concatenate([values, jnp.ones_like(values)], axis=1)
-    for head in range(heads):
-        acc = jnp.dot(p_ref[head], ext, preferred_element_type=jnp.float32)
-        out_ref[:, head * HEAD_WIDTH:(head + 1) * HEAD_WIDTH] = (
-            acc[:, :HEAD_WIDTH] / acc[:, HEAD_WIDTH:]
-        ).astype(jnp.bfloat16)
-
-
-def tiled_attention(queries, keys, values, key_pos, query_pos, starts, tile):
+def iota(shape, dim):
+    return lax.broadcasted_iota(jnp.int32, shape, dim)
+
+
+def visible_bias(own, owners, lengths_ref, places_ref, first_row, rows, shard_rows):
+    block_total = places_ref.shape[1]
+    block_rows = shard_rows * lax.axis_size("seq") // block_total
+    blocks = shard_rows // block_rows
+    places = places_ref[...]
+    row = iota((rows, block_total), 0) + first_row
+    hit = places == own * blocks + row // block_rows
+    at = jnp.where(hit, iota((rows, block_total), 1) * block_rows, 0).astype(jnp.float32)
+    query_pos = jnp.sum(at, axis=1, keepdims=True) + (
+        (iota((rows, 1), 0) + first_row) % block_rows
+    ).astype(jnp.float32)
+    starts = jnp.zeros_like(query_pos)
+    bound = jnp.int32(0)
+    for t in range(lengths_ref.shape[0]):
+        bound = bound + lengths_ref[t]
+        edge = bound.astype(jnp.float32)
+        starts = jnp.where(edge <= query_pos, edge, starts)
+    square = (block_total, block_total)
+    as_column = jnp.sum(
+        jnp.where(iota(square, 0) == iota(square, 1), places, 0).astype(jnp.float32),
+        axis=1, keepdims=True,
+    ).astype(jnp.int32)
+    parts = []
+    for owner in owners:
+        shape = (block_total, shard_rows)
+        hit = as_column == owner * blocks + iota(shape, 1) // block_rows
+        at = jnp.where(hit, iota(shape, 0) * block_rows, 0).astype(jnp.float32)
+        parts.append(
+            jnp.sum(at, axis=0, keepdims=True)
+            + (iota((1, shard_rows), 1) % block_rows).astype(jnp.float32)
+        )
+    key_pos = jnp.concatenate(parts, axis=1)
+    visible = (key_pos >= starts) & (key_pos <= query_pos)
+    return jnp.where(visible, 0.0, NEG_FILL)
+
+
+def scaled_scores(q_ref, rows, heads, keys, bias):
+    q = jnp.concatenate(
+        [q_ref[rows, head * HEAD_WIDTH:(head + 1) * HEAD_WIDTH] for head in range(heads)], axis=0
+    )
+    scores = lax.dot_general(
+        q, keys, (((1,), (1,)), ((), ())), preferred_element_type=jnp.float32
+    )
+    scores = scores.reshape(heads, bias.shape[0], bias.shape[1])
+    return scores * (HEAD_WIDTH ** -0.5 * LOG2_E) + bias[None]
+
+
+def weigh(scaled, peak, values):
+    heads, rows, key_count = scaled.shape
+    weights = jnp.exp2(scaled - peak).astype(jnp.bfloat16).reshape(heads * rows, key_count)
+    with_ones = jnp.concatenate([values, jnp.ones_like(values)], axis=1)
+    summed = jnp.dot(weights, with_ones, preferred_element_type=jnp.float32)
+    return summed.reshape(heads, rows, 2 * HEAD_WIDTH)
+
+
+def first_kernel(tile, masks, own_ref, lengths_ref, places_ref, q_ref, k_ref, v_ref, *refs):
+    pair_refs, (peak_ref, sum_ref, total_ref) = refs[:-3], refs[-3:]
+    heads = q_ref.shape[1] // HEAD_WIDTH
+    own = own_ref[0]
+    owners = [own] + [own ^ mask for mask in masks]
+    keys = jnp.concatenate([k_ref[...]] + [ref[:, :HEAD_WIDTH] for ref in pair_refs], axis=0)
+    values = jnp.concatenate([v_ref[...]] + [ref[:, HEAD_WIDTH:] for ref in pair_refs], axis=0)
+    for first_row in range(0, q_ref.shape[0], tile):
+        rows = slice(first_row, first_row + tile)
+        bias = visible_bias(own, owners, lengths_ref, places_ref, first_row, tile, k_ref.shape[0])
+        scaled = scaled_scores(q_ref, rows, heads, keys, bias)
+        peak = jnp.max(scaled, axis=2, keepdims=True)
+        summed = weigh(scaled, peak, values)
+        peak_ref[:, rows, :] = jnp.broadcast_to(peak, (heads, tile, HEAD_WIDTH))
+        sum_ref[:, rows, :] = summed[:, :, :HEAD_WIDTH]
+        total_ref[:, rows, :] = summed[:, :, HEAD_WIDTH:]
+
+
+def last_kernel(
+    tile, mask, own_ref, lengths_ref, places_ref, q_ref, peak_ref, sum_ref, total_ref, pair_ref,
+    out_ref, block_ref, sems,
+):
+    heads = q_ref.shape[1] // HEAD_WIDTH
+    own = own_ref[0]
+    keys = pair_ref[:, :HEAD_WIDTH]
+    values = pair_ref[:, HEAD_WIDTH:]
+    copies = []
+    for first_row in range(0, q_ref.shape[0], tile):
+        rows = slice(first_row, first_row + tile)
+        bias = visible_bias(own, [own ^ mask], lengths_ref, places_ref, first_row, tile, pair_ref.shape[0])
+        scaled = scaled_scores(q_ref, rows, heads, keys, bias)
+        before = peak_ref[:, rows, :]
+        peak = jnp.maximum(before, jnp.max(scaled, axis=2, keepdims=True))
+        summed = weigh(scaled, peak[:, :, :1], values)
+        rescale = jnp.exp2(before - peak)
+        out = (sum_ref[:, rows, :] * rescale + summed[:, :, :HEAD_WIDTH]) / (
+            total_ref[:, rows, :] * rescale + summed[:, :, HEAD_WIDTH:]
+        )
+        for head in range(heads):
+            block_ref[rows, head * HEAD_WIDTH:(head + 1) * HEAD_WIDTH] = out[head].astype(jnp.bfloat16)
+        copy = pltpu.make_async_copy(
+            block_ref.at[rows, :], out_ref.at[rows, :], sems.at[len(copies)]
+        )
+        copy.start()
+        copies.append(copy)
+    for copy in copies:
+        copy.wait()
+
+
+def estimate(rows, heads, key_count):
+    return pl.CostEstimate(
+        flops=6 * heads * rows * key_count * HEAD_WIDTH,
+        bytes_accessed=8 * heads * rows * HEAD_WIDTH,
+        transcendentals=heads * rows * key_count,
+    )
+
+
+def staged_attention(queries, keys, values, pairs, lengths, old_place, tile):
     rows, cols = queries.shape
     heads = cols // HEAD_WIDTH
-    key_count = keys.shape[0]
-    weights = pl.pallas_call(
-        lambda *refs: weights_kernel(heads, *refs),
-        grid=(rows // tile,),
-        in_specs=[
-            pl.BlockSpec((tile, cols), lambda i: (i, 0)),
-            pl.BlockSpec((key_count, HEAD_WIDTH), lambda i: (0, 0)),
-            pl.BlockSpec((1, key_count), lambda i: (0, 0)),
-            pl.BlockSpec((tile, 1), lambda i: (i, 0)),
-            pl.BlockSpec((tile, 1), lambda i: (i, 0)),
+    own = lax.axis_index("seq").astype(jnp.int32).reshape(1)
+    scalars = (own, lengths, old_place.reshape(1, -1))
+    scalar_specs = [
+        pl.BlockSpec(memory_space=pltpu.SMEM),
+        pl.BlockSpec(memory_space=pltpu.SMEM),
+        pl.BlockSpec(memory_space=pltpu.VMEM),
+    ]
+    in_vmem = pl.BlockSpec(memory_space=pltpu.VMEM)
+    *early, late = pairs
+    state = pltpu.VMEM((heads, rows, HEAD_WIDTH), jnp.float32)
+    carried = pl.pallas_call(
+        lambda *refs: first_kernel(tile, early, *refs),
+        in_specs=scalar_specs + [in_vmem] * (3 + len(early)),
+        out_specs=[in_vmem] * 3,
+        out_shape=[state] * 3,
+        compiler_params=pltpu.CompilerParams(vmem_limit_bytes=32 << 20),
+        cost_estimate=estimate(rows, heads, keys.shape[0] * (1 + len(early))),
+        name="first_shards",
+    )(*scalars, queries, keys, values, *[pairs[mask] for mask in early])
+    carried = [pltpu.with_memory_space_constraint(part, pltpu.VMEM) for part in carried]
+    return pl.pallas_call(
+        lambda *refs: last_kernel(tile, late, *refs),
+        in_specs=scalar_specs + [in_vmem] * 5,
+        out_specs=pl.BlockSpec(memory_space=pl.ANY),
+        out_shape=jax.ShapeDtypeStruct((rows, cols), jnp.bfloat16),
+        scratch_shapes=[
+            pltpu.VMEM((rows, cols), jnp.bfloat16),
+            pltpu.SemaphoreType.DMA((rows // tile,)),
         ],
-        out_specs=pl.BlockSpec((heads, tile, key_count), lambda i: (0, i, 0)),
-        out_shape=jax.ShapeDtypeStruct((heads, rows, key_count), jnp.bfloat16),
         compiler_params=pltpu.CompilerParams(vmem_limit_bytes=32 << 20),
-        cost_estimate=pl.CostEstimate(
-            flops=2 * heads * rows * key_count * HEAD_WIDTH,
-            bytes_accessed=2 * heads * rows * key_count,
-            transcendentals=heads * rows * key_count,
-        ),
-        name="weights",
-    )(queries, keys, key_pos, query_pos, starts)
-    return pl.pallas_call(
-        lambda *refs: mix_kernel(heads, *refs),
-        grid=(rows // tile,),
-        in_specs=[
-            pl.BlockSpec((heads, tile, key_count), lambda i: (0, i, 0)),
-            pl.BlockSpec((key_count, HEAD_WIDTH), lambda i: (0, 0)),
-        ],
-        out_specs=pl.BlockSpec((tile, cols), lambda i: (i, 0)),
-        out_shape=jax.ShapeDtypeStruct((rows, cols), jnp.bfloat16),
-        compiler_params=pltpu.CompilerParams(vmem_limit_bytes=32 << 20),
-        cost_estimate=pl.CostEstimate(
-            flops=4 * heads * rows * key_count * HEAD_WIDTH,
-            bytes_accessed=2 * heads * rows * key_count,
-            transcendentals=0,
-        ),
-        name="mix",
-    )(weights, values)
+        cost_estimate=estimate(rows, heads, keys.shape[0]),
+        name="last_shard",
+    )(*scalars, queries, *carried, pairs[late])
 
 
 def online_kernel(heads, q_ref, k_ref, v_ref, key_pos_ref, query_pos_ref, start_ref, out_ref, peak_ref, acc_ref):
@@ -154,14 +239,21 @@
 
 
 def body(queries, keys, values, lengths, old_place):
-    own_index = lax.axis_index("seq")
+    devices = lax.axis_size("seq")
     row_count = queries.shape[0]
-    key_count = row_count * lax.axis_size("seq")
+    key_count = row_count * devices
+    if devices == 4 and key_count <= 1024:
+        own_pair = jnp.concatenate([keys, values], axis=1)
+        pairs = {
+            mask: lax.ppermute(own_pair, "seq", [(i, i ^ mask) for i in range(devices)])
+            for mask in (2, 1, 3)
+        }
+        return staged_attention(queries, keys, values, pairs, lengths, old_place, 64)
     all_keys = lax.all_gather(keys, "seq", axis=0, tiled=True)
     all_values = lax.all_gather(values, "seq", axis=0, tiled=True)
-    key_pos, query_pos, starts = block_places(lengths, old_place, own_index, row_count, key_count)
-    if key_count <= 1024:
-        return tiled_attention(queries, all_keys, all_values, key_pos, query_pos, starts, 64)
+    key_pos, query_pos, starts = block_places(
+        lengths, old_place, lax.axis_index("seq"), row_count, key_count
+    )
     return online_attention(queries, all_keys, all_values, key_pos, query_pos, starts, 512)
 
 

time: 42.4 us -> 25.6 us (0.60)
  blocking collectives: 30.3 us -> 0 us
  waiting for transfers between devices: 0 us -> 10.3 us
  starting transfers between devices: 0 us -> 5.68 us
  Pallas kernels: 8.53 us -> 6.72 us
  other arithmetic: 1.78 us -> 0 us
  local copies, waits for them, and re-layouts: 1.59 us -> 2.62 us
    all_gather x2 -> x0, blocking collectives: 30.3 us -> none  [the longest x1 15.8 us: body(): all_keys = lax.all_gather(keys, 'seq', axis=0, tiled=True)]
    ppermute x0 -> x3, waiting for transfers between devices: none -> 10.3 us  [body(): lax.ppermute(own_pair, 'seq', [(i, i ^ mask) for i in range(devices)])]
    ppermute x0 -> x3, starting transfers between devices: none -> 5.68 us  [body(): lax.ppermute(own_pair, 'seq', [(i, i ^ mask) for i in range(devices)])]
    pallas_call x2, Pallas kernels: 8.53 us -> 6.72 us  [the longest x1 3.59 us: staged_attention(): pl.pallas_call(lambda *refs: last_kernel(tile, late, *refs), in_specs=sca...]
    unnamed x4 -> x11, local copies, waits for them, and re-layouts: 1.05 us -> 2.6 us
    another operation x1 -> x0, other arithmetic: 0.82 us -> none
    reduce_sum x1 -> x0, other arithmetic: 0.78 us -> none  [block_places(): new_block = jnp.sum(jnp.where(hit, ids[:, None], 0), axis=0)]
  transfers between devices with their start and end apart: 0 -> 3, of which waited for: 0 -> 2; matrix products, arithmetic and copies ran while one was open for 0% -> 0% of each run, Pallas kernels for 0% -> 12%
where the time goes in v3:
time: 25.6 us; the launch traced here: 25.4 us
  waiting for transfers between devices  10.3 us (40%)
  Pallas kernels  6.72 us (26%)
  starting transfers between devices  5.68 us (22%)
  local copies, waits for them, and re-layouts  2.62 us (10%)
    ppermute x3, waiting for transfers between devices, body(): lax.ppermute(own_pair, 'seq', [(i, i ^ mask) for i in range(devices)])  10.3 us
    ppermute x3, starting transfers between devices, body(): lax.ppermute(own_pair, 'seq', [(i, i ^ mask) for i in range(devices)])  5.68 us
    pallas_call x1, Pallas kernels, staged_attention(): pl.pallas_call(lambda *refs: last_kernel(tile, late, *refs), in_specs=sca...  3.59 us
    pallas_call x1, Pallas kernels, staged_attention(): pl.pallas_call(lambda *refs: first_kernel(tile, early, *refs), in_specs=s...  3.13 us
    unnamed x11, local copies, waits for them, and re-layouts  2.6 us
  transfers between devices with their start and end apart: 3, of which 2 were waited for; matrix products, arithmetic and copies ran while one was open for 0% of the time, Pallas kernels for 12%

profile of v3, /device:TPU:0, one launch (start us, length us, event | category | flops | bytes accessed | tf_op | source)
XLA Modules:
  0.0 25.4 jit_solution(8748702244116067501)
XLA Ops:
  0.0 0.0 copy-start.2
  0.0 0.9 %constant_dynamic-update-slice_fusion.1 = bf16[256,256]{1,0:T(8,128)(2,1)S(1)} fusion(bf16[256,128]{1,0:T(8,128)(2,1)} %refs_4_.1), kind=kLoop, calls=%fused_computation.1 | loop fusion | bytes 131072
  0.9 0.0 copy-done.2
  0.9 0.0 copy-start.1
  0.9 3.1 %collective-permute-start.1 = (bf16[256,256]{1,0:T(8,128)(2,1)S(1)}, bf16[256,256]{1,0:T(8,128)(2,1)S(1)}, u32[]{:S(2)}, u32[]{:S(2)}) collective-permute-start(bf16[256,256]{1,0:T(8,128)(2,1)S(1)} %constant_dynamic-update-slice_fusion), channel_id=1, source_target_pairs={{0,4},{4,0},{8,12},{12,8},{1,5},{5,1},{9,13},{13,9},{2,6},{6,2},{1... | collective-permute-start | bytes 393224 | tf_op jit(solution)/shard_map/ppermute | solution.py:248
  4.0 2.6 %collective-permute-start = (bf16[256,256]{1,0:T(8,128)(2,1)S(1)}, bf16[256,256]{1,0:T(8,128)(2,1)S(1)}, u32[]{:S(2)}, u32[]{:S(2)}) collective-permute-start(bf16[256,256]{1,0:T(8,128)(2,1)S(1)} %constant_dynamic-update-slice_fusion), channel_id=1, source_target_pairs={{0,8},{4,12},{8,0},{12,4},{1,9},{5,13},{9,1},{13,5},{2,10},{6,14},... | collective-permute-start | bytes 393224 | tf_op jit(solution)/shard_map/ppermute | solution.py:248
  6.6 0.0 collective-permute-start.2
  6.6 2.4 %collective-permute-done.1.refs_7_ = bf16[256,256]{1,0:T(8,128)(2,1)S(1)} collective-permute-done((bf16[256,256]{1,0:T(8,128)(2,1)S(1)}, bf16[256,256]{1,0:T(8,128)(2,1)S(1)}, u32[]{:S(2)}, u32[]{:S(2)}) %collective-permute-start.1) | collective-permute-done | bytes 131104 | tf_op jit(solution)/shard_map/ppermute | solution.py:248
  9.1 7.9 %collective-permute-done.refs_6_ = bf16[256,256]{1,0:T(8,128)(2,1)S(1)} collective-permute-done((bf16[256,256]{1,0:T(8,128)(2,1)S(1)}, bf16[256,256]{1,0:T(8,128)(2,1)S(1)}, u32[]{:S(2)}, u32[]{:S(2)}) %collective-permute-start) | collective-permute-done | bytes 131104 | tf_op jit(solution)/shard_map/ppermute | solution.py:248
  17.0 0.0 copy-start.3
  17.0 0.0 copy-start.4
  17.0 0.0 copy-done.1
  17.0 0.6 %copy-done.3 = s32[3]{0:T(128)S(1)} copy-done((s32[3]{0:T(128)S(1)}, s32[3]{0:T(128)}, u32[]{:S(2)}) %copy-start.3) | copy-done | bytes 36
  17.6 0.0 copy-done.4
  17.6 0.0 copy-start
  17.6 1.0 %copy-done = bf16[256,1024]{1,0:T(8,128)(2,1)S(1)} copy-done((bf16[256,1024]{1,0:T(8,128)(2,1)S(1)}, bf16[256,1024]{1,0:T(8,128)(2,1)}, u32[]{:S(2)}) %copy-start) | copy-done | bytes 524312
  18.7 3.1 %first_shards.1 = (f32[8,256,128]{2,1,0:T(8,128)S(1)}, f32[8,256,128]{2,1,0:T(8,128)S(1)}, f32[8,256,128]{2,1,0:T(8,128)S(1)}) custom-call(s32[1]{0:T(128)} %bitcast.refs_0_, s32[3]{0:T(128)S(1)} %copy-done.3, s32[1,128]{1,0:T(1,128)S(1)} %bitcast.2, bf16[256,1024]{1,0:T(8,128)(2,1)S(1)} %copy-done, bf16[256,128]{1,0:T(8,128)(2,1)S(1)} %copy-done.1, ...), custom_call_target="tpu_custom_call" | custom-call | flops 1207959552 | bytes 2097152 | tf_op jit(solution)/shard_map/first_shards/pallas_call | solution.py:155
  21.8 0.0 collective-permute-done.2.refs_7_
  21.8 3.6 %last_shard.1 = bf16[256,1024]{1,0:T(8,128)(2,1)} custom-call(s32[1]{0:T(128)} %bitcast.refs_0_, s32[3]{0:T(128)S(1)} %copy-done.3, s32[1,128]{1,0:T(1,128)S(1)} %bitcast.3, bf16[256,1024]{1,0:T(8,128)(2,1)S(1)} %copy-done, f32[8,256,128]{2,1,0:T(8,128)S(1)} %get-tuple-element.8.refs_4_, f32[8,256,128]{2,1,0:T(8,128)S(1)} %get-tuple-element.9.refs_5_, ...), custom_call_target="tpu_custom_call" | custom-call | flops 402653184 | bytes 2097152 | tf_op jit(solution)/shard_map/last_shard/pallas_call | solution.py:165
  (1 shorter events, 0.0 us)
Async XLA Ops:
  0.0 0.9 %copy-start.2 = (bf16[256,128]{1,0:T(8,128)(2,1)S(1)}, bf16[256,128]{1,0:T(8,128)(2,1)}, u32[]{:S(2)}) copy-start(bf16[256,128]{1,0:T(8,128)(2,1)} %refs_5_.1) | copy-start | bytes 196612
  0.9 16.1 %copy-start.1 = (bf16[256,128]{1,0:T(8,128)(2,1)S(1)}, bf16[256,128]{1,0:T(8,128)(2,1)}, u32[]{:S(2)}) copy-start(bf16[256,128]{1,0:T(8,128)(2,1)} %refs_4_.1) | copy-start | bytes 196612
  0.9 8.1 %collective-permute-start.1 = (bf16[256,256]{1,0:T(8,128)(2,1)S(1)}, bf16[256,256]{1,0:T(8,128)(2,1)S(1)}, u32[]{:S(2)}, u32[]{:S(2)}) collective-permute-start(bf16[256,256]{1,0:T(8,128)(2,1)S(1)} %constant_dynamic-update-slice_fusion), channel_id=1, source_target_pairs={{0,4},{4,0},{8,12},{12,8},{1,5},{5,1},{9,13},{13,9},{2,6},{6,2},{1... | collective-permute-start | bytes 393224 | tf_op jit(solution)/shard_map/ppermute | solution.py:248
  4.0 12.9 %collective-permute-start = (bf16[256,256]{1,0:T(8,128)(2,1)S(1)}, bf16[256,256]{1,0:T(8,128)(2,1)S(1)}, u32[]{:S(2)}, u32[]{:S(2)}) collective-permute-start(bf16[256,256]{1,0:T(8,128)(2,1)S(1)} %constant_dynamic-update-slice_fusion), channel_id=1, source_target_pairs={{0,8},{4,12},{8,0},{12,4},{1,9},{5,13},{9,1},{13,5},{2,10},{6,14},... | collective-permute-start | bytes 393224 | tf_op jit(solution)/shard_map/ppermute | solution.py:248
  6.6 15.2 %collective-permute-start.2 = (bf16[256,256]{1,0:T(8,128)(2,1)S(1)}, bf16[256,256]{1,0:T(8,128)(2,1)S(1)}, u32[]{:S(2)}, u32[]{:S(2)}) collective-permute-start(bf16[256,256]{1,0:T(8,128)(2,1)S(1)} %constant_dynamic-update-slice_fusion), channel_id=1, source_target_pairs={{0,12},{4,8},{8,4},{12,0},{1,13},{5,9},{9,5},{13,1},{2,14},{6,10},... | collective-permute-start | bytes 393224 | tf_op jit(solution)/shard_map/ppermute | solution.py:248
  17.0 0.7 %copy-start.3 = (s32[3]{0:T(128)S(1)}, s32[3]{0:T(128)}, u32[]{:S(2)}) copy-start(s32[3]{0:T(128)} %refs_1_.3) | copy-start | bytes 40
  17.0 0.7 %copy-start.4 = (s32[128]{0:T(128)S(1)}, s32[128]{0:T(128)}, u32[]{:S(2)}) copy-start(s32[128]{0:T(128)} %param.9) | copy-start | bytes 1540
  17.6 1.0 %copy-start = (bf16[256,1024]{1,0:T(8,128)(2,1)S(1)}, bf16[256,1024]{1,0:T(8,128)(2,1)}, u32[]{:S(2)}) copy-start(bf16[256,1024]{1,0:T(8,128)(2,1)} %refs_3_.3) | copy-start | bytes 1572868

commit v4 on v3

v4 whole, which is shorter than its diff:
```python
import jax
import jax.numpy as jnp
from jax import lax
from jax.experimental import pallas as pl
from jax.experimental.pallas import tpu as pltpu
from jax.sharding import PartitionSpec as P

HEAD_WIDTH = 128
LOG2_E = 1.4426950408889634
NEG_FILL = -1e30
ONES = 16


def block_places(lengths, old_place, own_index, row_count, key_count):
    block_total = old_place.shape[0]
    block_rows = key_count // block_total
    ids = jnp.arange(block_total, dtype=jnp.int32)
    hit = old_place[:, None] == ids[None, :]
    new_block = jnp.sum(jnp.where(hit, ids[:, None], 0), axis=0)
    key_pos = (new_block[:, None] * block_rows + jnp.arange(block_rows, dtype=jnp.int32)).reshape(-1)
    query_pos = lax.dynamic_slice_in_dim(key_pos, own_index * row_count, row_count)
    bounds = jnp.cumsum(lengths)
    starts = jnp.max(jnp.where(bounds[None, :] <= query_pos[:, None], bounds[None, :], 0), axis=1)
    return key_pos.reshape(1, -1), query_pos.reshape(-1, 1), starts.reshape(-1, 1)


def iota(shape, dim):
    return lax.broadcasted_iota(jnp.int32, shape, dim)


def mask_tables(own, owners, lengths_ref, places_ref, rows, bias_ref):
    block_total = places_ref.shape[1]
    block_rows = rows * lax.axis_size("seq") // block_total
    blocks = rows // block_rows
    places = places_ref[...]
    square = (block_total, block_total)
    as_column = jnp.sum(
        jnp.where(iota(square, 0) == iota(square, 1), places, 0).astype(jnp.float32),
        axis=1, keepdims=True,
    ).astype(jnp.int32)
    across = (block_total, rows)
    hit = as_column == own * blocks + iota(across, 1) // block_rows
    at = jnp.where(hit, iota(across, 0) * block_rows, 0).astype(jnp.float32)
    query_pos = jnp.sum(at, axis=0, keepdims=True) + (
        iota((1, rows), 1) % block_rows
    ).astype(jnp.float32)
    starts = jnp.zeros_like(query_pos)
    bound = jnp.int32(0)
    for t in range(lengths_ref.shape[0]):
        bound = bound + lengths_ref[t]
        edge = bound.astype(jnp.float32)
        starts = jnp.where(edge <= query_pos, edge, starts)
    down = (rows, block_total)
    for n, owner in enumerate(owners):
        hit = places == owner * blocks + iota(down, 0) // block_rows
        at = jnp.where(hit, iota(down, 1) * block_rows, 0).astype(jnp.float32)
        key_pos = jnp.sum(at, axis=1, keepdims=True) + (
            iota((rows, 1), 0) % block_rows
        ).astype(jnp.float32)
        visible = (key_pos >= starts) & (key_pos <= query_pos)
        bias_ref[n] = jnp.where(visible, 0.0, NEG_FILL)


def scaled_scores(keys, q_across, bias):
    scores = jnp.dot(keys, q_across, preferred_element_type=jnp.float32)
    return scores * (HEAD_WIDTH ** -0.5 * LOG2_E) + bias


def values_down(values):
    turned = jnp.transpose(values.astype(jnp.float32)).astype(jnp.bfloat16)
    return jnp.concatenate([turned, jnp.ones((ONES, values.shape[0]), jnp.bfloat16)], axis=0)


def weigh(scaled, peak, turned):
    weights = jnp.exp2(scaled - peak).astype(jnp.bfloat16)
    return jnp.dot(turned, weights, preferred_element_type=jnp.float32)


def own_kernel(
    masks, own_ref, lengths_ref, places_ref, q_ref, k_ref, v_ref,
    across_ref, bias_ref, peak_ref, sum_ref,
):
    heads = q_ref.shape[1] // HEAD_WIDTH
    own = own_ref[0]
    owners = [own] + [own ^ mask for mask in masks]
    mask_tables(own, owners, lengths_ref, places_ref, q_ref.shape[0], bias_ref)
    turned = values_down(v_ref[...])
    for head in range(heads):
        q = q_ref[:, head * HEAD_WIDTH:(head + 1) * HEAD_WIDTH]
        across = jnp.transpose(q.astype(jnp.float32)).astype(jnp.bfloat16)
        across_ref[head] = across
        scaled = scaled_scores(k_ref[...], across, bias_ref[0])
        peak = jnp.max(scaled, axis=0, keepdims=True)
        peak_ref[head:head + 1, :] = peak
        sum_ref[head] = weigh(scaled, peak, turned)


def add_shard(head, bias, keys, turned, across_ref, peak_ref, sum_ref):
    scaled = scaled_scores(keys, across_ref[head], bias)
    before = peak_ref[head:head + 1, :]
    peak = jnp.maximum(before, jnp.max(scaled, axis=0, keepdims=True))
    return peak, sum_ref[head] * jnp.exp2(before - peak) + weigh(scaled, peak, turned)


def next_kernel(at, across_ref, bias_ref, peak_ref, sum_ref, pair_ref, new_peak_ref, new_sum_ref):
    keys = pair_ref[:, :HEAD_WIDTH]
    turned = values_down(pair_ref[:, HEAD_WIDTH:])
    for head in range(across_ref.shape[0]):
        peak, summed = add_shard(head, bias_ref[at], keys, turned, across_ref, peak_ref, sum_ref)
        new_peak_ref[head:head + 1, :] = peak
        new_sum_ref[head] = summed


def last_kernel(at, across_ref, bias_ref, peak_ref, sum_ref, pair_ref, out_ref, block_ref, sems):
    keys = pair_ref[:, :HEAD_WIDTH]
    turned = values_down(pair_ref[:, HEAD_WIDTH:])
    copies = []
    for head in range(across_ref.shape[0]):
        _, summed = add_shard(head, bias_ref[at], keys, turned, across_ref, peak_ref, sum_ref)
        out = summed[:HEAD_WIDTH] / summed[HEAD_WIDTH:HEAD_WIDTH + 1]
        cols = slice(head * HEAD_WIDTH, (head + 1) * HEAD_WIDTH)
        block_ref[:, cols] = jnp.transpose(out).astype(jnp.bfloat16)
        copy = pltpu.make_async_copy(block_ref.at[:, cols], out_ref.at[:, cols], sems.at[head])
        copy.start()
        copies.append(copy)
    for copy in copies:
        copy.wait()


def estimate(rows, heads, key_count):
    return pl.CostEstimate(
        flops=6 * heads * rows * key_count * HEAD_WIDTH,
        bytes_accessed=8 * heads * rows * HEAD_WIDTH,
        transcendentals=heads * rows * key_count,
    )


def in_vmem(*arrays):
    return [pltpu.with_memory_space_constraint(array, pltpu.VMEM) for array in arrays]


def staged_attention(queries, keys, values, pairs, lengths, old_place):
    rows, cols = queries.shape
    heads = cols // HEAD_WIDTH
    own = lax.axis_index("seq").astype(jnp.int32).reshape(1)
    whole = pl.BlockSpec(memory_space=pltpu.VMEM)
    params = pltpu.CompilerParams(vmem_limit_bytes=32 << 20)
    state = [
        pltpu.VMEM((heads, rows), jnp.float32),
        pltpu.VMEM((heads, HEAD_WIDTH + ONES, rows), jnp.float32),
    ]
    across, bias, *carried = pl.pallas_call(
        lambda *refs: own_kernel(list(pairs), *refs),
        in_specs=[pl.BlockSpec(memory_space=pltpu.SMEM)] * 2 + [whole] * 4,
        out_specs=[whole] * 4,
        out_shape=[
            pltpu.VMEM((heads, HEAD_WIDTH, rows), jnp.bfloat16),
            pltpu.VMEM((1 + len(pairs), rows, rows), jnp.float32),
        ] + state,
        compiler_params=params,
        cost_estimate=estimate(rows, heads, rows),
        name="own_shard",
    )(own, lengths, old_place.reshape(1, -1), queries, keys, values)
    *early, last = pairs
    for at, mask in enumerate(early):
        carried = pl.pallas_call(
            lambda *refs, at=at: next_kernel(1 + at, *refs),
            in_specs=[whole] * 5,
            out_specs=[whole] * 2,
            out_shape=state,
            compiler_params=params,
            cost_estimate=estimate(rows, heads, rows),
            name="next_shard",
        )(*in_vmem(across, bias, *carried), pairs[mask])
    return pl.pallas_call(
        lambda *refs: last_kernel(1 + len(early), *refs),
        in_specs=[whole] * 5,
        out_specs=pl.BlockSpec(memory_space=pl.ANY),
        out_shape=jax.ShapeDtypeStruct((rows, cols), jnp.bfloat16),
        scratch_shapes=[
            pltpu.VMEM((rows, cols), jnp.bfloat16),
            pltpu.SemaphoreType.DMA((heads,)),
        ],
        compiler_params=params,
        cost_estimate=estimate(rows, heads, rows),
        name="last_shard",
    )(*in_vmem(across, bias, *carried), pairs[last])


def online_kernel(heads, q_ref, k_ref, v_ref, key_pos_ref, query_pos_ref, start_ref, out_ref, peak_ref, acc_ref):
    step = pl.program_id(0)

    @pl.when(step == 0)
    def _():
        peak_ref[...] = jnp.full(peak_ref.shape, NEG_FILL, jnp.float32)
        acc_ref[...] = jnp.zeros(acc_ref.shape, jnp.float32)

    key_pos = key_pos_ref[...]
    visible = (key_pos >= start_ref[...]) & (key_pos <= query_pos_ref[...])
    values = v_ref[...]
    ext = jnp.concatenate([values, jnp.ones_like(values)], axis=1)
    for head in range(heads):
        q = q_ref[:, head * HEAD_WIDTH:(head + 1) * HEAD_WIDTH]
        scores = lax.dot_general(
            q, k_ref[...], (((1,), (1,)), ((), ())), preferred_element_type=jnp.float32
        )
        scaled = jnp.where(visible, scores * (HEAD_WIDTH ** -0.5 * LOG2_E), NEG_FILL)
        before = peak_ref[head]
        peak = jnp.maximum(before, jnp.max(scaled, axis=1, keepdims=True))
        weights = jnp.where(visible, jnp.exp2(scaled - peak), 0.0).astype(jnp.bfloat16)
        peak_ref[head] = peak
        acc_ref[head] = acc_ref[head] * jnp.exp2(before - peak) + jnp.dot(
            weights, ext, preferred_element_type=jnp.float32
        )

    @pl.when(step == pl.num_programs(0) - 1)
    def _():
        for head in range(heads):
            acc = acc_ref[head]
            out_ref[:, head * HEAD_WIDTH:(head + 1) * HEAD_WIDTH] = (
                acc[:, :HEAD_WIDTH] / acc[:, HEAD_WIDTH:]
            ).astype(jnp.bfloat16)


def online_attention(queries, keys, values, key_pos, query_pos, starts, chunk):
    rows, cols = queries.shape
    heads = cols // HEAD_WIDTH
    key_count = keys.shape[0]
    return pl.pallas_call(
        lambda *refs: online_kernel(heads, *refs),
        grid=(key_count // chunk,),
        in_specs=[
            pl.BlockSpec((rows, cols), lambda j: (0, 0)),
            pl.BlockSpec((chunk, HEAD_WIDTH), lambda j: (j, 0)),
            pl.BlockSpec((chunk, HEAD_WIDTH), lambda j: (j, 0)),
            pl.BlockSpec((1, chunk), lambda j: (0, j)),
            pl.BlockSpec((rows, 1), lambda j: (0, 0)),
            pl.BlockSpec((rows, 1), lambda j: (0, 0)),
        ],
        out_specs=pl.BlockSpec((rows, cols), lambda j: (0, 0)),
        out_shape=jax.ShapeDtypeStruct((rows, cols), jnp.bfloat16),
        scratch_shapes=[
            pltpu.VMEM((heads, rows, 1), jnp.float32),
            pltpu.VMEM((heads, rows, 2 * HEAD_WIDTH), jnp.float32),
        ],
        compiler_params=pltpu.CompilerParams(vmem_limit_bytes=32 << 20),
        name="online",
    )(queries, keys, values, key_pos, query_pos, starts)


def body(queries, keys, values, lengths, old_place):
    devices = lax.axis_size("seq")
    row_count = queries.shape[0]
    key_count = row_count * devices
    if devices == 4 and key_count <= 1024:
        own_pair = jnp.concatenate([keys, values], axis=1)
        pairs = {
            mask: lax.ppermute(own_pair, "seq", [(i, i ^ mask) for i in range(devices)])
            for mask in (2, 1, 3)
        }
        return staged_attention(queries, keys, values, pairs, lengths, old_place)
    all_keys = lax.all_gather(keys, "seq", axis=0, tiled=True)
    all_values = lax.all_gather(values, "seq", axis=0, tiled=True)
    key_pos, query_pos, starts = block_places(
        lengths, old_place, lax.axis_index("seq"), row_count, key_count
    )
    return online_attention(queries, all_keys, all_values, key_pos, query_pos, starts, 512)


def solution(mesh):
    in_specs = (
        P(("groups", "seq"), "mp"),
        P(("groups", "seq"), "mp"),
        P(("groups", "seq"), "mp"),
        P("groups"),
        P("groups"),
    )
    out_specs = P(("groups", "seq"), "mp")
    return jax.shard_map(body, mesh=mesh, in_specs=in_specs, out_specs=out_specs, check_vma=False)
```

time: 25.6 us -> 22.9 us (0.89)
  waiting for transfers between devices: 10.3 us -> 0.01 us
  Pallas kernels: 6.72 us -> 11 us
  local copies, waits for them, and re-layouts: 2.62 us -> 5.74 us
    ppermute x3, waiting for transfers between devices: 10.3 us -> 0.01 us  [body(): lax.ppermute(own_pair, 'seq', [(i, i ^ mask) for i in range(devices)])]
    pallas_call x2 -> x4, Pallas kernels: 6.72 us -> 11 us  [the longest x2 4.75 us: staged_attention(): pl.pallas_call(lambda *refs, at=at: next_kernel(1 + at, *refs), in_specs=...]
    unnamed x11, local copies, waits for them, and re-layouts: 2.6 us -> 4.88 us
    concatenate x1, local copies, waits for them, and re-layouts: 0.02 us -> 0.86 us  [body(): own_pair = jnp.concatenate([keys, values], axis=1)]
  transfers between devices with their start and end apart: 3 -> 3, of which waited for: 2 -> 0; matrix products, arithmetic and copies ran while one was open for 0% -> 0% of each run, Pallas kernels for 12% -> 35%
where the time goes in v4:
time: 22.9 us; the launch traced here: 22.5 us
  Pallas kernels  11 us (48%)
  local copies, waits for them, and re-layouts  5.74 us (25%)
  starting transfers between devices  5.68 us (25%)
    ppermute x3, starting transfers between devices, body(): lax.ppermute(own_pair, 'seq', [(i, i ^ mask) for i in range(devices)])  5.68 us
    unnamed x11, local copies, waits for them, and re-layouts  4.88 us
    pallas_call x2, Pallas kernels, staged_attention(): pl.pallas_call(lambda *refs, at=at: next_kernel(1 + at, *refs), in_specs=...  4.75 us
    pallas_call x1, Pallas kernels, staged_attention(): pl.pallas_call(lambda *refs: last_kernel(1 + len(early), *refs), in_specs...  3.21 us
    pallas_call x1, Pallas kernels, staged_attention(): pl.pallas_call(lambda *refs: own_kernel(list(pairs), *refs), in_specs=[pl...  3.07 us
    concatenate x1, local copies, waits for them, and re-layouts, body(): own_pair = jnp.concatenate([keys, values], axis=1)  0.86 us
  transfers between devices with their start and end apart: 3, of which 0 were waited for; matrix products, arithmetic and copies ran while one was open for 0% of the time, Pallas kernels for 35%

profile of v4, /device:TPU:0, one launch (start us, length us, event | category | flops | bytes accessed | tf_op | source)
XLA Modules:
  0.0 22.5 jit_solution(8605391114480132965)
XLA Ops:
  0.0 0.9 %constant_dynamic-update-slice_fusion.1 = bf16[256,256]{1,0:T(8,128)(2,1)S(1)} fusion(bf16[256,128]{1,0:T(8,128)(2,1)} %refs_4_.1), kind=kLoop, calls=%fused_computation.1 | loop fusion | bytes 131072
  0.9 0.9 %constant_dynamic-update-slice_fusion = bf16[256,256]{1,0:T(8,128)(2,1)S(1)} fusion(bf16[256,256]{1,0:T(8,128)(2,1)S(1)} %constant_dynamic-update-slice_fusion.1, bf16[256,128]{1,0:T(8,128)(2,1)} %refs_5_.1), kind=kLoop, calls=%fused_computation | loop fusion | bytes 131072 | tf_op jit(solution)/shard_map/concatenate | solution.py:256
  1.7 4.1 %collective-permute-start = (bf16[256,256]{1,0:T(8,128)(2,1)S(1)}, bf16[256,256]{1,0:T(8,128)(2,1)S(1)}, u32[]{:S(2)}, u32[]{:S(2)}) collective-permute-start(bf16[256,256]{1,0:T(8,128)(2,1)S(1)} %constant_dynamic-update-slice_fusion), channel_id=1, source_target_pairs={{0,8},{4,12},{8,0},{12,4},{1,9},{5,13},{9,1},{13,5},{2,10},{6,14},... | collective-permute-start | bytes 393224 | tf_op jit(solution)/shard_map/ppermute | solution.py:258
  5.8 1.6 %collective-permute-start.1 = (bf16[256,256]{1,0:T(8,128)(2,1)S(1)}, bf16[256,256]{1,0:T(8,128)(2,1)S(1)}, u32[]{:S(2)}, u32[]{:S(2)}) collective-permute-start(bf16[256,256]{1,0:T(8,128)(2,1)S(1)} %constant_dynamic-update-slice_fusion), channel_id=1, source_target_pairs={{0,4},{4,0},{8,12},{12,8},{1,5},{5,1},{9,13},{13,9},{2,6},{6,2},{1... | collective-permute-start | bytes 393224 | tf_op jit(solution)/shard_map/ppermute | solution.py:258
  7.4 0.0 collective-permute-start.2
  7.4 0.0 copy-start
  7.4 0.8 %copy-done = bf16[256,128]{1,0:T(8,128)(2,1)S(1)} copy-done((bf16[256,128]{1,0:T(8,128)(2,1)S(1)}, bf16[256,128]{1,0:T(8,128)(2,1)}, u32[]{:S(2)}) %copy-start) | copy-done | bytes 65560
  8.2 0.0 copy-start.1
  8.2 0.8 %copy-done.1 = bf16[256,128]{1,0:T(8,128)(2,1)S(1)} copy-done((bf16[256,128]{1,0:T(8,128)(2,1)S(1)}, bf16[256,128]{1,0:T(8,128)(2,1)}, u32[]{:S(2)}) %copy-start.1) | copy-done | bytes 65560
  9.1 0.0 copy-start.2
  9.1 1.0 %copy-done.2 = bf16[256,1024]{1,0:T(8,128)(2,1)S(1)} copy-done((bf16[256,1024]{1,0:T(8,128)(2,1)S(1)}, bf16[256,1024]{1,0:T(8,128)(2,1)}, u32[]{:S(2)}) %copy-start.2) | copy-done | bytes 524312
  10.1 0.0 copy-start.3
  10.1 0.7 %copy-done.3 = s32[3]{0:T(128)S(1)} copy-done((s32[3]{0:T(128)S(1)}, s32[3]{0:T(128)}, u32[]{:S(2)}) %copy-start.3) | copy-done | bytes 36
  10.8 0.0 copy-start.4
  10.8 0.7 %copy-done.4 = s32[128]{0:T(128)S(1)} copy-done((s32[128]{0:T(128)S(1)}, s32[128]{0:T(128)}, u32[]{:S(2)}) %copy-start.4) | copy-done | bytes 536
  11.4 3.1 %own_shard.1 = (bf16[8,128,256]{2,1,0:T(8,128)(2,1)S(1)}, f32[4,256,256]{2,1,0:T(8,128)S(1)}, f32[8,256]{1,0:T(8,128)S(1)}, f32[8,144,256]{2,1,0:T(8,128)S(1)}) custom-call(s32[1]{0:T(128)} %bitcast.refs_0_, s32[3]{0:T(128)S(1)} %copy-done.3, s32[1,128]{1,0:T(1,128)S(1)} %bitcast.2, bf16[256,1024]{1,0:T(8,128)(2,1)S(1)} %copy-done.2, ...), custom_call_target="tpu_custom_call" | custom-call | flops 402653184 | bytes 2097152 | tf_op jit(solution)/shard_map/own_shard/pallas_call | solution.py:152
  14.5 0.0 collective-permute-done.refs_4_
  14.5 2.4 %next_shard.2 = (f32[8,256]{1,0:T(8,128)S(1)}, f32[8,144,256]{2,1,0:T(8,128)S(1)}) custom-call(bf16[8,128,256]{2,1,0:T(8,128)(2,1)S(1)} %get-tuple-element.13.refs_0_, f32[4,256,256]{2,1,0:T(8,128)S(1)} %get-tuple-element.14.refs_1_, f32[8,256]{1,0:T(8,128)S(1)} %get-tuple-element.15.refs_2_, f32[8,144,256]{2,1,0:T(8,128)S(1)} %get-tuple-element.16.refs_3_, ...), custom_call_target="tpu_custom_call" | custom-call | flops 402653184 | bytes 2097152 | tf_op jit(solution)/shard_map/next_shard/pallas_call | solution.py:166
  16.9 0.0 collective-permute-done.1.refs_4_
  16.9 2.4 %next_shard.3 = (f32[8,256]{1,0:T(8,128)S(1)}, f32[8,144,256]{2,1,0:T(8,128)S(1)}) custom-call(bf16[8,128,256]{2,1,0:T(8,128)(2,1)S(1)} %get-tuple-element.13.refs_0_, f32[4,256,256]{2,1,0:T(8,128)S(1)} %get-tuple-element.14.refs_1_, f32[8,256]{1,0:T(8,128)S(1)} %get-tuple-element.17.refs_2_, f32[8,144,256]{2,1,0:T(8,128)S(1)} %get-tuple-element.18.refs_3_, ...), custom_call_target="tpu_custom_call" | custom-call | flops 402653184 | bytes 2097152 | tf_op jit(solution)/shard_map/next_shard/pallas_call | solution.py:166
  19.3 0.0 collective-permute-done.2.refs_4_
  19.3 3.2 %last_shard.1 = bf16[256,1024]{1,0:T(8,128)(2,1)} custom-call(bf16[8,128,256]{2,1,0:T(8,128)(2,1)S(1)} %get-tuple-element.13.refs_0_, f32[4,256,256]{2,1,0:T(8,128)S(1)} %get-tuple-element.14.refs_1_, f32[8,256]{1,0:T(8,128)S(1)} %get-tuple-element.19.refs_2_, f32[8,144,256]{2,1,0:T(8,128)S(1)} %get-tuple-element.20.refs_3_, ...), custom_call_target="tpu_custom_call" | custom-call | flops 402653184 | bytes 2097152 | tf_op jit(solution)/shard_map/last_shard/pallas_call | solution.py:175
Async XLA Ops:
  1.7 12.8 %collective-permute-start = (bf16[256,256]{1,0:T(8,128)(2,1)S(1)}, bf16[256,256]{1,0:T(8,128)(2,1)S(1)}, u32[]{:S(2)}, u32[]{:S(2)}) collective-permute-start(bf16[256,256]{1,0:T(8,128)(2,1)S(1)} %constant_dynamic-update-slice_fusion), channel_id=1, source_target_pairs={{0,8},{4,12},{8,0},{12,4},{1,9},{5,13},{9,1},{13,5},{2,10},{6,14},... | collective-permute-start | bytes 393224 | tf_op jit(solution)/shard_map/ppermute | solution.py:258
  5.8 11.1 %collective-permute-start.1 = (bf16[256,256]{1,0:T(8,128)(2,1)S(1)}, bf16[256,256]{1,0:T(8,128)(2,1)S(1)}, u32[]{:S(2)}, u32[]{:S(2)}) collective-permute-start(bf16[256,256]{1,0:T(8,128)(2,1)S(1)} %constant_dynamic-update-slice_fusion), channel_id=1, source_target_pairs={{0,4},{4,0},{8,12},{12,8},{1,5},{5,1},{9,13},{13,9},{2,6},{6,2},{1... | collective-permute-start | bytes 393224 | tf_op jit(solution)/shard_map/ppermute | solution.py:258
  7.4 11.9 %collective-permute-start.2 = (bf16[256,256]{1,0:T(8,128)(2,1)S(1)}, bf16[256,256]{1,0:T(8,128)(2,1)S(1)}, u32[]{:S(2)}, u32[]{:S(2)}) collective-permute-start(bf16[256,256]{1,0:T(8,128)(2,1)S(1)} %constant_dynamic-update-slice_fusion), channel_id=1, source_target_pairs={{0,12},{4,8},{8,4},{12,0},{1,13},{5,9},{9,5},{13,1},{2,14},{6,10},... | collective-permute-start | bytes 393224 | tf_op jit(solution)/shard_map/ppermute | solution.py:258
  7.4 0.8 %copy-start = (bf16[256,128]{1,0:T(8,128)(2,1)S(1)}, bf16[256,128]{1,0:T(8,128)(2,1)}, u32[]{:S(2)}) copy-start(bf16[256,128]{1,0:T(8,128)(2,1)} %refs_4_.1) | copy-start | bytes 196612
  8.2 0.8 %copy-start.1 = (bf16[256,128]{1,0:T(8,128)(2,1)S(1)}, bf16[256,128]{1,0:T(8,128)(2,1)}, u32[]{:S(2)}) copy-start(bf16[256,128]{1,0:T(8,128)(2,1)} %refs_5_.1) | copy-start | bytes 196612
  9.1 1.0 %copy-start.2 = (bf16[256,1024]{1,0:T(8,128)(2,1)S(1)}, bf16[256,1024]{1,0:T(8,128)(2,1)}, u32[]{:S(2)}) copy-start(bf16[256,1024]{1,0:T(8,128)(2,1)} %refs_3_.1) | copy-start | bytes 1572868
  10.1 0.7 %copy-start.3 = (s32[3]{0:T(128)S(1)}, s32[3]{0:T(128)}, u32[]{:S(2)}) copy-start(s32[3]{0:T(128)} %refs_1_.1) | copy-start | bytes 40
  10.8 0.7 %copy-start.4 = (s32[128]{0:T(128)S(1)}, s32[128]{0:T(128)}, u32[]{:S(2)}) copy-start(s32[128]{0:T(128)} %param.9) | copy-start | bytes 1540

commit v5 on v4

--- a/solution.py
+++ b/solution.py
@@ -61,68 +61,138 @@
         bias_ref[n] = jnp.where(visible, 0.0, NEG_FILL)
 
 
-def scaled_scores(keys, q_across, bias):
-    scores = jnp.dot(keys, q_across, preferred_element_type=jnp.float32)
-    return scores * (HEAD_WIDTH ** -0.5 * LOG2_E) + bias
-
-
 def values_down(values):
     turned = jnp.transpose(values.astype(jnp.float32)).astype(jnp.bfloat16)
     return jnp.concatenate([turned, jnp.ones((ONES, values.shape[0]), jnp.bfloat16)], axis=0)
 
 
-def weigh(scaled, peak, turned):
-    weights = jnp.exp2(scaled - peak).astype(jnp.bfloat16)
-    return jnp.dot(turned, weights, preferred_element_type=jnp.float32)
+def in_stages(heads, stages):
+    results = [{} for _ in stages]
+    for step in range(heads + len(stages) - 1):
+        for late, stage in enumerate(stages):
+            head = step - late
+            if 0 <= head < heads:
+                before = results[late - 1].pop(head) if late else None
+                results[late][head] = stage(head, before)
+
+
+def score_stage(keys, across_ref, bias_ref, at, scaled_ref, old_peak):
+    def stage(head, _):
+        scores = jnp.dot(keys, across_ref[head], preferred_element_type=jnp.float32)
+        scaled = scores * (HEAD_WIDTH ** -0.5 * LOG2_E) + bias_ref[at]
+        scaled_ref[head] = scaled
+        peak = jnp.max(scaled, axis=0, keepdims=True)
+        return peak if old_peak is None else jnp.maximum(old_peak(head), peak)
+
+    return stage
+
+
+def weight_stage(scaled_ref, weight_ref):
+    def stage(head, peak):
+        weight_ref[head] = jnp.exp2(scaled_ref[head] - peak).astype(jnp.bfloat16)
+        return peak
+
+    return stage
+
+
+def pack_kernel(k_ref, v_ref, pair_ref, sems):
+    copies = [
+        pltpu.make_async_copy(ref, pair_ref.at[:, at * HEAD_WIDTH:(at + 1) * HEAD_WIDTH], sems.at[at])
+        for at, ref in enumerate((k_ref, v_ref))
+    ]
+    for copy in copies:
+        copy.start()
+    for copy in copies:
+        copy.wait()
 
 
 def own_kernel(
-    masks, own_ref, lengths_ref, places_ref, q_ref, k_ref, v_ref,
+    masks, own_ref, lengths_hbm, places_hbm, q_hbm, pair_ref,
     across_ref, bias_ref, peak_ref, sum_ref,
+    lengths_ref, places_ref, q_ref, scaled_ref, weight_ref, sems,
 ):
-    heads = q_ref.shape[1] // HEAD_WIDTH
+    moves = ((lengths_hbm, lengths_ref), (places_hbm, places_ref), (q_hbm, q_ref))
+    copies = [pltpu.make_async_copy(*move, sems.at[n]) for n, move in enumerate(moves)]
+    for copy in copies:
+        copy.start()
+    turned = values_down(pair_ref[:, HEAD_WIDTH:])
+    keys = pair_ref[:, :HEAD_WIDTH]
+    copies[0].wait()
+    copies[1].wait()
+    heads, _, rows = across_ref.shape
     own = own_ref[0]
     owners = [own] + [own ^ mask for mask in masks]
-    mask_tables(own, owners, lengths_ref, places_ref, q_ref.shape[0], bias_ref)
-    turned = values_down(v_ref[...])
-    for head in range(heads):
+    mask_tables(own, owners, lengths_ref, places_ref, rows, bias_ref)
+    copies[2].wait()
+
+    def turn(head, _):
         q = q_ref[:, head * HEAD_WIDTH:(head + 1) * HEAD_WIDTH]
-        across = jnp.transpose(q.astype(jnp.float32)).astype(jnp.bfloat16)
-        across_ref[head] = across
-        scaled = scaled_scores(k_ref[...], across, bias_ref[0])
-        peak = jnp.max(scaled, axis=0, keepdims=True)
+        across_ref[head] = jnp.transpose(q.astype(jnp.float32)).astype(jnp.bfloat16)
+
+    def mix(head, peak):
         peak_ref[head:head + 1, :] = peak
-        sum_ref[head] = weigh(scaled, peak, turned)
-
-
-def add_shard(head, bias, keys, turned, across_ref, peak_ref, sum_ref):
-    scaled = scaled_scores(keys, across_ref[head], bias)
-    before = peak_ref[head:head + 1, :]
-    peak = jnp.maximum(before, jnp.max(scaled, axis=0, keepdims=True))
-    return peak, sum_ref[head] * jnp.exp2(before - peak) + weigh(scaled, peak, turned)
-
-
-def next_kernel(at, across_ref, bias_ref, peak_ref, sum_ref, pair_ref, new_peak_ref, new_sum_ref):
-    keys = pair_ref[:, :HEAD_WIDTH]
+        sum_ref[head] = jnp.dot(turned, weight_ref[head], preferred_element_type=jnp.float32)
+
+    in_stages(heads, [
+        turn,
+        score_stage(keys, across_ref, bias_ref, 0, scaled_ref, None),
+        weight_stage(scaled_ref, weight_ref),
+        mix,
+    ])
+
+
+def joined(head, peak, turned, weight_ref, peak_ref, sum_ref):
+    added = jnp.dot(turned, weight_ref[head], preferred_element_type=jnp.float32)
+    return sum_ref[head] * jnp.exp2(peak_ref[head:head + 1, :] - peak) + added
+
+
+def next_kernel(
+    at, across_ref, bias_ref, peak_ref, sum_ref, pair_ref, new_peak_ref, new_sum_ref,
+    scaled_ref, weight_ref,
+):
     turned = values_down(pair_ref[:, HEAD_WIDTH:])
-    for head in range(across_ref.shape[0]):
-        peak, summed = add_shard(head, bias_ref[at], keys, turned, across_ref, peak_ref, sum_ref)
+
+    def mix(head, peak):
         new_peak_ref[head:head + 1, :] = peak
-        new_sum_ref[head] = summed
-
-
-def last_kernel(at, across_ref, bias_ref, peak_ref, sum_ref, pair_ref, out_ref, block_ref, sems):
-    keys = pair_ref[:, :HEAD_WIDTH]
+        new_sum_ref[head] = joined(head, peak, turned, weight_ref, peak_ref, sum_ref)
+
+    in_stages(across_ref.shape[0], [
+        score_stage(
+            pair_ref[:, :HEAD_WIDTH], across_ref, bias_ref, at, scaled_ref,
+            lambda head: peak_ref[head:head + 1, :],
+        ),
+        weight_stage(scaled_ref, weight_ref),
+        mix,
+    ])
+
+
+def last_kernel(
+    at, across_ref, bias_ref, peak_ref, sum_ref, pair_ref, out_ref,
+    scaled_ref, weight_ref, block_ref, sems,
+):
     turned = values_down(pair_ref[:, HEAD_WIDTH:])
     copies = []
-    for head in range(across_ref.shape[0]):
-        _, summed = add_shard(head, bias_ref[at], keys, turned, across_ref, peak_ref, sum_ref)
-        out = summed[:HEAD_WIDTH] / summed[HEAD_WIDTH:HEAD_WIDTH + 1]
+
+    def mix(head, peak):
+        summed = joined(head, peak, turned, weight_ref, peak_ref, sum_ref)
+        return summed[:HEAD_WIDTH] / summed[HEAD_WIDTH:HEAD_WIDTH + 1]
+
+    def send(head, out):
         cols = slice(head * HEAD_WIDTH, (head + 1) * HEAD_WIDTH)
         block_ref[:, cols] = jnp.transpose(out).astype(jnp.bfloat16)
         copy = pltpu.make_async_copy(block_ref.at[:, cols], out_ref.at[:, cols], sems.at[head])
         copy.start()
         copies.append(copy)
+
+    in_stages(across_ref.shape[0], [
+        score_stage(
+            pair_ref[:, :HEAD_WIDTH], across_ref, bias_ref, at, scaled_ref,
+            lambda head: peak_ref[head:head + 1, :],
+        ),
+        weight_stage(scaled_ref, weight_ref),
+        mix,
+        send,
+    ])
     for copy in copies:
         copy.wait()
 
@@ -139,50 +209,81 @@
     return [pltpu.with_memory_space_constraint(array, pltpu.VMEM) for array in arrays]
 
 
-def staged_attention(queries, keys, values, pairs, lengths, old_place):
+def in_hbm(*arrays):
+    return [pltpu.with_memory_space_constraint(array, pltpu.HBM) for array in arrays]
+
+
+VMEM_REF = pl.BlockSpec(memory_space=pltpu.VMEM)
+HBM_REF = pl.BlockSpec(memory_space=pltpu.HBM)
+PARAMS = pltpu.CompilerParams(vmem_limit_bytes=32 << 20)
+
+
+def packed_pair(keys, values):
+    return pl.pallas_call(
+        pack_kernel,
+        in_specs=[HBM_REF] * 2,
+        out_specs=VMEM_REF,
+        out_shape=pltpu.VMEM((keys.shape[0], 2 * HEAD_WIDTH), keys.dtype),
+        scratch_shapes=[pltpu.SemaphoreType.DMA((2,))],
+        compiler_params=PARAMS,
+        name="pack",
+    )(*in_hbm(keys, values))
+
+
+def staged_attention(queries, own_pair, pairs, lengths, old_place):
     rows, cols = queries.shape
     heads = cols // HEAD_WIDTH
     own = lax.axis_index("seq").astype(jnp.int32).reshape(1)
-    whole = pl.BlockSpec(memory_space=pltpu.VMEM)
-    params = pltpu.CompilerParams(vmem_limit_bytes=32 << 20)
+    places = old_place.reshape(1, -1)
     state = [
         pltpu.VMEM((heads, rows), jnp.float32),
         pltpu.VMEM((heads, HEAD_WIDTH + ONES, rows), jnp.float32),
     ]
+    work = [
+        pltpu.VMEM((heads, rows, rows), jnp.float32),
+        pltpu.VMEM((heads, rows, rows), jnp.bfloat16),
+    ]
+    cost = estimate(rows, heads, rows)
     across, bias, *carried = pl.pallas_call(
         lambda *refs: own_kernel(list(pairs), *refs),
-        in_specs=[pl.BlockSpec(memory_space=pltpu.SMEM)] * 2 + [whole] * 4,
-        out_specs=[whole] * 4,
+        in_specs=[pl.BlockSpec(memory_space=pltpu.SMEM)] + [HBM_REF] * 3 + [VMEM_REF],
+        out_specs=[VMEM_REF] * 4,
         out_shape=[
             pltpu.VMEM((heads, HEAD_WIDTH, rows), jnp.bfloat16),
             pltpu.VMEM((1 + len(pairs), rows, rows), jnp.float32),
         ] + state,
-        compiler_params=params,
-        cost_estimate=estimate(rows, heads, rows),
+        scratch_shapes=[
+            pltpu.SMEM(lengths.shape, jnp.int32),
+            pltpu.VMEM(places.shape, jnp.int32),
+            pltpu.VMEM(queries.shape, jnp.bfloat16),
+        ] + work + [pltpu.SemaphoreType.DMA((3,))],
+        compiler_params=PARAMS,
+        cost_estimate=cost,
         name="own_shard",
-    )(own, lengths, old_place.reshape(1, -1), queries, keys, values)
+    )(own, *in_hbm(lengths, places, queries), *in_vmem(own_pair))
     *early, last = pairs
     for at, mask in enumerate(early):
         carried = pl.pallas_call(
             lambda *refs, at=at: next_kernel(1 + at, *refs),
-            in_specs=[whole] * 5,
-            out_specs=[whole] * 2,
+            in_specs=[VMEM_REF] * 5,
+            out_specs=[VMEM_REF] * 2,
             out_shape=state,
-            compiler_params=params,
-            cost_estimate=estimate(rows, heads, rows),
+            scratch_shapes=work,
+            compiler_params=PARAMS,
+            cost_estimate=cost,
             name="next_shard",
         )(*in_vmem(across, bias, *carried), pairs[mask])
     return pl.pallas_call(
         lambda *refs: last_kernel(1 + len(early), *refs),
-        in_specs=[whole] * 5,
+        in_specs=[VMEM_REF] * 5,
         out_specs=pl.BlockSpec(memory_space=pl.ANY),
         out_shape=jax.ShapeDtypeStruct((rows, cols), jnp.bfloat16),
-        scratch_shapes=[
+        scratch_shapes=work + [
             pltpu.VMEM((rows, cols), jnp.bfloat16),
             pltpu.SemaphoreType.DMA((heads,)),
         ],
-        compiler_params=params,
-        cost_estimate=estimate(rows, heads, rows),
+        compiler_params=PARAMS,
+        cost_estimate=cost,
         name="last_shard",
     )(*in_vmem(across, bias, *carried), pairs[last])
 
@@ -253,12 +354,12 @@
     row_count = queries.shape[0]
     key_count = row_count * devices
     if devices == 4 and key_count <= 1024:
-        own_pair = jnp.concatenate([keys, values], axis=1)
+        own_pair = packed_pair(keys, values)
         pairs = {
             mask: lax.ppermute(own_pair, "seq", [(i, i ^ mask) for i in range(devices)])
             for mask in (2, 1, 3)
         }
-        return staged_attention(queries, keys, values, pairs, lengths, old_place)
+        return staged_attention(queries, own_pair, pairs, lengths, old_place)
     all_keys = lax.all_gather(keys, "seq", axis=0, tiled=True)
     all_values = lax.all_gather(values, "seq", axis=0, tiled=True)
     key_pos, query_pos, starts = block_places(

time: 22.9 us -> 17.8 us (0.78)
  the two profiles are of different devices: /device:TPU:0 before, /device:TPU:23 now
where the time goes in v5:
time: 17.8 us; the launch traced here: 17.7 us
  waiting for transfers between devices  7.51 us (42%)
  Pallas kernels  7.4 us (42%)
  starting transfers between devices  2.71 us (15%)
    ppermute x3, waiting for transfers between devices, body(): lax.ppermute(own_pair, 'seq', [(i, i ^ mask) for i in range(devices)])  7.51 us
    ppermute x3, starting transfers between devices, body(): lax.ppermute(own_pair, 'seq', [(i, i ^ mask) for i in range(devices)])  2.71 us
    pallas_call x1, Pallas kernels, staged_attention(): pl.pallas_call(lambda *refs: own_kernel(list(pairs), *refs), in_specs=[pl...  2.33 us
    pallas_call x2, Pallas kernels, staged_attention(): pl.pallas_call(lambda *refs, at=at: next_kernel(1 + at, *refs), in_specs=...  2.23 us
    pallas_call x1, Pallas kernels, staged_attention(): pl.pallas_call(lambda *refs: last_kernel(1 + len(early), *refs), in_specs...  1.95 us
    pallas_call x1, Pallas kernels, packed_pair(): pl.pallas_call(pack_kernel, in_specs=[HBM_REF] * 2, out_specs=VMEM_REF, o...  0.89 us
  transfers between devices with their start and end apart: 3, of which 3 were waited for; matrix products, arithmetic and copies ran while one was open for 0% of the time, Pallas kernels for 26%

profile of v5, /device:TPU:23, one launch (start us, length us, event | category | flops | bytes accessed | tf_op | source)
XLA Modules:
  0.0 17.7 jit_solution(8029722132920927092)
XLA Ops:
  0.0 0.9 %pack.1.refs_4_ = bf16[256,256]{1,0:T(8,128)(2,1)S(1)} custom-call(bf16[256,128]{1,0:T(8,128)(2,1)} %k_ref.1, bf16[256,128]{1,0:T(8,128)(2,1)} %v_ref.1), custom_call_target="tpu_custom_call" | custom-call | tf_op jit(solution)/shard_map/pack/pallas_call | solution.py:222
  0.9 0.1 collective-permute-start
  1.0 1.3 %collective-permute-start.1 = (bf16[256,256]{1,0:T(8,128)(2,1)S(1)}, bf16[256,256]{1,0:T(8,128)(2,1)S(1)}, u32[]{:S(2)}, u32[]{:S(2)}) collective-permute-start(bf16[256,256]{1,0:T(8,128)(2,1)S(1)} %pack.1.refs_4_), channel_id=1, source_target_pairs={{0,4},{4,0},{8,12},{12,8},{1,5},{5,1},{9,13},{13,9},{2,6},{6,2},{1... | collective-permute-start | bytes 393224 | tf_op jit(solution)/shard_map/ppermute | solution.py:359
  2.3 1.3 %collective-permute-start.2 = (bf16[256,256]{1,0:T(8,128)(2,1)S(1)}, bf16[256,256]{1,0:T(8,128)(2,1)S(1)}, u32[]{:S(2)}, u32[]{:S(2)}) collective-permute-start(bf16[256,256]{1,0:T(8,128)(2,1)S(1)} %pack.1.refs_4_), channel_id=1, source_target_pairs={{0,12},{4,8},{8,4},{12,0},{1,13},{5,9},{9,5},{13,1},{2,14},{6,10},... | collective-permute-start | bytes 393224 | tf_op jit(solution)/shard_map/ppermute | solution.py:359
  3.6 2.3 %own_shard.1 = (bf16[8,128,256]{2,1,0:T(8,128)(2,1)S(1)}, f32[4,256,256]{2,1,0:T(8,128)S(1)}, f32[8,256]{1,0:T(8,128)S(1)}, f32[8,144,256]{2,1,0:T(8,128)S(1)}) custom-call(s32[1]{0:T(128)} %bitcast.refs_0_, s32[3]{0:T(128)} %refs_1_.1, s32[1,128]{1,0:T(1,128)} %bitcast.2, bf16[256,1024]{1,0:T(8,128)(2,1)} %refs_3_.1, bf16[256,256]{1,0:T(8,128)(2,1)S(1)} %pack.1.refs_4_), custom_call_target="tpu_custom_call" | custom-call | flops 402653184 | bytes 2097152 | tf_op jit(solution)/shard_map/own_shard/pallas_call | solution.py:247
  5.9 0.3 %collective-permute-done.refs_4_ = bf16[256,256]{1,0:T(8,128)(2,1)S(1)} collective-permute-done((bf16[256,256]{1,0:T(8,128)(2,1)S(1)}, bf16[256,256]{1,0:T(8,128)(2,1)S(1)}, u32[]{:S(2)}, u32[]{:S(2)}) %collective-permute-start) | collective-permute-done | bytes 131104 | tf_op jit(solution)/shard_map/ppermute | solution.py:359
  6.2 1.1 %next_shard.2 = (f32[8,256]{1,0:T(8,128)S(1)}, f32[8,144,256]{2,1,0:T(8,128)S(1)}) custom-call(bf16[8,128,256]{2,1,0:T(8,128)(2,1)S(1)} %get-tuple-element.13.refs_0_, f32[4,256,256]{2,1,0:T(8,128)S(1)} %get-tuple-element.14.refs_1_, f32[8,256]{1,0:T(8,128)S(1)} %get-tuple-element.15.refs_2_, f32[8,144,256]{2,1,0:T(8,128)S(1)} %get-tuple-element.16.refs_3_, ...), custom_call_target="tpu_custom_call" | custom-call | flops 402653184 | bytes 2097152 | tf_op jit(solution)/shard_map/next_shard/pallas_call | solution.py:266
  7.3 0.8 %collective-permute-done.1.refs_4_ = bf16[256,256]{1,0:T(8,128)(2,1)S(1)} collective-permute-done((bf16[256,256]{1,0:T(8,128)(2,1)S(1)}, bf16[256,256]{1,0:T(8,128)(2,1)S(1)}, u32[]{:S(2)}, u32[]{:S(2)}) %collective-permute-start.1) | collective-permute-done | bytes 131104 | tf_op jit(solution)/shard_map/ppermute | solution.py:359
  8.1 1.1 %next_shard.3 = (f32[8,256]{1,0:T(8,128)S(1)}, f32[8,144,256]{2,1,0:T(8,128)S(1)}) custom-call(bf16[8,128,256]{2,1,0:T(8,128)(2,1)S(1)} %get-tuple-element.13.refs_0_, f32[4,256,256]{2,1,0:T(8,128)S(1)} %get-tuple-element.14.refs_1_, f32[8,256]{1,0:T(8,128)S(1)} %get-tuple-element.17.refs_2_, f32[8,144,256]{2,1,0:T(8,128)S(1)} %get-tuple-element.18.refs_3_, ...), custom_call_target="tpu_custom_call" | custom-call | flops 402653184 | bytes 2097152 | tf_op jit(solution)/shard_map/next_shard/pallas_call | solution.py:266
  9.2 6.5 %collective-permute-done.2.refs_4_ = bf16[256,256]{1,0:T(8,128)(2,1)S(1)} collective-permute-done((bf16[256,256]{1,0:T(8,128)(2,1)S(1)}, bf16[256,256]{1,0:T(8,128)(2,1)S(1)}, u32[]{:S(2)}, u32[]{:S(2)}) %collective-permute-start.2) | collective-permute-done | bytes 131104 | tf_op jit(solution)/shard_map/ppermute | solution.py:359
  15.7 1.9 %last_shard.1 = bf16[256,1024]{1,0:T(8,128)(2,1)} custom-call(bf16[8,128,256]{2,1,0:T(8,128)(2,1)S(1)} %get-tuple-element.13.refs_0_, f32[4,256,256]{2,1,0:T(8,128)S(1)} %get-tuple-element.14.refs_1_, f32[8,256]{1,0:T(8,128)S(1)} %get-tuple-element.19.refs_2_, f32[8,144,256]{2,1,0:T(8,128)S(1)} %get-tuple-element.20.refs_3_, ...), custom_call_target="tpu_custom_call" | custom-call | flops 402653184 | bytes 2097152 | tf_op jit(solution)/shard_map/last_shard/pallas_call | solution.py:276
Async XLA Ops:
  0.9 5.3 %collective-permute-start = (bf16[256,256]{1,0:T(8,128)(2,1)S(1)}, bf16[256,256]{1,0:T(8,128)(2,1)S(1)}, u32[]{:S(2)}, u32[]{:S(2)}) collective-permute-start(bf16[256,256]{1,0:T(8,128)(2,1)S(1)} %pack.1.refs_4_), channel_id=1, source_target_pairs={{0,8},{4,12},{8,0},{12,4},{1,9},{5,13},{9,1},{13,5},{2,10},{6,14},... | collective-permute-start | bytes 393224 | tf_op jit(solution)/shard_map/ppermute | solution.py:359
  1.0 7.1 %collective-permute-start.1 = (bf16[256,256]{1,0:T(8,128)(2,1)S(1)}, bf16[256,256]{1,0:T(8,128)(2,1)S(1)}, u32[]{:S(2)}, u32[]{:S(2)}) collective-permute-start(bf16[256,256]{1,0:T(8,128)(2,1)S(1)} %pack.1.refs_4_), channel_id=1, source_target_pairs={{0,4},{4,0},{8,12},{12,8},{1,5},{5,1},{9,13},{13,9},{2,6},{6,2},{1... | collective-permute-start | bytes 393224 | tf_op jit(solution)/shard_map/ppermute | solution.py:359
  2.3 13.4 %collective-permute-start.2 = (bf16[256,256]{1,0:T(8,128)(2,1)S(1)}, bf16[256,256]{1,0:T(8,128)(2,1)S(1)}, u32[]{:S(2)}, u32[]{:S(2)}) collective-permute-start(bf16[256,256]{1,0:T(8,128)(2,1)S(1)} %pack.1.refs_4_), channel_id=1, source_target_pairs={{0,12},{4,8},{8,4},{12,0},{1,13},{5,9},{9,5},{13,1},{2,14},{6,10},... | collective-permute-start | bytes 393224 | tf_op jit(solution)/shard_map/ppermute | solution.py:359

commit v6 on v5

--- a/solution.py
+++ b/solution.py
@@ -349,16 +349,20 @@
     )(queries, keys, values, key_pos, query_pos, starts)
 
 
+def moved(value, mask, devices):
+    return lax.ppermute(value, "seq", [(i, i ^ mask) for i in range(devices)])
+
+
 def body(queries, keys, values, lengths, old_place):
     devices = lax.axis_size("seq")
     row_count = queries.shape[0]
     key_count = row_count * devices
     if devices == 4 and key_count <= 1024:
         own_pair = packed_pair(keys, values)
-        pairs = {
-            mask: lax.ppermute(own_pair, "seq", [(i, i ^ mask) for i in range(devices)])
-            for mask in (2, 1, 3)
-        }
+        pairs = {}
+        pairs[2] = moved(own_pair, 2, devices)
+        pairs[1] = moved(own_pair, 1, devices)
+        pairs[3] = moved(pairs[2], 1, devices)
         return staged_attention(queries, own_pair, pairs, lengths, old_place)
     all_keys = lax.all_gather(keys, "seq", axis=0, tiled=True)
     all_values = lax.all_gather(values, "seq", axis=0, tiled=True)

time: 17.8 us -> 18.8 us (1.056)
  the two profiles are of different devices: /device:TPU:23 before, /device:TPU:0 now
where the time goes in v6:
time: 18.8 us; the launch traced here: 18.6 us
  Pallas kernels  7.41 us (39%)
  starting transfers between devices  6.29 us (33%)
  waiting for transfers between devices  4.84 us (26%)
    ppermute x3, starting transfers between devices, moved(): return lax.ppermute(value, 'seq', [(i, i ^ mask) for i in range(devices)])  6.29 us
    ppermute x3, waiting for transfers between devices, moved(): return lax.ppermute(value, 'seq', [(i, i ^ mask) for i in range(devices)])  4.84 us
    pallas_call x1, Pallas kernels, staged_attention(): pl.pallas_call(lambda *refs: own_kernel(list(pairs), *refs), in_specs=[pl...  2.33 us
    pallas_call x2, Pallas kernels, staged_attention(): pl.pallas_call(lambda *refs, at=at: next_kernel(1 + at, *refs), in_specs=...  2.24 us
    pallas_call x1, Pallas kernels, staged_attention(): pl.pallas_call(lambda *refs: last_kernel(1 + len(early), *refs), in_specs...  1.95 us
    pallas_call x1, Pallas kernels, packed_pair(): pl.pallas_call(pack_kernel, in_specs=[HBM_REF] * 2, out_specs=VMEM_REF, o...  0.89 us
  transfers between devices with their start and end apart: 3, of which 1 were waited for; matrix products, arithmetic and copies ran while one was open for 0% of the time, Pallas kernels for 25%

profile of v6, /device:TPU:0, one launch (start us, length us, event | category | flops | bytes accessed | tf_op | source)
XLA Modules:
  0.0 18.6 jit_solution(8995893490578159972)
XLA Ops:
  0.0 0.9 %pack.1.refs_4_ = bf16[256,256]{1,0:T(8,128)(2,1)S(1)} custom-call(bf16[256,128]{1,0:T(8,128)(2,1)} %k_ref.1, bf16[256,128]{1,0:T(8,128)(2,1)} %v_ref.1), custom_call_target="tpu_custom_call" | custom-call | tf_op jit(solution)/shard_map/pack/pallas_call | solution.py:222
  0.9 4.1 %collective-permute-start = (bf16[256,256]{1,0:T(8,128)(2,1)S(1)}, bf16[256,256]{1,0:T(8,128)(2,1)S(1)}, u32[]{:S(2)}, u32[]{:S(2)}) collective-permute-start(bf16[256,256]{1,0:T(8,128)(2,1)S(1)} %pack.1.refs_4_), channel_id=1, source_target_pairs={{0,8},{4,12},{8,0},{12,4},{1,9},{5,13},{9,1},{13,5},{2,10},{6,14},... | collective-permute-start | bytes 393224 | tf_op jit(solution)/shard_map/ppermute | solution.py:353
  5.0 1.6 %collective-permute-start.1 = (bf16[256,256]{1,0:T(8,128)(2,1)S(1)}, bf16[256,256]{1,0:T(8,128)(2,1)S(1)}, u32[]{:S(2)}, u32[]{:S(2)}) collective-permute-start(bf16[256,256]{1,0:T(8,128)(2,1)S(1)} %pack.1.refs_4_), channel_id=1, source_target_pairs={{0,4},{4,0},{8,12},{12,8},{1,5},{5,1},{9,13},{13,9},{2,6},{6,2},{1... | collective-permute-start | bytes 393224 | tf_op jit(solution)/shard_map/ppermute | solution.py:353
  6.6 4.8 %collective-permute-done.refs_4_ = bf16[256,256]{1,0:T(8,128)(2,1)S(1)} collective-permute-done((bf16[256,256]{1,0:T(8,128)(2,1)S(1)}, bf16[256,256]{1,0:T(8,128)(2,1)S(1)}, u32[]{:S(2)}, u32[]{:S(2)}) %collective-permute-start) | collective-permute-done | bytes 131104 | tf_op jit(solution)/shard_map/ppermute | solution.py:353
  11.4 0.6 %collective-permute-start.2 = (bf16[256,256]{1,0:T(8,128)(2,1)S(1)}, bf16[256,256]{1,0:T(8,128)(2,1)S(1)}, u32[]{:S(2)}, u32[]{:S(2)}) collective-permute-start(bf16[256,256]{1,0:T(8,128)(2,1)S(1)} %collective-permute-done.refs_4_), channel_id=1, source_target_pairs={{0,4},{4,0},{8,12},{12,8},{1,5},{5,1},{9,13},{13,9},{2,6},{6,2},{1... | collective-permute-start | bytes 393224 | tf_op jit(solution)/shard_map/ppermute | solution.py:353
  12.0 2.3 %own_shard.1 = (bf16[8,128,256]{2,1,0:T(8,128)(2,1)S(1)}, f32[4,256,256]{2,1,0:T(8,128)S(1)}, f32[8,256]{1,0:T(8,128)S(1)}, f32[8,144,256]{2,1,0:T(8,128)S(1)}) custom-call(s32[1]{0:T(128)} %bitcast.refs_0_, s32[3]{0:T(128)} %refs_1_.1, s32[1,128]{1,0:T(1,128)} %bitcast.2, bf16[256,1024]{1,0:T(8,128)(2,1)} %refs_3_.1, bf16[256,256]{1,0:T(8,128)(2,1)S(1)} %pack.1.refs_4_), custom_call_target="tpu_custom_call" | custom-call | flops 402653184 | bytes 2097152 | tf_op jit(solution)/shard_map/own_shard/pallas_call | solution.py:247
  14.4 1.1 %next_shard.2 = (f32[8,256]{1,0:T(8,128)S(1)}, f32[8,144,256]{2,1,0:T(8,128)S(1)}) custom-call(bf16[8,128,256]{2,1,0:T(8,128)(2,1)S(1)} %get-tuple-element.13.refs_0_, f32[4,256,256]{2,1,0:T(8,128)S(1)} %get-tuple-element.14.refs_1_, f32[8,256]{1,0:T(8,128)S(1)} %get-tuple-element.15.refs_2_, f32[8,144,256]{2,1,0:T(8,128)S(1)} %get-tuple-element.16.refs_3_, ...), custom_call_target="tpu_custom_call" | custom-call | flops 402653184 | bytes 2097152 | tf_op jit(solution)/shard_map/next_shard/pallas_call | solution.py:266
  15.5 0.0 collective-permute-done.1.refs_4_
  15.5 1.1 %next_shard.3 = (f32[8,256]{1,0:T(8,128)S(1)}, f32[8,144,256]{2,1,0:T(8,128)S(1)}) custom-call(bf16[8,128,256]{2,1,0:T(8,128)(2,1)S(1)} %get-tuple-element.13.refs_0_, f32[4,256,256]{2,1,0:T(8,128)S(1)} %get-tuple-element.14.refs_1_, f32[8,256]{1,0:T(8,128)S(1)} %get-tuple-element.17.refs_2_, f32[8,144,256]{2,1,0:T(8,128)S(1)} %get-tuple-element.18.refs_3_, ...), custom_call_target="tpu_custom_call" | custom-call | flops 402653184 | bytes 2097152 | tf_op jit(solution)/shard_map/next_shard/pallas_call | solution.py:266
  16.6 0.0 collective-permute-done.2.refs_4_
  16.6 2.0 %last_shard.1 = bf16[256,1024]{1,0:T(8,128)(2,1)} custom-call(bf16[8,128,256]{2,1,0:T(8,128)(2,1)S(1)} %get-tuple-element.13.refs_0_, f32[4,256,256]{2,1,0:T(8,128)S(1)} %get-tuple-element.14.refs_1_, f32[8,256]{1,0:T(8,128)S(1)} %get-tuple-element.19.refs_2_, f32[8,144,256]{2,1,0:T(8,128)S(1)} %get-tuple-element.20.refs_3_, ...), custom_call_target="tpu_custom_call" | custom-call | flops 402653184 | bytes 2097152 | tf_op jit(solution)/shard_map/last_shard/pallas_call | solution.py:276
Async XLA Ops:
  0.9 10.5 %collective-permute-start = (bf16[256,256]{1,0:T(8,128)(2,1)S(1)}, bf16[256,256]{1,0:T(8,128)(2,1)S(1)}, u32[]{:S(2)}, u32[]{:S(2)}) collective-permute-start(bf16[256,256]{1,0:T(8,128)(2,1)S(1)} %pack.1.refs_4_), channel_id=1, source_target_pairs={{0,8},{4,12},{8,0},{12,4},{1,9},{5,13},{9,1},{13,5},{2,10},{6,14},... | collective-permute-start | bytes 393224 | tf_op jit(solution)/shard_map/ppermute | solution.py:353
  5.0 10.5 %collective-permute-start.1 = (bf16[256,256]{1,0:T(8,128)(2,1)S(1)}, bf16[256,256]{1,0:T(8,128)(2,1)S(1)}, u32[]{:S(2)}, u32[]{:S(2)}) collective-permute-start(bf16[256,256]{1,0:T(8,128)(2,1)S(1)} %pack.1.refs_4_), channel_id=1, source_target_pairs={{0,4},{4,0},{8,12},{12,8},{1,5},{5,1},{9,13},{13,9},{2,6},{6,2},{1... | collective-permute-start | bytes 393224 | tf_op jit(solution)/shard_map/ppermute | solution.py:353
  11.4 5.2 %collective-permute-start.2 = (bf16[256,256]{1,0:T(8,128)(2,1)S(1)}, bf16[256,256]{1,0:T(8,128)(2,1)S(1)}, u32[]{:S(2)}, u32[]{:S(2)}) collective-permute-start(bf16[256,256]{1,0:T(8,128)(2,1)S(1)} %collective-permute-done.refs_4_), channel_id=1, source_target_pairs={{0,4},{4,0},{8,12},{12,8},{1,5},{5,1},{9,13},{13,9},{2,6},{6,2},{1... | collective-permute-start | bytes 393224 | tf_op jit(solution)/shard_map/ppermute | solution.py:353

commit v7 on v6

--- a/solution.py
+++ b/solution.py
@@ -233,6 +233,8 @@
 def staged_attention(queries, own_pair, pairs, lengths, old_place):
     rows, cols = queries.shape
     heads = cols // HEAD_WIDTH
+    devices = lax.axis_size("seq")
+    masks = (1, 2, 3)
     own = lax.axis_index("seq").astype(jnp.int32).reshape(1)
     places = old_place.reshape(1, -1)
     state = [
@@ -245,12 +247,12 @@
     ]
     cost = estimate(rows, heads, rows)
     across, bias, *carried = pl.pallas_call(
-        lambda *refs: own_kernel(list(pairs), *refs),
+        lambda *refs: own_kernel(masks, *refs),
         in_specs=[pl.BlockSpec(memory_space=pltpu.SMEM)] + [HBM_REF] * 3 + [VMEM_REF],
         out_specs=[VMEM_REF] * 4,
         out_shape=[
             pltpu.VMEM((heads, HEAD_WIDTH, rows), jnp.bfloat16),
-            pltpu.VMEM((1 + len(pairs), rows, rows), jnp.float32),
+            pltpu.VMEM((devices, rows, rows), jnp.float32),
         ] + state,
         scratch_shapes=[
             pltpu.SMEM(lengths.shape, jnp.int32),
@@ -261,10 +263,11 @@
         cost_estimate=cost,
         name="own_shard",
     )(own, *in_hbm(lengths, places, queries), *in_vmem(own_pair))
-    *early, last = pairs
-    for at, mask in enumerate(early):
+    relayed, *carried = lax.optimization_barrier((pairs[2], *carried))
+    pairs[3] = moved(relayed, 1, devices)
+    for mask in (2, 1):
         carried = pl.pallas_call(
-            lambda *refs, at=at: next_kernel(1 + at, *refs),
+            lambda *refs, mask=mask: next_kernel(mask, *refs),
             in_specs=[VMEM_REF] * 5,
             out_specs=[VMEM_REF] * 2,
             out_shape=state,
@@ -274,7 +277,7 @@
             name="next_shard",
         )(*in_vmem(across, bias, *carried), pairs[mask])
     return pl.pallas_call(
-        lambda *refs: last_kernel(1 + len(early), *refs),
+        lambda *refs: last_kernel(3, *refs),
         in_specs=[VMEM_REF] * 5,
         out_specs=pl.BlockSpec(memory_space=pl.ANY),
         out_shape=jax.ShapeDtypeStruct((rows, cols), jnp.bfloat16),
@@ -285,7 +288,7 @@
         compiler_params=PARAMS,
         cost_estimate=cost,
         name="last_shard",
-    )(*in_vmem(across, bias, *carried), pairs[last])
+    )(*in_vmem(across, bias, *carried), pairs[3])
 
 
 def online_kernel(heads, q_ref, k_ref, v_ref, key_pos_ref, query_pos_ref, start_ref, out_ref, peak_ref, acc_ref):
@@ -362,7 +365,6 @@
         pairs = {}
         pairs[2] = moved(own_pair, 2, devices)
         pairs[1] = moved(own_pair, 1, devices)
-        pairs[3] = moved(pairs[2], 1, devices)
         return staged_attention(queries, own_pair, pairs, lengths, old_place)
     all_keys = lax.all_gather(keys, "seq", axis=0, tiled=True)
     all_values = lax.all_gather(values, "seq", axis=0, tiled=True)

time: 18.8 us -> 18.5 us (0.984)
  waiting for transfers between devices: 4.84 us -> 4.59 us
    ppermute x3, waiting for transfers between devices: 4.84 us -> 4.59 us  [moved(): return lax.ppermute(value, 'seq', [(i, i ^ mask) for i in range(devices)])]
  transfers between devices with their start and end apart: 3 -> 3, of which waited for: 1 -> 2; matrix products, arithmetic and copies ran while one was open for 0% -> 0% of each run, Pallas kernels for 25% -> 25%
where the time goes in v7:
time: 18.5 us; the launch traced here: 18.3 us
  Pallas kernels  7.4 us (40%)
  starting transfers between devices  6.29 us (34%)
  waiting for transfers between devices  4.59 us (25%)
    ppermute x3, starting transfers between devices, moved(): return lax.ppermute(value, 'seq', [(i, i ^ mask) for i in range(devices)])  6.29 us
    ppermute x3, waiting for transfers between devices, moved(): return lax.ppermute(value, 'seq', [(i, i ^ mask) for i in range(devices)])  4.59 us
    pallas_call x1, Pallas kernels, staged_attention(): pl.pallas_call(lambda *refs: own_kernel(masks, *refs), in_specs=[pl.Block...  2.33 us
    pallas_call x2, Pallas kernels, staged_attention(): pl.pallas_call(lambda *refs, mask=mask: next_kernel(mask, *refs), in_spec...  2.24 us
    pallas_call x1, Pallas kernels, staged_attention(): pl.pallas_call(lambda *refs: last_kernel(3, *refs), in_specs=[VMEM_REF] *...  1.95 us
    pallas_call x1, Pallas kernels, packed_pair(): pl.pallas_call(pack_kernel, in_specs=[HBM_REF] * 2, out_specs=VMEM_REF, o...  0.89 us
  transfers between devices with their start and end apart: 3, of which 2 were waited for; matrix products, arithmetic and copies ran while one was open for 0% of the time, Pallas kernels for 25%

profile of v7, /device:TPU:0, one launch (start us, length us, event | category | flops | bytes accessed | tf_op | source)
XLA Modules:
  0.0 18.3 jit_solution(770292115544979911)
XLA Ops:
  0.0 0.9 %pack.1.refs_4_ = bf16[256,256]{1,0:T(8,128)(2,1)S(1)} custom-call(bf16[256,128]{1,0:T(8,128)(2,1)} %k_ref.1, bf16[256,128]{1,0:T(8,128)(2,1)} %v_ref.1), custom_call_target="tpu_custom_call" | custom-call | tf_op jit(solution)/shard_map/pack/pallas_call | solution.py:222
  0.9 4.1 %collective-permute-start = (bf16[256,256]{1,0:T(8,128)(2,1)S(1)}, bf16[256,256]{1,0:T(8,128)(2,1)S(1)}, u32[]{:S(2)}, u32[]{:S(2)}) collective-permute-start(bf16[256,256]{1,0:T(8,128)(2,1)S(1)} %pack.1.refs_4_), channel_id=1, source_target_pairs={{0,8},{4,12},{8,0},{12,4},{1,9},{5,13},{9,1},{13,5},{2,10},{6,14},... | collective-permute-start | bytes 393224 | tf_op jit(solution)/shard_map/ppermute | solution.py:356
  5.0 1.6 %collective-permute-start.1 = (bf16[256,256]{1,0:T(8,128)(2,1)S(1)}, bf16[256,256]{1,0:T(8,128)(2,1)S(1)}, u32[]{:S(2)}, u32[]{:S(2)}) collective-permute-start(bf16[256,256]{1,0:T(8,128)(2,1)S(1)} %pack.1.refs_4_), channel_id=1, source_target_pairs={{0,4},{4,0},{8,12},{12,8},{1,5},{5,1},{9,13},{13,9},{2,6},{6,2},{1... | collective-permute-start | bytes 393224 | tf_op jit(solution)/shard_map/ppermute | solution.py:356
  6.6 2.3 %own_shard.1 = (bf16[8,128,256]{2,1,0:T(8,128)(2,1)S(1)}, f32[4,256,256]{2,1,0:T(8,128)S(1)}, f32[8,256]{1,0:T(8,128)S(1)}, f32[8,144,256]{2,1,0:T(8,128)S(1)}) custom-call(s32[1]{0:T(128)} %bitcast.refs_0_, s32[3]{0:T(128)} %refs_1_.1, s32[1,128]{1,0:T(1,128)} %bitcast.2, bf16[256,1024]{1,0:T(8,128)(2,1)} %refs_3_.1, bf16[256,256]{1,0:T(8,128)(2,1)S(1)} %pack.1.refs_4_), custom_call_target="tpu_custom_call" | custom-call | flops 402653184 | bytes 2097152 | tf_op jit(solution)/shard_map/own_shard/pallas_call | solution.py:249
  8.9 2.5 %collective-permute-done.refs_4_ = bf16[256,256]{1,0:T(8,128)(2,1)S(1)} collective-permute-done((bf16[256,256]{1,0:T(8,128)(2,1)S(1)}, bf16[256,256]{1,0:T(8,128)(2,1)S(1)}, u32[]{:S(2)}, u32[]{:S(2)}) %collective-permute-start) | collective-permute-done | bytes 131104 | tf_op jit(solution)/shard_map/ppermute | solution.py:356
  11.4 0.6 %collective-permute-start.2 = (bf16[256,256]{1,0:T(8,128)(2,1)S(1)}, bf16[256,256]{1,0:T(8,128)(2,1)S(1)}, u32[]{:S(2)}, u32[]{:S(2)}) collective-permute-start(bf16[256,256]{1,0:T(8,128)(2,1)S(1)} %collective-permute-done.refs_4_), channel_id=1, source_target_pairs={{0,4},{4,0},{8,12},{12,8},{1,5},{5,1},{9,13},{13,9},{2,6},{6,2},{1... | collective-permute-start | bytes 393224 | tf_op jit(solution)/shard_map/ppermute | solution.py:356
  12.0 1.1 %next_shard.2 = (f32[8,256]{1,0:T(8,128)S(1)}, f32[8,144,256]{2,1,0:T(8,128)S(1)}) custom-call(bf16[8,128,256]{2,1,0:T(8,128)(2,1)S(1)} %get-tuple-element.16.refs_0_, f32[4,256,256]{2,1,0:T(8,128)S(1)} %get-tuple-element.17.refs_1_, f32[8,256]{1,0:T(8,128)S(1)} %get-tuple-element.20.refs_2_, f32[8,144,256]{2,1,0:T(8,128)S(1)} %get-tuple-element.21.refs_3_, ...), custom_call_target="tpu_custom_call" | custom-call | flops 402653184 | bytes 2097152 | tf_op jit(solution)/shard_map/next_shard/pallas_call | solution.py:269
  13.1 0.0 collective-permute-done.1.refs_4_
  13.2 1.1 %next_shard.3 = (f32[8,256]{1,0:T(8,128)S(1)}, f32[8,144,256]{2,1,0:T(8,128)S(1)}) custom-call(bf16[8,128,256]{2,1,0:T(8,128)(2,1)S(1)} %get-tuple-element.16.refs_0_, f32[4,256,256]{2,1,0:T(8,128)S(1)} %get-tuple-element.17.refs_1_, f32[8,256]{1,0:T(8,128)S(1)} %get-tuple-element.22.refs_2_, f32[8,144,256]{2,1,0:T(8,128)S(1)} %get-tuple-element.23.refs_3_, ...), custom_call_target="tpu_custom_call" | custom-call | flops 402653184 | bytes 2097152 | tf_op jit(solution)/shard_map/next_shard/pallas_call | solution.py:269
  14.3 2.1 %collective-permute-done.2.refs_4_ = bf16[256,256]{1,0:T(8,128)(2,1)S(1)} collective-permute-done((bf16[256,256]{1,0:T(8,128)(2,1)S(1)}, bf16[256,256]{1,0:T(8,128)(2,1)S(1)}, u32[]{:S(2)}, u32[]{:S(2)}) %collective-permute-start.2) | collective-permute-done | bytes 131104 | tf_op jit(solution)/shard_map/ppermute | solution.py:356
  16.4 1.9 %last_shard.1 = bf16[256,1024]{1,0:T(8,128)(2,1)} custom-call(bf16[8,128,256]{2,1,0:T(8,128)(2,1)S(1)} %get-tuple-element.16.refs_0_, f32[4,256,256]{2,1,0:T(8,128)S(1)} %get-tuple-element.17.refs_1_, f32[8,256]{1,0:T(8,128)S(1)} %get-tuple-element.24.refs_2_, f32[8,144,256]{2,1,0:T(8,128)S(1)} %get-tuple-element.25.refs_3_, ...), custom_call_target="tpu_custom_call" | custom-call | flops 402653184 | bytes 2097152 | tf_op jit(solution)/shard_map/last_shard/pallas_call | solution.py:279
Async XLA Ops:
  0.9 10.5 %collective-permute-start = (bf16[256,256]{1,0:T(8,128)(2,1)S(1)}, bf16[256,256]{1,0:T(8,128)(2,1)S(1)}, u32[]{:S(2)}, u32[]{:S(2)}) collective-permute-start(bf16[256,256]{1,0:T(8,128)(2,1)S(1)} %pack.1.refs_4_), channel_id=1, source_target_pairs={{0,8},{4,12},{8,0},{12,4},{1,9},{5,13},{9,1},{13,5},{2,10},{6,14},... | collective-permute-start | bytes 393224 | tf_op jit(solution)/shard_map/ppermute | solution.py:356
  5.0 8.2 %collective-permute-start.1 = (bf16[256,256]{1,0:T(8,128)(2,1)S(1)}, bf16[256,256]{1,0:T(8,128)(2,1)S(1)}, u32[]{:S(2)}, u32[]{:S(2)}) collective-permute-start(bf16[256,256]{1,0:T(8,128)(2,1)S(1)} %pack.1.refs_4_), channel_id=1, source_target_pairs={{0,4},{4,0},{8,12},{12,8},{1,5},{5,1},{9,13},{13,9},{2,6},{6,2},{1... | collective-permute-start | bytes 393224 | tf_op jit(solution)/shard_map/ppermute | solution.py:356
  11.4 5.0 %collective-permute-start.2 = (bf16[256,256]{1,0:T(8,128)(2,1)S(1)}, bf16[256,256]{1,0:T(8,128)(2,1)S(1)}, u32[]{:S(2)}, u32[]{:S(2)}) collective-permute-start(bf16[256,256]{1,0:T(8,128)(2,1)S(1)} %collective-permute-done.refs_4_), channel_id=1, source_target_pairs={{0,4},{4,0},{8,12},{12,8},{1,5},{5,1},{9,13},{13,9},{2,6},{6,2},{1... | collective-permute-start | bytes 393224 | tf_op jit(solution)/shard_map/ppermute | solution.py:356

commit v8 on v5

--- a/solution.py
+++ b/solution.py
@@ -141,20 +141,13 @@
     ])
 
 
-def joined(head, peak, turned, weight_ref, peak_ref, sum_ref):
-    added = jnp.dot(turned, weight_ref[head], preferred_element_type=jnp.float32)
-    return sum_ref[head] * jnp.exp2(peak_ref[head:head + 1, :] - peak) + added
-
-
-def next_kernel(
-    at, across_ref, bias_ref, peak_ref, sum_ref, pair_ref, new_peak_ref, new_sum_ref,
-    scaled_ref, weight_ref,
-):
+def join_shard(at, across_ref, bias_ref, pair_ref, peak_ref, sum_ref, scaled_ref, weight_ref):
     turned = values_down(pair_ref[:, HEAD_WIDTH:])
 
     def mix(head, peak):
-        new_peak_ref[head:head + 1, :] = peak
-        new_sum_ref[head] = joined(head, peak, turned, weight_ref, peak_ref, sum_ref)
+        added = jnp.dot(turned, weight_ref[head], preferred_element_type=jnp.float32)
+        sum_ref[head] = sum_ref[head] * jnp.exp2(peak_ref[head:head + 1, :] - peak) + added
+        peak_ref[head:head + 1, :] = peak
 
     in_stages(across_ref.shape[0], [
         score_stage(
@@ -166,35 +159,65 @@
     ])
 
 
+def is_one_of(own, members):
+    found = own == members[0]
+    for member in members[1:]:
+        found = found | (own == member)
+    return found
+
+
+def next_kernel(
+    at, members, own_ref, across_ref, bias_ref, pair_ref, old_peak_ref, old_sum_ref,
+    peak_ref, sum_ref, scaled_ref, weight_ref,
+):
+    @pl.when(is_one_of(own_ref[0], members))
+    def _():
+        join_shard(at, across_ref, bias_ref, pair_ref, peak_ref, sum_ref, scaled_ref, weight_ref)
+
+
 def last_kernel(
-    at, across_ref, bias_ref, peak_ref, sum_ref, pair_ref, out_ref,
-    scaled_ref, weight_ref, block_ref, sems,
+    at, members, own_ref, across_ref, bias_ref, pair_ref, old_peak_ref, old_sum_ref,
+    peak_ref, sum_ref, out_ref, scaled_ref, weight_ref, block_ref, sems,
 ):
-    turned = values_down(pair_ref[:, HEAD_WIDTH:])
-    copies = []
-
-    def mix(head, peak):
-        summed = joined(head, peak, turned, weight_ref, peak_ref, sum_ref)
-        return summed[:HEAD_WIDTH] / summed[HEAD_WIDTH:HEAD_WIDTH + 1]
-
-    def send(head, out):
+    heads = across_ref.shape[0]
+
+    def copy_of(head):
         cols = slice(head * HEAD_WIDTH, (head + 1) * HEAD_WIDTH)
+        return pltpu.make_async_copy(block_ref.at[:, cols], out_ref.at[:, cols], sems.at[head])
+
+    def finish(head, summed):
+        cols = slice(head * HEAD_WIDTH, (head + 1) * HEAD_WIDTH)
+        out = summed[:HEAD_WIDTH] / summed[HEAD_WIDTH:HEAD_WIDTH + 1]
         block_ref[:, cols] = jnp.transpose(out).astype(jnp.bfloat16)
-        copy = pltpu.make_async_copy(block_ref.at[:, cols], out_ref.at[:, cols], sems.at[head])
-        copy.start()
-        copies.append(copy)
-
-    in_stages(across_ref.shape[0], [
-        score_stage(
-            pair_ref[:, :HEAD_WIDTH], across_ref, bias_ref, at, scaled_ref,
-            lambda head: peak_ref[head:head + 1, :],
-        ),
-        weight_stage(scaled_ref, weight_ref),
-        mix,
-        send,
-    ])
-    for copy in copies:
-        copy.wait()
+        copy_of(head).start()
+
+    active = is_one_of(own_ref[0], members)
+
+    @pl.when(active)
+    def _():
+        turned = values_down(pair_ref[:, HEAD_WIDTH:])
+
+        def mix(head, peak):
+            added = jnp.dot(turned, weight_ref[head], preferred_element_type=jnp.float32)
+            return sum_ref[head] * jnp.exp2(peak_ref[head:head + 1, :] - peak) + added
+
+        in_stages(heads, [
+            score_stage(
+                pair_ref[:, :HEAD_WIDTH], across_ref, bias_ref, at, scaled_ref,
+                lambda head: peak_ref[head:head + 1, :],
+            ),
+            weight_stage(scaled_ref, weight_ref),
+            mix,
+            finish,
+        ])
+
+    @pl.when(jnp.logical_not(active))
+    def _():
+        for head in range(heads):
+            finish(head, sum_ref[head])
+
+    for head in range(heads):
+        copy_of(head).wait()
 
 
 def estimate(rows, heads, key_count):
@@ -230,7 +253,7 @@
     )(*in_hbm(keys, values))
 
 
-def staged_attention(queries, own_pair, pairs, lengths, old_place):
+def staged_attention(queries, own_pair, lengths, old_place):
     rows, cols = queries.shape
     heads = cols // HEAD_WIDTH
     own = lax.axis_index("seq").astype(jnp.int32).reshape(1)
@@ -244,13 +267,14 @@
         pltpu.VMEM((heads, rows, rows), jnp.bfloat16),
     ]
     cost = estimate(rows, heads, rows)
+    scalar = pl.BlockSpec(memory_space=pltpu.SMEM)
     across, bias, *carried = pl.pallas_call(
-        lambda *refs: own_kernel(list(pairs), *refs),
-        in_specs=[pl.BlockSpec(memory_space=pltpu.SMEM)] + [HBM_REF] * 3 + [VMEM_REF],
+        lambda *refs: own_kernel((1, 2, 3), *refs),
+        in_specs=[scalar] + [HBM_REF] * 3 + [VMEM_REF],
         out_specs=[VMEM_REF] * 4,
         out_shape=[
             pltpu.VMEM((heads, HEAD_WIDTH, rows), jnp.bfloat16),
-            pltpu.VMEM((1 + len(pairs), rows, rows), jnp.float32),
+            pltpu.VMEM((4, rows, rows), jnp.float32),
         ] + state,
         scratch_shapes=[
             pltpu.SMEM(lengths.shape, jnp.int32),
@@ -261,23 +285,28 @@
         cost_estimate=cost,
         name="own_shard",
     )(own, *in_hbm(lengths, places, queries), *in_vmem(own_pair))
-    *early, last = pairs
-    for at, mask in enumerate(early):
+    *early, last = EXCHANGES
+    for mask, members in early:
+        pair = exchanged(own_pair, mask, members)
         carried = pl.pallas_call(
-            lambda *refs, at=at: next_kernel(1 + at, *refs),
-            in_specs=[VMEM_REF] * 5,
+            lambda *refs, mask=mask, members=members: next_kernel(mask, members, *refs),
+            in_specs=[scalar] + [VMEM_REF] * 5,
             out_specs=[VMEM_REF] * 2,
             out_shape=state,
+            input_output_aliases={4: 0, 5: 1},
             scratch_shapes=work,
             compiler_params=PARAMS,
             cost_estimate=cost,
             name="next_shard",
-        )(*in_vmem(across, bias, *carried), pairs[mask])
-    return pl.pallas_call(
-        lambda *refs: last_kernel(1 + len(early), *refs),
-        in_specs=[VMEM_REF] * 5,
-        out_specs=pl.BlockSpec(memory_space=pl.ANY),
-        out_shape=jax.ShapeDtypeStruct((rows, cols), jnp.bfloat16),
+        )(own, *in_vmem(across, bias, pair, *carried))
+    mask, members = last
+    pair = exchanged(own_pair, mask, members)
+    *_, out = pl.pallas_call(
+        lambda *refs: last_kernel(mask, members, *refs),
+        in_specs=[scalar] + [VMEM_REF] * 5,
+        out_specs=[VMEM_REF] * 2 + [pl.BlockSpec(memory_space=pl.ANY)],
+        out_shape=state + [jax.ShapeDtypeStruct((rows, cols), jnp.bfloat16)],
+        input_output_aliases={4: 0, 5: 1},
         scratch_shapes=work + [
             pltpu.VMEM((rows, cols), jnp.bfloat16),
             pltpu.SemaphoreType.DMA((heads,)),
@@ -285,7 +314,8 @@
         compiler_params=PARAMS,
         cost_estimate=cost,
         name="last_shard",
-    )(*in_vmem(across, bias, *carried), pairs[last])
+    )(own, *in_vmem(across, bias, pair, *carried))
+    return out
 
 
 def online_kernel(heads, q_ref, k_ref, v_ref, key_pos_ref, query_pos_ref, start_ref, out_ref, peak_ref, acc_ref):
@@ -349,17 +379,20 @@
     )(queries, keys, values, key_pos, query_pos, starts)
 
 
+EXCHANGES = ((1, (0, 1)), (3, (0, 3)), (2, (0, 1, 2, 3)), (1, (2, 3)), (3, (1, 2)))
+
+
+def exchanged(value, mask, members):
+    return lax.ppermute(value, "seq", [(i, i ^ mask) for i in members])
+
+
 def body(queries, keys, values, lengths, old_place):
     devices = lax.axis_size("seq")
     row_count = queries.shape[0]
     key_count = row_count * devices
     if devices == 4 and key_count <= 1024:
         own_pair = packed_pair(keys, values)
-        pairs = {
-            mask: lax.ppermute(own_pair, "seq", [(i, i ^ mask) for i in range(devices)])
-            for mask in (2, 1, 3)
-        }
-        return staged_attention(queries, own_pair, pairs, lengths, old_place)
+        return staged_attention(queries, own_pair, lengths, old_place)
     all_keys = lax.all_gather(keys, "seq", axis=0, tiled=True)
     all_values = lax.all_gather(values, "seq", axis=0, tiled=True)
     key_pos, query_pos, starts = block_places(

time: 17.8 us -> 22.8 us (1.28)
  the two profiles are of different devices: /device:TPU:23 before, /device:TPU:13 now
where the time goes in v8:
time: 22.8 us; the launch traced here: 22.6 us
  starting transfers between devices  11.5 us (50%)
  Pallas kernels  7.48 us (33%)
  waiting for transfers between devices  3.42 us (15%)
    ppermute x5, starting transfers between devices, exchanged(): return lax.ppermute(value, 'seq', [(i, i ^ mask) for i in members])  11.5 us
    ppermute x5, waiting for transfers between devices, exchanged(): return lax.ppermute(value, 'seq', [(i, i ^ mask) for i in members])  3.42 us
    pallas_call x1, Pallas kernels, staged_attention(): pl.pallas_call(lambda *refs: own_kernel((1, 2, 3), *refs), in_specs=[scal...  2.33 us
    pallas_call x4, Pallas kernels, staged_attention(): pl.pallas_call(lambda *refs, mask=mask, members=members: next_kernel(mask...  2.28 us
    pallas_call x1, Pallas kernels, staged_attention(): pl.pallas_call(lambda *refs: last_kernel(mask, members, *refs), in_specs=...  1.98 us
    pallas_call x1, Pallas kernels, packed_pair(): pl.pallas_call(pack_kernel, in_specs=[HBM_REF] * 2, out_specs=VMEM_REF, o...  0.89 us
  transfers between devices with their start and end apart: 5, of which 1 were waited for; matrix products, arithmetic and copies ran while one was open for 0% of the time, Pallas kernels for 20%

profile of v8, /device:TPU:13, one launch (start us, length us, event | category | flops | bytes accessed | tf_op | source)
XLA Modules:
  0.0 22.6 jit_solution(12367983065271524399)
XLA Ops:
  0.0 0.9 %pack.1.refs_4_ = bf16[256,256]{1,0:T(8,128)(2,1)S(1)} custom-call(bf16[256,128]{1,0:T(8,128)(2,1)} %k_ref.1, bf16[256,128]{1,0:T(8,128)(2,1)} %v_ref.1), custom_call_target="tpu_custom_call" | custom-call | tf_op jit(solution)/shard_map/pack/pallas_call | solution.py:245
  0.9 2.1 %collective-permute-start.4 = (bf16[256,256]{1,0:T(8,128)(2,1)S(1)}, bf16[256,256]{1,0:T(8,128)(2,1)S(1)}, u32[]{:S(2)}, u32[]{:S(2)}) collective-permute-start(bf16[256,256]{1,0:T(8,128)(2,1)S(1)} %pack.1.refs_4_), channel_id=1, source_target_pairs={{0,4},{4,0},{1,5},{5,1},{2,6},{6,2},{3,7},{7,3},{16,20},{20,16},{1... | collective-permute-start | bytes 393224 | tf_op jit(solution)/shard_map/ppermute | solution.py:386
  3.0 0.7 %collective-permute-start.3 = (bf16[256,256]{1,0:T(8,128)(2,1)S(1)}, bf16[256,256]{1,0:T(8,128)(2,1)S(1)}, u32[]{:S(2)}, u32[]{:S(2)}) collective-permute-start(bf16[256,256]{1,0:T(8,128)(2,1)S(1)} %pack.1.refs_4_), channel_id=1, source_target_pairs={{0,12},{12,0},{1,13},{13,1},{2,14},{14,2},{3,15},{15,3},{16,28},{2... | collective-permute-start | bytes 393224 | tf_op jit(solution)/shard_map/ppermute | solution.py:386
  3.7 4.7 %collective-permute-start.2 = (bf16[256,256]{1,0:T(8,128)(2,1)S(1)}, bf16[256,256]{1,0:T(8,128)(2,1)S(1)}, u32[]{:S(2)}, u32[]{:S(2)}) collective-permute-start(bf16[256,256]{1,0:T(8,128)(2,1)S(1)} %pack.1.refs_4_), channel_id=1, source_target_pairs={{0,8},{4,12},{8,0},{12,4},{1,9},{5,13},{9,1},{13,5},{2,10},{6,14},... | collective-permute-start | bytes 393224 | tf_op jit(solution)/shard_map/ppermute | solution.py:386
  8.3 0.7 %collective-permute-start.1 = (bf16[256,256]{1,0:T(8,128)(2,1)S(1)}, bf16[256,256]{1,0:T(8,128)(2,1)S(1)}, u32[]{:S(2)}, u32[]{:S(2)}) collective-permute-start(bf16[256,256]{1,0:T(8,128)(2,1)S(1)} %pack.1.refs_4_), channel_id=1, source_target_pairs={{8,12},{12,8},{9,13},{13,9},{10,14},{14,10},{11,15},{15,11},{24,28... | collective-permute-start | bytes 393224 | tf_op jit(solution)/shard_map/ppermute | solution.py:386
  9.0 3.5 %collective-permute-start = (bf16[256,256]{1,0:T(8,128)(2,1)S(1)}, bf16[256,256]{1,0:T(8,128)(2,1)S(1)}, u32[]{:S(2)}, u32[]{:S(2)}) collective-permute-start(bf16[256,256]{1,0:T(8,128)(2,1)S(1)} %pack.1.refs_4_), channel_id=1, source_target_pairs={{4,8},{8,4},{5,9},{9,5},{6,10},{10,6},{7,11},{11,7},{20,24},{24,20... | collective-permute-start | bytes 393224 | tf_op jit(solution)/shard_map/ppermute | solution.py:386
  12.5 2.3 %own_shard.1 = (bf16[8,128,256]{2,1,0:T(8,128)(2,1)S(1)}, f32[4,256,256]{2,1,0:T(8,128)S(1)}, f32[8,256]{1,0:T(8,128)S(1)}, f32[8,144,256]{2,1,0:T(8,128)S(1)}) custom-call(s32[1]{0:T(128)} %bitcast.refs_0_, s32[3]{0:T(128)} %refs_1_.1, s32[1,128]{1,0:T(1,128)} %bitcast.2, bf16[256,1024]{1,0:T(8,128)(2,1)} %refs_3_.1, bf16[256,256]{1,0:T(8,128)(2,1)S(1)} %pack.1.refs_4_), custom_call_target="tpu_custom_call" | custom-call | flops 402653184 | bytes 2097152 | tf_op jit(solution)/shard_map/own_shard/pallas_call | solution.py:271
  14.8 0.0 collective-permute-done.4.refs_3_
  14.8 1.1 %next_shard.4 = (f32[8,256]{1,0:T(8,128)S(1)}, f32[8,144,256]{2,1,0:T(8,128)S(1)}) custom-call(s32[1]{0:T(128)} %bitcast.refs_0_, bf16[8,128,256]{2,1,0:T(8,128)(2,1)S(1)} %get-tuple-element.18.refs_1_, f32[4,256,256]{2,1,0:T(8,128)S(1)} %get-tuple-element.19.refs_2_, ...), custom_call_target="tpu_custom_call", output_to_operand_aliasing={{0}: (4, {}), {1}: (5, {})} | custom-call | flops 402653184 | bytes 2097152 | tf_op jit(solution)/shard_map/next_shard/pallas_call | solution.py:291
  16.0 0.0 collective-permute-done.3.refs_3_
  16.0 0.0 collective-permute-done.2.refs_3_
  16.0 1.1 %next_shard.6 = (f32[8,256]{1,0:T(8,128)S(1)}, f32[8,144,256]{2,1,0:T(8,128)S(1)}) custom-call(s32[1]{0:T(128)} %bitcast.refs_0_, bf16[8,128,256]{2,1,0:T(8,128)(2,1)S(1)} %get-tuple-element.18.refs_1_, f32[4,256,256]{2,1,0:T(8,128)S(1)} %get-tuple-element.19.refs_2_, ...), custom_call_target="tpu_custom_call", output_to_operand_aliasing={{0}: (4, {}), {1}: (5, {})} | custom-call | flops 402653184 | bytes 2097152 | tf_op jit(solution)/shard_map/next_shard/pallas_call | solution.py:291
  17.1 0.0 collective-permute-done.1.refs_3_
  17.2 3.4 %collective-permute-done.refs_3_ = bf16[256,256]{1,0:T(8,128)(2,1)S(1)} collective-permute-done((bf16[256,256]{1,0:T(8,128)(2,1)S(1)}, bf16[256,256]{1,0:T(8,128)(2,1)S(1)}, u32[]{:S(2)}, u32[]{:S(2)}) %collective-permute-start) | collective-permute-done | bytes 131104 | tf_op jit(solution)/shard_map/ppermute | solution.py:386
  20.6 2.0 %last_shard.1 = (f32[8,256]{1,0:T(8,128)S(1)}, f32[8,144,256]{2,1,0:T(8,128)S(1)}, bf16[256,1024]{1,0:T(8,128)(2,1)}) custom-call(s32[1]{0:T(128)} %bitcast.refs_0_, bf16[8,128,256]{2,1,0:T(8,128)(2,1)S(1)} %get-tuple-element.18.refs_1_, f32[4,256,256]{2,1,0:T(8,128)S(1)} %get-tuple-element.19.refs_2_, ...), custom_call_target="tpu_custom_call", output_to_operand_aliasing={{0}: (4, {}), {1}: (5, {})} | custom-call | flops 402653184 | bytes 2097152 | tf_op jit(solution)/shard_map/last_shard/pallas_call | solution.py:304
  (2 shorter events, 0.0 us)
Async XLA Ops:
  0.9 13.9 %collective-permute-start.4 = (bf16[256,256]{1,0:T(8,128)(2,1)S(1)}, bf16[256,256]{1,0:T(8,128)(2,1)S(1)}, u32[]{:S(2)}, u32[]{:S(2)}) collective-permute-start(bf16[256,256]{1,0:T(8,128)(2,1)S(1)} %pack.1.refs_4_), channel_id=1, source_target_pairs={{0,4},{4,0},{1,5},{5,1},{2,6},{6,2},{3,7},{7,3},{16,20},{20,16},{1... | collective-permute-start | bytes 393224 | tf_op jit(solution)/shard_map/ppermute | solution.py:386
  3.0 13.0 %collective-permute-start.3 = (bf16[256,256]{1,0:T(8,128)(2,1)S(1)}, bf16[256,256]{1,0:T(8,128)(2,1)S(1)}, u32[]{:S(2)}, u32[]{:S(2)}) collective-permute-start(bf16[256,256]{1,0:T(8,128)(2,1)S(1)} %pack.1.refs_4_), channel_id=1, source_target_pairs={{0,12},{12,0},{1,13},{13,1},{2,14},{14,2},{3,15},{15,3},{16,28},{2... | collective-permute-start | bytes 393224 | tf_op jit(solution)/shard_map/ppermute | solution.py:386
  3.7 12.3 %collective-permute-start.2 = (bf16[256,256]{1,0:T(8,128)(2,1)S(1)}, bf16[256,256]{1,0:T(8,128)(2,1)S(1)}, u32[]{:S(2)}, u32[]{:S(2)}) collective-permute-start(bf16[256,256]{1,0:T(8,128)(2,1)S(1)} %pack.1.refs_4_), channel_id=1, source_target_pairs={{0,8},{4,12},{8,0},{12,4},{1,9},{5,13},{9,1},{13,5},{2,10},{6,14},... | collective-permute-start | bytes 393224 | tf_op jit(solution)/shard_map/ppermute | solution.py:386
  8.3 8.8 %collective-permute-start.1 = (bf16[256,256]{1,0:T(8,128)(2,1)S(1)}, bf16[256,256]{1,0:T(8,128)(2,1)S(1)}, u32[]{:S(2)}, u32[]{:S(2)}) collective-permute-start(bf16[256,256]{1,0:T(8,128)(2,1)S(1)} %pack.1.refs_4_), channel_id=1, source_target_pairs={{8,12},{12,8},{9,13},{13,9},{10,14},{14,10},{11,15},{15,11},{24,28... | collective-permute-start | bytes 393224 | tf_op jit(solution)/shard_map/ppermute | solution.py:386
  9.0 11.6 %collective-permute-start = (bf16[256,256]{1,0:T(8,128)(2,1)S(1)}, bf16[256,256]{1,0:T(8,128)(2,1)S(1)}, u32[]{:S(2)}, u32[]{:S(2)}) collective-permute-start(bf16[256,256]{1,0:T(8,128)(2,1)S(1)} %pack.1.refs_4_), channel_id=1, source_target_pairs={{4,8},{8,4},{5,9},{9,5},{6,10},{10,6},{7,11},{11,7},{20,24},{24,20... | collective-permute-start | bytes 393224 | tf_op jit(solution)/shard_map/ppermute | solution.py:386

commit v9 on v7

--- a/solution.py
+++ b/solution.py
@@ -95,35 +95,28 @@
     return stage
 
 
-def pack_kernel(k_ref, v_ref, pair_ref, sems):
-    copies = [
-        pltpu.make_async_copy(ref, pair_ref.at[:, at * HEAD_WIDTH:(at + 1) * HEAD_WIDTH], sems.at[at])
-        for at, ref in enumerate((k_ref, v_ref))
-    ]
-    for copy in copies:
-        copy.start()
-    for copy in copies:
-        copy.wait()
-
-
 def own_kernel(
-    masks, own_ref, lengths_hbm, places_hbm, q_hbm, pair_ref,
+    masks, own_ref, lengths_hbm, places_hbm, q_hbm, k_hbm, v_hbm,
     across_ref, bias_ref, peak_ref, sum_ref,
-    lengths_ref, places_ref, q_ref, scaled_ref, weight_ref, sems,
+    lengths_ref, places_ref, q_ref, k_ref, v_ref, scaled_ref, weight_ref, sems,
 ):
-    moves = ((lengths_hbm, lengths_ref), (places_hbm, places_ref), (q_hbm, q_ref))
+    moves = (
+        (lengths_hbm, lengths_ref), (places_hbm, places_ref),
+        (k_hbm, k_ref), (v_hbm, v_ref), (q_hbm, q_ref),
+    )
     copies = [pltpu.make_async_copy(*move, sems.at[n]) for n, move in enumerate(moves)]
     for copy in copies:
         copy.start()
-    turned = values_down(pair_ref[:, HEAD_WIDTH:])
-    keys = pair_ref[:, :HEAD_WIDTH]
     copies[0].wait()
     copies[1].wait()
     heads, _, rows = across_ref.shape
     own = own_ref[0]
     owners = [own] + [own ^ mask for mask in masks]
     mask_tables(own, owners, lengths_ref, places_ref, rows, bias_ref)
-    copies[2].wait()
+    for copy in copies[2:]:
+        copy.wait()
+    keys = k_ref[...]
+    turned = values_down(v_ref[...])
 
     def turn(head, _):
         q = q_ref[:, head * HEAD_WIDTH:(head + 1) * HEAD_WIDTH]
@@ -147,10 +140,10 @@
 
 
 def next_kernel(
-    at, across_ref, bias_ref, peak_ref, sum_ref, pair_ref, new_peak_ref, new_sum_ref,
+    at, across_ref, bias_ref, peak_ref, sum_ref, k_ref, v_ref, new_peak_ref, new_sum_ref,
     scaled_ref, weight_ref,
 ):
-    turned = values_down(pair_ref[:, HEAD_WIDTH:])
+    turned = values_down(v_ref[...])
 
     def mix(head, peak):
         new_peak_ref[head:head + 1, :] = peak
@@ -158,7 +151,7 @@
 
     in_stages(across_ref.shape[0], [
         score_stage(
-            pair_ref[:, :HEAD_WIDTH], across_ref, bias_ref, at, scaled_ref,
+            k_ref[...], across_ref, bias_ref, at, scaled_ref,
             lambda head: peak_ref[head:head + 1, :],
         ),
         weight_stage(scaled_ref, weight_ref),
@@ -167,10 +160,10 @@
 
 
 def last_kernel(
-    at, across_ref, bias_ref, peak_ref, sum_ref, pair_ref, out_ref,
+    at, across_ref, bias_ref, peak_ref, sum_ref, k_ref, v_ref, out_ref,
     scaled_ref, weight_ref, block_ref, sems,
 ):
-    turned = values_down(pair_ref[:, HEAD_WIDTH:])
+    turned = values_down(v_ref[...])
     copies = []
 
     def mix(head, peak):
@@ -186,7 +179,7 @@
 
     in_stages(across_ref.shape[0], [
         score_stage(
-            pair_ref[:, :HEAD_WIDTH], across_ref, bias_ref, at, scaled_ref,
+            k_ref[...], across_ref, bias_ref, at, scaled_ref,
             lambda head: peak_ref[head:head + 1, :],
         ),
         weight_stage(scaled_ref, weight_ref),
@@ -218,19 +211,13 @@
 PARAMS = pltpu.CompilerParams(vmem_limit_bytes=32 << 20)
 
 
-def packed_pair(keys, values):
-    return pl.pallas_call(
-        pack_kernel,
-        in_specs=[HBM_REF] * 2,
-        out_specs=VMEM_REF,
-        out_shape=pltpu.VMEM((keys.shape[0], 2 * HEAD_WIDTH), keys.dtype),
-        scratch_shapes=[pltpu.SemaphoreType.DMA((2,))],
-        compiler_params=PARAMS,
-        name="pack",
-    )(*in_hbm(keys, values))
-
-
-def staged_attention(queries, own_pair, pairs, lengths, old_place):
+def moved(value, mask):
+    return lax.ppermute(value, "seq", [(i, i ^ mask) for i in range(lax.axis_size("seq"))])
+
+
+def staged_attention(queries, keys, values, lengths, old_place):
+    pairs = {mask: [moved(part, mask) for part in (keys, values)] for mask in (2, 1)}
+    relayed_keys = moved(pairs[2][0], 1)
     rows, cols = queries.shape
     heads = cols // HEAD_WIDTH
     devices = lax.axis_size("seq")
@@ -248,7 +235,7 @@
     cost = estimate(rows, heads, rows)
     across, bias, *carried = pl.pallas_call(
         lambda *refs: own_kernel(masks, *refs),
-        in_specs=[pl.BlockSpec(memory_space=pltpu.SMEM)] + [HBM_REF] * 3 + [VMEM_REF],
+        in_specs=[pl.BlockSpec(memory_space=pltpu.SMEM)] + [HBM_REF] * 5,
         out_specs=[VMEM_REF] * 4,
         out_shape=[
             pltpu.VMEM((heads, HEAD_WIDTH, rows), jnp.bfloat16),
@@ -258,27 +245,29 @@
             pltpu.SMEM(lengths.shape, jnp.int32),
             pltpu.VMEM(places.shape, jnp.int32),
             pltpu.VMEM(queries.shape, jnp.bfloat16),
-        ] + work + [pltpu.SemaphoreType.DMA((3,))],
+            pltpu.VMEM(keys.shape, jnp.bfloat16),
+            pltpu.VMEM(values.shape, jnp.bfloat16),
+        ] + work + [pltpu.SemaphoreType.DMA((5,))],
         compiler_params=PARAMS,
         cost_estimate=cost,
         name="own_shard",
-    )(own, *in_hbm(lengths, places, queries), *in_vmem(own_pair))
-    relayed, *carried = lax.optimization_barrier((pairs[2], *carried))
-    pairs[3] = moved(relayed, 1, devices)
+    )(own, *in_hbm(lengths, places, queries, keys, values))
+    relayed, *carried = lax.optimization_barrier((pairs[2][1], *carried))
+    pairs[3] = [relayed_keys, moved(relayed, 1)]
     for mask in (2, 1):
         carried = pl.pallas_call(
             lambda *refs, mask=mask: next_kernel(mask, *refs),
-            in_specs=[VMEM_REF] * 5,
+            in_specs=[VMEM_REF] * 6,
             out_specs=[VMEM_REF] * 2,
             out_shape=state,
             scratch_shapes=work,
             compiler_params=PARAMS,
             cost_estimate=cost,
             name="next_shard",
-        )(*in_vmem(across, bias, *carried), pairs[mask])
+        )(*in_vmem(across, bias, *carried), *pairs[mask])
     return pl.pallas_call(
         lambda *refs: last_kernel(3, *refs),
-        in_specs=[VMEM_REF] * 5,
+        in_specs=[VMEM_REF] * 6,
         out_specs=pl.BlockSpec(memory_space=pl.ANY),
         out_shape=jax.ShapeDtypeStruct((rows, cols), jnp.bfloat16),
         scratch_shapes=work + [
@@ -288,7 +277,7 @@
         compiler_params=PARAMS,
         cost_estimate=cost,
         name="last_shard",
-    )(*in_vmem(across, bias, *carried), pairs[3])
+    )(*in_vmem(across, bias, *carried), *pairs[3])
 
 
 def online_kernel(heads, q_ref, k_ref, v_ref, key_pos_ref, query_pos_ref, start_ref, out_ref, peak_ref, acc_ref):
@@ -352,20 +341,12 @@
     )(queries, keys, values, key_pos, query_pos, starts)
 
 
-def moved(value, mask, devices):
-    return lax.ppermute(value, "seq", [(i, i ^ mask) for i in range(devices)])
-
-
 def body(queries, keys, values, lengths, old_place):
     devices = lax.axis_size("seq")
     row_count = queries.shape[0]
     key_count = row_count * devices
     if devices == 4 and key_count <= 1024:
-        own_pair = packed_pair(keys, values)
-        pairs = {}
-        pairs[2] = moved(own_pair, 2, devices)
-        pairs[1] = moved(own_pair, 1, devices)
-        return staged_attention(queries, own_pair, pairs, lengths, old_place)
+        return staged_attention(queries, keys, values, lengths, old_place)
     all_keys = lax.all_gather(keys, "seq", axis=0, tiled=True)
     all_values = lax.all_gather(values, "seq", axis=0, tiled=True)
     key_pos, query_pos, starts = block_places(

time: 18.5 us -> 16.8 us (0.908)
  waiting for transfers between devices: 4.59 us -> 0.82 us
  starting transfers between devices: 6.29 us -> 9.22 us
  Pallas kernels: 7.4 us -> 6.59 us
    ppermute x3 -> x6, waiting for transfers between devices: 4.59 us -> 0.82 us  [moved(): lax.ppermute(value, 'seq', [(i, i ^ mask) for i in range(lax.axis_size('s...]
    ppermute x3 -> x6, starting transfers between devices: 6.29 us -> 9.22 us  [moved(): lax.ppermute(value, 'seq', [(i, i ^ mask) for i in range(lax.axis_size('s...]
    pallas_call x1 -> x0, Pallas kernels: 0.89 us -> none  [packed_pair(): pl.pallas_call(pack_kernel, in_specs=[HBM_REF] * 2, out_specs=VMEM_REF, o...]
  transfers between devices with their start and end apart: 3 -> 6, of which waited for: 2 -> 1; matrix products, arithmetic and copies ran while one was open for 0% -> 0% of each run, Pallas kernels for 25% -> 28%
where the time goes in v9:
time: 16.8 us; the launch traced here: 16.7 us
  starting transfers between devices  9.22 us (55%)
  Pallas kernels  6.59 us (39%)
  waiting for transfers between devices  0.82 us (5%)
    ppermute x6, starting transfers between devices, moved(): lax.ppermute(value, 'seq', [(i, i ^ mask) for i in range(lax.axis_size('s...  9.22 us
    pallas_call x1, Pallas kernels, staged_attention(): pl.pallas_call(lambda *refs: own_kernel(masks, *refs), in_specs=[pl.Block...  2.4 us
    pallas_call x2, Pallas kernels, staged_attention(): pl.pallas_call(lambda *refs, mask=mask: next_kernel(mask, *refs), in_spec...  2.24 us
    pallas_call x1, Pallas kernels, staged_attention(): pl.pallas_call(lambda *refs: last_kernel(3, *refs), in_specs=[VMEM_REF] *...  1.95 us
    ppermute x6, waiting for transfers between devices, moved(): lax.ppermute(value, 'seq', [(i, i ^ mask) for i in range(lax.axis_size('s...  0.82 us
  transfers between devices with their start and end apart: 6, of which 1 were waited for; matrix products, arithmetic and copies ran while one was open for 0% of the time, Pallas kernels for 28%

profile of v9, /device:TPU:0, one launch (start us, length us, event | category | flops | bytes accessed | tf_op | source)
XLA Modules:
  0.0 16.7 jit_solution(3238932709536919)
XLA Ops:
  0.0 4.0 %collective-permute-start = (bf16[256,128]{1,0:T(8,128)(2,1)}, bf16[256,128]{1,0:T(8,128)(2,1)S(1)}, u32[]{:S(2)}, u32[]{:S(2)}) collective-permute-start(bf16[256,128]{1,0:T(8,128)(2,1)} %refs_5_.1), channel_id=1, source_target_pairs={{0,8},{4,12},{8,0},{12,4},{1,9},{5,13},{9,1},{13,5},{2,10},{6,14},... | collective-permute-start | bytes 196616 | tf_op jit(solution)/shard_map/ppermute | solution.py:215
  4.0 0.0 collective-permute-start.1
  4.1 1.9 %collective-permute-start.2 = (bf16[256,128]{1,0:T(8,128)(2,1)}, bf16[256,128]{1,0:T(8,128)(2,1)S(1)}, u32[]{:S(2)}, u32[]{:S(2)}) collective-permute-start(bf16[256,128]{1,0:T(8,128)(2,1)} %refs_4_.1), channel_id=1, source_target_pairs={{0,4},{4,0},{8,12},{12,8},{1,5},{5,1},{9,13},{13,9},{2,6},{6,2},{1... | collective-permute-start | bytes 196616 | tf_op jit(solution)/shard_map/ppermute | solution.py:215
  6.0 0.1 collective-permute-start.3
  6.1 2.4 %own_shard.1 = (bf16[8,128,256]{2,1,0:T(8,128)(2,1)S(1)}, f32[4,256,256]{2,1,0:T(8,128)S(1)}, f32[8,256]{1,0:T(8,128)S(1)}, f32[8,144,256]{2,1,0:T(8,128)S(1)}) custom-call(s32[1]{0:T(128)} %bitcast.refs_0_, s32[3]{0:T(128)} %refs_1_.1, s32[1,128]{1,0:T(1,128)} %bitcast.2, bf16[256,1024]{1,0:T(8,128)(2,1)} %refs_3_.1, bf16[256,128]{1,0:T(8,128)(2,1)} %refs_4_.1, ...), custom_call_target="tpu_custom_call" | custom-call | flops 402653184 | bytes 2097152 | tf_op jit(solution)/shard_map/own_shard/pallas_call | solution.py:236
  8.5 0.0 collective-permute-done.refs_5_
  8.5 1.9 %collective-permute-start.5 = (bf16[256,128]{1,0:T(8,128)(2,1)S(1)}, bf16[256,128]{1,0:T(8,128)(2,1)S(1)}, u32[]{:S(2)}, u32[]{:S(2)}) collective-permute-start(bf16[256,128]{1,0:T(8,128)(2,1)S(1)} %collective-permute-done.refs_5_), channel_id=1, source_target_pairs={{0,4},{4,0},{8,12},{12,8},{1,5},{5,1},{9,13},{13,9},{2,6},{6,2},{1... | collective-permute-start | bytes 196616 | tf_op jit(solution)/shard_map/ppermute | solution.py:215
  10.5 0.0 collective-permute-done.1.refs_4_
  10.5 1.2 %collective-permute-start.4 = (bf16[256,128]{1,0:T(8,128)(2,1)S(1)}, bf16[256,128]{1,0:T(8,128)(2,1)S(1)}, u32[]{:S(2)}, u32[]{:S(2)}) collective-permute-start(bf16[256,128]{1,0:T(8,128)(2,1)S(1)} %collective-permute-done.1.refs_4_), channel_id=1, source_target_pairs={{0,4},{4,0},{8,12},{12,8},{1,5},{5,1},{9,13},{13,9},{2,6},{6,2},{1... | collective-permute-start | bytes 196616 | tf_op jit(solution)/shard_map/ppermute | solution.py:215
  11.6 1.1 %next_shard.2 = (f32[8,256]{1,0:T(8,128)S(1)}, f32[8,144,256]{2,1,0:T(8,128)S(1)}) custom-call(bf16[8,128,256]{2,1,0:T(8,128)(2,1)S(1)} %get-tuple-element.16.refs_0_, f32[4,256,256]{2,1,0:T(8,128)S(1)} %get-tuple-element.17.refs_1_, f32[8,256]{1,0:T(8,128)S(1)} %get-tuple-element.20.refs_2_, f32[8,144,256]{2,1,0:T(8,128)S(1)} %get-tuple-element.21.refs_3_, ...), custom_call_target="tpu_custom_call" | custom-call | flops 402653184 | bytes 2097152 | tf_op jit(solution)/shard_map/next_shard/pallas_call | solution.py:258
  12.8 0.0 collective-permute-done.2.refs_4_
  12.8 0.0 collective-permute-done.3.refs_5_
  12.8 1.1 %next_shard.3 = (f32[8,256]{1,0:T(8,128)S(1)}, f32[8,144,256]{2,1,0:T(8,128)S(1)}) custom-call(bf16[8,128,256]{2,1,0:T(8,128)(2,1)S(1)} %get-tuple-element.16.refs_0_, f32[4,256,256]{2,1,0:T(8,128)S(1)} %get-tuple-element.17.refs_1_, f32[8,256]{1,0:T(8,128)S(1)} %get-tuple-element.22.refs_2_, f32[8,144,256]{2,1,0:T(8,128)S(1)} %get-tuple-element.23.refs_3_, ...), custom_call_target="tpu_custom_call" | custom-call | flops 402653184 | bytes 2097152 | tf_op jit(solution)/shard_map/next_shard/pallas_call | solution.py:258
  13.9 0.0 collective-permute-done.5.refs_5_
  13.9 0.8 %collective-permute-done.4.refs_4_ = bf16[256,128]{1,0:T(8,128)(2,1)S(1)} collective-permute-done((bf16[256,128]{1,0:T(8,128)(2,1)S(1)}, bf16[256,128]{1,0:T(8,128)(2,1)S(1)}, u32[]{:S(2)}, u32[]{:S(2)}) %collective-permute-start.4) | collective-permute-done | bytes 65568 | tf_op jit(solution)/shard_map/ppermute | solution.py:215
  14.7 2.0 %last_shard.1 = bf16[256,1024]{1,0:T(8,128)(2,1)} custom-call(bf16[8,128,256]{2,1,0:T(8,128)(2,1)S(1)} %get-tuple-element.16.refs_0_, f32[4,256,256]{2,1,0:T(8,128)S(1)} %get-tuple-element.17.refs_1_, f32[8,256]{1,0:T(8,128)S(1)} %get-tuple-element.24.refs_2_, f32[8,144,256]{2,1,0:T(8,128)S(1)} %get-tuple-element.25.refs_3_, ...), custom_call_target="tpu_custom_call" | custom-call | flops 402653184 | bytes 2097152 | tf_op jit(solution)/shard_map/last_shard/pallas_call | solution.py:268
Async XLA Ops:
  0.0 8.5 %collective-permute-start = (bf16[256,128]{1,0:T(8,128)(2,1)}, bf16[256,128]{1,0:T(8,128)(2,1)S(1)}, u32[]{:S(2)}, u32[]{:S(2)}) collective-permute-start(bf16[256,128]{1,0:T(8,128)(2,1)} %refs_5_.1), channel_id=1, source_target_pairs={{0,8},{4,12},{8,0},{12,4},{1,9},{5,13},{9,1},{13,5},{2,10},{6,14},... | collective-permute-start | bytes 196616 | tf_op jit(solution)/shard_map/ppermute | solution.py:215
  4.0 6.4 %collective-permute-start.1 = (bf16[256,128]{1,0:T(8,128)(2,1)}, bf16[256,128]{1,0:T(8,128)(2,1)S(1)}, u32[]{:S(2)}, u32[]{:S(2)}) collective-permute-start(bf16[256,128]{1,0:T(8,128)(2,1)} %refs_4_.1), channel_id=1, source_target_pairs={{0,8},{4,12},{8,0},{12,4},{1,9},{5,13},{9,1},{13,5},{2,10},{6,14},... | collective-permute-start | bytes 196616 | tf_op jit(solution)/shard_map/ppermute | solution.py:215
  4.1 8.7 %collective-permute-start.2 = (bf16[256,128]{1,0:T(8,128)(2,1)}, bf16[256,128]{1,0:T(8,128)(2,1)S(1)}, u32[]{:S(2)}, u32[]{:S(2)}) collective-permute-start(bf16[256,128]{1,0:T(8,128)(2,1)} %refs_4_.1), channel_id=1, source_target_pairs={{0,4},{4,0},{8,12},{12,8},{1,5},{5,1},{9,13},{13,9},{2,6},{6,2},{1... | collective-permute-start | bytes 196616 | tf_op jit(solution)/shard_map/ppermute | solution.py:215
  6.0 6.8 %collective-permute-start.3 = (bf16[256,128]{1,0:T(8,128)(2,1)}, bf16[256,128]{1,0:T(8,128)(2,1)S(1)}, u32[]{:S(2)}, u32[]{:S(2)}) collective-permute-start(bf16[256,128]{1,0:T(8,128)(2,1)} %refs_5_.1), channel_id=1, source_target_pairs={{0,4},{4,0},{8,12},{12,8},{1,5},{5,1},{9,13},{13,9},{2,6},{6,2},{1... | collective-permute-start | bytes 196616 | tf_op jit(solution)/shard_map/ppermute | solution.py:215
  8.5 5.4 %collective-permute-start.5 = (bf16[256,128]{1,0:T(8,128)(2,1)S(1)}, bf16[256,128]{1,0:T(8,128)(2,1)S(1)}, u32[]{:S(2)}, u32[]{:S(2)}) collective-permute-start(bf16[256,128]{1,0:T(8,128)(2,1)S(1)} %collective-permute-done.refs_5_), channel_id=1, source_target_pairs={{0,4},{4,0},{8,12},{12,8},{1,5},{5,1},{9,13},{13,9},{2,6},{6,2},{1... | collective-permute-start | bytes 196616 | tf_op jit(solution)/shard_map/ppermute | solution.py:215
  10.5 4.3 %collective-permute-start.4 = (bf16[256,128]{1,0:T(8,128)(2,1)S(1)}, bf16[256,128]{1,0:T(8,128)(2,1)S(1)}, u32[]{:S(2)}, u32[]{:S(2)}) collective-permute-start(bf16[256,128]{1,0:T(8,128)(2,1)S(1)} %collective-permute-done.1.refs_4_), channel_id=1, source_target_pairs={{0,4},{4,0},{8,12},{12,8},{1,5},{5,1},{9,13},{13,9},{2,6},{6,2},{1... | collective-permute-start | bytes 196616 | tf_op jit(solution)/shard_map/ppermute | solution.py:215

commit v10 on v9

--- a/solution.py
+++ b/solution.py
@@ -159,15 +159,38 @@
     ])
 
 
-def last_kernel(
-    at, across_ref, bias_ref, peak_ref, sum_ref, k_ref, v_ref, out_ref,
-    scaled_ref, weight_ref, block_ref, sems,
+def weights_kernel(
+    at, across_ref, bias_ref, peak_ref, sum_ref, k_ref,
+    new_peak_ref, new_sum_ref, weight_ref, scaled_ref,
 ):
+    def rescale(head, peak):
+        new_peak_ref[head:head + 1, :] = peak
+        new_sum_ref[head] = sum_ref[head] * jnp.exp2(peak_ref[head:head + 1, :] - peak)
+
+    in_stages(across_ref.shape[0], [
+        score_stage(
+            k_ref[...], across_ref, bias_ref, at, scaled_ref,
+            lambda head: peak_ref[head:head + 1, :],
+        ),
+        weight_stage(scaled_ref, weight_ref),
+        rescale,
+    ])
+
+
+def values_kernel(sum_ref, weight_ref, v_ref, new_sum_ref):
+    turned = values_down(v_ref[...])
+    for head in range(sum_ref.shape[0]):
+        added = jnp.dot(turned, weight_ref[head], preferred_element_type=jnp.float32)
+        new_sum_ref[head] = sum_ref[head] + added
+
+
+def last_kernel(sum_ref, weight_ref, v_ref, out_ref, block_ref, sems):
     turned = values_down(v_ref[...])
     copies = []
 
-    def mix(head, peak):
-        summed = joined(head, peak, turned, weight_ref, peak_ref, sum_ref)
+    def mix(head, _):
+        added = jnp.dot(turned, weight_ref[head], preferred_element_type=jnp.float32)
+        summed = sum_ref[head] + added
         return summed[:HEAD_WIDTH] / summed[HEAD_WIDTH:HEAD_WIDTH + 1]
 
     def send(head, out):
@@ -177,15 +200,7 @@
         copy.start()
         copies.append(copy)
 
-    in_stages(across_ref.shape[0], [
-        score_stage(
-            k_ref[...], across_ref, bias_ref, at, scaled_ref,
-            lambda head: peak_ref[head:head + 1, :],
-        ),
-        weight_stage(scaled_ref, weight_ref),
-        mix,
-        send,
-    ])
+    in_stages(sum_ref.shape[0], [mix, send])
     for copy in copies:
         copy.wait()
 
@@ -217,7 +232,6 @@
 
 def staged_attention(queries, keys, values, lengths, old_place):
     pairs = {mask: [moved(part, mask) for part in (keys, values)] for mask in (2, 1)}
-    relayed_keys = moved(pairs[2][0], 1)
     rows, cols = queries.shape
     heads = cols // HEAD_WIDTH
     devices = lax.axis_size("seq")
@@ -252,32 +266,57 @@
         cost_estimate=cost,
         name="own_shard",
     )(own, *in_hbm(lengths, places, queries, keys, values))
-    relayed, *carried = lax.optimization_barrier((pairs[2][1], *carried))
-    pairs[3] = [relayed_keys, moved(relayed, 1)]
-    for mask in (2, 1):
-        carried = pl.pallas_call(
-            lambda *refs, mask=mask: next_kernel(mask, *refs),
-            in_specs=[VMEM_REF] * 6,
-            out_specs=[VMEM_REF] * 2,
-            out_shape=state,
-            scratch_shapes=work,
+
+    def shard_weights(at, keys, peak, summed):
+        return pl.pallas_call(
+            lambda *refs: weights_kernel(at, *refs),
+            in_specs=[VMEM_REF] * 5,
+            out_specs=[VMEM_REF] * 3,
+            out_shape=state + work[1:],
+            scratch_shapes=work[:1],
             compiler_params=PARAMS,
             cost_estimate=cost,
-            name="next_shard",
-        )(*in_vmem(across, bias, *carried), *pairs[mask])
+            name="shard_weights",
+        )(*in_vmem(across, bias, peak, summed), keys)
+
+    far_keys, peak, summed = lax.optimization_barrier((pairs[2][0], *carried))
+    third_keys = moved(far_keys, 1)
+    peak, summed, weights = shard_weights(2, far_keys, peak, summed)
+    far_values, summed, weights = lax.optimization_barrier((pairs[2][1], summed, weights))
+    third_values = moved(far_values, 1)
+    summed = pl.pallas_call(
+        values_kernel,
+        in_specs=[VMEM_REF] * 3,
+        out_specs=VMEM_REF,
+        out_shape=state[1],
+        compiler_params=PARAMS,
+        cost_estimate=cost,
+        name="shard_values",
+    )(*in_vmem(summed, weights), far_values)
+    peak, summed = pl.pallas_call(
+        lambda *refs: next_kernel(1, *refs),
+        in_specs=[VMEM_REF] * 6,
+        out_specs=[VMEM_REF] * 2,
+        out_shape=state,
+        scratch_shapes=work,
+        compiler_params=PARAMS,
+        cost_estimate=cost,
+        name="next_shard",
+    )(*in_vmem(across, bias, peak, summed), *pairs[1])
+    peak, summed, weights = shard_weights(3, third_keys, peak, summed)
     return pl.pallas_call(
-        lambda *refs: last_kernel(3, *refs),
-        in_specs=[VMEM_REF] * 6,
+        last_kernel,
+        in_specs=[VMEM_REF] * 3,
         out_specs=pl.BlockSpec(memory_space=pl.ANY),
         out_shape=jax.ShapeDtypeStruct((rows, cols), jnp.bfloat16),
-        scratch_shapes=work + [
+        scratch_shapes=[
             pltpu.VMEM((rows, cols), jnp.bfloat16),
             pltpu.SemaphoreType.DMA((heads,)),
         ],
         compiler_params=PARAMS,
         cost_estimate=cost,
-        name="last_shard",
-    )(*in_vmem(across, bias, *carried), *pairs[3])
+        name="last_values",
+    )(*in_vmem(summed, weights), third_values)
 
 
 def online_kernel(heads, q_ref, k_ref, v_ref, key_pos_ref, query_pos_ref, start_ref, out_ref, peak_ref, acc_ref):

time: 16.8 us -> 17.3 us (1.030)
  starting transfers between devices: 9.22 us -> 8.25 us
  waiting for transfers between devices: 0.82 us -> 1.66 us
  Pallas kernels: 6.59 us -> 7.16 us
    ppermute x6, starting transfers between devices: 9.22 us -> 8.25 us  [moved(): lax.ppermute(value, 'seq', [(i, i ^ mask) for i in range(lax.axis_size('s...]
    ppermute x6, waiting for transfers between devices: 0.82 us -> 1.66 us  [moved(): lax.ppermute(value, 'seq', [(i, i ^ mask) for i in range(lax.axis_size('s...]
    pallas_call x3 -> x5, Pallas kernels: 4.19 us -> 4.76 us  [the longest x2 2.03 us: shard_weights(): pl.pallas_call(lambda *refs: weights_kernel(at, *refs), in_specs=[VMEM_RE...]
  transfers between devices with their start and end apart: 6 -> 6, of which waited for: 1 -> 2; matrix products, arithmetic and copies ran while one was open for 0% -> 0% of each run, Pallas kernels for 28% -> 35%
where the time goes in v10:
time: 17.3 us; the launch traced here: 17.1 us
  starting transfers between devices  8.25 us (48%)
  Pallas kernels  7.16 us (41%)
  waiting for transfers between devices  1.66 us (10%)
    ppermute x6, starting transfers between devices, moved(): lax.ppermute(value, 'seq', [(i, i ^ mask) for i in range(lax.axis_size('s...  8.25 us
    pallas_call x1, Pallas kernels, staged_attention(): pl.pallas_call(lambda *refs: own_kernel(masks, *refs), in_specs=[pl.Block...  2.4 us
    pallas_call x2, Pallas kernels, shard_weights(): pl.pallas_call(lambda *refs: weights_kernel(at, *refs), in_specs=[VMEM_RE...  2.03 us
    ppermute x6, waiting for transfers between devices, moved(): lax.ppermute(value, 'seq', [(i, i ^ mask) for i in range(lax.axis_size('s...  1.66 us
    pallas_call x1, Pallas kernels, staged_attention(): pl.pallas_call(last_kernel, in_specs=[VMEM_REF] * 3, out_specs=pl.BlockSp...  1.24 us
    pallas_call x1, Pallas kernels, staged_attention(): pl.pallas_call(lambda *refs: next_kernel(1, *refs), in_specs=[VMEM_REF] *...  1.12 us
    pallas_call x1, Pallas kernels, staged_attention(): pl.pallas_call(values_kernel, in_specs=[VMEM_REF] * 3, out_specs=VMEM_REF...  0.37 us
  transfers between devices with their start and end apart: 6, of which 2 were waited for; matrix products, arithmetic and copies ran while one was open for 0% of the time, Pallas kernels for 35%

profile of v10, /device:TPU:0, one launch (start us, length us, event | category | flops | bytes accessed | tf_op | source)
XLA Modules:
  0.0 17.1 jit_solution(10216465869130085960)
XLA Ops:
  0.0 4.0 %collective-permute-start = (bf16[256,128]{1,0:T(8,128)(2,1)}, bf16[256,128]{1,0:T(8,128)(2,1)S(1)}, u32[]{:S(2)}, u32[]{:S(2)}) collective-permute-start(bf16[256,128]{1,0:T(8,128)(2,1)} %refs_4_.1), channel_id=1, source_target_pairs={{0,8},{4,12},{8,0},{12,4},{1,9},{5,13},{9,1},{13,5},{2,10},{6,14},... | collective-permute-start | bytes 196616 | tf_op jit(solution)/shard_map/ppermute | solution.py:230
  4.0 1.6 %collective-permute-start.2 = (bf16[256,128]{1,0:T(8,128)(2,1)}, bf16[256,128]{1,0:T(8,128)(2,1)S(1)}, u32[]{:S(2)}, u32[]{:S(2)}) collective-permute-start(bf16[256,128]{1,0:T(8,128)(2,1)} %refs_4_.1), channel_id=1, source_target_pairs={{0,4},{4,0},{8,12},{12,8},{1,5},{5,1},{9,13},{13,9},{2,6},{6,2},{1... | collective-permute-start | bytes 196616 | tf_op jit(solution)/shard_map/ppermute | solution.py:230
  5.6 0.3 %collective-permute-start.1 = (bf16[256,128]{1,0:T(8,128)(2,1)}, bf16[256,128]{1,0:T(8,128)(2,1)S(1)}, u32[]{:S(2)}, u32[]{:S(2)}) collective-permute-start(bf16[256,128]{1,0:T(8,128)(2,1)} %refs_5_.1), channel_id=1, source_target_pairs={{0,8},{4,12},{8,0},{12,4},{1,9},{5,13},{9,1},{13,5},{2,10},{6,14},... | collective-permute-start | bytes 196616 | tf_op jit(solution)/shard_map/ppermute | solution.py:230
  6.0 0.1 collective-permute-start.3
  6.1 2.4 %own_shard.1 = (bf16[8,128,256]{2,1,0:T(8,128)(2,1)S(1)}, f32[4,256,256]{2,1,0:T(8,128)S(1)}, f32[8,256]{1,0:T(8,128)S(1)}, f32[8,144,256]{2,1,0:T(8,128)S(1)}) custom-call(s32[1]{0:T(128)} %bitcast.refs_0_, s32[3]{0:T(128)} %refs_1_.1, s32[1,128]{1,0:T(1,128)} %bitcast.2, bf16[256,1024]{1,0:T(8,128)(2,1)} %refs_3_.1, bf16[256,128]{1,0:T(8,128)(2,1)} %refs_4_.1, ...), custom_call_target="tpu_custom_call" | custom-call | flops 402653184 | bytes 2097152 | tf_op jit(solution)/shard_map/own_shard/pallas_call | solution.py:250
  8.5 0.0 collective-permute-done.refs_4_
  8.5 2.0 %collective-permute-start.4 = (bf16[256,128]{1,0:T(8,128)(2,1)S(1)}, bf16[256,128]{1,0:T(8,128)(2,1)S(1)}, u32[]{:S(2)}, u32[]{:S(2)}) collective-permute-start(bf16[256,128]{1,0:T(8,128)(2,1)S(1)} %collective-permute-done.refs_4_), channel_id=1, source_target_pairs={{0,4},{4,0},{8,12},{12,8},{1,5},{5,1},{9,13},{13,9},{2,6},{6,2},{1... | collective-permute-start | bytes 196616 | tf_op jit(solution)/shard_map/ppermute | solution.py:230
  10.5 0.7 %shard_weights.2 = (f32[8,256]{1,0:T(8,128)S(1)}, f32[8,144,256]{2,1,0:T(8,128)S(1)}, bf16[8,256,256]{2,1,0:T(8,128)(2,1)S(1)}) custom-call(bf16[8,128,256]{2,1,0:T(8,128)(2,1)S(1)} %get-tuple-element.22.refs_0_, f32[4,256,256]{2,1,0:T(8,128)S(1)} %get-tuple-element.23.refs_1_, f32[8,256]{1,0:T(8,128)S(1)} %get-tuple-element.26.refs_2_, ...), custom_call_target="tpu_custom_call" | custom-call | flops 402653184 | bytes 2097152 | tf_op jit(solution)/shard_map/shard_weights/pallas_call | solution.py:271
  11.2 0.4 %collective-permute-done.1.v_ref = bf16[256,128]{1,0:T(8,128)(2,1)S(1)} collective-permute-done((bf16[256,128]{1,0:T(8,128)(2,1)}, bf16[256,128]{1,0:T(8,128)(2,1)S(1)}, u32[]{:S(2)}, u32[]{:S(2)}) %collective-permute-start.1) | collective-permute-done | bytes 65568 | tf_op jit(solution)/shard_map/ppermute | solution.py:230
  11.6 0.2 %collective-permute-start.5 = (bf16[256,128]{1,0:T(8,128)(2,1)S(1)}, bf16[256,128]{1,0:T(8,128)(2,1)S(1)}, u32[]{:S(2)}, u32[]{:S(2)}) collective-permute-start(bf16[256,128]{1,0:T(8,128)(2,1)S(1)} %collective-permute-done.1.v_ref), channel_id=1, source_target_pairs={{0,4},{4,0},{8,12},{12,8},{1,5},{5,1},{9,13},{13,9},{2,6},{6,2},{1... | collective-permute-start | bytes 196616 | tf_op jit(solution)/shard_map/ppermute | solution.py:230
  11.8 0.4 %shard_values.1.refs_3_ = f32[8,144,256]{2,1,0:T(8,128)S(1)} custom-call(f32[8,144,256]{2,1,0:T(8,128)S(1)} %get-tuple-element.32.sum_ref, bf16[8,256,256]{2,1,0:T(8,128)(2,1)S(1)} %get-tuple-element.33.weight_ref, bf16[256,128]{1,0:T(8,128)(2,1)S(1)} %collective-permute-done.1.v_ref), custom_call_target="tpu_custom_call" | custom-call | flops 402653184 | bytes 2097152 | tf_op jit(solution)/shard_map/shard_values/pallas_call | solution.py:287
  12.2 0.0 collective-permute-done.2.refs_4_
  12.2 0.0 collective-permute-done.3.refs_5_
  12.2 1.1 %next_shard.1 = (f32[8,256]{1,0:T(8,128)S(1)}, f32[8,144,256]{2,1,0:T(8,128)S(1)}) custom-call(bf16[8,128,256]{2,1,0:T(8,128)(2,1)S(1)} %get-tuple-element.22.refs_0_, f32[4,256,256]{2,1,0:T(8,128)S(1)} %get-tuple-element.23.refs_1_, f32[8,256]{1,0:T(8,128)S(1)} %get-tuple-element.29.refs_2_, f32[8,144,256]{2,1,0:T(8,128)S(1)} %shard_values.1.refs_3_, ...), custom_call_target="tpu_custom_call" | custom-call | flops 402653184 | bytes 2097152 | tf_op jit(solution)/shard_map/next_shard/pallas_call | solution.py:296
  13.4 0.0 collective-permute-done.4.refs_4_
  13.4 1.3 %shard_weights.3 = (f32[8,256]{1,0:T(8,128)}, f32[8,144,256]{2,1,0:T(8,128)S(1)}, bf16[8,256,256]{2,1,0:T(8,128)(2,1)S(1)}) custom-call(bf16[8,128,256]{2,1,0:T(8,128)(2,1)S(1)} %get-tuple-element.22.refs_0_, f32[4,256,256]{2,1,0:T(8,128)S(1)} %get-tuple-element.23.refs_1_, f32[8,256]{1,0:T(8,128)S(1)} %get-tuple-element.35.refs_2_, ...), custom_call_target="tpu_custom_call" | custom-call | flops 402653184 | bytes 2097152 | tf_op jit(solution)/shard_map/shard_weights/pallas_call | solution.py:271
  14.7 1.2 %collective-permute-done.5.v_ref = bf16[256,128]{1,0:T(8,128)(2,1)S(1)} collective-permute-done((bf16[256,128]{1,0:T(8,128)(2,1)S(1)}, bf16[256,128]{1,0:T(8,128)(2,1)S(1)}, u32[]{:S(2)}, u32[]{:S(2)}) %collective-permute-start.5) | collective-permute-done | bytes 65568 | tf_op jit(solution)/shard_map/ppermute | solution.py:230
  15.9 1.2 %last_values.1 = bf16[256,1024]{1,0:T(8,128)(2,1)} custom-call(f32[8,144,256]{2,1,0:T(8,128)S(1)} %get-tuple-element.37.sum_ref, bf16[8,256,256]{2,1,0:T(8,128)(2,1)S(1)} %get-tuple-element.38.weight_ref, bf16[256,128]{1,0:T(8,128)(2,1)S(1)} %collective-permute-done.5.v_ref), custom_call_target="tpu_custom_call" | custom-call | flops 402653184 | bytes 2097152 | tf_op jit(solution)/shard_map/last_values/pallas_call | solution.py:307
Async XLA Ops:
  0.0 8.5 %collective-permute-start = (bf16[256,128]{1,0:T(8,128)(2,1)}, bf16[256,128]{1,0:T(8,128)(2,1)S(1)}, u32[]{:S(2)}, u32[]{:S(2)}) collective-permute-start(bf16[256,128]{1,0:T(8,128)(2,1)} %refs_4_.1), channel_id=1, source_target_pairs={{0,8},{4,12},{8,0},{12,4},{1,9},{5,13},{9,1},{13,5},{2,10},{6,14},... | collective-permute-start | bytes 196616 | tf_op jit(solution)/shard_map/ppermute | solution.py:230
  4.0 8.2 %collective-permute-start.2 = (bf16[256,128]{1,0:T(8,128)(2,1)}, bf16[256,128]{1,0:T(8,128)(2,1)S(1)}, u32[]{:S(2)}, u32[]{:S(2)}) collective-permute-start(bf16[256,128]{1,0:T(8,128)(2,1)} %refs_4_.1), channel_id=1, source_target_pairs={{0,4},{4,0},{8,12},{12,8},{1,5},{5,1},{9,13},{13,9},{2,6},{6,2},{1... | collective-permute-start | bytes 196616 | tf_op jit(solution)/shard_map/ppermute | solution.py:230
  5.6 6.0 %collective-permute-start.1 = (bf16[256,128]{1,0:T(8,128)(2,1)}, bf16[256,128]{1,0:T(8,128)(2,1)S(1)}, u32[]{:S(2)}, u32[]{:S(2)}) collective-permute-start(bf16[256,128]{1,0:T(8,128)(2,1)} %refs_5_.1), channel_id=1, source_target_pairs={{0,8},{4,12},{8,0},{12,4},{1,9},{5,13},{9,1},{13,5},{2,10},{6,14},... | collective-permute-start | bytes 196616 | tf_op jit(solution)/shard_map/ppermute | solution.py:230
  6.0 6.3 %collective-permute-start.3 = (bf16[256,128]{1,0:T(8,128)(2,1)}, bf16[256,128]{1,0:T(8,128)(2,1)S(1)}, u32[]{:S(2)}, u32[]{:S(2)}) collective-permute-start(bf16[256,128]{1,0:T(8,128)(2,1)} %refs_5_.1), channel_id=1, source_target_pairs={{0,4},{4,0},{8,12},{12,8},{1,5},{5,1},{9,13},{13,9},{2,6},{6,2},{1... | collective-permute-start | bytes 196616 | tf_op jit(solution)/shard_map/ppermute | solution.py:230
  8.5 4.9 %collective-permute-start.4 = (bf16[256,128]{1,0:T(8,128)(2,1)S(1)}, bf16[256,128]{1,0:T(8,128)(2,1)S(1)}, u32[]{:S(2)}, u32[]{:S(2)}) collective-permute-start(bf16[256,128]{1,0:T(8,128)(2,1)S(1)} %collective-permute-done.refs_4_), channel_id=1, source_target_pairs={{0,4},{4,0},{8,12},{12,8},{1,5},{5,1},{9,13},{13,9},{2,6},{6,2},{1... | collective-permute-start | bytes 196616 | tf_op jit(solution)/shard_map/ppermute | solution.py:230
  11.6 4.3 %collective-permute-start.5 = (bf16[256,128]{1,0:T(8,128)(2,1)S(1)}, bf16[256,128]{1,0:T(8,128)(2,1)S(1)}, u32[]{:S(2)}, u32[]{:S(2)}) collective-permute-start(bf16[256,128]{1,0:T(8,128)(2,1)S(1)} %collective-permute-done.1.v_ref), channel_id=1, source_target_pairs={{0,4},{4,0},{8,12},{12,8},{1,5},{5,1},{9,13},{13,9},{2,6},{6,2},{1... | collective-permute-start | bytes 196616 | tf_op jit(solution)/shard_map/ppermute | solution.py:230

commit v11 on v10

--- a/solution.py
+++ b/solution.py
@@ -28,7 +28,7 @@
     return lax.broadcasted_iota(jnp.int32, shape, dim)
 
 
-def mask_tables(own, owners, lengths_ref, places_ref, rows, bias_ref):
+def mask_tables(owners, lengths_ref, places_ref, rows, bias_ref):
     block_total = places_ref.shape[1]
     block_rows = rows * lax.axis_size("seq") // block_total
     blocks = rows // block_rows
@@ -39,7 +39,7 @@
         axis=1, keepdims=True,
     ).astype(jnp.int32)
     across = (block_total, rows)
-    hit = as_column == own * blocks + iota(across, 1) // block_rows
+    hit = as_column == owners[0] * blocks + iota(across, 1) // block_rows
     at = jnp.where(hit, iota(across, 0) * block_rows, 0).astype(jnp.float32)
     query_pos = jnp.sum(at, axis=0, keepdims=True) + (
         iota((1, rows), 1) % block_rows
@@ -96,7 +96,7 @@
 
 
 def own_kernel(
-    masks, own_ref, lengths_hbm, places_hbm, q_hbm, k_hbm, v_hbm,
+    own_ref, first_ref, lengths_hbm, places_hbm, q_hbm, k_hbm, v_hbm,
     across_ref, bias_ref, peak_ref, sum_ref,
     lengths_ref, places_ref, q_ref, k_ref, v_ref, scaled_ref, weight_ref, sems,
 ):
@@ -110,9 +110,9 @@
     copies[0].wait()
     copies[1].wait()
     heads, _, rows = across_ref.shape
-    own = own_ref[0]
-    owners = [own] + [own ^ mask for mask in masks]
-    mask_tables(own, owners, lengths_ref, places_ref, rows, bias_ref)
+    own, first = own_ref[0], first_ref[0]
+    owners = [own, own ^ first, own ^ 3 ^ first, own ^ 3]
+    mask_tables(owners, lengths_ref, places_ref, rows, bias_ref)
     for copy in copies[2:]:
         copy.wait()
     keys = k_ref[...]
@@ -160,11 +160,9 @@
 
 
 def weights_kernel(
-    at, across_ref, bias_ref, peak_ref, sum_ref, k_ref,
-    new_peak_ref, new_sum_ref, weight_ref, scaled_ref,
+    at, across_ref, bias_ref, peak_ref, sum_ref, k_ref, new_sum_ref, weight_ref, scaled_ref,
 ):
     def rescale(head, peak):
-        new_peak_ref[head:head + 1, :] = peak
         new_sum_ref[head] = sum_ref[head] * jnp.exp2(peak_ref[head:head + 1, :] - peak)
 
     in_stages(across_ref.shape[0], [
@@ -177,13 +175,6 @@
     ])
 
 
-def values_kernel(sum_ref, weight_ref, v_ref, new_sum_ref):
-    turned = values_down(v_ref[...])
-    for head in range(sum_ref.shape[0]):
-        added = jnp.dot(turned, weight_ref[head], preferred_element_type=jnp.float32)
-        new_sum_ref[head] = sum_ref[head] + added
-
-
 def last_kernel(sum_ref, weight_ref, v_ref, out_ref, block_ref, sems):
     turned = values_down(v_ref[...])
     copies = []
@@ -205,12 +196,7 @@
         copy.wait()
 
 
-def estimate(rows, heads, key_count):
-    return pl.CostEstimate(
-        flops=6 * heads * rows * key_count * HEAD_WIDTH,
-        bytes_accessed=8 * heads * rows * HEAD_WIDTH,
-        transcendentals=heads * rows * key_count,
-    )
+SHORT = pl.CostEstimate(flops=0, bytes_accessed=0, transcendentals=0)
 
 
 def in_vmem(*arrays):
@@ -226,17 +212,25 @@
 PARAMS = pltpu.CompilerParams(vmem_limit_bytes=32 << 20)
 
 
-def moved(value, mask):
-    return lax.ppermute(value, "seq", [(i, i ^ mask) for i in range(lax.axis_size("seq"))])
+def moved(value, *masks):
+    seq_size, mp_size = lax.axis_size("seq"), lax.axis_size("mp")
+    pairs = [
+        (index * mp_size + place, (index ^ masks[place % len(masks)]) * mp_size + place)
+        for index in range(seq_size)
+        for place in range(mp_size)
+    ]
+    return lax.ppermute(value, ("seq", "mp"), pairs)
 
 
 def staged_attention(queries, keys, values, lengths, old_place):
-    pairs = {mask: [moved(part, mask) for part in (keys, values)] for mask in (2, 1)}
+    first_keys, second_keys = moved(keys, 2, 1), moved(keys, 1, 2)
+    first_values, second_values = moved(values, 2, 1), moved(values, 1, 2)
     rows, cols = queries.shape
     heads = cols // HEAD_WIDTH
     devices = lax.axis_size("seq")
-    masks = (1, 2, 3)
-    own = lax.axis_index("seq").astype(jnp.int32).reshape(1)
+    own = lax.axis_index("seq").astype(jnp.int32)
+    far_first = lax.axis_index("mp") % 2 == 0
+    first = jnp.where(far_first, 2, 1).astype(jnp.int32)
     places = old_place.reshape(1, -1)
     state = [
         pltpu.VMEM((heads, rows), jnp.float32),
@@ -246,10 +240,9 @@
         pltpu.VMEM((heads, rows, rows), jnp.float32),
         pltpu.VMEM((heads, rows, rows), jnp.bfloat16),
     ]
-    cost = estimate(rows, heads, rows)
     across, bias, *carried = pl.pallas_call(
-        lambda *refs: own_kernel(masks, *refs),
-        in_specs=[pl.BlockSpec(memory_space=pltpu.SMEM)] + [HBM_REF] * 5,
+        own_kernel,
+        in_specs=[pl.BlockSpec(memory_space=pltpu.SMEM)] * 2 + [HBM_REF] * 5,
         out_specs=[VMEM_REF] * 4,
         out_shape=[
             pltpu.VMEM((heads, HEAD_WIDTH, rows), jnp.bfloat16),
@@ -263,47 +256,41 @@
             pltpu.VMEM(values.shape, jnp.bfloat16),
         ] + work + [pltpu.SemaphoreType.DMA((5,))],
         compiler_params=PARAMS,
-        cost_estimate=cost,
+        cost_estimate=SHORT,
         name="own_shard",
-    )(own, *in_hbm(lengths, places, queries, keys, values))
-
-    def shard_weights(at, keys, peak, summed):
+    )(own.reshape(1), first.reshape(1), *in_hbm(lengths, places, queries, keys, values))
+
+    def add_shard(at, keys, values, carried):
         return pl.pallas_call(
-            lambda *refs: weights_kernel(at, *refs),
-            in_specs=[VMEM_REF] * 5,
-            out_specs=[VMEM_REF] * 3,
-            out_shape=state + work[1:],
-            scratch_shapes=work[:1],
+            lambda *refs: next_kernel(at, *refs),
+            in_specs=[VMEM_REF] * 6,
+            out_specs=[VMEM_REF] * 2,
+            out_shape=state,
+            scratch_shapes=work,
             compiler_params=PARAMS,
-            cost_estimate=cost,
-            name="shard_weights",
-        )(*in_vmem(across, bias, peak, summed), keys)
-
-    far_keys, peak, summed = lax.optimization_barrier((pairs[2][0], *carried))
-    third_keys = moved(far_keys, 1)
-    peak, summed, weights = shard_weights(2, far_keys, peak, summed)
-    far_values, summed, weights = lax.optimization_barrier((pairs[2][1], summed, weights))
-    third_values = moved(far_values, 1)
-    summed = pl.pallas_call(
-        values_kernel,
-        in_specs=[VMEM_REF] * 3,
-        out_specs=VMEM_REF,
-        out_shape=state[1],
+            cost_estimate=SHORT,
+            name="next_shard",
+        )(*in_vmem(across, bias, *carried), keys, values)
+
+    carried = add_shard(1, first_keys, first_values, carried)
+    relayed = []
+    for one, other in ((first_keys, second_keys), (first_values, second_values)):
+        one, other, *carried = lax.optimization_barrier((one, other, *carried))
+        far = jnp.where(far_first, one, other)
+        far, *carried = lax.optimization_barrier((far, *carried))
+        relayed.append(moved(far, 1))
+    third_keys, third_values = relayed
+    carried = add_shard(2, second_keys, second_values, carried)
+    summed, weights = pl.pallas_call(
+        lambda *refs: weights_kernel(3, *refs),
+        in_specs=[VMEM_REF] * 5,
+        out_specs=[VMEM_REF] * 2,
+        out_shape=state[1:] + work[1:],
+        scratch_shapes=work[:1],
         compiler_params=PARAMS,
-        cost_estimate=cost,
-        name="shard_values",
-    )(*in_vmem(summed, weights), far_values)
-    peak, summed = pl.pallas_call(
-        lambda *refs: next_kernel(1, *refs),
-        in_specs=[VMEM_REF] * 6,
-        out_specs=[VMEM_REF] * 2,
-        out_shape=state,
-        scratch_shapes=work,
-        compiler_params=PARAMS,
-        cost_estimate=cost,
-        name="next_shard",
-    )(*in_vmem(across, bias, peak, summed), *pairs[1])
-    peak, summed, weights = shard_weights(3, third_keys, peak, summed)
+        cost_estimate=SHORT,
+        name="last_weights",
+    )(*in_vmem(across, bias, *carried), third_keys)
     return pl.pallas_call(
         last_kernel,
         in_specs=[VMEM_REF] * 3,
@@ -314,7 +301,7 @@
             pltpu.SemaphoreType.DMA((heads,)),
         ],
         compiler_params=PARAMS,
-        cost_estimate=cost,
+        cost_estimate=SHORT,
         name="last_values",
     )(*in_vmem(summed, weights), third_values)
 

time: 17.3 us -> 19.8 us (1.14)
  waiting for transfers between devices: 1.66 us -> 4.54 us
  Pallas kernels: 7.16 us -> 6.72 us
    ppermute x6, waiting for transfers between devices: 1.66 us -> 4.54 us  [moved(): return lax.ppermute(value, ('seq', 'mp'), pairs)]
    pallas_call x5 -> x4, Pallas kernels: 5.92 us -> 5.46 us  [the longest x1 2.43 us: staged_attention(): pl.pallas_call(own_kernel, in_specs=[pl.BlockSpec(memory_space=pltpu.SMEM...]
  transfers between devices with their start and end apart: 6 -> 6, of which waited for: 2 -> 2; matrix products, arithmetic and copies ran while one was open for 0% -> 0% of each run, Pallas kernels for 35% -> 28%
where the time goes in v11:
time: 19.8 us; the launch traced here: 19.6 us
  starting transfers between devices  8.25 us (42%)
  Pallas kernels  6.72 us (34%)
  waiting for transfers between devices  4.54 us (23%)
    ppermute x6, starting transfers between devices, moved(): return lax.ppermute(value, ('seq', 'mp'), pairs)  8.25 us
    ppermute x6, waiting for transfers between devices, moved(): return lax.ppermute(value, ('seq', 'mp'), pairs)  4.54 us
    pallas_call x1, Pallas kernels, staged_attention(): pl.pallas_call(own_kernel, in_specs=[pl.BlockSpec(memory_space=pltpu.SMEM...  2.43 us
    pallas_call x2, Pallas kernels, add_shard(): pl.pallas_call(lambda *refs: next_kernel(at, *refs), in_specs=[VMEM_REF]...  2.24 us
    pallas_call x1, Pallas kernels, staged_attention(): pl.pallas_call(last_kernel, in_specs=[VMEM_REF] * 3, out_specs=pl.BlockSp...  1.26 us
    pallas_call x1, Pallas kernels, staged_attention(): pl.pallas_call(lambda *refs: weights_kernel(3, *refs), in_specs=[VMEM_REF...  0.79 us
  transfers between devices with their start and end apart: 6, of which 2 were waited for; matrix products, arithmetic and copies ran while one was open for 0% of the time, Pallas kernels for 28%

profile of v11, /device:TPU:0, one launch (start us, length us, event | category | flops | bytes accessed | tf_op | source)
XLA Modules:
  0.0 19.6 jit_solution(17677424168620932726)
XLA Ops:
  0.0 4.0 %collective-permute-start.2 = (bf16[256,128]{1,0:T(8,128)(2,1)}, bf16[256,128]{1,0:T(8,128)(2,1)S(1)}, u32[]{:S(2)}, u32[]{:S(2)}) collective-permute-start(bf16[256,128]{1,0:T(8,128)(2,1)} %k_hbm.1), channel_id=1, source_target_pairs={{0,8},{1,5},{2,10},{3,7},{4,12},{5,1},{6,14},{7,3},{8,0},{9,13},{1... | collective-permute-start | bytes 196616 | tf_op jit(solution)/shard_map/ppermute | solution.py:222
  4.0 0.0 collective-permute-start
  4.1 1.9 %collective-permute-start.3 = (bf16[256,128]{1,0:T(8,128)(2,1)}, bf16[256,128]{1,0:T(8,128)(2,1)S(1)}, u32[]{:S(2)}, u32[]{:S(2)}) collective-permute-start(bf16[256,128]{1,0:T(8,128)(2,1)} %k_hbm.1), channel_id=1, source_target_pairs={{0,4},{1,9},{2,6},{3,11},{4,0},{5,13},{6,2},{7,15},{8,12},{9,1},{1... | collective-permute-start | bytes 196616 | tf_op jit(solution)/shard_map/ppermute | solution.py:222
  6.0 0.1 collective-permute-start.1
  6.1 2.4 %own_shard.1 = (bf16[8,128,256]{2,1,0:T(8,128)(2,1)S(1)}, f32[4,256,256]{2,1,0:T(8,128)S(1)}, f32[8,256]{1,0:T(8,128)S(1)}, f32[8,144,256]{2,1,0:T(8,128)S(1)}) custom-call(s32[1]{0:T(128)} %bitcast.own_ref, s32[1]{0:T(128)} %bitcast.1.first_ref, s32[3]{0:T(128)} %lengths_hbm.1, s32[1,128]{1,0:T(1,128)} %bitcast.3, bf16[256,1024]{1,0:T(8,128)(2,1)} %q_hbm.1, ...), custom_call_target="tpu_custom_call" | custom-call | tf_op jit(solution)/shard_map/own_shard/pallas_call | solution.py:243
  8.5 0.0 collective-permute-done.2.refs_4_
  8.5 3.5 %collective-permute-done.refs_5_ = bf16[256,128]{1,0:T(8,128)(2,1)S(1)} collective-permute-done((bf16[256,128]{1,0:T(8,128)(2,1)}, bf16[256,128]{1,0:T(8,128)(2,1)S(1)}, u32[]{:S(2)}, u32[]{:S(2)}) %collective-permute-start) | collective-permute-done | bytes 65568 | tf_op jit(solution)/shard_map/ppermute | solution.py:222
  12.0 1.1 %next_shard.2 = (f32[8,256]{1,0:T(8,128)S(1)}, f32[8,144,256]{2,1,0:T(8,128)S(1)}) custom-call(bf16[8,128,256]{2,1,0:T(8,128)(2,1)S(1)} %get-tuple-element.29.refs_0_, f32[4,256,256]{2,1,0:T(8,128)S(1)} %get-tuple-element.30.refs_1_, f32[8,256]{1,0:T(8,128)S(1)} %get-tuple-element.31.refs_2_, f32[8,144,256]{2,1,0:T(8,128)S(1)} %get-tuple-element.32.refs_3_, ...), custom_call_target="tpu_custom_call" | custom-call | tf_op jit(solution)/shard_map/next_shard/pallas_call | solution.py:264
  13.2 0.0 collective-permute-done.3.refs_4_
  13.2 0.0 collective-permute-done.1.refs_5_
  13.2 0.5 %collective-permute-start.4 = (bf16[256,128]{1,0:T(8,128)(2,1)S(1)}, bf16[256,128]{1,0:T(8,128)(2,1)S(1)}, u32[]{:S(2)}, u32[]{:S(2)}) collective-permute-start(bf16[256,128]{1,0:T(8,128)(2,1)S(1)} %broadcast_select_fusion.1), channel_id=1, source_target_pairs={{0,4},{1,5},{2,6},{3,7},{4,0},{5,1},{6,2},{7,3},{8,12},{9,13},{10,... | collective-permute-start | bytes 196616 | tf_op jit(solution)/shard_map/ppermute | solution.py:222
  13.8 1.6 %collective-permute-start.5 = (bf16[256,128]{1,0:T(8,128)(2,1)S(1)}, bf16[256,128]{1,0:T(8,128)(2,1)S(1)}, u32[]{:S(2)}, u32[]{:S(2)}) collective-permute-start(bf16[256,128]{1,0:T(8,128)(2,1)S(1)} %broadcast_select_fusion), channel_id=1, source_target_pairs={{0,4},{1,5},{2,6},{3,7},{4,0},{5,1},{6,2},{7,3},{8,12},{9,13},{10,... | collective-permute-start | bytes 196616 | tf_op jit(solution)/shard_map/ppermute | solution.py:222
  15.4 1.1 %next_shard.3 = (f32[8,256]{1,0:T(8,128)S(1)}, f32[8,144,256]{2,1,0:T(8,128)S(1)}) custom-call(bf16[8,128,256]{2,1,0:T(8,128)(2,1)S(1)} %get-tuple-element.29.refs_0_, f32[4,256,256]{2,1,0:T(8,128)S(1)} %get-tuple-element.30.refs_1_, f32[8,256]{1,0:T(8,128)S(1)} %get-tuple-element.45.refs_2_, f32[8,144,256]{2,1,0:T(8,128)S(1)} %get-tuple-element.46.refs_3_, ...), custom_call_target="tpu_custom_call" | custom-call | tf_op jit(solution)/shard_map/next_shard/pallas_call | solution.py:264
  16.5 1.0 %collective-permute-done.4.refs_4_ = bf16[256,128]{1,0:T(8,128)(2,1)S(1)} collective-permute-done((bf16[256,128]{1,0:T(8,128)(2,1)S(1)}, bf16[256,128]{1,0:T(8,128)(2,1)S(1)}, u32[]{:S(2)}, u32[]{:S(2)}) %collective-permute-start.4) | collective-permute-done | bytes 65568 | tf_op jit(solution)/shard_map/ppermute | solution.py:222
  17.5 0.8 %last_weights.1 = (f32[8,144,256]{2,1,0:T(8,128)S(1)}, bf16[8,256,256]{2,1,0:T(8,128)(2,1)S(1)}) custom-call(bf16[8,128,256]{2,1,0:T(8,128)(2,1)S(1)} %get-tuple-element.29.refs_0_, f32[4,256,256]{2,1,0:T(8,128)S(1)} %get-tuple-element.30.refs_1_, f32[8,256]{1,0:T(8,128)S(1)} %get-tuple-element.47.refs_2_, f32[8,144,256]{2,1,0:T(8,128)S(1)} %get-tuple-element.48.refs_3_, ...), custom_call_target="tpu_custom_call" | custom-call | tf_op jit(solution)/shard_map/last_weights/pallas_call | solution.py:284
  18.3 0.0 collective-permute-done.5.v_ref
  18.4 1.3 %last_values.1 = bf16[256,1024]{1,0:T(8,128)(2,1)} custom-call(f32[8,144,256]{2,1,0:T(8,128)S(1)} %get-tuple-element.50.sum_ref, bf16[8,256,256]{2,1,0:T(8,128)(2,1)S(1)} %get-tuple-element.51.weight_ref, bf16[256,128]{1,0:T(8,128)(2,1)S(1)} %collective-permute-done.5.v_ref), custom_call_target="tpu_custom_call" | custom-call | tf_op jit(solution)/shard_map/last_values/pallas_call | solution.py:294
  (2 shorter events, 0.0 us)
Async XLA Ops:
  0.0 8.5 %collective-permute-start.2 = (bf16[256,128]{1,0:T(8,128)(2,1)}, bf16[256,128]{1,0:T(8,128)(2,1)S(1)}, u32[]{:S(2)}, u32[]{:S(2)}) collective-permute-start(bf16[256,128]{1,0:T(8,128)(2,1)} %k_hbm.1), channel_id=1, source_target_pairs={{0,8},{1,5},{2,10},{3,7},{4,12},{5,1},{6,14},{7,3},{8,0},{9,13},{1... | collective-permute-start | bytes 196616 | tf_op jit(solution)/shard_map/ppermute | solution.py:222
  4.0 8.0 %collective-permute-start = (bf16[256,128]{1,0:T(8,128)(2,1)}, bf16[256,128]{1,0:T(8,128)(2,1)S(1)}, u32[]{:S(2)}, u32[]{:S(2)}) collective-permute-start(bf16[256,128]{1,0:T(8,128)(2,1)} %v_hbm.1), channel_id=1, source_target_pairs={{0,8},{1,5},{2,10},{3,7},{4,12},{5,1},{6,14},{7,3},{8,0},{9,13},{1... | collective-permute-start | bytes 196616 | tf_op jit(solution)/shard_map/ppermute | solution.py:222
  4.1 9.1 %collective-permute-start.3 = (bf16[256,128]{1,0:T(8,128)(2,1)}, bf16[256,128]{1,0:T(8,128)(2,1)S(1)}, u32[]{:S(2)}, u32[]{:S(2)}) collective-permute-start(bf16[256,128]{1,0:T(8,128)(2,1)} %k_hbm.1), channel_id=1, source_target_pairs={{0,4},{1,9},{2,6},{3,11},{4,0},{5,13},{6,2},{7,15},{8,12},{9,1},{1... | collective-permute-start | bytes 196616 | tf_op jit(solution)/shard_map/ppermute | solution.py:222
  6.0 7.3 %collective-permute-start.1 = (bf16[256,128]{1,0:T(8,128)(2,1)}, bf16[256,128]{1,0:T(8,128)(2,1)S(1)}, u32[]{:S(2)}, u32[]{:S(2)}) collective-permute-start(bf16[256,128]{1,0:T(8,128)(2,1)} %v_hbm.1), channel_id=1, source_target_pairs={{0,4},{1,9},{2,6},{3,11},{4,0},{5,13},{6,2},{7,15},{8,12},{9,1},{1... | collective-permute-start | bytes 196616 | tf_op jit(solution)/shard_map/ppermute | solution.py:222
  13.2 4.3 %collective-permute-start.4 = (bf16[256,128]{1,0:T(8,128)(2,1)S(1)}, bf16[256,128]{1,0:T(8,128)(2,1)S(1)}, u32[]{:S(2)}, u32[]{:S(2)}) collective-permute-start(bf16[256,128]{1,0:T(8,128)(2,1)S(1)} %broadcast_select_fusion.1), channel_id=1, source_target_pairs={{0,4},{1,5},{2,6},{3,7},{4,0},{5,1},{6,2},{7,3},{8,12},{9,13},{10,... | collective-permute-start | bytes 196616 | tf_op jit(solution)/shard_map/ppermute | solution.py:222
  13.8 4.6 %collective-permute-start.5 = (bf16[256,128]{1,0:T(8,128)(2,1)S(1)}, bf16[256,128]{1,0:T(8,128)(2,1)S(1)}, u32[]{:S(2)}, u32[]{:S(2)}) collective-permute-start(bf16[256,128]{1,0:T(8,128)(2,1)S(1)} %broadcast_select_fusion), channel_id=1, source_target_pairs={{0,4},{1,5},{2,6},{3,7},{4,0},{5,1},{6,2},{7,3},{8,12},{9,13},{10,... | collective-permute-start | bytes 196616 | tf_op jit(solution)/shard_map/ppermute | solution.py:222

commit v12 on v11

--- a/solution.py
+++ b/solution.py
@@ -96,7 +96,7 @@
 
 
 def own_kernel(
-    own_ref, first_ref, lengths_hbm, places_hbm, q_hbm, k_hbm, v_hbm,
+    own_ref, lengths_hbm, places_hbm, q_hbm, k_hbm, v_hbm,
     across_ref, bias_ref, peak_ref, sum_ref,
     lengths_ref, places_ref, q_ref, k_ref, v_ref, scaled_ref, weight_ref, sems,
 ):
@@ -110,8 +110,7 @@
     copies[0].wait()
     copies[1].wait()
     heads, _, rows = across_ref.shape
-    own, first = own_ref[0], first_ref[0]
-    owners = [own, own ^ first, own ^ 3 ^ first, own ^ 3]
+    owners = [own_ref[0] ^ mask for mask in range(bias_ref.shape[0])]
     mask_tables(owners, lengths_ref, places_ref, rows, bias_ref)
     for copy in copies[2:]:
         copy.wait()
@@ -212,25 +211,17 @@
 PARAMS = pltpu.CompilerParams(vmem_limit_bytes=32 << 20)
 
 
-def moved(value, *masks):
-    seq_size, mp_size = lax.axis_size("seq"), lax.axis_size("mp")
-    pairs = [
-        (index * mp_size + place, (index ^ masks[place % len(masks)]) * mp_size + place)
-        for index in range(seq_size)
-        for place in range(mp_size)
-    ]
-    return lax.ppermute(value, ("seq", "mp"), pairs)
+def moved(value, mask):
+    return lax.ppermute(value, "seq", [(i, i ^ mask) for i in range(lax.axis_size("seq"))])
 
 
 def staged_attention(queries, keys, values, lengths, old_place):
-    first_keys, second_keys = moved(keys, 2, 1), moved(keys, 1, 2)
-    first_values, second_values = moved(values, 2, 1), moved(values, 1, 2)
+    far_keys, far_values = moved(keys, 2), moved(values, 2)
+    near_keys, near_values = moved(keys, 1), moved(values, 1)
     rows, cols = queries.shape
     heads = cols // HEAD_WIDTH
     devices = lax.axis_size("seq")
     own = lax.axis_index("seq").astype(jnp.int32)
-    far_first = lax.axis_index("mp") % 2 == 0
-    first = jnp.where(far_first, 2, 1).astype(jnp.int32)
     places = old_place.reshape(1, -1)
     state = [
         pltpu.VMEM((heads, rows), jnp.float32),
@@ -242,7 +233,7 @@
     ]
     across, bias, *carried = pl.pallas_call(
         own_kernel,
-        in_specs=[pl.BlockSpec(memory_space=pltpu.SMEM)] * 2 + [HBM_REF] * 5,
+        in_specs=[pl.BlockSpec(memory_space=pltpu.SMEM)] + [HBM_REF] * 5,
         out_specs=[VMEM_REF] * 4,
         out_shape=[
             pltpu.VMEM((heads, HEAD_WIDTH, rows), jnp.bfloat16),
@@ -258,7 +249,7 @@
         compiler_params=PARAMS,
         cost_estimate=SHORT,
         name="own_shard",
-    )(own.reshape(1), first.reshape(1), *in_hbm(lengths, places, queries, keys, values))
+    )(own.reshape(1), *in_hbm(lengths, places, queries, keys, values))
 
     def add_shard(at, keys, values, carried):
         return pl.pallas_call(
@@ -272,15 +263,12 @@
             name="next_shard",
         )(*in_vmem(across, bias, *carried), keys, values)
 
-    carried = add_shard(1, first_keys, first_values, carried)
-    relayed = []
-    for one, other in ((first_keys, second_keys), (first_values, second_values)):
-        one, other, *carried = lax.optimization_barrier((one, other, *carried))
-        far = jnp.where(far_first, one, other)
-        far, *carried = lax.optimization_barrier((far, *carried))
-        relayed.append(moved(far, 1))
-    third_keys, third_values = relayed
-    carried = add_shard(2, second_keys, second_values, carried)
+    far_keys, *carried = lax.optimization_barrier((far_keys, *carried))
+    third_keys = moved(far_keys, 1)
+    far_values, *carried = lax.optimization_barrier((far_values, *carried))
+    third_values = moved(far_values, 1)
+    carried = add_shard(2, far_keys, far_values, carried)
+    carried = add_shard(1, near_keys, near_values, carried)
     summed, weights = pl.pallas_call(
         lambda *refs: weights_kernel(3, *refs),
         in_specs=[VMEM_REF] * 5,

time: 19.8 us -> 16.2 us (0.82)
  waiting for transfers between devices: 4.54 us -> 0.03 us
  starting transfers between devices: 8.25 us -> 9.19 us
    ppermute x6, waiting for transfers between devices: 4.54 us -> 0.03 us  [moved(): lax.ppermute(value, 'seq', [(i, i ^ mask) for i in range(lax.axis_size('s...]
    ppermute x6, starting transfers between devices: 8.25 us -> 9.19 us  [moved(): lax.ppermute(value, 'seq', [(i, i ^ mask) for i in range(lax.axis_size('s...]
  transfers between devices with their start and end apart: 6 -> 6, of which waited for: 2 -> 0; matrix products, arithmetic and copies ran while one was open for 0% -> 0% of each run, Pallas kernels for 28% -> 34%
where the time goes in v12:
time: 16.2 us; the launch traced here: 16 us
  starting transfers between devices  9.19 us (57%)
  Pallas kernels  6.73 us (42%)
    ppermute x6, starting transfers between devices, moved(): lax.ppermute(value, 'seq', [(i, i ^ mask) for i in range(lax.axis_size('s...  9.19 us
    pallas_call x1, Pallas kernels, staged_attention(): pl.pallas_call(own_kernel, in_specs=[pl.BlockSpec(memory_space=pltpu.SMEM...  2.42 us
    pallas_call x2, Pallas kernels, add_shard(): pl.pallas_call(lambda *refs: next_kernel(at, *refs), in_specs=[VMEM_REF]...  2.25 us
    pallas_call x1, Pallas kernels, staged_attention(): pl.pallas_call(last_kernel, in_specs=[VMEM_REF] * 3, out_specs=pl.BlockSp...  1.26 us
    pallas_call x1, Pallas kernels, staged_attention(): pl.pallas_call(lambda *refs: weights_kernel(3, *refs), in_specs=[VMEM_REF...  0.8 us
  transfers between devices with their start and end apart: 6, of which 0 were waited for; matrix products, arithmetic and copies ran while one was open for 0% of the time, Pallas kernels for 34%

profile of v12, /device:TPU:0, one launch (start us, length us, event | category | flops | bytes accessed | tf_op | source)
XLA Modules:
  0.0 16.0 jit_solution(7367311946831083109)
XLA Ops:
  0.0 4.0 %collective-permute-start.1 = (bf16[256,128]{1,0:T(8,128)(2,1)}, bf16[256,128]{1,0:T(8,128)(2,1)S(1)}, u32[]{:S(2)}, u32[]{:S(2)}) collective-permute-start(bf16[256,128]{1,0:T(8,128)(2,1)} %k_hbm.1), channel_id=1, source_target_pairs={{0,8},{4,12},{8,0},{12,4},{1,9},{5,13},{9,1},{13,5},{2,10},{6,14},... | collective-permute-start | bytes 196616 | tf_op jit(solution)/shard_map/ppermute | solution.py:215
  4.0 0.0 collective-permute-start
  4.1 1.9 %collective-permute-start.2 = (bf16[256,128]{1,0:T(8,128)(2,1)}, bf16[256,128]{1,0:T(8,128)(2,1)S(1)}, u32[]{:S(2)}, u32[]{:S(2)}) collective-permute-start(bf16[256,128]{1,0:T(8,128)(2,1)} %k_hbm.1), channel_id=1, source_target_pairs={{0,4},{4,0},{8,12},{12,8},{1,5},{5,1},{9,13},{13,9},{2,6},{6,2},{1... | collective-permute-start | bytes 196616 | tf_op jit(solution)/shard_map/ppermute | solution.py:215
  6.0 0.1 collective-permute-start.3
  6.1 2.4 %own_shard.1 = (bf16[8,128,256]{2,1,0:T(8,128)(2,1)S(1)}, f32[4,256,256]{2,1,0:T(8,128)S(1)}, f32[8,256]{1,0:T(8,128)S(1)}, f32[8,144,256]{2,1,0:T(8,128)S(1)}) custom-call(s32[1]{0:T(128)} %bitcast.own_ref, s32[3]{0:T(128)} %lengths_hbm.1, s32[1,128]{1,0:T(1,128)} %bitcast.2, bf16[256,1024]{1,0:T(8,128)(2,1)} %q_hbm.1, bf16[256,128]{1,0:T(8,128)(2,1)} %k_hbm.1, ...), custom_call_target="tpu_custom_call" | custom-call | tf_op jit(solution)/shard_map/own_shard/pallas_call | solution.py:234
  8.5 0.0 collective-permute-done.1.refs_4_
  8.5 1.9 %collective-permute-start.4 = (bf16[256,128]{1,0:T(8,128)(2,1)S(1)}, bf16[256,128]{1,0:T(8,128)(2,1)S(1)}, u32[]{:S(2)}, u32[]{:S(2)}) collective-permute-start(bf16[256,128]{1,0:T(8,128)(2,1)S(1)} %collective-permute-done.1.refs_4_), channel_id=1, source_target_pairs={{0,4},{4,0},{8,12},{12,8},{1,5},{5,1},{9,13},{13,9},{2,6},{6,2},{1... | collective-permute-start | bytes 196616 | tf_op jit(solution)/shard_map/ppermute | solution.py:215
  10.5 0.0 collective-permute-done.refs_5_
  10.5 1.2 %collective-permute-start.5 = (bf16[256,128]{1,0:T(8,128)(2,1)S(1)}, bf16[256,128]{1,0:T(8,128)(2,1)S(1)}, u32[]{:S(2)}, u32[]{:S(2)}) collective-permute-start(bf16[256,128]{1,0:T(8,128)(2,1)S(1)} %collective-permute-done.refs_5_), channel_id=1, source_target_pairs={{0,4},{4,0},{8,12},{12,8},{1,5},{5,1},{9,13},{13,9},{2,6},{6,2},{1... | collective-permute-start | bytes 196616 | tf_op jit(solution)/shard_map/ppermute | solution.py:215
  11.6 1.1 %next_shard.2 = (f32[8,256]{1,0:T(8,128)S(1)}, f32[8,144,256]{2,1,0:T(8,128)S(1)}) custom-call(bf16[8,128,256]{2,1,0:T(8,128)(2,1)S(1)} %get-tuple-element.21.refs_0_, f32[4,256,256]{2,1,0:T(8,128)S(1)} %get-tuple-element.22.refs_1_, f32[8,256]{1,0:T(8,128)S(1)} %get-tuple-element.27.refs_2_, f32[8,144,256]{2,1,0:T(8,128)S(1)} %get-tuple-element.28.refs_3_, ...), custom_call_target="tpu_custom_call" | custom-call | tf_op jit(solution)/shard_map/next_shard/pallas_call | solution.py:255
  12.8 0.0 collective-permute-done.2.refs_4_
  12.8 0.0 collective-permute-done.3.refs_5_
  12.8 1.1 %next_shard.3 = (f32[8,256]{1,0:T(8,128)S(1)}, f32[8,144,256]{2,1,0:T(8,128)S(1)}) custom-call(bf16[8,128,256]{2,1,0:T(8,128)(2,1)S(1)} %get-tuple-element.21.refs_0_, f32[4,256,256]{2,1,0:T(8,128)S(1)} %get-tuple-element.22.refs_1_, f32[8,256]{1,0:T(8,128)S(1)} %get-tuple-element.31.refs_2_, f32[8,144,256]{2,1,0:T(8,128)S(1)} %get-tuple-element.32.refs_3_, ...), custom_call_target="tpu_custom_call" | custom-call | tf_op jit(solution)/shard_map/next_shard/pallas_call | solution.py:255
  13.9 0.0 collective-permute-done.4.refs_4_
  13.9 0.8 %last_weights.1 = (f32[8,144,256]{2,1,0:T(8,128)S(1)}, bf16[8,256,256]{2,1,0:T(8,128)(2,1)S(1)}) custom-call(bf16[8,128,256]{2,1,0:T(8,128)(2,1)S(1)} %get-tuple-element.21.refs_0_, f32[4,256,256]{2,1,0:T(8,128)S(1)} %get-tuple-element.22.refs_1_, f32[8,256]{1,0:T(8,128)S(1)} %get-tuple-element.33.refs_2_, f32[8,144,256]{2,1,0:T(8,128)S(1)} %get-tuple-element.34.refs_3_, ...), custom_call_target="tpu_custom_call" | custom-call | tf_op jit(solution)/shard_map/last_weights/pallas_call | solution.py:272
  14.7 0.0 collective-permute-done.5.v_ref
  14.8 1.3 %last_values.1 = bf16[256,1024]{1,0:T(8,128)(2,1)} custom-call(f32[8,144,256]{2,1,0:T(8,128)S(1)} %get-tuple-element.35.sum_ref, bf16[8,256,256]{2,1,0:T(8,128)(2,1)S(1)} %get-tuple-element.36.weight_ref, bf16[256,128]{1,0:T(8,128)(2,1)S(1)} %collective-permute-done.5.v_ref), custom_call_target="tpu_custom_call" | custom-call | tf_op jit(solution)/shard_map/last_values/pallas_call | solution.py:282
Async XLA Ops:
  0.0 8.5 %collective-permute-start.1 = (bf16[256,128]{1,0:T(8,128)(2,1)}, bf16[256,128]{1,0:T(8,128)(2,1)S(1)}, u32[]{:S(2)}, u32[]{:S(2)}) collective-permute-start(bf16[256,128]{1,0:T(8,128)(2,1)} %k_hbm.1), channel_id=1, source_target_pairs={{0,8},{4,12},{8,0},{12,4},{1,9},{5,13},{9,1},{13,5},{2,10},{6,14},... | collective-permute-start | bytes 196616 | tf_op jit(solution)/shard_map/ppermute | solution.py:215
  4.0 6.4 %collective-permute-start = (bf16[256,128]{1,0:T(8,128)(2,1)}, bf16[256,128]{1,0:T(8,128)(2,1)S(1)}, u32[]{:S(2)}, u32[]{:S(2)}) collective-permute-start(bf16[256,128]{1,0:T(8,128)(2,1)} %v_hbm.1), channel_id=1, source_target_pairs={{0,8},{4,12},{8,0},{12,4},{1,9},{5,13},{9,1},{13,5},{2,10},{6,14},... | collective-permute-start | bytes 196616 | tf_op jit(solution)/shard_map/ppermute | solution.py:215
  4.1 8.7 %collective-permute-start.2 = (bf16[256,128]{1,0:T(8,128)(2,1)}, bf16[256,128]{1,0:T(8,128)(2,1)S(1)}, u32[]{:S(2)}, u32[]{:S(2)}) collective-permute-start(bf16[256,128]{1,0:T(8,128)(2,1)} %k_hbm.1), channel_id=1, source_target_pairs={{0,4},{4,0},{8,12},{12,8},{1,5},{5,1},{9,13},{13,9},{2,6},{6,2},{1... | collective-permute-start | bytes 196616 | tf_op jit(solution)/shard_map/ppermute | solution.py:215
  6.0 6.8 %collective-permute-start.3 = (bf16[256,128]{1,0:T(8,128)(2,1)}, bf16[256,128]{1,0:T(8,128)(2,1)S(1)}, u32[]{:S(2)}, u32[]{:S(2)}) collective-permute-start(bf16[256,128]{1,0:T(8,128)(2,1)} %v_hbm.1), channel_id=1, source_target_pairs={{0,4},{4,0},{8,12},{12,8},{1,5},{5,1},{9,13},{13,9},{2,6},{6,2},{1... | collective-permute-start | bytes 196616 | tf_op jit(solution)/shard_map/ppermute | solution.py:215
  8.5 5.4 %collective-permute-start.4 = (bf16[256,128]{1,0:T(8,128)(2,1)S(1)}, bf16[256,128]{1,0:T(8,128)(2,1)S(1)}, u32[]{:S(2)}, u32[]{:S(2)}) collective-permute-start(bf16[256,128]{1,0:T(8,128)(2,1)S(1)} %collective-permute-done.1.refs_4_), channel_id=1, source_target_pairs={{0,4},{4,0},{8,12},{12,8},{1,5},{5,1},{9,13},{13,9},{2,6},{6,2},{1... | collective-permute-start | bytes 196616 | tf_op jit(solution)/shard_map/ppermute | solution.py:215
  10.5 4.3 %collective-permute-start.5 = (bf16[256,128]{1,0:T(8,128)(2,1)S(1)}, bf16[256,128]{1,0:T(8,128)(2,1)S(1)}, u32[]{:S(2)}, u32[]{:S(2)}) collective-permute-start(bf16[256,128]{1,0:T(8,128)(2,1)S(1)} %collective-permute-done.refs_5_), channel_id=1, source_target_pairs={{0,4},{4,0},{8,12},{12,8},{1,5},{5,1},{9,13},{13,9},{2,6},{6,2},{1... | collective-permute-start | bytes 196616 | tf_op jit(solution)/shard_map/ppermute | solution.py:215

commit v13 on v11

--- a/solution.py
+++ b/solution.py
@@ -212,25 +212,20 @@
 PARAMS = pltpu.CompilerParams(vmem_limit_bytes=32 << 20)
 
 
-def moved(value, *masks):
-    seq_size, mp_size = lax.axis_size("seq"), lax.axis_size("mp")
-    pairs = [
-        (index * mp_size + place, (index ^ masks[place % len(masks)]) * mp_size + place)
-        for index in range(seq_size)
-        for place in range(mp_size)
-    ]
-    return lax.ppermute(value, ("seq", "mp"), pairs)
+CYCLE = ((0, 2), (2, 3), (3, 1), (1, 0))
+BACK = tuple((target, source) for source, target in CYCLE)
+SWAP = ((0, 1), (1, 0), (2, 3), (3, 2))
 
 
 def staged_attention(queries, keys, values, lengths, old_place):
-    first_keys, second_keys = moved(keys, 2, 1), moved(keys, 1, 2)
-    first_values, second_values = moved(values, 2, 1), moved(values, 1, 2)
+    first_keys, first_values = (lax.ppermute(part, "seq", CYCLE) for part in (keys, values))
+    second_keys, second_values = (lax.ppermute(part, "seq", BACK) for part in (keys, values))
     rows, cols = queries.shape
     heads = cols // HEAD_WIDTH
     devices = lax.axis_size("seq")
     own = lax.axis_index("seq").astype(jnp.int32)
-    far_first = lax.axis_index("mp") % 2 == 0
-    first = jnp.where(far_first, 2, 1).astype(jnp.int32)
+    inner = (own == 1) | (own == 2)
+    first = jnp.where(inner, 2, 1).astype(jnp.int32)
     places = old_place.reshape(1, -1)
     state = [
         pltpu.VMEM((heads, rows), jnp.float32),
@@ -273,13 +268,12 @@
         )(*in_vmem(across, bias, *carried), keys, values)
 
     carried = add_shard(1, first_keys, first_values, carried)
-    relayed = []
-    for one, other in ((first_keys, second_keys), (first_values, second_values)):
-        one, other, *carried = lax.optimization_barrier((one, other, *carried))
-        far = jnp.where(far_first, one, other)
-        far, *carried = lax.optimization_barrier((far, *carried))
-        relayed.append(moved(far, 1))
-    third_keys, third_values = relayed
+    second_keys, *carried = lax.optimization_barrier((second_keys, *carried))
+    far_keys = jnp.where(inner, first_keys, second_keys)
+    third_keys = lax.ppermute(far_keys, "seq", SWAP)
+    second_values, second_keys, far_keys, *carried = lax.optimization_barrier((second_values, second_keys, far_keys, *carried))
+    far_values = jnp.where(inner, first_values, second_values)
+    third_values = lax.ppermute(far_values, "seq", SWAP)
     carried = add_shard(2, second_keys, second_values, carried)
     summed, weights = pl.pallas_call(
         lambda *refs: weights_kernel(3, *refs),

time: 19.8 us -> 17.9 us (0.904)
  waiting for transfers between devices: 4.54 us -> 2.74 us
    ppermute x6, waiting for transfers between devices: 4.54 us -> 2.74 us  [the longest x2 1.7 us: staged_attention(): lax.ppermute(part, 'seq', BACK)]
  transfers between devices with their start and end apart: 6 -> 6, of which waited for: 2 -> 2; matrix products, arithmetic and copies ran while one was open for 0% -> 0% of each run, Pallas kernels for 28% -> 31%
where the time goes in v13:
time: 17.9 us; the launch traced here: 17.8 us
  starting transfers between devices  8.25 us (46%)
  Pallas kernels  6.71 us (37%)
  waiting for transfers between devices  2.74 us (15%)
    ppermute x2, starting transfers between devices, staged_attention(): lax.ppermute(part, 'seq', CYCLE)  5.61 us
    pallas_call x1, Pallas kernels, staged_attention(): pl.pallas_call(own_kernel, in_specs=[pl.BlockSpec(memory_space=pltpu.SMEM...  2.43 us
    pallas_call x2, Pallas kernels, add_shard(): pl.pallas_call(lambda *refs: next_kernel(at, *refs), in_specs=[VMEM_REF]...  2.25 us
    ppermute x2, waiting for transfers between devices, staged_attention(): lax.ppermute(part, 'seq', BACK)  1.7 us
    ppermute x1, starting transfers between devices, staged_attention(): third_values = lax.ppermute(far_values, 'seq', SWAP)  1.45 us
    pallas_call x1, Pallas kernels, staged_attention(): pl.pallas_call(last_kernel, in_specs=[VMEM_REF] * 3, out_specs=pl.BlockSp...  1.25 us
    ppermute x1, waiting for transfers between devices, staged_attention(): third_keys = lax.ppermute(far_keys, 'seq', SWAP)  1.03 us
    pallas_call x1, Pallas kernels, staged_attention(): pl.pallas_call(lambda *refs: weights_kernel(3, *refs), in_specs=[VMEM_REF...  0.79 us
  transfers between devices with their start and end apart: 6, of which 2 were waited for; matrix products, arithmetic and copies ran while one was open for 0% of the time, Pallas kernels for 31%

profile of v13, /device:TPU:0, one launch (start us, length us, event | category | flops | bytes accessed | tf_op | source)
XLA Modules:
  0.0 17.8 jit_solution(15289408445580283321)
XLA Ops:
  0.0 4.0 %collective-permute-start.2 = (bf16[256,128]{1,0:T(8,128)(2,1)}, bf16[256,128]{1,0:T(8,128)(2,1)S(1)}, u32[]{:S(2)}, u32[]{:S(2)}) collective-permute-start(bf16[256,128]{1,0:T(8,128)(2,1)} %k_hbm.1), channel_id=1, source_target_pairs={{0,8},{8,12},{12,4},{4,0},{1,9},{9,13},{13,5},{5,1},{2,10},{10,14}... | collective-permute-start | bytes 196616 | tf_op jit(solution)/shard_map/ppermute | solution.py:221
  4.0 1.6 %collective-permute-start.3 = (bf16[256,128]{1,0:T(8,128)(2,1)}, bf16[256,128]{1,0:T(8,128)(2,1)S(1)}, u32[]{:S(2)}, u32[]{:S(2)}) collective-permute-start(bf16[256,128]{1,0:T(8,128)(2,1)} %v_hbm.1), channel_id=1, source_target_pairs={{0,8},{8,12},{12,4},{4,0},{1,9},{9,13},{13,5},{5,1},{2,10},{10,14}... | collective-permute-start | bytes 196616 | tf_op jit(solution)/shard_map/ppermute | solution.py:221
  5.6 0.4 %collective-permute-start.1 = (bf16[256,128]{1,0:T(8,128)(2,1)}, bf16[256,128]{1,0:T(8,128)(2,1)S(1)}, u32[]{:S(2)}, u32[]{:S(2)}) collective-permute-start(bf16[256,128]{1,0:T(8,128)(2,1)} %k_hbm.1), channel_id=1, source_target_pairs={{8,0},{12,8},{4,12},{0,4},{9,1},{13,9},{5,13},{1,5},{10,2},{14,10}... | collective-permute-start | bytes 196616 | tf_op jit(solution)/shard_map/ppermute | solution.py:222
  6.1 0.0 collective-permute-start
  6.1 2.4 %own_shard.1 = (bf16[8,128,256]{2,1,0:T(8,128)(2,1)S(1)}, f32[4,256,256]{2,1,0:T(8,128)S(1)}, f32[8,256]{1,0:T(8,128)S(1)}, f32[8,144,256]{2,1,0:T(8,128)S(1)}) custom-call(s32[1]{0:T(128)} %bitcast.own_ref, s32[1]{0:T(128)} %bitcast.1.first_ref, s32[3]{0:T(128)} %lengths_hbm.1, s32[1,128]{1,0:T(1,128)} %bitcast.3, bf16[256,1024]{1,0:T(8,128)(2,1)} %q_hbm.1, ...), custom_call_target="tpu_custom_call" | custom-call | tf_op jit(solution)/shard_map/own_shard/pallas_call | solution.py:238
  8.5 0.0 collective-permute-done.2.refs_4_
  8.5 0.0 collective-permute-done.3.refs_5_
  8.6 1.1 %next_shard.2 = (f32[8,256]{1,0:T(8,128)S(1)}, f32[8,144,256]{2,1,0:T(8,128)S(1)}) custom-call(bf16[8,128,256]{2,1,0:T(8,128)(2,1)S(1)} %get-tuple-element.22.refs_0_, f32[4,256,256]{2,1,0:T(8,128)S(1)} %get-tuple-element.23.refs_1_, f32[8,256]{1,0:T(8,128)S(1)} %get-tuple-element.24.refs_2_, f32[8,144,256]{2,1,0:T(8,128)S(1)} %get-tuple-element.25.refs_3_, ...), custom_call_target="tpu_custom_call" | custom-call | tf_op jit(solution)/shard_map/next_shard/pallas_call | solution.py:259
  9.7 1.7 %collective-permute-done.1.refs_4_ = bf16[256,128]{1,0:T(8,128)(2,1)S(1)} collective-permute-done((bf16[256,128]{1,0:T(8,128)(2,1)}, bf16[256,128]{1,0:T(8,128)(2,1)S(1)}, u32[]{:S(2)}, u32[]{:S(2)}) %collective-permute-start.1) | collective-permute-done | bytes 65568 | tf_op jit(solution)/shard_map/ppermute | solution.py:222
  11.4 0.7 %collective-permute-start.4 = (bf16[256,128]{1,0:T(8,128)(2,1)S(1)}, bf16[256,128]{1,0:T(8,128)(2,1)S(1)}, u32[]{:S(2)}, u32[]{:S(2)}) collective-permute-start(bf16[256,128]{1,0:T(8,128)(2,1)S(1)} %broadcast_select_fusion.1), channel_id=1, source_target_pairs={{0,4},{4,0},{8,12},{12,8},{1,5},{5,1},{9,13},{13,9},{2,6},{6,2},{1... | collective-permute-start | bytes 196616 | tf_op jit(solution)/shard_map/ppermute | solution.py:273
  12.1 0.0 collective-permute-done.refs_5_
  12.1 1.4 %collective-permute-start.5 = (bf16[256,128]{1,0:T(8,128)(2,1)S(1)}, bf16[256,128]{1,0:T(8,128)(2,1)S(1)}, u32[]{:S(2)}, u32[]{:S(2)}) collective-permute-start(bf16[256,128]{1,0:T(8,128)(2,1)S(1)} %broadcast_select_fusion), channel_id=1, source_target_pairs={{0,4},{4,0},{8,12},{12,8},{1,5},{5,1},{9,13},{13,9},{2,6},{6,2},{1... | collective-permute-start | bytes 196616 | tf_op jit(solution)/shard_map/ppermute | solution.py:276
  13.6 1.1 %next_shard.3 = (f32[8,256]{1,0:T(8,128)S(1)}, f32[8,144,256]{2,1,0:T(8,128)S(1)}) custom-call(bf16[8,128,256]{2,1,0:T(8,128)(2,1)S(1)} %get-tuple-element.22.refs_0_, f32[4,256,256]{2,1,0:T(8,128)S(1)} %get-tuple-element.23.refs_1_, f32[8,256]{1,0:T(8,128)S(1)} %get-tuple-element.31.refs_2_, f32[8,144,256]{2,1,0:T(8,128)S(1)} %get-tuple-element.32.refs_3_, ...), custom_call_target="tpu_custom_call" | custom-call | tf_op jit(solution)/shard_map/next_shard/pallas_call | solution.py:259
  14.7 1.0 %collective-permute-done.4.refs_4_ = bf16[256,128]{1,0:T(8,128)(2,1)S(1)} collective-permute-done((bf16[256,128]{1,0:T(8,128)(2,1)S(1)}, bf16[256,128]{1,0:T(8,128)(2,1)S(1)}, u32[]{:S(2)}, u32[]{:S(2)}) %collective-permute-start.4) | collective-permute-done | bytes 65568 | tf_op jit(solution)/shard_map/ppermute | solution.py:273
  15.7 0.8 %last_weights.1 = (f32[8,144,256]{2,1,0:T(8,128)S(1)}, bf16[8,256,256]{2,1,0:T(8,128)(2,1)S(1)}) custom-call(bf16[8,128,256]{2,1,0:T(8,128)(2,1)S(1)} %get-tuple-element.22.refs_0_, f32[4,256,256]{2,1,0:T(8,128)S(1)} %get-tuple-element.23.refs_1_, f32[8,256]{1,0:T(8,128)S(1)} %get-tuple-element.35.refs_2_, f32[8,144,256]{2,1,0:T(8,128)S(1)} %get-tuple-element.36.refs_3_, ...), custom_call_target="tpu_custom_call" | custom-call | tf_op jit(solution)/shard_map/last_weights/pallas_call | solution.py:278
  16.5 0.0 collective-permute-done.5.v_ref
  16.5 1.3 %last_values.1 = bf16[256,1024]{1,0:T(8,128)(2,1)} custom-call(f32[8,144,256]{2,1,0:T(8,128)S(1)} %get-tuple-element.37.sum_ref, bf16[8,256,256]{2,1,0:T(8,128)(2,1)S(1)} %get-tuple-element.38.weight_ref, bf16[256,128]{1,0:T(8,128)(2,1)S(1)} %collective-permute-done.5.v_ref), custom_call_target="tpu_custom_call" | custom-call | tf_op jit(solution)/shard_map/last_values/pallas_call | solution.py:288
  (2 shorter events, 0.0 us)
Async XLA Ops:
  0.0 8.5 %collective-permute-start.2 = (bf16[256,128]{1,0:T(8,128)(2,1)}, bf16[256,128]{1,0:T(8,128)(2,1)S(1)}, u32[]{:S(2)}, u32[]{:S(2)}) collective-permute-start(bf16[256,128]{1,0:T(8,128)(2,1)} %k_hbm.1), channel_id=1, source_target_pairs={{0,8},{8,12},{12,4},{4,0},{1,9},{9,13},{13,5},{5,1},{2,10},{10,14}... | collective-permute-start | bytes 196616 | tf_op jit(solution)/shard_map/ppermute | solution.py:221
  4.0 4.5 %collective-permute-start.3 = (bf16[256,128]{1,0:T(8,128)(2,1)}, bf16[256,128]{1,0:T(8,128)(2,1)S(1)}, u32[]{:S(2)}, u32[]{:S(2)}) collective-permute-start(bf16[256,128]{1,0:T(8,128)(2,1)} %v_hbm.1), channel_id=1, source_target_pairs={{0,8},{8,12},{12,4},{4,0},{1,9},{9,13},{13,5},{5,1},{2,10},{10,14}... | collective-permute-start | bytes 196616 | tf_op jit(solution)/shard_map/ppermute | solution.py:221
  5.6 5.8 %collective-permute-start.1 = (bf16[256,128]{1,0:T(8,128)(2,1)}, bf16[256,128]{1,0:T(8,128)(2,1)S(1)}, u32[]{:S(2)}, u32[]{:S(2)}) collective-permute-start(bf16[256,128]{1,0:T(8,128)(2,1)} %k_hbm.1), channel_id=1, source_target_pairs={{8,0},{12,8},{4,12},{0,4},{9,1},{13,9},{5,13},{1,5},{10,2},{14,10}... | collective-permute-start | bytes 196616 | tf_op jit(solution)/shard_map/ppermute | solution.py:222
  6.1 6.0 %collective-permute-start = (bf16[256,128]{1,0:T(8,128)(2,1)}, bf16[256,128]{1,0:T(8,128)(2,1)S(1)}, u32[]{:S(2)}, u32[]{:S(2)}) collective-permute-start(bf16[256,128]{1,0:T(8,128)(2,1)} %v_hbm.1), channel_id=1, source_target_pairs={{8,0},{12,8},{4,12},{0,4},{9,1},{13,9},{5,13},{1,5},{10,2},{14,10}... | collective-permute-start | bytes 196616 | tf_op jit(solution)/shard_map/ppermute | solution.py:222
  11.4 4.3 %collective-permute-start.4 = (bf16[256,128]{1,0:T(8,128)(2,1)S(1)}, bf16[256,128]{1,0:T(8,128)(2,1)S(1)}, u32[]{:S(2)}, u32[]{:S(2)}) collective-permute-start(bf16[256,128]{1,0:T(8,128)(2,1)S(1)} %broadcast_select_fusion.1), channel_id=1, source_target_pairs={{0,4},{4,0},{8,12},{12,8},{1,5},{5,1},{9,13},{13,9},{2,6},{6,2},{1... | collective-permute-start | bytes 196616 | tf_op jit(solution)/shard_map/ppermute | solution.py:273
  12.1 4.4 %collective-permute-start.5 = (bf16[256,128]{1,0:T(8,128)(2,1)S(1)}, bf16[256,128]{1,0:T(8,128)(2,1)S(1)}, u32[]{:S(2)}, u32[]{:S(2)}) collective-permute-start(bf16[256,128]{1,0:T(8,128)(2,1)S(1)} %broadcast_select_fusion), channel_id=1, source_target_pairs={{0,4},{4,0},{8,12},{12,8},{1,5},{5,1},{9,13},{13,9},{2,6},{6,2},{1... | collective-permute-start | bytes 196616 | tf_op jit(solution)/shard_map/ppermute | solution.py:276

commit v14 on v12

--- a/solution.py
+++ b/solution.py
@@ -216,8 +216,9 @@
 
 
 def staged_attention(queries, keys, values, lengths, old_place):
-    far_keys, far_values = moved(keys, 2), moved(values, 2)
+    far_values, far_keys = moved(values, 2), moved(keys, 2)
     near_keys, near_values = moved(keys, 1), moved(values, 1)
+    third_keys = moved(keys, 3)
     rows, cols = queries.shape
     heads = cols // HEAD_WIDTH
     devices = lax.axis_size("seq")
@@ -263,8 +264,6 @@
             name="next_shard",
         )(*in_vmem(across, bias, *carried), keys, values)
 
-    far_keys, *carried = lax.optimization_barrier((far_keys, *carried))
-    third_keys = moved(far_keys, 1)
     far_values, *carried = lax.optimization_barrier((far_values, *carried))
     third_values = moved(far_values, 1)
     carried = add_shard(2, far_keys, far_values, carried)

time: 16.2 us -> 17.6 us (1.086)
  starting transfers between devices: 9.19 us -> 10.5 us
    ppermute x6, starting transfers between devices: 9.19 us -> 10.5 us  [moved(): lax.ppermute(value, 'seq', [(i, i ^ mask) for i in range(lax.axis_size('s...]
  transfers between devices with their start and end apart: 6 -> 6, of which waited for: 0 -> 1; matrix products, arithmetic and copies ran while one was open for 0% -> 0% of each run, Pallas kernels for 34% -> 32%
where the time goes in v14:
time: 17.6 us; the launch traced here: 17.4 us
  starting transfers between devices  10.5 us (60%)
  Pallas kernels  6.74 us (38%)
    ppermute x6, starting transfers between devices, moved(): lax.ppermute(value, 'seq', [(i, i ^ mask) for i in range(lax.axis_size('s...  10.5 us
    pallas_call x1, Pallas kernels, staged_attention(): pl.pallas_call(own_kernel, in_specs=[pl.BlockSpec(memory_space=pltpu.SMEM...  2.43 us
    pallas_call x2, Pallas kernels, add_shard(): pl.pallas_call(lambda *refs: next_kernel(at, *refs), in_specs=[VMEM_REF]...  2.25 us
    pallas_call x1, Pallas kernels, staged_attention(): pl.pallas_call(last_kernel, in_specs=[VMEM_REF] * 3, out_specs=pl.BlockSp...  1.26 us
    pallas_call x1, Pallas kernels, staged_attention(): pl.pallas_call(lambda *refs: weights_kernel(3, *refs), in_specs=[VMEM_REF...  0.8 us
  transfers between devices with their start and end apart: 6, of which 1 were waited for; matrix products, arithmetic and copies ran while one was open for 0% of the time, Pallas kernels for 32%

profile of v14, /device:TPU:0, one launch (start us, length us, event | category | flops | bytes accessed | tf_op | source)
XLA Modules:
  0.0 17.4 jit_solution(4712950304348043545)
XLA Ops:
  0.0 4.0 %collective-permute-start = (bf16[256,128]{1,0:T(8,128)(2,1)}, bf16[256,128]{1,0:T(8,128)(2,1)S(1)}, u32[]{:S(2)}, u32[]{:S(2)}) collective-permute-start(bf16[256,128]{1,0:T(8,128)(2,1)} %v_hbm.1), channel_id=1, source_target_pairs={{0,8},{4,12},{8,0},{12,4},{1,9},{5,13},{9,1},{13,5},{2,10},{6,14},... | collective-permute-start | bytes 196616 | tf_op jit(solution)/shard_map/ppermute | solution.py:215
  4.0 1.6 %collective-permute-start.3 = (bf16[256,128]{1,0:T(8,128)(2,1)}, bf16[256,128]{1,0:T(8,128)(2,1)S(1)}, u32[]{:S(2)}, u32[]{:S(2)}) collective-permute-start(bf16[256,128]{1,0:T(8,128)(2,1)} %v_hbm.1), channel_id=1, source_target_pairs={{0,4},{4,0},{8,12},{12,8},{1,5},{5,1},{9,13},{13,9},{2,6},{6,2},{1... | collective-permute-start | bytes 196616 | tf_op jit(solution)/shard_map/ppermute | solution.py:215
  5.6 0.3 %collective-permute-start.1 = (bf16[256,128]{1,0:T(8,128)(2,1)}, bf16[256,128]{1,0:T(8,128)(2,1)S(1)}, u32[]{:S(2)}, u32[]{:S(2)}) collective-permute-start(bf16[256,128]{1,0:T(8,128)(2,1)} %k_hbm.1), channel_id=1, source_target_pairs={{0,8},{4,12},{8,0},{12,4},{1,9},{5,13},{9,1},{13,5},{2,10},{6,14},... | collective-permute-start | bytes 196616 | tf_op jit(solution)/shard_map/ppermute | solution.py:215
  6.0 2.5 %collective-permute-start.4 = (bf16[256,128]{1,0:T(8,128)(2,1)}, bf16[256,128]{1,0:T(8,128)(2,1)S(1)}, u32[]{:S(2)}, u32[]{:S(2)}) collective-permute-start(bf16[256,128]{1,0:T(8,128)(2,1)} %k_hbm.1), channel_id=1, source_target_pairs={{0,12},{4,8},{8,4},{12,0},{1,13},{5,9},{9,5},{13,1},{2,14},{6,10},... | collective-permute-start | bytes 196616 | tf_op jit(solution)/shard_map/ppermute | solution.py:215
  8.4 0.7 %collective-permute-start.2 = (bf16[256,128]{1,0:T(8,128)(2,1)}, bf16[256,128]{1,0:T(8,128)(2,1)S(1)}, u32[]{:S(2)}, u32[]{:S(2)}) collective-permute-start(bf16[256,128]{1,0:T(8,128)(2,1)} %k_hbm.1), channel_id=1, source_target_pairs={{0,4},{4,0},{8,12},{12,8},{1,5},{5,1},{9,13},{13,9},{2,6},{6,2},{1... | collective-permute-start | bytes 196616 | tf_op jit(solution)/shard_map/ppermute | solution.py:215
  9.1 2.4 %own_shard.1 = (bf16[8,128,256]{2,1,0:T(8,128)(2,1)S(1)}, f32[4,256,256]{2,1,0:T(8,128)S(1)}, f32[8,256]{1,0:T(8,128)S(1)}, f32[8,144,256]{2,1,0:T(8,128)S(1)}) custom-call(s32[1]{0:T(128)} %bitcast.own_ref, s32[3]{0:T(128)} %lengths_hbm.1, s32[1,128]{1,0:T(1,128)} %bitcast.2, bf16[256,1024]{1,0:T(8,128)(2,1)} %q_hbm.1, bf16[256,128]{1,0:T(8,128)(2,1)} %k_hbm.1, ...), custom_call_target="tpu_custom_call" | custom-call | tf_op jit(solution)/shard_map/own_shard/pallas_call | solution.py:235
  11.5 0.0 collective-permute-done.refs_5_
  11.6 1.4 %collective-permute-start.5 = (bf16[256,128]{1,0:T(8,128)(2,1)S(1)}, bf16[256,128]{1,0:T(8,128)(2,1)S(1)}, u32[]{:S(2)}, u32[]{:S(2)}) collective-permute-start(bf16[256,128]{1,0:T(8,128)(2,1)S(1)} %collective-permute-done.refs_5_), channel_id=1, source_target_pairs={{0,4},{4,0},{8,12},{12,8},{1,5},{5,1},{9,13},{13,9},{2,6},{6,2},{1... | collective-permute-start | bytes 196616 | tf_op jit(solution)/shard_map/ppermute | solution.py:215
  13.0 0.1 collective-permute-done.1.refs_4_
  13.1 1.1 %next_shard.2 = (f32[8,256]{1,0:T(8,128)S(1)}, f32[8,144,256]{2,1,0:T(8,128)S(1)}) custom-call(bf16[8,128,256]{2,1,0:T(8,128)(2,1)S(1)} %get-tuple-element.18.refs_0_, f32[4,256,256]{2,1,0:T(8,128)S(1)} %get-tuple-element.19.refs_1_, f32[8,256]{1,0:T(8,128)S(1)} %get-tuple-element.22.refs_2_, f32[8,144,256]{2,1,0:T(8,128)S(1)} %get-tuple-element.23.refs_3_, ...), custom_call_target="tpu_custom_call" | custom-call | tf_op jit(solution)/shard_map/next_shard/pallas_call | solution.py:256
  14.2 0.0 collective-permute-done.3.refs_5_
  14.2 0.0 collective-permute-done.2.refs_4_
  14.2 1.1 %next_shard.3 = (f32[8,256]{1,0:T(8,128)S(1)}, f32[8,144,256]{2,1,0:T(8,128)S(1)}) custom-call(bf16[8,128,256]{2,1,0:T(8,128)(2,1)S(1)} %get-tuple-element.18.refs_0_, f32[4,256,256]{2,1,0:T(8,128)S(1)} %get-tuple-element.19.refs_1_, f32[8,256]{1,0:T(8,128)S(1)} %get-tuple-element.25.refs_2_, f32[8,144,256]{2,1,0:T(8,128)S(1)} %get-tuple-element.26.refs_3_, ...), custom_call_target="tpu_custom_call" | custom-call | tf_op jit(solution)/shard_map/next_shard/pallas_call | solution.py:256
  15.3 0.0 collective-permute-done.4.refs_4_
  15.3 0.8 %last_weights.1 = (f32[8,144,256]{2,1,0:T(8,128)S(1)}, bf16[8,256,256]{2,1,0:T(8,128)(2,1)S(1)}) custom-call(bf16[8,128,256]{2,1,0:T(8,128)(2,1)S(1)} %get-tuple-element.18.refs_0_, f32[4,256,256]{2,1,0:T(8,128)S(1)} %get-tuple-element.19.refs_1_, f32[8,256]{1,0:T(8,128)S(1)} %get-tuple-element.27.refs_2_, f32[8,144,256]{2,1,0:T(8,128)S(1)} %get-tuple-element.28.refs_3_, ...), custom_call_target="tpu_custom_call" | custom-call | tf_op jit(solution)/shard_map/last_weights/pallas_call | solution.py:271
  16.2 0.0 collective-permute-done.5.v_ref
  16.2 1.3 %last_values.1 = bf16[256,1024]{1,0:T(8,128)(2,1)} custom-call(f32[8,144,256]{2,1,0:T(8,128)S(1)} %get-tuple-element.29.sum_ref, bf16[8,256,256]{2,1,0:T(8,128)(2,1)S(1)} %get-tuple-element.30.weight_ref, bf16[256,128]{1,0:T(8,128)(2,1)S(1)} %collective-permute-done.5.v_ref), custom_call_target="tpu_custom_call" | custom-call | tf_op jit(solution)/shard_map/last_values/pallas_call | solution.py:281
Async XLA Ops:
  0.0 11.5 %collective-permute-start = (bf16[256,128]{1,0:T(8,128)(2,1)}, bf16[256,128]{1,0:T(8,128)(2,1)S(1)}, u32[]{:S(2)}, u32[]{:S(2)}) collective-permute-start(bf16[256,128]{1,0:T(8,128)(2,1)} %v_hbm.1), channel_id=1, source_target_pairs={{0,8},{4,12},{8,0},{12,4},{1,9},{5,13},{9,1},{13,5},{2,10},{6,14},... | collective-permute-start | bytes 196616 | tf_op jit(solution)/shard_map/ppermute | solution.py:215
  4.0 10.1 %collective-permute-start.3 = (bf16[256,128]{1,0:T(8,128)(2,1)}, bf16[256,128]{1,0:T(8,128)(2,1)S(1)}, u32[]{:S(2)}, u32[]{:S(2)}) collective-permute-start(bf16[256,128]{1,0:T(8,128)(2,1)} %v_hbm.1), channel_id=1, source_target_pairs={{0,4},{4,0},{8,12},{12,8},{1,5},{5,1},{9,13},{13,9},{2,6},{6,2},{1... | collective-permute-start | bytes 196616 | tf_op jit(solution)/shard_map/ppermute | solution.py:215
  5.6 7.4 %collective-permute-start.1 = (bf16[256,128]{1,0:T(8,128)(2,1)}, bf16[256,128]{1,0:T(8,128)(2,1)S(1)}, u32[]{:S(2)}, u32[]{:S(2)}) collective-permute-start(bf16[256,128]{1,0:T(8,128)(2,1)} %k_hbm.1), channel_id=1, source_target_pairs={{0,8},{4,12},{8,0},{12,4},{1,9},{5,13},{9,1},{13,5},{2,10},{6,14},... | collective-permute-start | bytes 196616 | tf_op jit(solution)/shard_map/ppermute | solution.py:215
  6.0 9.4 %collective-permute-start.4 = (bf16[256,128]{1,0:T(8,128)(2,1)}, bf16[256,128]{1,0:T(8,128)(2,1)S(1)}, u32[]{:S(2)}, u32[]{:S(2)}) collective-permute-start(bf16[256,128]{1,0:T(8,128)(2,1)} %k_hbm.1), channel_id=1, source_target_pairs={{0,12},{4,8},{8,4},{12,0},{1,13},{5,9},{9,5},{13,1},{2,14},{6,10},... | collective-permute-start | bytes 196616 | tf_op jit(solution)/shard_map/ppermute | solution.py:215
  8.4 5.8 %collective-permute-start.2 = (bf16[256,128]{1,0:T(8,128)(2,1)}, bf16[256,128]{1,0:T(8,128)(2,1)S(1)}, u32[]{:S(2)}, u32[]{:S(2)}) collective-permute-start(bf16[256,128]{1,0:T(8,128)(2,1)} %k_hbm.1), channel_id=1, source_target_pairs={{0,4},{4,0},{8,12},{12,8},{1,5},{5,1},{9,13},{13,9},{2,6},{6,2},{1... | collective-permute-start | bytes 196616 | tf_op jit(solution)/shard_map/ppermute | solution.py:215
  11.6 4.6 %collective-permute-start.5 = (bf16[256,128]{1,0:T(8,128)(2,1)S(1)}, bf16[256,128]{1,0:T(8,128)(2,1)S(1)}, u32[]{:S(2)}, u32[]{:S(2)}) collective-permute-start(bf16[256,128]{1,0:T(8,128)(2,1)S(1)} %collective-permute-done.refs_5_), channel_id=1, source_target_pairs={{0,4},{4,0},{8,12},{12,8},{1,5},{5,1},{9,13},{13,9},{2,6},{6,2},{1... | collective-permute-start | bytes 196616 | tf_op jit(solution)/shard_map/ppermute | solution.py:215

commit v15 on v14

--- a/solution.py
+++ b/solution.py
@@ -216,9 +216,9 @@
 
 
 def staged_attention(queries, keys, values, lengths, old_place):
-    far_values, far_keys = moved(values, 2), moved(keys, 2)
-    near_keys, near_values = moved(keys, 1), moved(values, 1)
-    third_keys = moved(keys, 3)
+    (far_keys, far_values), (near_keys, near_values), (third_keys, third_values) = (
+        (moved(keys, mask), moved(values, mask)) for mask in (2, 1, 3)
+    )
     rows, cols = queries.shape
     heads = cols // HEAD_WIDTH
     devices = lax.axis_size("seq")
@@ -264,8 +264,6 @@
             name="next_shard",
         )(*in_vmem(across, bias, *carried), keys, values)
 
-    far_values, *carried = lax.optimization_barrier((far_values, *carried))
-    third_values = moved(far_values, 1)
     carried = add_shard(2, far_keys, far_values, carried)
     carried = add_shard(1, near_keys, near_values, carried)
     summed, weights = pl.pallas_call(

time: 17.6 us -> 19.8 us (1.12)
  starting transfers between devices: 10.5 us -> 12.9 us
    ppermute x6, starting transfers between devices: 10.5 us -> 12.9 us  [moved(): lax.ppermute(value, 'seq', [(i, i ^ mask) for i in range(lax.axis_size('s...]
  transfers between devices with their start and end apart: 6 -> 6, of which waited for: 1 -> 0; matrix products, arithmetic and copies ran while one was open for 0% -> 0% of each run, Pallas kernels for 32% -> 28%
where the time goes in v15:
time: 19.8 us; the launch traced here: 19.7 us
  starting transfers between devices  12.9 us (65%)
  Pallas kernels  6.72 us (34%)
    ppermute x6, starting transfers between devices, moved(): lax.ppermute(value, 'seq', [(i, i ^ mask) for i in range(lax.axis_size('s...  12.9 us
    pallas_call x1, Pallas kernels, staged_attention(): pl.pallas_call(own_kernel, in_specs=[pl.BlockSpec(memory_space=pltpu.SMEM...  2.42 us
    pallas_call x2, Pallas kernels, add_shard(): pl.pallas_call(lambda *refs: next_kernel(at, *refs), in_specs=[VMEM_REF]...  2.25 us
    pallas_call x1, Pallas kernels, staged_attention(): pl.pallas_call(last_kernel, in_specs=[VMEM_REF] * 3, out_specs=pl.BlockSp...  1.26 us
    pallas_call x1, Pallas kernels, staged_attention(): pl.pallas_call(lambda *refs: weights_kernel(3, *refs), in_specs=[VMEM_REF...  0.79 us
  transfers between devices with their start and end apart: 6, of which 0 were waited for; matrix products, arithmetic and copies ran while one was open for 0% of the time, Pallas kernels for 28%

profile of v15, /device:TPU:0, one launch (start us, length us, event | category | flops | bytes accessed | tf_op | source)
XLA Modules:
  0.0 19.7 jit_solution(14097415757172978818)
XLA Ops:
  0.0 4.0 %collective-permute-start = (bf16[256,128]{1,0:T(8,128)(2,1)}, bf16[256,128]{1,0:T(8,128)(2,1)S(1)}, u32[]{:S(2)}, u32[]{:S(2)}) collective-permute-start(bf16[256,128]{1,0:T(8,128)(2,1)} %k_hbm.1), channel_id=1, source_target_pairs={{0,8},{4,12},{8,0},{12,4},{1,9},{5,13},{9,1},{13,5},{2,10},{6,14},... | collective-permute-start | bytes 196616 | tf_op jit(solution)/shard_map/ppermute | solution.py:215
  4.0 0.0 collective-permute-start.1
  4.1 1.9 %collective-permute-start.2 = (bf16[256,128]{1,0:T(8,128)(2,1)}, bf16[256,128]{1,0:T(8,128)(2,1)S(1)}, u32[]{:S(2)}, u32[]{:S(2)}) collective-permute-start(bf16[256,128]{1,0:T(8,128)(2,1)} %k_hbm.1), channel_id=1, source_target_pairs={{0,4},{4,0},{8,12},{12,8},{1,5},{5,1},{9,13},{13,9},{2,6},{6,2},{1... | collective-permute-start | bytes 196616 | tf_op jit(solution)/shard_map/ppermute | solution.py:215
  6.0 0.1 collective-permute-start.3
  6.1 3.9 %collective-permute-start.4 = (bf16[256,128]{1,0:T(8,128)(2,1)}, bf16[256,128]{1,0:T(8,128)(2,1)S(1)}, u32[]{:S(2)}, u32[]{:S(2)}) collective-permute-start(bf16[256,128]{1,0:T(8,128)(2,1)} %k_hbm.1), channel_id=1, source_target_pairs={{0,12},{4,8},{8,4},{12,0},{1,13},{5,9},{9,5},{13,1},{2,14},{6,10},... | collective-permute-start | bytes 196616 | tf_op jit(solution)/shard_map/ppermute | solution.py:215
  10.0 0.0 collective-permute-done.refs_4_
  10.0 2.9 %collective-permute-start.5 = (bf16[256,128]{1,0:T(8,128)(2,1)}, bf16[256,128]{1,0:T(8,128)(2,1)S(1)}, u32[]{:S(2)}, u32[]{:S(2)}) collective-permute-start(bf16[256,128]{1,0:T(8,128)(2,1)} %v_hbm.1), channel_id=1, source_target_pairs={{0,12},{4,8},{8,4},{12,0},{1,13},{5,9},{9,5},{13,1},{2,14},{6,10},... | collective-permute-start | bytes 196616 | tf_op jit(solution)/shard_map/ppermute | solution.py:215
  12.9 2.4 %own_shard.1 = (bf16[8,128,256]{2,1,0:T(8,128)(2,1)S(1)}, f32[4,256,256]{2,1,0:T(8,128)S(1)}, f32[8,256]{1,0:T(8,128)S(1)}, f32[8,144,256]{2,1,0:T(8,128)S(1)}) custom-call(s32[1]{0:T(128)} %bitcast.own_ref, s32[3]{0:T(128)} %lengths_hbm.1, s32[1,128]{1,0:T(1,128)} %bitcast.2, bf16[256,1024]{1,0:T(8,128)(2,1)} %q_hbm.1, bf16[256,128]{1,0:T(8,128)(2,1)} %k_hbm.1, ...), custom_call_target="tpu_custom_call" | custom-call | tf_op jit(solution)/shard_map/own_shard/pallas_call | solution.py:235
  15.3 0.0 collective-permute-done.1.refs_5_
  15.3 1.1 %next_shard.2 = (f32[8,256]{1,0:T(8,128)S(1)}, f32[8,144,256]{2,1,0:T(8,128)S(1)}) custom-call(bf16[8,128,256]{2,1,0:T(8,128)(2,1)S(1)} %get-tuple-element.15.refs_0_, f32[4,256,256]{2,1,0:T(8,128)S(1)} %get-tuple-element.16.refs_1_, f32[8,256]{1,0:T(8,128)S(1)} %get-tuple-element.17.refs_2_, f32[8,144,256]{2,1,0:T(8,128)S(1)} %get-tuple-element.18.refs_3_, ...), custom_call_target="tpu_custom_call" | custom-call | tf_op jit(solution)/shard_map/next_shard/pallas_call | solution.py:256
  16.5 0.0 collective-permute-done.2.refs_4_
  16.5 0.0 collective-permute-done.3.refs_5_
  16.5 1.1 %next_shard.3 = (f32[8,256]{1,0:T(8,128)S(1)}, f32[8,144,256]{2,1,0:T(8,128)S(1)}) custom-call(bf16[8,128,256]{2,1,0:T(8,128)(2,1)S(1)} %get-tuple-element.15.refs_0_, f32[4,256,256]{2,1,0:T(8,128)S(1)} %get-tuple-element.16.refs_1_, f32[8,256]{1,0:T(8,128)S(1)} %get-tuple-element.19.refs_2_, f32[8,144,256]{2,1,0:T(8,128)S(1)} %get-tuple-element.20.refs_3_, ...), custom_call_target="tpu_custom_call" | custom-call | tf_op jit(solution)/shard_map/next_shard/pallas_call | solution.py:256
  17.6 0.0 collective-permute-done.4.refs_4_
  17.6 0.8 %last_weights.1 = (f32[8,144,256]{2,1,0:T(8,128)S(1)}, bf16[8,256,256]{2,1,0:T(8,128)(2,1)S(1)}) custom-call(bf16[8,128,256]{2,1,0:T(8,128)(2,1)S(1)} %get-tuple-element.15.refs_0_, f32[4,256,256]{2,1,0:T(8,128)S(1)} %get-tuple-element.16.refs_1_, f32[8,256]{1,0:T(8,128)S(1)} %get-tuple-element.21.refs_2_, f32[8,144,256]{2,1,0:T(8,128)S(1)} %get-tuple-element.22.refs_3_, ...), custom_call_target="tpu_custom_call" | custom-call | tf_op jit(solution)/shard_map/last_weights/pallas_call | solution.py:269
  18.4 0.0 collective-permute-done.5.v_ref
  18.4 1.3 %last_values.1 = bf16[256,1024]{1,0:T(8,128)(2,1)} custom-call(f32[8,144,256]{2,1,0:T(8,128)S(1)} %get-tuple-element.23.sum_ref, bf16[8,256,256]{2,1,0:T(8,128)(2,1)S(1)} %get-tuple-element.24.weight_ref, bf16[256,128]{1,0:T(8,128)(2,1)S(1)} %collective-permute-done.5.v_ref), custom_call_target="tpu_custom_call" | custom-call | tf_op jit(solution)/shard_map/last_values/pallas_call | solution.py:279
Async XLA Ops:
  0.0 10.0 %collective-permute-start = (bf16[256,128]{1,0:T(8,128)(2,1)}, bf16[256,128]{1,0:T(8,128)(2,1)S(1)}, u32[]{:S(2)}, u32[]{:S(2)}) collective-permute-start(bf16[256,128]{1,0:T(8,128)(2,1)} %k_hbm.1), channel_id=1, source_target_pairs={{0,8},{4,12},{8,0},{12,4},{1,9},{5,13},{9,1},{13,5},{2,10},{6,14},... | collective-permute-start | bytes 196616 | tf_op jit(solution)/shard_map/ppermute | solution.py:215
  4.0 11.3 %collective-permute-start.1 = (bf16[256,128]{1,0:T(8,128)(2,1)}, bf16[256,128]{1,0:T(8,128)(2,1)S(1)}, u32[]{:S(2)}, u32[]{:S(2)}) collective-permute-start(bf16[256,128]{1,0:T(8,128)(2,1)} %v_hbm.1), channel_id=1, source_target_pairs={{0,8},{4,12},{8,0},{12,4},{1,9},{5,13},{9,1},{13,5},{2,10},{6,14},... | collective-permute-start | bytes 196616 | tf_op jit(solution)/shard_map/ppermute | solution.py:215
  4.1 12.4 %collective-permute-start.2 = (bf16[256,128]{1,0:T(8,128)(2,1)}, bf16[256,128]{1,0:T(8,128)(2,1)S(1)}, u32[]{:S(2)}, u32[]{:S(2)}) collective-permute-start(bf16[256,128]{1,0:T(8,128)(2,1)} %k_hbm.1), channel_id=1, source_target_pairs={{0,4},{4,0},{8,12},{12,8},{1,5},{5,1},{9,13},{13,9},{2,6},{6,2},{1... | collective-permute-start | bytes 196616 | tf_op jit(solution)/shard_map/ppermute | solution.py:215
  6.0 10.5 %collective-permute-start.3 = (bf16[256,128]{1,0:T(8,128)(2,1)}, bf16[256,128]{1,0:T(8,128)(2,1)S(1)}, u32[]{:S(2)}, u32[]{:S(2)}) collective-permute-start(bf16[256,128]{1,0:T(8,128)(2,1)} %v_hbm.1), channel_id=1, source_target_pairs={{0,4},{4,0},{8,12},{12,8},{1,5},{5,1},{9,13},{13,9},{2,6},{6,2},{1... | collective-permute-start | bytes 196616 | tf_op jit(solution)/shard_map/ppermute | solution.py:215
  6.1 11.5 %collective-permute-start.4 = (bf16[256,128]{1,0:T(8,128)(2,1)}, bf16[256,128]{1,0:T(8,128)(2,1)S(1)}, u32[]{:S(2)}, u32[]{:S(2)}) collective-permute-start(bf16[256,128]{1,0:T(8,128)(2,1)} %k_hbm.1), channel_id=1, source_target_pairs={{0,12},{4,8},{8,4},{12,0},{1,13},{5,9},{9,5},{13,1},{2,14},{6,10},... | collective-permute-start | bytes 196616 | tf_op jit(solution)/shard_map/ppermute | solution.py:215
  10.0 8.4 %collective-permute-start.5 = (bf16[256,128]{1,0:T(8,128)(2,1)}, bf16[256,128]{1,0:T(8,128)(2,1)S(1)}, u32[]{:S(2)}, u32[]{:S(2)}) collective-permute-start(bf16[256,128]{1,0:T(8,128)(2,1)} %v_hbm.1), channel_id=1, source_target_pairs={{0,12},{4,8},{8,4},{12,0},{1,13},{5,9},{9,5},{13,1},{2,14},{6,10},... | collective-permute-start | bytes 196616 | tf_op jit(solution)/shard_map/ppermute | solution.py:215

commit v16 on v12

--- a/solution.py
+++ b/solution.py
@@ -28,19 +28,18 @@
     return lax.broadcasted_iota(jnp.int32, shape, dim)
 
 
-def mask_tables(owners, lengths_ref, places_ref, rows, bias_ref):
-    block_total = places_ref.shape[1]
+def row_sum_as_column(places):
+    square = (places.shape[1],) * 2
+    spread = jnp.where(iota(square, 0) == iota(square, 1), places, 0).astype(jnp.float32)
+    return jnp.sum(spread, axis=1, keepdims=True).astype(jnp.int32)
+
+
+def query_places(own, lengths_ref, places, rows):
+    block_total = places.shape[1]
     block_rows = rows * lax.axis_size("seq") // block_total
-    blocks = rows // block_rows
-    places = places_ref[...]
-    square = (block_total, block_total)
-    as_column = jnp.sum(
-        jnp.where(iota(square, 0) == iota(square, 1), places, 0).astype(jnp.float32),
-        axis=1, keepdims=True,
-    ).astype(jnp.int32)
-    across = (block_total, rows)
-    hit = as_column == owners[0] * blocks + iota(across, 1) // block_rows
-    at = jnp.where(hit, iota(across, 0) * block_rows, 0).astype(jnp.float32)
+    shape = (block_total, rows)
+    hit = row_sum_as_column(places) == own * (rows // block_rows) + iota(shape, 1) // block_rows
+    at = jnp.where(hit, iota(shape, 0) * block_rows, 0).astype(jnp.float32)
     query_pos = jnp.sum(at, axis=0, keepdims=True) + (
         iota((1, rows), 1) % block_rows
     ).astype(jnp.float32)
@@ -50,19 +49,23 @@
         bound = bound + lengths_ref[t]
         edge = bound.astype(jnp.float32)
         starts = jnp.where(edge <= query_pos, edge, starts)
-    down = (rows, block_total)
-    for n, owner in enumerate(owners):
-        hit = places == owner * blocks + iota(down, 0) // block_rows
-        at = jnp.where(hit, iota(down, 1) * block_rows, 0).astype(jnp.float32)
-        key_pos = jnp.sum(at, axis=1, keepdims=True) + (
-            iota((rows, 1), 0) % block_rows
-        ).astype(jnp.float32)
-        visible = (key_pos >= starts) & (key_pos <= query_pos)
-        bias_ref[n] = jnp.where(visible, 0.0, NEG_FILL)
+    return query_pos, starts
+
+
+def mask_table(owner, query_pos, starts, places):
+    block_total, rows = places.shape[1], query_pos.shape[1]
+    block_rows = rows * lax.axis_size("seq") // block_total
+    shape = (rows, block_total)
+    hit = places == owner * (rows // block_rows) + iota(shape, 0) // block_rows
+    at = jnp.where(hit, iota(shape, 1) * block_rows, 0).astype(jnp.float32)
+    key_pos = jnp.sum(at, axis=1, keepdims=True) + (
+        iota((rows, 1), 0) % block_rows
+    ).astype(jnp.float32)
+    return jnp.where((key_pos >= starts) & (key_pos <= query_pos), 0.0, NEG_FILL)
 
 
 def values_down(values):
-    turned = jnp.transpose(values.astype(jnp.float32)).astype(jnp.bfloat16)
+    turned = jnp.transpose(values)
     return jnp.concatenate([turned, jnp.ones((ONES, values.shape[0]), jnp.bfloat16)], axis=0)
 
 
@@ -107,19 +110,20 @@
     copies = [pltpu.make_async_copy(*move, sems.at[n]) for n, move in enumerate(moves)]
     for copy in copies:
         copy.start()
-    copies[0].wait()
-    copies[1].wait()
+    for copy in copies:
+        copy.wait()
     heads, _, rows = across_ref.shape
-    owners = [own_ref[0] ^ mask for mask in range(bias_ref.shape[0])]
-    mask_tables(owners, lengths_ref, places_ref, rows, bias_ref)
-    for copy in copies[2:]:
-        copy.wait()
+    own, places = own_ref[0], places_ref[...]
     keys = k_ref[...]
+    query_pos, starts = query_places(own, lengths_ref, places, rows)
+    bias_ref[0] = mask_table(own, query_pos, starts, places)
     turned = values_down(v_ref[...])
 
     def turn(head, _):
         q = q_ref[:, head * HEAD_WIDTH:(head + 1) * HEAD_WIDTH]
-        across_ref[head] = jnp.transpose(q.astype(jnp.float32)).astype(jnp.bfloat16)
+        across_ref[head] = jnp.transpose(q)
+        if 0 < head < bias_ref.shape[0]:
+            bias_ref[head] = mask_table(own ^ head, query_pos, starts, places)
 
     def mix(head, peak):
         peak_ref[head:head + 1, :] = peak
@@ -159,10 +163,18 @@
 
 
 def weights_kernel(
-    at, across_ref, bias_ref, peak_ref, sum_ref, k_ref, new_sum_ref, weight_ref, scaled_ref,
+    at, across_ref, bias_ref, peak_ref, sum_ref, k_ref,
+    new_sum_ref, weight_ref, share_ref, scaled_ref,
 ):
+    ones = jnp.ones((ONES, k_ref.shape[0]), jnp.bfloat16)
+
     def rescale(head, peak):
-        new_sum_ref[head] = sum_ref[head] * jnp.exp2(peak_ref[head:head + 1, :] - peak)
+        factor = jnp.exp2(peak_ref[head:head + 1, :] - peak)
+        added = jnp.dot(ones, weight_ref[head], preferred_element_type=jnp.float32)
+        total = sum_ref[head, HEAD_WIDTH:HEAD_WIDTH + 1, :] * factor + added[:1]
+        share = 1.0 / total
+        share_ref[head:head + 1, :] = share
+        new_sum_ref[head] = sum_ref[head, :HEAD_WIDTH, :] * (factor * share)
 
     in_stages(across_ref.shape[0], [
         score_stage(
@@ -174,18 +186,17 @@
     ])
 
 
-def last_kernel(sum_ref, weight_ref, v_ref, out_ref, block_ref, sems):
-    turned = values_down(v_ref[...])
+def last_kernel(sum_ref, weight_ref, share_ref, v_ref, out_ref, block_ref, sems):
+    turned = jnp.transpose(v_ref[...])
     copies = []
 
     def mix(head, _):
         added = jnp.dot(turned, weight_ref[head], preferred_element_type=jnp.float32)
-        summed = sum_ref[head] + added
-        return summed[:HEAD_WIDTH] / summed[HEAD_WIDTH:HEAD_WIDTH + 1]
+        return (sum_ref[head] + added * share_ref[head:head + 1, :]).astype(jnp.bfloat16)
 
     def send(head, out):
         cols = slice(head * HEAD_WIDTH, (head + 1) * HEAD_WIDTH)
-        block_ref[:, cols] = jnp.transpose(out).astype(jnp.bfloat16)
+        block_ref[:, cols] = jnp.transpose(out)
         copy = pltpu.make_async_copy(block_ref.at[:, cols], out_ref.at[:, cols], sems.at[head])
         copy.start()
         copies.append(copy)
@@ -269,11 +280,12 @@
     third_values = moved(far_values, 1)
     carried = add_shard(2, far_keys, far_values, carried)
     carried = add_shard(1, near_keys, near_values, carried)
-    summed, weights = pl.pallas_call(
+    scaled_sum = pltpu.VMEM((heads, HEAD_WIDTH, rows), jnp.float32)
+    last = pl.pallas_call(
         lambda *refs: weights_kernel(3, *refs),
         in_specs=[VMEM_REF] * 5,
-        out_specs=[VMEM_REF] * 2,
-        out_shape=state[1:] + work[1:],
+        out_specs=[VMEM_REF] * 3,
+        out_shape=[scaled_sum, work[1], state[0]],
         scratch_shapes=work[:1],
         compiler_params=PARAMS,
         cost_estimate=SHORT,
@@ -281,7 +293,7 @@
     )(*in_vmem(across, bias, *carried), third_keys)
     return pl.pallas_call(
         last_kernel,
-        in_specs=[VMEM_REF] * 3,
+        in_specs=[VMEM_REF] * 4,
         out_specs=pl.BlockSpec(memory_space=pl.ANY),
         out_shape=jax.ShapeDtypeStruct((rows, cols), jnp.bfloat16),
         scratch_shapes=[
@@ -291,7 +303,7 @@
         compiler_params=PARAMS,
         cost_estimate=SHORT,
         name="last_values",
-    )(*in_vmem(summed, weights), third_values)
+    )(*in_vmem(*last), third_values)
 
 
 def online_kernel(heads, q_ref, k_ref, v_ref, key_pos_ref, query_pos_ref, start_ref, out_ref, peak_ref, acc_ref):

time: 16.2 us -> 16.3 us (level)
    pallas_call x1, Pallas kernels: 0.8 us -> 1.06 us  [staged_attention(): pl.pallas_call(lambda *refs: weights_kernel(3, *refs), in_specs=[VMEM_REF...]
  transfers between devices with their start and end apart: 6 -> 6, of which waited for: 0 -> 0; matrix products, arithmetic and copies ran while one was open for 0% -> 0% of each run, Pallas kernels for 34% -> 35%
where the time goes in v16:
time: 16.3 us; the launch traced here: 16.1 us
  starting transfers between devices  9.2 us (56%)
  Pallas kernels  6.83 us (42%)
    ppermute x6, starting transfers between devices, moved(): lax.ppermute(value, 'seq', [(i, i ^ mask) for i in range(lax.axis_size('s...  9.2 us
    pallas_call x1, Pallas kernels, staged_attention(): pl.pallas_call(own_kernel, in_specs=[pl.BlockSpec(memory_space=pltpu.SMEM...  2.41 us
    pallas_call x2, Pallas kernels, add_shard(): pl.pallas_call(lambda *refs: next_kernel(at, *refs), in_specs=[VMEM_REF]...  2.22 us
    pallas_call x1, Pallas kernels, staged_attention(): pl.pallas_call(last_kernel, in_specs=[VMEM_REF] * 4, out_specs=pl.BlockSp...  1.14 us
    pallas_call x1, Pallas kernels, staged_attention(): pl.pallas_call(lambda *refs: weights_kernel(3, *refs), in_specs=[VMEM_REF...  1.06 us
  transfers between devices with their start and end apart: 6, of which 0 were waited for; matrix products, arithmetic and copies ran while one was open for 0% of the time, Pallas kernels for 35%

profile of v16, /device:TPU:0, one launch (start us, length us, event | category | flops | bytes accessed | tf_op | source)
XLA Modules:
  0.0 16.1 jit_solution(10938348799813307093)
XLA Ops:
  0.0 4.0 %collective-permute-start.1 = (bf16[256,128]{1,0:T(8,128)(2,1)}, bf16[256,128]{1,0:T(8,128)(2,1)S(1)}, u32[]{:S(2)}, u32[]{:S(2)}) collective-permute-start(bf16[256,128]{1,0:T(8,128)(2,1)} %k_hbm.1), channel_id=1, source_target_pairs={{0,8},{4,12},{8,0},{12,4},{1,9},{5,13},{9,1},{13,5},{2,10},{6,14},... | collective-permute-start | bytes 196616 | tf_op jit(solution)/shard_map/ppermute | solution.py:226
  4.0 0.0 collective-permute-start
  4.1 1.9 %collective-permute-start.2 = (bf16[256,128]{1,0:T(8,128)(2,1)}, bf16[256,128]{1,0:T(8,128)(2,1)S(1)}, u32[]{:S(2)}, u32[]{:S(2)}) collective-permute-start(bf16[256,128]{1,0:T(8,128)(2,1)} %k_hbm.1), channel_id=1, source_target_pairs={{0,4},{4,0},{8,12},{12,8},{1,5},{5,1},{9,13},{13,9},{2,6},{6,2},{1... | collective-permute-start | bytes 196616 | tf_op jit(solution)/shard_map/ppermute | solution.py:226
  6.0 0.1 collective-permute-start.3
  6.1 2.4 %own_shard.1 = (bf16[8,128,256]{2,1,0:T(8,128)(2,1)S(1)}, f32[4,256,256]{2,1,0:T(8,128)S(1)}, f32[8,256]{1,0:T(8,128)S(1)}, f32[8,144,256]{2,1,0:T(8,128)S(1)}) custom-call(s32[1]{0:T(128)} %bitcast.own_ref, s32[3]{0:T(128)} %lengths_hbm.1, s32[1,128]{1,0:T(1,128)} %bitcast.2, bf16[256,1024]{1,0:T(8,128)(2,1)} %q_hbm.1, bf16[256,128]{1,0:T(8,128)(2,1)} %k_hbm.1, ...), custom_call_target="tpu_custom_call" | custom-call | tf_op jit(solution)/shard_map/own_shard/pallas_call | solution.py:245
  8.5 0.0 collective-permute-done.1.refs_4_
  8.5 1.9 %collective-permute-start.4 = (bf16[256,128]{1,0:T(8,128)(2,1)S(1)}, bf16[256,128]{1,0:T(8,128)(2,1)S(1)}, u32[]{:S(2)}, u32[]{:S(2)}) collective-permute-start(bf16[256,128]{1,0:T(8,128)(2,1)S(1)} %collective-permute-done.1.refs_4_), channel_id=1, source_target_pairs={{0,4},{4,0},{8,12},{12,8},{1,5},{5,1},{9,13},{13,9},{2,6},{6,2},{1... | collective-permute-start | bytes 196616 | tf_op jit(solution)/shard_map/ppermute | solution.py:226
  10.5 0.0 collective-permute-done.refs_5_
  10.5 1.2 %collective-permute-start.5 = (bf16[256,128]{1,0:T(8,128)(2,1)S(1)}, bf16[256,128]{1,0:T(8,128)(2,1)S(1)}, u32[]{:S(2)}, u32[]{:S(2)}) collective-permute-start(bf16[256,128]{1,0:T(8,128)(2,1)S(1)} %collective-permute-done.refs_5_), channel_id=1, source_target_pairs={{0,4},{4,0},{8,12},{12,8},{1,5},{5,1},{9,13},{13,9},{2,6},{6,2},{1... | collective-permute-start | bytes 196616 | tf_op jit(solution)/shard_map/ppermute | solution.py:226
  11.6 1.1 %next_shard.2 = (f32[8,256]{1,0:T(8,128)S(1)}, f32[8,144,256]{2,1,0:T(8,128)S(1)}) custom-call(bf16[8,128,256]{2,1,0:T(8,128)(2,1)S(1)} %get-tuple-element.22.refs_0_, f32[4,256,256]{2,1,0:T(8,128)S(1)} %get-tuple-element.23.refs_1_, f32[8,256]{1,0:T(8,128)S(1)} %get-tuple-element.28.refs_2_, f32[8,144,256]{2,1,0:T(8,128)S(1)} %get-tuple-element.29.refs_3_, ...), custom_call_target="tpu_custom_call" | custom-call | tf_op jit(solution)/shard_map/next_shard/pallas_call | solution.py:266
  12.8 0.0 collective-permute-done.2.refs_4_
  12.8 0.0 collective-permute-done.3.refs_5_
  12.8 1.1 %next_shard.3 = (f32[8,256]{1,0:T(8,128)S(1)}, f32[8,144,256]{2,1,0:T(8,128)S(1)}) custom-call(bf16[8,128,256]{2,1,0:T(8,128)(2,1)S(1)} %get-tuple-element.22.refs_0_, f32[4,256,256]{2,1,0:T(8,128)S(1)} %get-tuple-element.23.refs_1_, f32[8,256]{1,0:T(8,128)S(1)} %get-tuple-element.32.refs_2_, f32[8,144,256]{2,1,0:T(8,128)S(1)} %get-tuple-element.33.refs_3_, ...), custom_call_target="tpu_custom_call" | custom-call | tf_op jit(solution)/shard_map/next_shard/pallas_call | solution.py:266
  13.9 0.0 collective-permute-done.4.refs_4_
  13.9 1.1 %last_weights.1 = (f32[8,128,256]{2,1,0:T(8,128)S(1)}, bf16[8,256,256]{2,1,0:T(8,128)(2,1)S(1)}, f32[8,256]{1,0:T(8,128)S(1)}) custom-call(bf16[8,128,256]{2,1,0:T(8,128)(2,1)S(1)} %get-tuple-element.22.refs_0_, f32[4,256,256]{2,1,0:T(8,128)S(1)} %get-tuple-element.23.refs_1_, f32[8,256]{1,0:T(8,128)S(1)} %get-tuple-element.34.refs_2_, ...), custom_call_target="tpu_custom_call" | custom-call | tf_op jit(solution)/shard_map/last_weights/pallas_call | solution.py:284
  15.0 0.0 collective-permute-done.5.v_ref
  15.0 1.1 %last_values.1 = bf16[256,1024]{1,0:T(8,128)(2,1)} custom-call(f32[8,128,256]{2,1,0:T(8,128)S(1)} %get-tuple-element.36.sum_ref, bf16[8,256,256]{2,1,0:T(8,128)(2,1)S(1)} %get-tuple-element.37.weight_ref, f32[8,256]{1,0:T(8,128)S(1)} %get-tuple-element.38.share_ref, bf16[256,128]{1,0:T(8,128)(2,1)S(1)} %collective-permute-done.5.v_ref), custom_call_target="tpu_custom_call" | custom-call | tf_op jit(solution)/shard_map/last_values/pallas_call | solution.py:294
Async XLA Ops:
  0.0 8.5 %collective-permute-start.1 = (bf16[256,128]{1,0:T(8,128)(2,1)}, bf16[256,128]{1,0:T(8,128)(2,1)S(1)}, u32[]{:S(2)}, u32[]{:S(2)}) collective-permute-start(bf16[256,128]{1,0:T(8,128)(2,1)} %k_hbm.1), channel_id=1, source_target_pairs={{0,8},{4,12},{8,0},{12,4},{1,9},{5,13},{9,1},{13,5},{2,10},{6,14},... | collective-permute-start | bytes 196616 | tf_op jit(solution)/shard_map/ppermute | solution.py:226
  4.0 6.4 %collective-permute-start = (bf16[256,128]{1,0:T(8,128)(2,1)}, bf16[256,128]{1,0:T(8,128)(2,1)S(1)}, u32[]{:S(2)}, u32[]{:S(2)}) collective-permute-start(bf16[256,128]{1,0:T(8,128)(2,1)} %v_hbm.1), channel_id=1, source_target_pairs={{0,8},{4,12},{8,0},{12,4},{1,9},{5,13},{9,1},{13,5},{2,10},{6,14},... | collective-permute-start | bytes 196616 | tf_op jit(solution)/shard_map/ppermute | solution.py:226
  4.1 8.7 %collective-permute-start.2 = (bf16[256,128]{1,0:T(8,128)(2,1)}, bf16[256,128]{1,0:T(8,128)(2,1)S(1)}, u32[]{:S(2)}, u32[]{:S(2)}) collective-permute-start(bf16[256,128]{1,0:T(8,128)(2,1)} %k_hbm.1), channel_id=1, source_target_pairs={{0,4},{4,0},{8,12},{12,8},{1,5},{5,1},{9,13},{13,9},{2,6},{6,2},{1... | collective-permute-start | bytes 196616 | tf_op jit(solution)/shard_map/ppermute | solution.py:226
  6.0 6.8 %collective-permute-start.3 = (bf16[256,128]{1,0:T(8,128)(2,1)}, bf16[256,128]{1,0:T(8,128)(2,1)S(1)}, u32[]{:S(2)}, u32[]{:S(2)}) collective-permute-start(bf16[256,128]{1,0:T(8,128)(2,1)} %v_hbm.1), channel_id=1, source_target_pairs={{0,4},{4,0},{8,12},{12,8},{1,5},{5,1},{9,13},{13,9},{2,6},{6,2},{1... | collective-permute-start | bytes 196616 | tf_op jit(solution)/shard_map/ppermute | solution.py:226
  8.5 5.4 %collective-permute-start.4 = (bf16[256,128]{1,0:T(8,128)(2,1)S(1)}, bf16[256,128]{1,0:T(8,128)(2,1)S(1)}, u32[]{:S(2)}, u32[]{:S(2)}) collective-permute-start(bf16[256,128]{1,0:T(8,128)(2,1)S(1)} %collective-permute-done.1.refs_4_), channel_id=1, source_target_pairs={{0,4},{4,0},{8,12},{12,8},{1,5},{5,1},{9,13},{13,9},{2,6},{6,2},{1... | collective-permute-start | bytes 196616 | tf_op jit(solution)/shard_map/ppermute | solution.py:226
  10.5 4.5 %collective-permute-start.5 = (bf16[256,128]{1,0:T(8,128)(2,1)S(1)}, bf16[256,128]{1,0:T(8,128)(2,1)S(1)}, u32[]{:S(2)}, u32[]{:S(2)}) collective-permute-start(bf16[256,128]{1,0:T(8,128)(2,1)S(1)} %collective-permute-done.refs_5_), channel_id=1, source_target_pairs={{0,4},{4,0},{8,12},{12,8},{1,5},{5,1},{9,13},{13,9},{2,6},{6,2},{1... | collective-permute-start | bytes 196616 | tf_op jit(solution)/shard_map/ppermute | solution.py:226

commit v17 on v16

--- a/solution.py
+++ b/solution.py
@@ -98,14 +98,13 @@
     return stage
 
 
-def own_kernel(
+def prepare_kernel(
     own_ref, lengths_hbm, places_hbm, q_hbm, k_hbm, v_hbm,
-    across_ref, bias_ref, peak_ref, sum_ref,
-    lengths_ref, places_ref, q_ref, k_ref, v_ref, scaled_ref, weight_ref, sems,
+    across_ref, bias_ref, k_ref, v_ref, lengths_ref, places_ref, q_ref, sems,
 ):
     moves = (
         (lengths_hbm, lengths_ref), (places_hbm, places_ref),
-        (k_hbm, k_ref), (v_hbm, v_ref), (q_hbm, q_ref),
+        (q_hbm, q_ref), (k_hbm, k_ref), (v_hbm, v_ref),
     )
     copies = [pltpu.make_async_copy(*move, sems.at[n]) for n, move in enumerate(moves)]
     for copy in copies:
@@ -114,43 +113,78 @@
         copy.wait()
     heads, _, rows = across_ref.shape
     own, places = own_ref[0], places_ref[...]
-    keys = k_ref[...]
     query_pos, starts = query_places(own, lengths_ref, places, rows)
-    bias_ref[0] = mask_table(own, query_pos, starts, places)
+    for mask in range(bias_ref.shape[0]):
+        bias_ref[mask] = mask_table(own ^ mask, query_pos, starts, places)
+    for head in range(heads):
+        across_ref[head] = jnp.transpose(q_ref[:, head * HEAD_WIDTH:(head + 1) * HEAD_WIDTH])
+
+
+def only_for(members, own_ref):
+    found = own_ref[0] == members[0]
+    for member in members[1:]:
+        found = found | (own_ref[0] == member)
+    return pl.when(found)
+
+
+def own_kernel(members, own_ref, across_ref, bias_ref, k_ref, v_ref, *refs):
+    peak_ref, sum_ref, scaled_ref, weight_ref = refs[-4:]
+
+    @only_for(members, own_ref)
+    def _():
+        turned = values_down(v_ref[...])
+
+        def mix(head, peak):
+            peak_ref[head:head + 1, :] = peak
+            sum_ref[head] = jnp.dot(turned, weight_ref[head], preferred_element_type=jnp.float32)
+
+        in_stages(across_ref.shape[0], [
+            score_stage(k_ref[...], across_ref, bias_ref, 0, scaled_ref, None),
+            weight_stage(scaled_ref, weight_ref),
+            mix,
+        ])
+
+
+def shrink(head, peak, peak_ref, sum_ref):
+    summed = sum_ref[head] * jnp.exp2(peak_ref[head:head + 1, :] - peak)
+    peak_ref[head:head + 1, :] = peak
+    return summed
+
+
+def weights_kernel(at, members, own_ref, across_ref, bias_ref, k_ref, *refs):
+    peak_ref, sum_ref, weight_ref, scaled_ref = refs[-4:]
+
+    @only_for(members, own_ref)
+    def _():
+        def rescale(head, peak):
+            sum_ref[head] = shrink(head, peak, peak_ref, sum_ref)
+
+        in_stages(across_ref.shape[0], [
+            score_stage(
+                k_ref[...], across_ref, bias_ref, at, scaled_ref,
+                lambda head: peak_ref[head:head + 1, :],
+            ),
+            weight_stage(scaled_ref, weight_ref),
+            rescale,
+        ])
+
+
+def values_kernel(weight_ref, v_ref, old_sum_ref, sum_ref):
     turned = values_down(v_ref[...])
-
-    def turn(head, _):
-        q = q_ref[:, head * HEAD_WIDTH:(head + 1) * HEAD_WIDTH]
-        across_ref[head] = jnp.transpose(q)
-        if 0 < head < bias_ref.shape[0]:
-            bias_ref[head] = mask_table(own ^ head, query_pos, starts, places)
-
-    def mix(head, peak):
-        peak_ref[head:head + 1, :] = peak
-        sum_ref[head] = jnp.dot(turned, weight_ref[head], preferred_element_type=jnp.float32)
-
-    in_stages(heads, [
-        turn,
-        score_stage(keys, across_ref, bias_ref, 0, scaled_ref, None),
-        weight_stage(scaled_ref, weight_ref),
-        mix,
-    ])
-
-
-def joined(head, peak, turned, weight_ref, peak_ref, sum_ref):
-    added = jnp.dot(turned, weight_ref[head], preferred_element_type=jnp.float32)
-    return sum_ref[head] * jnp.exp2(peak_ref[head:head + 1, :] - peak) + added
+    for head in range(sum_ref.shape[0]):
+        sum_ref[head] += jnp.dot(turned, weight_ref[head], preferred_element_type=jnp.float32)
 
 
 def next_kernel(
-    at, across_ref, bias_ref, peak_ref, sum_ref, k_ref, v_ref, new_peak_ref, new_sum_ref,
-    scaled_ref, weight_ref,
+    at, across_ref, bias_ref, k_ref, v_ref, old_peak_ref, old_sum_ref,
+    peak_ref, sum_ref, scaled_ref, weight_ref,
 ):
     turned = values_down(v_ref[...])
 
     def mix(head, peak):
-        new_peak_ref[head:head + 1, :] = peak
-        new_sum_ref[head] = joined(head, peak, turned, weight_ref, peak_ref, sum_ref)
+        sum_ref[head] = shrink(head, peak, peak_ref, sum_ref) + jnp.dot(
+            turned, weight_ref[head], preferred_element_type=jnp.float32
+        )
 
     in_stages(across_ref.shape[0], [
         score_stage(
@@ -162,37 +196,15 @@
     ])
 
 
-def weights_kernel(
-    at, across_ref, bias_ref, peak_ref, sum_ref, k_ref,
-    new_sum_ref, weight_ref, share_ref, scaled_ref,
-):
-    ones = jnp.ones((ONES, k_ref.shape[0]), jnp.bfloat16)
-
-    def rescale(head, peak):
-        factor = jnp.exp2(peak_ref[head:head + 1, :] - peak)
-        added = jnp.dot(ones, weight_ref[head], preferred_element_type=jnp.float32)
-        total = sum_ref[head, HEAD_WIDTH:HEAD_WIDTH + 1, :] * factor + added[:1]
-        share = 1.0 / total
-        share_ref[head:head + 1, :] = share
-        new_sum_ref[head] = sum_ref[head, :HEAD_WIDTH, :] * (factor * share)
-
-    in_stages(across_ref.shape[0], [
-        score_stage(
-            k_ref[...], across_ref, bias_ref, at, scaled_ref,
-            lambda head: peak_ref[head:head + 1, :],
-        ),
-        weight_stage(scaled_ref, weight_ref),
-        rescale,
-    ])
-
-
-def last_kernel(sum_ref, weight_ref, share_ref, v_ref, out_ref, block_ref, sems):
-    turned = jnp.transpose(v_ref[...])
+def last_kernel(weight_ref, v_ref, sum_ref, out_ref, block_ref, sems):
+    turned = values_down(v_ref[...])
     copies = []
 
     def mix(head, _):
         added = jnp.dot(turned, weight_ref[head], preferred_element_type=jnp.float32)
-        return (sum_ref[head] + added * share_ref[head:head + 1, :]).astype(jnp.bfloat16)
+        summed = sum_ref[head] + added
+        share = 1.0 / summed[HEAD_WIDTH:HEAD_WIDTH + 1]
+        return (summed[:HEAD_WIDTH] * share).astype(jnp.bfloat16)
 
     def send(head, out):
         cols = slice(head * HEAD_WIDTH, (head + 1) * HEAD_WIDTH)
@@ -232,68 +244,82 @@
     rows, cols = queries.shape
     heads = cols // HEAD_WIDTH
     devices = lax.axis_size("seq")
-    own = lax.axis_index("seq").astype(jnp.int32)
+    own = lax.axis_index("seq").astype(jnp.int32).reshape(1)
     places = old_place.reshape(1, -1)
-    state = [
-        pltpu.VMEM((heads, rows), jnp.float32),
-        pltpu.VMEM((heads, HEAD_WIDTH + ONES, rows), jnp.float32),
-    ]
-    work = [
-        pltpu.VMEM((heads, rows, rows), jnp.float32),
-        pltpu.VMEM((heads, rows, rows), jnp.bfloat16),
-    ]
-    across, bias, *carried = pl.pallas_call(
-        own_kernel,
-        in_specs=[pl.BlockSpec(memory_space=pltpu.SMEM)] + [HBM_REF] * 5,
+    scalar = pl.BlockSpec(memory_space=pltpu.SMEM)
+    peak_type = pltpu.VMEM((heads, rows), jnp.float32)
+    sum_type = pltpu.VMEM((heads, HEAD_WIDTH + ONES, rows), jnp.float32)
+    scaled_type = pltpu.VMEM((heads, rows, rows), jnp.float32)
+    weight_type = pltpu.VMEM((heads, rows, rows), jnp.bfloat16)
+
+    def call(kernel, name, ins, outs, scratch, state=(), scalars=()):
+        first = len(scalars) + len(ins)
+        return pl.pallas_call(
+            kernel,
+            in_specs=[scalar] * len(scalars) + [VMEM_REF] * (len(ins) + len(state)),
+            out_specs=[VMEM_REF] * len(outs),
+            out_shape=outs,
+            input_output_aliases={first + n: n for n in range(len(state))},
+            scratch_shapes=scratch,
+            compiler_params=PARAMS,
+            cost_estimate=SHORT,
+            name=name,
+        )(*scalars, *in_vmem(*ins, *state))
+
+    across, bias, own_keys, own_values = pl.pallas_call(
+        prepare_kernel,
+        in_specs=[scalar] + [HBM_REF] * 5,
         out_specs=[VMEM_REF] * 4,
         out_shape=[
             pltpu.VMEM((heads, HEAD_WIDTH, rows), jnp.bfloat16),
             pltpu.VMEM((devices, rows, rows), jnp.float32),
-        ] + state,
+            pltpu.VMEM(keys.shape, jnp.bfloat16),
+            pltpu.VMEM(values.shape, jnp.bfloat16),
+        ],
         scratch_shapes=[
             pltpu.SMEM(lengths.shape, jnp.int32),
             pltpu.VMEM(places.shape, jnp.int32),
             pltpu.VMEM(queries.shape, jnp.bfloat16),
-            pltpu.VMEM(keys.shape, jnp.bfloat16),
-            pltpu.VMEM(values.shape, jnp.bfloat16),
-        ] + work + [pltpu.SemaphoreType.DMA((5,))],
+            pltpu.SemaphoreType.DMA((5,)),
+        ],
         compiler_params=PARAMS,
         cost_estimate=SHORT,
-        name="own_shard",
-    )(own.reshape(1), *in_hbm(lengths, places, queries, keys, values))
-
-    def add_shard(at, keys, values, carried):
-        return pl.pallas_call(
-            lambda *refs: next_kernel(at, *refs),
-            in_specs=[VMEM_REF] * 6,
-            out_specs=[VMEM_REF] * 2,
-            out_shape=state,
-            scratch_shapes=work,
-            compiler_params=PARAMS,
-            cost_estimate=SHORT,
-            name="next_shard",
-        )(*in_vmem(across, bias, *carried), keys, values)
-
-    far_keys, *carried = lax.optimization_barrier((far_keys, *carried))
+        name="prepare",
+    )(own, *in_hbm(lengths, places, queries, keys, values))
+
+    def own_shard(members, state):
+        return call(
+            lambda *refs: own_kernel(members, *refs), "own_shard",
+            (across, bias, own_keys, own_values), [peak_type, sum_type],
+            [scaled_type, weight_type], state, (own,),
+        )
+
+    def shard_weights(at, members, keys, state):
+        return call(
+            lambda *refs: weights_kernel(at, members, *refs), "shard_weights",
+            (across, bias, keys), [peak_type, sum_type, weight_type],
+            [scaled_type], state, (own,),
+        )
+
+    state = own_shard((0, 2, 3), ())
+    state = shard_weights(2, (0, 2), far_keys, state)
+    far_keys, *state = lax.optimization_barrier((far_keys, *state))
     third_keys = moved(far_keys, 1)
-    far_values, *carried = lax.optimization_barrier((far_values, *carried))
+    state = [*own_shard((1,), state[:2]), state[2]]
+    state = shard_weights(2, (3,), far_keys, state)
+    far_values, far_keys, *state = lax.optimization_barrier((far_values, far_keys, *state))
     third_values = moved(far_values, 1)
-    carried = add_shard(2, far_keys, far_values, carried)
-    carried = add_shard(1, near_keys, near_values, carried)
-    scaled_sum = pltpu.VMEM((heads, HEAD_WIDTH, rows), jnp.float32)
-    last = pl.pallas_call(
-        lambda *refs: weights_kernel(3, *refs),
-        in_specs=[VMEM_REF] * 5,
-        out_specs=[VMEM_REF] * 3,
-        out_shape=[scaled_sum, work[1], state[0]],
-        scratch_shapes=work[:1],
-        compiler_params=PARAMS,
-        cost_estimate=SHORT,
-        name="last_weights",
-    )(*in_vmem(across, bias, *carried), third_keys)
+    peak, summed, weights = shard_weights(2, (1,), far_keys, state)
+    summed, = call(values_kernel, "shard_values", (weights, far_values), [sum_type], [], (summed,))
+    state = call(
+        lambda *refs: next_kernel(1, *refs), "next_shard",
+        (across, bias, near_keys, near_values), [peak_type, sum_type],
+        [scaled_type, weight_type], (peak, summed),
+    )
+    _, summed, weights = shard_weights(3, (0, 1, 2, 3), third_keys, state)
     return pl.pallas_call(
         last_kernel,
-        in_specs=[VMEM_REF] * 4,
+        in_specs=[VMEM_REF] * 3,
         out_specs=pl.BlockSpec(memory_space=pl.ANY),
         out_shape=jax.ShapeDtypeStruct((rows, cols), jnp.bfloat16),
         scratch_shapes=[
@@ -303,7 +329,7 @@
         compiler_params=PARAMS,
         cost_estimate=SHORT,
         name="last_values",
-    )(*in_vmem(*last), third_values)
+    )(*in_vmem(weights, third_values, summed))
 
 
 def online_kernel(heads, q_ref, k_ref, v_ref, key_pos_ref, query_pos_ref, start_ref, out_ref, peak_ref, acc_ref):

time: 16.3 us -> 16.6 us (1.018)
  waiting for transfers between devices: 0.02 us -> 0.33 us
    ppermute x6, waiting for transfers between devices: 0.02 us -> 0.33 us  [moved(): lax.ppermute(value, 'seq', [(i, i ^ mask) for i in range(lax.axis_size('s...]
    pallas_call x5 -> x10, Pallas kernels: 6.83 us -> 6.97 us  [the longest x8 4.2 us: call(): pl.pallas_call(kernel, in_specs=[scalar] * len(scalars) + [VMEM_REF] * (l...]
  transfers between devices with their start and end apart: 6 -> 6, of which waited for: 0 -> 1; matrix products, arithmetic and copies ran while one was open for 0% -> 0% of each run, Pallas kernels for 35% -> 35%
where the time goes in v17:
time: 16.6 us; the launch traced here: 16.5 us
  starting transfers between devices  9.1 us (55%)
  Pallas kernels  6.97 us (42%)
  waiting for transfers between devices  0.33 us (2%)
    ppermute x6, starting transfers between devices, moved(): lax.ppermute(value, 'seq', [(i, i ^ mask) for i in range(lax.axis_size('s...  9.1 us
    pallas_call x8, Pallas kernels, call(): pl.pallas_call(kernel, in_specs=[scalar] * len(scalars) + [VMEM_REF] * (l...  4.2 us
    pallas_call x1, Pallas kernels, staged_attention(): pl.pallas_call(prepare_kernel, in_specs=[scalar] + [HBM_REF] * 5, out_spe...  1.56 us
    pallas_call x1, Pallas kernels, staged_attention(): pl.pallas_call(last_kernel, in_specs=[VMEM_REF] * 3, out_specs=pl.BlockSp...  1.21 us
  transfers between devices with their start and end apart: 6, of which 1 were waited for; matrix products, arithmetic and copies ran while one was open for 0% of the time, Pallas kernels for 35%

profile of v17, /device:TPU:0, one launch (start us, length us, event | category | flops | bytes accessed | tf_op | source)
XLA Modules:
  0.0 16.5 jit_solution(7504947333632165054)
XLA Ops:
  0.0 4.0 %collective-permute-start = (bf16[256,128]{1,0:T(8,128)(2,1)}, bf16[256,128]{1,0:T(8,128)(2,1)S(1)}, u32[]{:S(2)}, u32[]{:S(2)}) collective-permute-start(bf16[256,128]{1,0:T(8,128)(2,1)} %k_hbm.1), channel_id=1, source_target_pairs={{0,8},{4,12},{8,0},{12,4},{1,9},{5,13},{9,1},{13,5},{2,10},{6,14},... | collective-permute-start | bytes 196616 | tf_op jit(solution)/shard_map/ppermute | solution.py:238
  4.0 0.0 collective-permute-start.4
  4.1 1.9 %collective-permute-start.2 = (bf16[256,128]{1,0:T(8,128)(2,1)}, bf16[256,128]{1,0:T(8,128)(2,1)S(1)}, u32[]{:S(2)}, u32[]{:S(2)}) collective-permute-start(bf16[256,128]{1,0:T(8,128)(2,1)} %k_hbm.1), channel_id=1, source_target_pairs={{0,4},{4,0},{8,12},{12,8},{1,5},{5,1},{9,13},{13,9},{2,6},{6,2},{1... | collective-permute-start | bytes 196616 | tf_op jit(solution)/shard_map/ppermute | solution.py:238
  6.0 0.1 collective-permute-start.3
  6.1 1.6 %prepare.1 = (bf16[8,128,256]{2,1,0:T(8,128)(2,1)S(1)}, f32[4,256,256]{2,1,0:T(8,128)S(1)}, bf16[256,128]{1,0:T(8,128)(2,1)S(1)}, bf16[256,128]{1,0:T(8,128)(2,1)S(1)}) custom-call(s32[1]{0:T(128)} %bitcast.own_ref.refs_0_, s32[3]{0:T(128)} %lengths_hbm.1, s32[1,128]{1,0:T(1,128)} %bitcast.2, bf16[256,1024]{1,0:T(8,128)(2,1)} %q_hbm.1, ...), custom_call_target="tpu_custom_call" | custom-call | tf_op jit(solution)/shard_map/prepare/pallas_call | solution.py:269
  7.7 1.1 %own_shard.2 = (f32[8,256]{1,0:T(8,128)S(1)}, f32[8,144,256]{2,1,0:T(8,128)S(1)}) custom-call(s32[1]{0:T(128)} %bitcast.own_ref.refs_0_, bf16[8,128,256]{2,1,0:T(8,128)(2,1)S(1)} %get-tuple-element.35.refs_1_.refs_0_, f32[4,256,256]{2,1,0:T(8,128)S(1)} %get-tuple-element.36.refs_2_.refs_1_, bf16[256,128]{1,0:T(8,128)(2,1)S(1)} %get-tuple-element.37.refs_3_, ...), custom_call_target="tpu_custom_call" | custom-call | tf_op jit(solution)/shard_map/own_shard/pallas_call | solution.py:257
  8.8 0.0 collective-permute-done.refs_3_
  8.8 0.8 %shard_weights.4 = (f32[8,256]{1,0:T(8,128)S(1)}, f32[8,144,256]{2,1,0:T(8,128)S(1)}, bf16[8,256,256]{2,1,0:T(8,128)(2,1)S(1)}) custom-call(s32[1]{0:T(128)} %bitcast.own_ref.refs_0_, bf16[8,128,256]{2,1,0:T(8,128)(2,1)S(1)} %get-tuple-element.35.refs_1_.refs_0_, ...), custom_call_target="tpu_custom_call", output_to_operand_aliasing={{0}: (4, {}), {1}: (5, {})} | custom-call | tf_op jit(solution)/shard_map/shard_weights/pallas_call | solution.py:257
  9.6 0.4 %collective-permute-start.1 = (bf16[256,128]{1,0:T(8,128)(2,1)S(1)}, bf16[256,128]{1,0:T(8,128)(2,1)S(1)}, u32[]{:S(2)}, u32[]{:S(2)}) collective-permute-start(bf16[256,128]{1,0:T(8,128)(2,1)S(1)} %collective-permute-done.refs_3_), channel_id=1, source_target_pairs={{0,4},{4,0},{8,12},{12,8},{1,5},{5,1},{9,13},{13,9},{2,6},{6,2},{1... | collective-permute-start | bytes 196616 | tf_op jit(solution)/shard_map/ppermute | solution.py:238
  10.0 0.3 %collective-permute-done.4.v_ref = bf16[256,128]{1,0:T(8,128)(2,1)S(1)} collective-permute-done((bf16[256,128]{1,0:T(8,128)(2,1)}, bf16[256,128]{1,0:T(8,128)(2,1)S(1)}, u32[]{:S(2)}, u32[]{:S(2)}) %collective-permute-start.4) | collective-permute-done | bytes 65568 | tf_op jit(solution)/shard_map/ppermute | solution.py:238
  10.3 2.6 %collective-permute-start.5 = (bf16[256,128]{1,0:T(8,128)(2,1)S(1)}, bf16[256,128]{1,0:T(8,128)(2,1)S(1)}, u32[]{:S(2)}, u32[]{:S(2)}) collective-permute-start(bf16[256,128]{1,0:T(8,128)(2,1)S(1)} %collective-permute-done.4.v_ref), channel_id=1, source_target_pairs={{0,4},{4,0},{8,12},{12,8},{1,5},{5,1},{9,13},{13,9},{2,6},{6,2},{1... | collective-permute-start | bytes 196616 | tf_op jit(solution)/shard_map/ppermute | solution.py:238
  13.0 0.3 %shard_values.1.refs_5_ = f32[8,144,256]{2,1,0:T(8,128)S(1)} custom-call(bf16[8,256,256]{2,1,0:T(8,128)(2,1)S(1)} %get-tuple-element.58.weight_ref, bf16[256,128]{1,0:T(8,128)(2,1)S(1)} %collective-permute-done.4.v_ref, f32[8,144,256]{2,1,0:T(8,128)S(1)} %get-tuple-element.60.old_sum_ref), custom_call_target="tpu_custom_call", output_to_operand_aliasing={{}: (2, {})} | custom-call | tf_op jit(solution)/shard_map/shard_values/pallas_call | solution.py:257
  13.3 0.0 collective-permute-done.2.refs_2_
  13.3 0.0 collective-permute-done.3.refs_3_
  13.3 1.1 %next_shard.1 = (f32[8,256]{1,0:T(8,128)S(1)}, f32[8,144,256]{2,1,0:T(8,128)S(1)}) custom-call(bf16[8,128,256]{2,1,0:T(8,128)(2,1)S(1)} %get-tuple-element.35.refs_1_.refs_0_, f32[4,256,256]{2,1,0:T(8,128)S(1)} %get-tuple-element.36.refs_2_.refs_1_, ...), custom_call_target="tpu_custom_call", output_to_operand_aliasing={{0}: (4, {}), {1}: (5, {})} | custom-call | tf_op jit(solution)/shard_map/next_shard/pallas_call | solution.py:257
  14.5 0.0 collective-permute-done.1.refs_3_
  14.5 0.8 %shard_weights.7 = (f32[8,256]{1,0:T(8,128)S(1)}, f32[8,144,256]{2,1,0:T(8,128)S(1)}, bf16[8,256,256]{2,1,0:T(8,128)(2,1)S(1)}) custom-call(s32[1]{0:T(128)} %bitcast.own_ref.refs_0_, bf16[8,128,256]{2,1,0:T(8,128)(2,1)S(1)} %get-tuple-element.35.refs_1_.refs_0_, ...), custom_call_target="tpu_custom_call", output_to_operand_aliasing={{0}: (4, {}), {1}: (5, {})} | custom-call | tf_op jit(solution)/shard_map/shard_weights/pallas_call | solution.py:257
  15.3 0.0 collective-permute-done.5.v_ref
  15.3 1.2 %last_values.1 = bf16[256,1024]{1,0:T(8,128)(2,1)} custom-call(bf16[8,256,256]{2,1,0:T(8,128)(2,1)S(1)} %get-tuple-element.63.weight_ref, bf16[256,128]{1,0:T(8,128)(2,1)S(1)} %collective-permute-done.5.v_ref, f32[8,144,256]{2,1,0:T(8,128)S(1)} %get-tuple-element.64.sum_ref), custom_call_target="tpu_custom_call" | custom-call | tf_op jit(solution)/shard_map/last_values/pallas_call | solution.py:320
  (3 shorter events, 0.0 us)
Async XLA Ops:
  0.0 8.8 %collective-permute-start = (bf16[256,128]{1,0:T(8,128)(2,1)}, bf16[256,128]{1,0:T(8,128)(2,1)S(1)}, u32[]{:S(2)}, u32[]{:S(2)}) collective-permute-start(bf16[256,128]{1,0:T(8,128)(2,1)} %k_hbm.1), channel_id=1, source_target_pairs={{0,8},{4,12},{8,0},{12,4},{1,9},{5,13},{9,1},{13,5},{2,10},{6,14},... | collective-permute-start | bytes 196616 | tf_op jit(solution)/shard_map/ppermute | solution.py:238
  4.0 6.3 %collective-permute-start.4 = (bf16[256,128]{1,0:T(8,128)(2,1)}, bf16[256,128]{1,0:T(8,128)(2,1)S(1)}, u32[]{:S(2)}, u32[]{:S(2)}) collective-permute-start(bf16[256,128]{1,0:T(8,128)(2,1)} %v_hbm.1), channel_id=1, source_target_pairs={{0,8},{4,12},{8,0},{12,4},{1,9},{5,13},{9,1},{13,5},{2,10},{6,14},... | collective-permute-start | bytes 196616 | tf_op jit(solution)/shard_map/ppermute | solution.py:238
  4.1 9.2 %collective-permute-start.2 = (bf16[256,128]{1,0:T(8,128)(2,1)}, bf16[256,128]{1,0:T(8,128)(2,1)S(1)}, u32[]{:S(2)}, u32[]{:S(2)}) collective-permute-start(bf16[256,128]{1,0:T(8,128)(2,1)} %k_hbm.1), channel_id=1, source_target_pairs={{0,4},{4,0},{8,12},{12,8},{1,5},{5,1},{9,13},{13,9},{2,6},{6,2},{1... | collective-permute-start | bytes 196616 | tf_op jit(solution)/shard_map/ppermute | solution.py:238
  6.0 7.4 %collective-permute-start.3 = (bf16[256,128]{1,0:T(8,128)(2,1)}, bf16[256,128]{1,0:T(8,128)(2,1)S(1)}, u32[]{:S(2)}, u32[]{:S(2)}) collective-permute-start(bf16[256,128]{1,0:T(8,128)(2,1)} %v_hbm.1), channel_id=1, source_target_pairs={{0,4},{4,0},{8,12},{12,8},{1,5},{5,1},{9,13},{13,9},{2,6},{6,2},{1... | collective-permute-start | bytes 196616 | tf_op jit(solution)/shard_map/ppermute | solution.py:238
  9.6 4.8 %collective-permute-start.1 = (bf16[256,128]{1,0:T(8,128)(2,1)S(1)}, bf16[256,128]{1,0:T(8,128)(2,1)S(1)}, u32[]{:S(2)}, u32[]{:S(2)}) collective-permute-start(bf16[256,128]{1,0:T(8,128)(2,1)S(1)} %collective-permute-done.refs_3_), channel_id=1, source_target_pairs={{0,4},{4,0},{8,12},{12,8},{1,5},{5,1},{9,13},{13,9},{2,6},{6,2},{1... | collective-permute-start | bytes 196616 | tf_op jit(solution)/shard_map/ppermute | solution.py:238
  10.3 4.9 %collective-permute-start.5 = (bf16[256,128]{1,0:T(8,128)(2,1)S(1)}, bf16[256,128]{1,0:T(8,128)(2,1)S(1)}, u32[]{:S(2)}, u32[]{:S(2)}) collective-permute-start(bf16[256,128]{1,0:T(8,128)(2,1)S(1)} %collective-permute-done.4.v_ref), channel_id=1, source_target_pairs={{0,4},{4,0},{8,12},{12,8},{1,5},{5,1},{9,13},{13,9},{2,6},{6,2},{1... | collective-permute-start | bytes 196616 | tf_op jit(solution)/shard_map/ppermute | solution.py:238

commit v18 on v17

--- a/solution.py
+++ b/solution.py
@@ -305,11 +305,10 @@
     state = shard_weights(2, (0, 2), far_keys, state)
     far_keys, *state = lax.optimization_barrier((far_keys, *state))
     third_keys = moved(far_keys, 1)
-    state = [*own_shard((1,), state[:2]), state[2]]
-    state = shard_weights(2, (3,), far_keys, state)
     far_values, far_keys, *state = lax.optimization_barrier((far_values, far_keys, *state))
     third_values = moved(far_values, 1)
-    peak, summed, weights = shard_weights(2, (1,), far_keys, state)
+    state = [*own_shard((1,), state[:2]), state[2]]
+    peak, summed, weights = shard_weights(2, (1, 3), far_keys, state)
     summed, = call(values_kernel, "shard_values", (weights, far_values), [sum_type], [], (summed,))
     state = call(
         lambda *refs: next_kernel(1, *refs), "next_shard",

time: 16.6 us -> 16.1 us (0.970)
  starting transfers between devices: 9.1 us -> 7.87 us
  waiting for transfers between devices: 0.33 us -> 1.06 us
    ppermute x6, starting transfers between devices: 9.1 us -> 7.87 us  [moved(): lax.ppermute(value, 'seq', [(i, i ^ mask) for i in range(lax.axis_size('s...]
    ppermute x6, waiting for transfers between devices: 0.33 us -> 1.06 us  [moved(): lax.ppermute(value, 'seq', [(i, i ^ mask) for i in range(lax.axis_size('s...]
    pallas_call x8 -> x7, Pallas kernels: 4.2 us -> 4.19 us  [call(): pl.pallas_call(kernel, in_specs=[scalar] * len(scalars) + [VMEM_REF] * (l...]
  transfers between devices with their start and end apart: 6 -> 6, of which waited for: 1 -> 2; matrix products, arithmetic and copies ran while one was open for 0% -> 0% of each run, Pallas kernels for 35% -> 36%
where the time goes in v18:
time: 16.1 us; the launch traced here: 16 us
  starting transfers between devices  7.87 us (49%)
  Pallas kernels  6.97 us (43%)
  waiting for transfers between devices  1.06 us (7%)
    ppermute x6, starting transfers between devices, moved(): lax.ppermute(value, 'seq', [(i, i ^ mask) for i in range(lax.axis_size('s...  7.87 us
    pallas_call x7, Pallas kernels, call(): pl.pallas_call(kernel, in_specs=[scalar] * len(scalars) + [VMEM_REF] * (l...  4.19 us
    pallas_call x1, Pallas kernels, staged_attention(): pl.pallas_call(prepare_kernel, in_specs=[scalar] + [HBM_REF] * 5, out_spe...  1.56 us
    pallas_call x1, Pallas kernels, staged_attention(): pl.pallas_call(last_kernel, in_specs=[VMEM_REF] * 3, out_specs=pl.BlockSp...  1.22 us
    ppermute x6, waiting for transfers between devices, moved(): lax.ppermute(value, 'seq', [(i, i ^ mask) for i in range(lax.axis_size('s...  1.06 us
  transfers between devices with their start and end apart: 6, of which 2 were waited for; matrix products, arithmetic and copies ran while one was open for 0% of the time, Pallas kernels for 36%

profile of v18, /device:TPU:0, one launch (start us, length us, event | category | flops | bytes accessed | tf_op | source)
XLA Modules:
  0.0 16.0 jit_solution(10678432644447919104)
XLA Ops:
  0.0 4.0 %collective-permute-start = (bf16[256,128]{1,0:T(8,128)(2,1)}, bf16[256,128]{1,0:T(8,128)(2,1)S(1)}, u32[]{:S(2)}, u32[]{:S(2)}) collective-permute-start(bf16[256,128]{1,0:T(8,128)(2,1)} %k_hbm.1), channel_id=1, source_target_pairs={{0,8},{4,12},{8,0},{12,4},{1,9},{5,13},{9,1},{13,5},{2,10},{6,14},... | collective-permute-start | bytes 196616 | tf_op jit(solution)/shard_map/ppermute | solution.py:238
  4.0 0.0 collective-permute-start.4
  4.1 1.9 %collective-permute-start.2 = (bf16[256,128]{1,0:T(8,128)(2,1)}, bf16[256,128]{1,0:T(8,128)(2,1)S(1)}, u32[]{:S(2)}, u32[]{:S(2)}) collective-permute-start(bf16[256,128]{1,0:T(8,128)(2,1)} %k_hbm.1), channel_id=1, source_target_pairs={{0,4},{4,0},{8,12},{12,8},{1,5},{5,1},{9,13},{13,9},{2,6},{6,2},{1... | collective-permute-start | bytes 196616 | tf_op jit(solution)/shard_map/ppermute | solution.py:238
  6.0 0.1 collective-permute-start.3
  6.1 1.6 %prepare.1 = (bf16[8,128,256]{2,1,0:T(8,128)(2,1)S(1)}, f32[4,256,256]{2,1,0:T(8,128)S(1)}, bf16[256,128]{1,0:T(8,128)(2,1)S(1)}, bf16[256,128]{1,0:T(8,128)(2,1)S(1)}) custom-call(s32[1]{0:T(128)} %bitcast.own_ref.refs_0_, s32[3]{0:T(128)} %lengths_hbm.1, s32[1,128]{1,0:T(1,128)} %bitcast.2, bf16[256,1024]{1,0:T(8,128)(2,1)} %q_hbm.1, ...), custom_call_target="tpu_custom_call" | custom-call | tf_op jit(solution)/shard_map/prepare/pallas_call | solution.py:269
  7.7 1.1 %own_shard.2 = (f32[8,256]{1,0:T(8,128)S(1)}, f32[8,144,256]{2,1,0:T(8,128)S(1)}) custom-call(s32[1]{0:T(128)} %bitcast.own_ref.refs_0_, bf16[8,128,256]{2,1,0:T(8,128)(2,1)S(1)} %get-tuple-element.32.refs_1_.refs_0_, f32[4,256,256]{2,1,0:T(8,128)S(1)} %get-tuple-element.33.refs_2_.refs_1_, bf16[256,128]{1,0:T(8,128)(2,1)S(1)} %get-tuple-element.34.refs_3_, ...), custom_call_target="tpu_custom_call" | custom-call | tf_op jit(solution)/shard_map/own_shard/pallas_call | solution.py:257
  8.8 0.0 collective-permute-done.refs_3_
  8.8 0.8 %shard_weights.3 = (f32[8,256]{1,0:T(8,128)S(1)}, f32[8,144,256]{2,1,0:T(8,128)S(1)}, bf16[8,256,256]{2,1,0:T(8,128)(2,1)S(1)}) custom-call(s32[1]{0:T(128)} %bitcast.own_ref.refs_0_, bf16[8,128,256]{2,1,0:T(8,128)(2,1)S(1)} %get-tuple-element.32.refs_1_.refs_0_, ...), custom_call_target="tpu_custom_call", output_to_operand_aliasing={{0}: (4, {}), {1}: (5, {})} | custom-call | tf_op jit(solution)/shard_map/shard_weights/pallas_call | solution.py:257
  9.6 0.4 %collective-permute-start.1 = (bf16[256,128]{1,0:T(8,128)(2,1)S(1)}, bf16[256,128]{1,0:T(8,128)(2,1)S(1)}, u32[]{:S(2)}, u32[]{:S(2)}) collective-permute-start(bf16[256,128]{1,0:T(8,128)(2,1)S(1)} %collective-permute-done.refs_3_), channel_id=1, source_target_pairs={{0,4},{4,0},{8,12},{12,8},{1,5},{5,1},{9,13},{13,9},{2,6},{6,2},{1... | collective-permute-start | bytes 196616 | tf_op jit(solution)/shard_map/ppermute | solution.py:238
  10.0 0.3 %collective-permute-done.4.v_ref = bf16[256,128]{1,0:T(8,128)(2,1)S(1)} collective-permute-done((bf16[256,128]{1,0:T(8,128)(2,1)}, bf16[256,128]{1,0:T(8,128)(2,1)S(1)}, u32[]{:S(2)}, u32[]{:S(2)}) %collective-permute-start.4) | collective-permute-done | bytes 65568 | tf_op jit(solution)/shard_map/ppermute | solution.py:238
  10.3 1.4 %collective-permute-start.5 = (bf16[256,128]{1,0:T(8,128)(2,1)S(1)}, bf16[256,128]{1,0:T(8,128)(2,1)S(1)}, u32[]{:S(2)}, u32[]{:S(2)}) collective-permute-start(bf16[256,128]{1,0:T(8,128)(2,1)S(1)} %collective-permute-done.4.v_ref), channel_id=1, source_target_pairs={{0,4},{4,0},{8,12},{12,8},{1,5},{5,1},{9,13},{13,9},{2,6},{6,2},{1... | collective-permute-start | bytes 196616 | tf_op jit(solution)/shard_map/ppermute | solution.py:238
  11.7 0.3 %shard_values.1.refs_5_ = f32[8,144,256]{2,1,0:T(8,128)S(1)} custom-call(bf16[8,256,256]{2,1,0:T(8,128)(2,1)S(1)} %get-tuple-element.52.weight_ref, bf16[256,128]{1,0:T(8,128)(2,1)S(1)} %collective-permute-done.4.v_ref, f32[8,144,256]{2,1,0:T(8,128)S(1)} %get-tuple-element.54.old_sum_ref), custom_call_target="tpu_custom_call", output_to_operand_aliasing={{}: (2, {})} | custom-call | tf_op jit(solution)/shard_map/shard_values/pallas_call | solution.py:257
  12.1 0.0 collective-permute-done.2.refs_2_
  12.1 0.0 collective-permute-done.3.refs_3_
  12.1 1.1 %next_shard.1 = (f32[8,256]{1,0:T(8,128)S(1)}, f32[8,144,256]{2,1,0:T(8,128)S(1)}) custom-call(bf16[8,128,256]{2,1,0:T(8,128)(2,1)S(1)} %get-tuple-element.32.refs_1_.refs_0_, f32[4,256,256]{2,1,0:T(8,128)S(1)} %get-tuple-element.33.refs_2_.refs_1_, ...), custom_call_target="tpu_custom_call", output_to_operand_aliasing={{0}: (4, {}), {1}: (5, {})} | custom-call | tf_op jit(solution)/shard_map/next_shard/pallas_call | solution.py:257
  13.2 0.7 %collective-permute-done.1.refs_3_ = bf16[256,128]{1,0:T(8,128)(2,1)S(1)} collective-permute-done((bf16[256,128]{1,0:T(8,128)(2,1)S(1)}, bf16[256,128]{1,0:T(8,128)(2,1)S(1)}, u32[]{:S(2)}, u32[]{:S(2)}) %collective-permute-start.1) | collective-permute-done | bytes 65568 | tf_op jit(solution)/shard_map/ppermute | solution.py:238
  14.0 0.8 %shard_weights.5 = (f32[8,256]{1,0:T(8,128)S(1)}, f32[8,144,256]{2,1,0:T(8,128)S(1)}, bf16[8,256,256]{2,1,0:T(8,128)(2,1)S(1)}) custom-call(s32[1]{0:T(128)} %bitcast.own_ref.refs_0_, bf16[8,128,256]{2,1,0:T(8,128)(2,1)S(1)} %get-tuple-element.32.refs_1_.refs_0_, ...), custom_call_target="tpu_custom_call", output_to_operand_aliasing={{0}: (4, {}), {1}: (5, {})} | custom-call | tf_op jit(solution)/shard_map/shard_weights/pallas_call | solution.py:257
  14.8 0.0 collective-permute-done.5.v_ref
  14.8 1.2 %last_values.1 = bf16[256,1024]{1,0:T(8,128)(2,1)} custom-call(bf16[8,256,256]{2,1,0:T(8,128)(2,1)S(1)} %get-tuple-element.57.weight_ref, bf16[256,128]{1,0:T(8,128)(2,1)S(1)} %collective-permute-done.5.v_ref, f32[8,144,256]{2,1,0:T(8,128)S(1)} %get-tuple-element.58.sum_ref), custom_call_target="tpu_custom_call" | custom-call | tf_op jit(solution)/shard_map/last_values/pallas_call | solution.py:319
  (2 shorter events, 0.0 us)
Async XLA Ops:
  0.0 8.8 %collective-permute-start = (bf16[256,128]{1,0:T(8,128)(2,1)}, bf16[256,128]{1,0:T(8,128)(2,1)S(1)}, u32[]{:S(2)}, u32[]{:S(2)}) collective-permute-start(bf16[256,128]{1,0:T(8,128)(2,1)} %k_hbm.1), channel_id=1, source_target_pairs={{0,8},{4,12},{8,0},{12,4},{1,9},{5,13},{9,1},{13,5},{2,10},{6,14},... | collective-permute-start | bytes 196616 | tf_op jit(solution)/shard_map/ppermute | solution.py:238
  4.0 6.3 %collective-permute-start.4 = (bf16[256,128]{1,0:T(8,128)(2,1)}, bf16[256,128]{1,0:T(8,128)(2,1)S(1)}, u32[]{:S(2)}, u32[]{:S(2)}) collective-permute-start(bf16[256,128]{1,0:T(8,128)(2,1)} %v_hbm.1), channel_id=1, source_target_pairs={{0,8},{4,12},{8,0},{12,4},{1,9},{5,13},{9,1},{13,5},{2,10},{6,14},... | collective-permute-start | bytes 196616 | tf_op jit(solution)/shard_map/ppermute | solution.py:238
  4.1 8.0 %collective-permute-start.2 = (bf16[256,128]{1,0:T(8,128)(2,1)}, bf16[256,128]{1,0:T(8,128)(2,1)S(1)}, u32[]{:S(2)}, u32[]{:S(2)}) collective-permute-start(bf16[256,128]{1,0:T(8,128)(2,1)} %k_hbm.1), channel_id=1, source_target_pairs={{0,4},{4,0},{8,12},{12,8},{1,5},{5,1},{9,13},{13,9},{2,6},{6,2},{1... | collective-permute-start | bytes 196616 | tf_op jit(solution)/shard_map/ppermute | solution.py:238
  6.0 6.1 %collective-permute-start.3 = (bf16[256,128]{1,0:T(8,128)(2,1)}, bf16[256,128]{1,0:T(8,128)(2,1)S(1)}, u32[]{:S(2)}, u32[]{:S(2)}) collective-permute-start(bf16[256,128]{1,0:T(8,128)(2,1)} %v_hbm.1), channel_id=1, source_target_pairs={{0,4},{4,0},{8,12},{12,8},{1,5},{5,1},{9,13},{13,9},{2,6},{6,2},{1... | collective-permute-start | bytes 196616 | tf_op jit(solution)/shard_map/ppermute | solution.py:238
  9.6 4.3 %collective-permute-start.1 = (bf16[256,128]{1,0:T(8,128)(2,1)S(1)}, bf16[256,128]{1,0:T(8,128)(2,1)S(1)}, u32[]{:S(2)}, u32[]{:S(2)}) collective-permute-start(bf16[256,128]{1,0:T(8,128)(2,1)S(1)} %collective-permute-done.refs_3_), channel_id=1, source_target_pairs={{0,4},{4,0},{8,12},{12,8},{1,5},{5,1},{9,13},{13,9},{2,6},{6,2},{1... | collective-permute-start | bytes 196616 | tf_op jit(solution)/shard_map/ppermute | solution.py:238
  10.3 4.4 %collective-permute-start.5 = (bf16[256,128]{1,0:T(8,128)(2,1)S(1)}, bf16[256,128]{1,0:T(8,128)(2,1)S(1)}, u32[]{:S(2)}, u32[]{:S(2)}) collective-permute-start(bf16[256,128]{1,0:T(8,128)(2,1)S(1)} %collective-permute-done.4.v_ref), channel_id=1, source_target_pairs={{0,4},{4,0},{8,12},{12,8},{1,5},{5,1},{9,13},{13,9},{2,6},{6,2},{1... | collective-permute-start | bytes 196616 | tf_op jit(solution)/shard_map/ppermute | solution.py:238

commit v19 on v18

--- a/solution.py
+++ b/solution.py
@@ -71,10 +71,10 @@
 
 def in_stages(heads, stages):
     results = [{} for _ in stages]
-    for step in range(heads + len(stages) - 1):
+    for step in range(len(heads) + len(stages) - 1):
         for late, stage in enumerate(stages):
-            head = step - late
-            if 0 <= head < heads:
+            if 0 <= step - late < len(heads):
+                head = heads[step - late]
                 before = results[late - 1].pop(head) if late else None
                 results[late][head] = stage(head, before)
 
@@ -138,7 +138,7 @@
             peak_ref[head:head + 1, :] = peak
             sum_ref[head] = jnp.dot(turned, weight_ref[head], preferred_element_type=jnp.float32)
 
-        in_stages(across_ref.shape[0], [
+        in_stages(range(across_ref.shape[0]), [
             score_stage(k_ref[...], across_ref, bias_ref, 0, scaled_ref, None),
             weight_stage(scaled_ref, weight_ref),
             mix,
@@ -151,7 +151,7 @@
     return summed
 
 
-def weights_kernel(at, members, own_ref, across_ref, bias_ref, k_ref, *refs):
+def weights_kernel(at, members, heads, own_ref, across_ref, bias_ref, k_ref, *refs):
     peak_ref, sum_ref, weight_ref, scaled_ref = refs[-4:]
 
     @only_for(members, own_ref)
@@ -159,7 +159,7 @@
         def rescale(head, peak):
             sum_ref[head] = shrink(head, peak, peak_ref, sum_ref)
 
-        in_stages(across_ref.shape[0], [
+        in_stages(heads, [
             score_stage(
                 k_ref[...], across_ref, bias_ref, at, scaled_ref,
                 lambda head: peak_ref[head:head + 1, :],
@@ -186,7 +186,7 @@
             turned, weight_ref[head], preferred_element_type=jnp.float32
         )
 
-    in_stages(across_ref.shape[0], [
+    in_stages(range(across_ref.shape[0]), [
         score_stage(
             k_ref[...], across_ref, bias_ref, at, scaled_ref,
             lambda head: peak_ref[head:head + 1, :],
@@ -213,7 +213,7 @@
         copy.start()
         copies.append(copy)
 
-    in_stages(sum_ref.shape[0], [mix, send])
+    in_stages(range(sum_ref.shape[0]), [mix, send])
     for copy in copies:
         copy.wait()
 
@@ -294,17 +294,18 @@
             [scaled_type, weight_type], state, (own,),
         )
 
-    def shard_weights(at, members, keys, state):
+    def shard_weights(at, members, keys, state, first=0, end=heads):
         return call(
-            lambda *refs: weights_kernel(at, members, *refs), "shard_weights",
+            lambda *refs: weights_kernel(at, members, range(first, end), *refs), "shard_weights",
             (across, bias, keys), [peak_type, sum_type, weight_type],
             [scaled_type], state, (own,),
         )
 
     state = own_shard((0, 2, 3), ())
-    state = shard_weights(2, (0, 2), far_keys, state)
+    state = shard_weights(2, (0, 2), far_keys, state, end=heads // 2)
     far_keys, *state = lax.optimization_barrier((far_keys, *state))
     third_keys = moved(far_keys, 1)
+    state = shard_weights(2, (0, 2), far_keys, state, first=heads // 2)
     far_values, far_keys, *state = lax.optimization_barrier((far_values, far_keys, *state))
     third_values = moved(far_values, 1)
     state = [*own_shard((1,), state[:2]), state[2]]

time: 16.1 us -> 16.2 us (level)
    pallas_call x7 -> x8, Pallas kernels: 4.19 us -> 4.33 us  [call(): pl.pallas_call(kernel, in_specs=[scalar] * len(scalars) + [VMEM_REF] * (l...]
  transfers between devices with their start and end apart: 6 -> 6, of which waited for: 2 -> 2; matrix products, arithmetic and copies ran while one was open for 0% -> 0% of each run, Pallas kernels for 36% -> 37%
where the time goes in v19:
time: 16.2 us; the launch traced here: 16 us
  starting transfers between devices  7.95 us (49%)
  Pallas kernels  7.1 us (44%)
  waiting for transfers between devices  0.91 us (6%)
    ppermute x6, starting transfers between devices, moved(): lax.ppermute(value, 'seq', [(i, i ^ mask) for i in range(lax.axis_size('s...  7.95 us
    pallas_call x8, Pallas kernels, call(): pl.pallas_call(kernel, in_specs=[scalar] * len(scalars) + [VMEM_REF] * (l...  4.33 us
    pallas_call x1, Pallas kernels, staged_attention(): pl.pallas_call(prepare_kernel, in_specs=[scalar] + [HBM_REF] * 5, out_spe...  1.56 us
    pallas_call x1, Pallas kernels, staged_attention(): pl.pallas_call(last_kernel, in_specs=[VMEM_REF] * 3, out_specs=pl.BlockSp...  1.21 us
    ppermute x6, waiting for transfers between devices, moved(): lax.ppermute(value, 'seq', [(i, i ^ mask) for i in range(lax.axis_size('s...  0.91 us
  transfers between devices with their start and end apart: 6, of which 2 were waited for; matrix products, arithmetic and copies ran while one was open for 0% of the time, Pallas kernels for 37%

profile of v19, /device:TPU:0, one launch (start us, length us, event | category | flops | bytes accessed | tf_op | source)
XLA Modules:
  0.0 16.0 jit_solution(15615855287802959538)
XLA Ops:
  0.0 4.0 %collective-permute-start = (bf16[256,128]{1,0:T(8,128)(2,1)}, bf16[256,128]{1,0:T(8,128)(2,1)S(1)}, u32[]{:S(2)}, u32[]{:S(2)}) collective-permute-start(bf16[256,128]{1,0:T(8,128)(2,1)} %k_hbm.1), channel_id=1, source_target_pairs={{0,8},{4,12},{8,0},{12,4},{1,9},{5,13},{9,1},{13,5},{2,10},{6,14},... | collective-permute-start | bytes 196616 | tf_op jit(solution)/shard_map/ppermute | solution.py:238
  4.0 0.0 collective-permute-start.4
  4.1 1.9 %collective-permute-start.2 = (bf16[256,128]{1,0:T(8,128)(2,1)}, bf16[256,128]{1,0:T(8,128)(2,1)S(1)}, u32[]{:S(2)}, u32[]{:S(2)}) collective-permute-start(bf16[256,128]{1,0:T(8,128)(2,1)} %k_hbm.1), channel_id=1, source_target_pairs={{0,4},{4,0},{8,12},{12,8},{1,5},{5,1},{9,13},{13,9},{2,6},{6,2},{1... | collective-permute-start | bytes 196616 | tf_op jit(solution)/shard_map/ppermute | solution.py:238
  6.0 0.1 collective-permute-start.3
  6.1 1.6 %prepare.1 = (bf16[8,128,256]{2,1,0:T(8,128)(2,1)S(1)}, f32[4,256,256]{2,1,0:T(8,128)S(1)}, bf16[256,128]{1,0:T(8,128)(2,1)S(1)}, bf16[256,128]{1,0:T(8,128)(2,1)S(1)}) custom-call(s32[1]{0:T(128)} %bitcast.own_ref.refs_0_, s32[3]{0:T(128)} %lengths_hbm.1, s32[1,128]{1,0:T(1,128)} %bitcast.2, bf16[256,1024]{1,0:T(8,128)(2,1)} %q_hbm.1, ...), custom_call_target="tpu_custom_call" | custom-call | tf_op jit(solution)/shard_map/prepare/pallas_call | solution.py:269
  7.7 1.1 %own_shard.2 = (f32[8,256]{1,0:T(8,128)S(1)}, f32[8,144,256]{2,1,0:T(8,128)S(1)}) custom-call(s32[1]{0:T(128)} %bitcast.own_ref.refs_0_, bf16[8,128,256]{2,1,0:T(8,128)(2,1)S(1)} %get-tuple-element.35.refs_1_.refs_0_, f32[4,256,256]{2,1,0:T(8,128)S(1)} %get-tuple-element.36.refs_2_.refs_1_, bf16[256,128]{1,0:T(8,128)(2,1)S(1)} %get-tuple-element.37.refs_3_, ...), custom_call_target="tpu_custom_call" | custom-call | tf_op jit(solution)/shard_map/own_shard/pallas_call | solution.py:257
  8.8 0.0 collective-permute-done.refs_3_
  8.8 0.5 %shard_weights.4 = (f32[8,256]{1,0:T(8,128)S(1)}, f32[8,144,256]{2,1,0:T(8,128)S(1)}, bf16[8,256,256]{2,1,0:T(8,128)(2,1)S(1)}) custom-call(s32[1]{0:T(128)} %bitcast.own_ref.refs_0_, bf16[8,128,256]{2,1,0:T(8,128)(2,1)S(1)} %get-tuple-element.35.refs_1_.refs_0_, ...), custom_call_target="tpu_custom_call", output_to_operand_aliasing={{0}: (4, {}), {1}: (5, {})} | custom-call | tf_op jit(solution)/shard_map/shard_weights/pallas_call | solution.py:257
  9.3 0.7 %collective-permute-start.1 = (bf16[256,128]{1,0:T(8,128)(2,1)S(1)}, bf16[256,128]{1,0:T(8,128)(2,1)S(1)}, u32[]{:S(2)}, u32[]{:S(2)}) collective-permute-start(bf16[256,128]{1,0:T(8,128)(2,1)S(1)} %collective-permute-done.refs_3_), channel_id=1, source_target_pairs={{0,4},{4,0},{8,12},{12,8},{1,5},{5,1},{9,13},{13,9},{2,6},{6,2},{1... | collective-permute-start | bytes 196616 | tf_op jit(solution)/shard_map/ppermute | solution.py:238
  10.0 0.5 %shard_weights.5 = (f32[8,256]{1,0:T(8,128)S(1)}, f32[8,144,256]{2,1,0:T(8,128)S(1)}, bf16[8,256,256]{2,1,0:T(8,128)(2,1)S(1)}) custom-call(s32[1]{0:T(128)} %bitcast.own_ref.refs_0_, bf16[8,128,256]{2,1,0:T(8,128)(2,1)S(1)} %get-tuple-element.35.refs_1_.refs_0_, ...), custom_call_target="tpu_custom_call", output_to_operand_aliasing={{0}: (4, {}), {1}: (5, {}), {2}: (6, {})} | custom-call | tf_op jit(solution)/shard_map/shard_weights/pallas_call | solution.py:257
  10.5 0.0 collective-permute-done.4.v_ref
  10.5 1.1 %collective-permute-start.5 = (bf16[256,128]{1,0:T(8,128)(2,1)S(1)}, bf16[256,128]{1,0:T(8,128)(2,1)S(1)}, u32[]{:S(2)}, u32[]{:S(2)}) collective-permute-start(bf16[256,128]{1,0:T(8,128)(2,1)S(1)} %collective-permute-done.4.v_ref), channel_id=1, source_target_pairs={{0,4},{4,0},{8,12},{12,8},{1,5},{5,1},{9,13},{13,9},{2,6},{6,2},{1... | collective-permute-start | bytes 196616 | tf_op jit(solution)/shard_map/ppermute | solution.py:238
  11.6 0.3 %shard_values.1.refs_5_ = f32[8,144,256]{2,1,0:T(8,128)S(1)} custom-call(bf16[8,256,256]{2,1,0:T(8,128)(2,1)S(1)} %get-tuple-element.58.weight_ref, bf16[256,128]{1,0:T(8,128)(2,1)S(1)} %collective-permute-done.4.v_ref, f32[8,144,256]{2,1,0:T(8,128)S(1)} %get-tuple-element.60.old_sum_ref), custom_call_target="tpu_custom_call", output_to_operand_aliasing={{}: (2, {})} | custom-call | tf_op jit(solution)/shard_map/shard_values/pallas_call | solution.py:257
  12.0 0.0 collective-permute-done.2.refs_2_
  12.0 0.0 collective-permute-done.3.refs_3_
  12.0 1.1 %next_shard.1 = (f32[8,256]{1,0:T(8,128)S(1)}, f32[8,144,256]{2,1,0:T(8,128)S(1)}) custom-call(bf16[8,128,256]{2,1,0:T(8,128)(2,1)S(1)} %get-tuple-element.35.refs_1_.refs_0_, f32[4,256,256]{2,1,0:T(8,128)S(1)} %get-tuple-element.36.refs_2_.refs_1_, ...), custom_call_target="tpu_custom_call", output_to_operand_aliasing={{0}: (4, {}), {1}: (5, {})} | custom-call | tf_op jit(solution)/shard_map/next_shard/pallas_call | solution.py:257
  13.1 0.8 %collective-permute-done.1.refs_3_ = bf16[256,128]{1,0:T(8,128)(2,1)S(1)} collective-permute-done((bf16[256,128]{1,0:T(8,128)(2,1)S(1)}, bf16[256,128]{1,0:T(8,128)(2,1)S(1)}, u32[]{:S(2)}, u32[]{:S(2)}) %collective-permute-start.1) | collective-permute-done | bytes 65568 | tf_op jit(solution)/shard_map/ppermute | solution.py:238
  13.9 0.8 %shard_weights.7 = (f32[8,256]{1,0:T(8,128)S(1)}, f32[8,144,256]{2,1,0:T(8,128)S(1)}, bf16[8,256,256]{2,1,0:T(8,128)(2,1)S(1)}) custom-call(s32[1]{0:T(128)} %bitcast.own_ref.refs_0_, bf16[8,128,256]{2,1,0:T(8,128)(2,1)S(1)} %get-tuple-element.35.refs_1_.refs_0_, ...), custom_call_target="tpu_custom_call", output_to_operand_aliasing={{0}: (4, {}), {1}: (5, {})} | custom-call | tf_op jit(solution)/shard_map/shard_weights/pallas_call | solution.py:257
  14.7 0.1 collective-permute-done.5.v_ref
  14.8 1.2 %last_values.1 = bf16[256,1024]{1,0:T(8,128)(2,1)} custom-call(bf16[8,256,256]{2,1,0:T(8,128)(2,1)S(1)} %get-tuple-element.63.weight_ref, bf16[256,128]{1,0:T(8,128)(2,1)S(1)} %collective-permute-done.5.v_ref, f32[8,144,256]{2,1,0:T(8,128)S(1)} %get-tuple-element.64.sum_ref), custom_call_target="tpu_custom_call" | custom-call | tf_op jit(solution)/shard_map/last_values/pallas_call | solution.py:320
  (2 shorter events, 0.0 us)
Async XLA Ops:
  0.0 8.8 %collective-permute-start = (bf16[256,128]{1,0:T(8,128)(2,1)}, bf16[256,128]{1,0:T(8,128)(2,1)S(1)}, u32[]{:S(2)}, u32[]{:S(2)}) collective-permute-start(bf16[256,128]{1,0:T(8,128)(2,1)} %k_hbm.1), channel_id=1, source_target_pairs={{0,8},{4,12},{8,0},{12,4},{1,9},{5,13},{9,1},{13,5},{2,10},{6,14},... | collective-permute-start | bytes 196616 | tf_op jit(solution)/shard_map/ppermute | solution.py:238
  4.0 6.5 %collective-permute-start.4 = (bf16[256,128]{1,0:T(8,128)(2,1)}, bf16[256,128]{1,0:T(8,128)(2,1)S(1)}, u32[]{:S(2)}, u32[]{:S(2)}) collective-permute-start(bf16[256,128]{1,0:T(8,128)(2,1)} %v_hbm.1), channel_id=1, source_target_pairs={{0,8},{4,12},{8,0},{12,4},{1,9},{5,13},{9,1},{13,5},{2,10},{6,14},... | collective-permute-start | bytes 196616 | tf_op jit(solution)/shard_map/ppermute | solution.py:238
  4.1 7.9 %collective-permute-start.2 = (bf16[256,128]{1,0:T(8,128)(2,1)}, bf16[256,128]{1,0:T(8,128)(2,1)S(1)}, u32[]{:S(2)}, u32[]{:S(2)}) collective-permute-start(bf16[256,128]{1,0:T(8,128)(2,1)} %k_hbm.1), channel_id=1, source_target_pairs={{0,4},{4,0},{8,12},{12,8},{1,5},{5,1},{9,13},{13,9},{2,6},{6,2},{1... | collective-permute-start | bytes 196616 | tf_op jit(solution)/shard_map/ppermute | solution.py:238
  6.0 6.1 %collective-permute-start.3 = (bf16[256,128]{1,0:T(8,128)(2,1)}, bf16[256,128]{1,0:T(8,128)(2,1)S(1)}, u32[]{:S(2)}, u32[]{:S(2)}) collective-permute-start(bf16[256,128]{1,0:T(8,128)(2,1)} %v_hbm.1), channel_id=1, source_target_pairs={{0,4},{4,0},{8,12},{12,8},{1,5},{5,1},{9,13},{13,9},{2,6},{6,2},{1... | collective-permute-start | bytes 196616 | tf_op jit(solution)/shard_map/ppermute | solution.py:238
  9.3 4.6 %collective-permute-start.1 = (bf16[256,128]{1,0:T(8,128)(2,1)S(1)}, bf16[256,128]{1,0:T(8,128)(2,1)S(1)}, u32[]{:S(2)}, u32[]{:S(2)}) collective-permute-start(bf16[256,128]{1,0:T(8,128)(2,1)S(1)} %collective-permute-done.refs_3_), channel_id=1, source_target_pairs={{0,4},{4,0},{8,12},{12,8},{1,5},{5,1},{9,13},{13,9},{2,6},{6,2},{1... | collective-permute-start | bytes 196616 | tf_op jit(solution)/shard_map/ppermute | solution.py:238
  10.5 4.3 %collective-permute-start.5 = (bf16[256,128]{1,0:T(8,128)(2,1)S(1)}, bf16[256,128]{1,0:T(8,128)(2,1)S(1)}, u32[]{:S(2)}, u32[]{:S(2)}) collective-permute-start(bf16[256,128]{1,0:T(8,128)(2,1)S(1)} %collective-permute-done.4.v_ref), channel_id=1, source_target_pairs={{0,4},{4,0},{8,12},{12,8},{1,5},{5,1},{9,13},{13,9},{2,6},{6,2},{1... | collective-permute-start | bytes 196616 | tf_op jit(solution)/shard_map/ppermute | solution.py:238

commit v20 on v13

--- a/solution.py
+++ b/solution.py
@@ -267,13 +267,13 @@
             name="next_shard",
         )(*in_vmem(across, bias, *carried), keys, values)
 
+    far_keys = jnp.where(~inner, second_keys, first_keys)
+    far_keys, *carried = lax.optimization_barrier((far_keys, *carried))
+    third_keys = lax.ppermute(far_keys, "seq", SWAP)
+    second_values, first_values, far_keys, *carried = lax.optimization_barrier((second_values, first_values, far_keys, *carried))
+    far_values = jnp.where(~inner, second_values, first_values)
+    third_values = lax.ppermute(far_values, "seq", SWAP)
     carried = add_shard(1, first_keys, first_values, carried)
-    second_keys, *carried = lax.optimization_barrier((second_keys, *carried))
-    far_keys = jnp.where(inner, first_keys, second_keys)
-    third_keys = lax.ppermute(far_keys, "seq", SWAP)
-    second_values, second_keys, far_keys, *carried = lax.optimization_barrier((second_values, second_keys, far_keys, *carried))
-    far_values = jnp.where(inner, first_values, second_values)
-    third_values = lax.ppermute(far_values, "seq", SWAP)
     carried = add_shard(2, second_keys, second_values, carried)
     summed, weights = pl.pallas_call(
         lambda *refs: weights_kernel(3, *refs),

time: 17.9 us -> 18.2 us (1.017)
  waiting for transfers between devices: 2.74 us -> 3.04 us
    ppermute x1, starting transfers between devices: 1.45 us -> 0.07 us  [staged_attention(): third_values = lax.ppermute(far_values, 'seq', SWAP)]
    ppermute x2, starting transfers between devices: 5.61 us -> 6.96 us  [staged_attention(): lax.ppermute(part, 'seq', CYCLE)]
    ppermute x1, waiting for transfers between devices: 0.01 us -> 1.09 us  [staged_attention(): third_values = lax.ppermute(far_values, 'seq', SWAP)]
    ppermute x1, waiting for transfers between devices: 1.03 us -> 0.1 us  [staged_attention(): third_keys = lax.ppermute(far_keys, 'seq', SWAP)]
    ppermute x2, starting transfers between devices: 0.48 us -> 0.01 us  [staged_attention(): lax.ppermute(part, 'seq', BACK)]
    ppermute x1, starting transfers between devices: 0.71 us -> 1.17 us  [staged_attention(): third_keys = lax.ppermute(far_keys, 'seq', SWAP)]
  transfers between devices with their start and end apart: 6 -> 6, of which waited for: 2 -> 4; matrix products, arithmetic and copies ran while one was open for 0% -> 0% of each run, Pallas kernels for 31% -> 30%
where the time goes in v20:
time: 18.2 us; the launch traced here: 18 us
  starting transfers between devices  8.2 us (45%)
  Pallas kernels  6.72 us (37%)
  waiting for transfers between devices  3.04 us (17%)
    ppermute x2, starting transfers between devices, staged_attention(): lax.ppermute(part, 'seq', CYCLE)  6.96 us
    pallas_call x1, Pallas kernels, staged_attention(): pl.pallas_call(own_kernel, in_specs=[pl.BlockSpec(memory_space=pltpu.SMEM...  2.43 us
    pallas_call x2, Pallas kernels, add_shard(): pl.pallas_call(lambda *refs: next_kernel(at, *refs), in_specs=[VMEM_REF]...  2.25 us
    ppermute x2, waiting for transfers between devices, staged_attention(): lax.ppermute(part, 'seq', BACK)  1.84 us
    pallas_call x1, Pallas kernels, staged_attention(): pl.pallas_call(last_kernel, in_specs=[VMEM_REF] * 3, out_specs=pl.BlockSp...  1.25 us
    ppermute x1, starting transfers between devices, staged_attention(): third_keys = lax.ppermute(far_keys, 'seq', SWAP)  1.17 us
    ppermute x1, waiting for transfers between devices, staged_attention(): third_values = lax.ppermute(far_values, 'seq', SWAP)  1.09 us
    pallas_call x1, Pallas kernels, staged_attention(): pl.pallas_call(lambda *refs: weights_kernel(3, *refs), in_specs=[VMEM_REF...  0.79 us
  transfers between devices with their start and end apart: 6, of which 4 were waited for; matrix products, arithmetic and copies ran while one was open for 0% of the time, Pallas kernels for 30%

profile of v20, /device:TPU:0, one launch (start us, length us, event | category | flops | bytes accessed | tf_op | source)
XLA Modules:
  0.0 18.0 jit_solution(3429964400819156498)
XLA Ops:
  0.0 4.0 %collective-permute-start.3 = (bf16[256,128]{1,0:T(8,128)(2,1)}, bf16[256,128]{1,0:T(8,128)(2,1)S(1)}, u32[]{:S(2)}, u32[]{:S(2)}) collective-permute-start(bf16[256,128]{1,0:T(8,128)(2,1)} %k_hbm.1), channel_id=1, source_target_pairs={{0,8},{8,12},{12,4},{4,0},{1,9},{9,13},{13,5},{5,1},{2,10},{10,14}... | collective-permute-start | bytes 196616 | tf_op jit(solution)/shard_map/ppermute | solution.py:221
  4.0 0.0 collective-permute-start.2
  4.0 2.9 %collective-permute-start.1 = (bf16[256,128]{1,0:T(8,128)(2,1)}, bf16[256,128]{1,0:T(8,128)(2,1)S(1)}, u32[]{:S(2)}, u32[]{:S(2)}) collective-permute-start(bf16[256,128]{1,0:T(8,128)(2,1)} %v_hbm.1), channel_id=1, source_target_pairs={{0,8},{8,12},{12,4},{4,0},{1,9},{9,13},{13,5},{5,1},{2,10},{10,14}... | collective-permute-start | bytes 196616 | tf_op jit(solution)/shard_map/ppermute | solution.py:221
  7.0 0.0 collective-permute-start
  7.0 2.4 %own_shard.1 = (bf16[8,128,256]{2,1,0:T(8,128)(2,1)S(1)}, f32[4,256,256]{2,1,0:T(8,128)S(1)}, f32[8,256]{1,0:T(8,128)S(1)}, f32[8,144,256]{2,1,0:T(8,128)S(1)}) custom-call(s32[1]{0:T(128)} %bitcast.own_ref, s32[1]{0:T(128)} %bitcast.1.first_ref, s32[3]{0:T(128)} %lengths_hbm.1, s32[1,128]{1,0:T(1,128)} %bitcast.3, bf16[256,1024]{1,0:T(8,128)(2,1)} %q_hbm.1, ...), custom_call_target="tpu_custom_call" | custom-call | tf_op jit(solution)/shard_map/own_shard/pallas_call | solution.py:238
  9.4 0.0 collective-permute-done.3.refs_4_
  9.4 0.8 %collective-permute-done.2.refs_4_ = bf16[256,128]{1,0:T(8,128)(2,1)S(1)} collective-permute-done((bf16[256,128]{1,0:T(8,128)(2,1)}, bf16[256,128]{1,0:T(8,128)(2,1)S(1)}, u32[]{:S(2)}, u32[]{:S(2)}) %collective-permute-start.2) | collective-permute-done | bytes 65568 | tf_op jit(solution)/shard_map/ppermute | solution.py:222
  10.2 1.2 %collective-permute-start.4 = (bf16[256,128]{1,0:T(8,128)(2,1)S(1)}, bf16[256,128]{1,0:T(8,128)(2,1)S(1)}, u32[]{:S(2)}, u32[]{:S(2)}) collective-permute-start(bf16[256,128]{1,0:T(8,128)(2,1)S(1)} %broadcast_select_fusion.1), channel_id=1, source_target_pairs={{0,4},{4,0},{8,12},{12,8},{1,5},{5,1},{9,13},{13,9},{2,6},{6,2},{1... | collective-permute-start | bytes 196616 | tf_op jit(solution)/shard_map/ppermute | solution.py:272
  11.4 0.0 collective-permute-done.1.refs_5_
  11.4 1.0 %collective-permute-done.refs_5_ = bf16[256,128]{1,0:T(8,128)(2,1)S(1)} collective-permute-done((bf16[256,128]{1,0:T(8,128)(2,1)}, bf16[256,128]{1,0:T(8,128)(2,1)S(1)}, u32[]{:S(2)}, u32[]{:S(2)}) %collective-permute-start) | collective-permute-done | bytes 65568 | tf_op jit(solution)/shard_map/ppermute | solution.py:222
  12.5 0.1 collective-permute-start.5
  12.5 1.1 %next_shard.2 = (f32[8,256]{1,0:T(8,128)S(1)}, f32[8,144,256]{2,1,0:T(8,128)S(1)}) custom-call(bf16[8,128,256]{2,1,0:T(8,128)(2,1)S(1)} %get-tuple-element.22.refs_0_, f32[4,256,256]{2,1,0:T(8,128)S(1)} %get-tuple-element.23.refs_1_, f32[8,256]{1,0:T(8,128)S(1)} %get-tuple-element.29.refs_2_, f32[8,144,256]{2,1,0:T(8,128)S(1)} %get-tuple-element.30.refs_3_, ...), custom_call_target="tpu_custom_call" | custom-call | tf_op jit(solution)/shard_map/next_shard/pallas_call | solution.py:259
  13.7 1.1 %next_shard.3 = (f32[8,256]{1,0:T(8,128)S(1)}, f32[8,144,256]{2,1,0:T(8,128)S(1)}) custom-call(bf16[8,128,256]{2,1,0:T(8,128)(2,1)S(1)} %get-tuple-element.22.refs_0_, f32[4,256,256]{2,1,0:T(8,128)S(1)} %get-tuple-element.23.refs_1_, f32[8,256]{1,0:T(8,128)S(1)} %get-tuple-element.32.refs_2_, f32[8,144,256]{2,1,0:T(8,128)S(1)} %get-tuple-element.33.refs_3_, ...), custom_call_target="tpu_custom_call" | custom-call | tf_op jit(solution)/shard_map/next_shard/pallas_call | solution.py:259
  14.8 0.1 collective-permute-done.4.refs_4_
  14.9 0.8 %last_weights.1 = (f32[8,144,256]{2,1,0:T(8,128)S(1)}, bf16[8,256,256]{2,1,0:T(8,128)(2,1)S(1)}) custom-call(bf16[8,128,256]{2,1,0:T(8,128)(2,1)S(1)} %get-tuple-element.22.refs_0_, f32[4,256,256]{2,1,0:T(8,128)S(1)} %get-tuple-element.23.refs_1_, f32[8,256]{1,0:T(8,128)S(1)} %get-tuple-element.35.refs_2_, f32[8,144,256]{2,1,0:T(8,128)S(1)} %get-tuple-element.36.refs_3_, ...), custom_call_target="tpu_custom_call" | custom-call | tf_op jit(solution)/shard_map/last_weights/pallas_call | solution.py:278
  15.7 1.1 %collective-permute-done.5.v_ref = bf16[256,128]{1,0:T(8,128)(2,1)S(1)} collective-permute-done((bf16[256,128]{1,0:T(8,128)(2,1)S(1)}, bf16[256,128]{1,0:T(8,128)(2,1)S(1)}, u32[]{:S(2)}, u32[]{:S(2)}) %collective-permute-start.5) | collective-permute-done | bytes 65568 | tf_op jit(solution)/shard_map/ppermute | solution.py:275
  16.8 1.3 %last_values.1 = bf16[256,1024]{1,0:T(8,128)(2,1)} custom-call(f32[8,144,256]{2,1,0:T(8,128)S(1)} %get-tuple-element.37.sum_ref, bf16[8,256,256]{2,1,0:T(8,128)(2,1)S(1)} %get-tuple-element.38.weight_ref, bf16[256,128]{1,0:T(8,128)(2,1)S(1)} %collective-permute-done.5.v_ref), custom_call_target="tpu_custom_call" | custom-call | tf_op jit(solution)/shard_map/last_values/pallas_call | solution.py:288
  (2 shorter events, 0.0 us)
Async XLA Ops:
  0.0 9.4 %collective-permute-start.3 = (bf16[256,128]{1,0:T(8,128)(2,1)}, bf16[256,128]{1,0:T(8,128)(2,1)S(1)}, u32[]{:S(2)}, u32[]{:S(2)}) collective-permute-start(bf16[256,128]{1,0:T(8,128)(2,1)} %k_hbm.1), channel_id=1, source_target_pairs={{0,8},{8,12},{12,4},{4,0},{1,9},{9,13},{13,5},{5,1},{2,10},{10,14}... | collective-permute-start | bytes 196616 | tf_op jit(solution)/shard_map/ppermute | solution.py:221
  4.0 6.2 %collective-permute-start.2 = (bf16[256,128]{1,0:T(8,128)(2,1)}, bf16[256,128]{1,0:T(8,128)(2,1)S(1)}, u32[]{:S(2)}, u32[]{:S(2)}) collective-permute-start(bf16[256,128]{1,0:T(8,128)(2,1)} %k_hbm.1), channel_id=1, source_target_pairs={{8,0},{12,8},{4,12},{0,4},{9,1},{13,9},{5,13},{1,5},{10,2},{14,10}... | collective-permute-start | bytes 196616 | tf_op jit(solution)/shard_map/ppermute | solution.py:222
  4.0 7.4 %collective-permute-start.1 = (bf16[256,128]{1,0:T(8,128)(2,1)}, bf16[256,128]{1,0:T(8,128)(2,1)S(1)}, u32[]{:S(2)}, u32[]{:S(2)}) collective-permute-start(bf16[256,128]{1,0:T(8,128)(2,1)} %v_hbm.1), channel_id=1, source_target_pairs={{0,8},{8,12},{12,4},{4,0},{1,9},{9,13},{13,5},{5,1},{2,10},{10,14}... | collective-permute-start | bytes 196616 | tf_op jit(solution)/shard_map/ppermute | solution.py:221
  7.0 5.5 %collective-permute-start = (bf16[256,128]{1,0:T(8,128)(2,1)}, bf16[256,128]{1,0:T(8,128)(2,1)S(1)}, u32[]{:S(2)}, u32[]{:S(2)}) collective-permute-start(bf16[256,128]{1,0:T(8,128)(2,1)} %v_hbm.1), channel_id=1, source_target_pairs={{8,0},{12,8},{4,12},{0,4},{9,1},{13,9},{5,13},{1,5},{10,2},{14,10}... | collective-permute-start | bytes 196616 | tf_op jit(solution)/shard_map/ppermute | solution.py:222
  10.2 4.7 %collective-permute-start.4 = (bf16[256,128]{1,0:T(8,128)(2,1)S(1)}, bf16[256,128]{1,0:T(8,128)(2,1)S(1)}, u32[]{:S(2)}, u32[]{:S(2)}) collective-permute-start(bf16[256,128]{1,0:T(8,128)(2,1)S(1)} %broadcast_select_fusion.1), channel_id=1, source_target_pairs={{0,4},{4,0},{8,12},{12,8},{1,5},{5,1},{9,13},{13,9},{2,6},{6,2},{1... | collective-permute-start | bytes 196616 | tf_op jit(solution)/shard_map/ppermute | solution.py:272
  12.5 4.3 %collective-permute-start.5 = (bf16[256,128]{1,0:T(8,128)(2,1)S(1)}, bf16[256,128]{1,0:T(8,128)(2,1)S(1)}, u32[]{:S(2)}, u32[]{:S(2)}) collective-permute-start(bf16[256,128]{1,0:T(8,128)(2,1)S(1)} %broadcast_select_fusion), channel_id=1, source_target_pairs={{0,4},{4,0},{8,12},{12,8},{1,5},{5,1},{9,13},{13,9},{2,6},{6,2},{1... | collective-permute-start | bytes 196616 | tf_op jit(solution)/shard_map/ppermute | solution.py:275

commit v21 on v19

--- a/solution.py
+++ b/solution.py
@@ -302,13 +302,13 @@
         )
 
     state = own_shard((0, 2, 3), ())
-    state = shard_weights(2, (0, 2), far_keys, state, end=heads // 2)
     far_keys, *state = lax.optimization_barrier((far_keys, *state))
     third_keys = moved(far_keys, 1)
-    state = shard_weights(2, (0, 2), far_keys, state, first=heads // 2)
+    state = shard_weights(2, (0, 2), far_keys, state, end=heads // 2)
     far_values, far_keys, *state = lax.optimization_barrier((far_values, far_keys, *state))
     third_values = moved(far_values, 1)
     state = [*own_shard((1,), state[:2]), state[2]]
+    state = shard_weights(2, (0, 2), far_keys, state, first=heads // 2)
     peak, summed, weights = shard_weights(2, (1, 3), far_keys, state)
     summed, = call(values_kernel, "shard_values", (weights, far_values), [sum_type], [], (summed,))
     state = call(

time: 16.2 us -> 16.2 us (level)
  waiting for transfers between devices: 0.91 us -> 0.42 us
  starting transfers between devices: 7.95 us -> 8.42 us
    ppermute x6, waiting for transfers between devices: 0.91 us -> 0.42 us  [moved(): lax.ppermute(value, 'seq', [(i, i ^ mask) for i in range(lax.axis_size('s...]
    ppermute x6, starting transfers between devices: 7.95 us -> 8.42 us  [moved(): lax.ppermute(value, 'seq', [(i, i ^ mask) for i in range(lax.axis_size('s...]
where the time goes in v21:
time: 16.2 us; the launch traced here: 16 us
  starting transfers between devices  8.42 us (52%)
  Pallas kernels  7.11 us (44%)
  waiting for transfers between devices  0.42 us (3%)
    ppermute x6, starting transfers between devices, moved(): lax.ppermute(value, 'seq', [(i, i ^ mask) for i in range(lax.axis_size('s...  8.42 us
    pallas_call x8, Pallas kernels, call(): pl.pallas_call(kernel, in_specs=[scalar] * len(scalars) + [VMEM_REF] * (l...  4.34 us
    pallas_call x1, Pallas kernels, staged_attention(): pl.pallas_call(prepare_kernel, in_specs=[scalar] + [HBM_REF] * 5, out_spe...  1.56 us
    pallas_call x1, Pallas kernels, staged_attention(): pl.pallas_call(last_kernel, in_specs=[VMEM_REF] * 3, out_specs=pl.BlockSp...  1.21 us
    ppermute x6, waiting for transfers between devices, moved(): lax.ppermute(value, 'seq', [(i, i ^ mask) for i in range(lax.axis_size('s...  0.42 us
  transfers between devices with their start and end apart: 6, of which 2 were waited for; matrix products, arithmetic and copies ran while one was open for 0% of the time, Pallas kernels for 37%

profile of v21, /device:TPU:0, one launch (start us, length us, event | category | flops | bytes accessed | tf_op | source)
XLA Modules:
  0.0 16.0 jit_solution(3948046503123326726)
XLA Ops:
  0.0 4.0 %collective-permute-start = (bf16[256,128]{1,0:T(8,128)(2,1)}, bf16[256,128]{1,0:T(8,128)(2,1)S(1)}, u32[]{:S(2)}, u32[]{:S(2)}) collective-permute-start(bf16[256,128]{1,0:T(8,128)(2,1)} %k_hbm.1), channel_id=1, source_target_pairs={{0,8},{4,12},{8,0},{12,4},{1,9},{5,13},{9,1},{13,5},{2,10},{6,14},... | collective-permute-start | bytes 196616 | tf_op jit(solution)/shard_map/ppermute | solution.py:238
  4.0 0.0 collective-permute-start.4
  4.1 1.9 %collective-permute-start.2 = (bf16[256,128]{1,0:T(8,128)(2,1)}, bf16[256,128]{1,0:T(8,128)(2,1)S(1)}, u32[]{:S(2)}, u32[]{:S(2)}) collective-permute-start(bf16[256,128]{1,0:T(8,128)(2,1)} %k_hbm.1), channel_id=1, source_target_pairs={{0,4},{4,0},{8,12},{12,8},{1,5},{5,1},{9,13},{13,9},{2,6},{6,2},{1... | collective-permute-start | bytes 196616 | tf_op jit(solution)/shard_map/ppermute | solution.py:238
  6.0 0.1 collective-permute-start.3
  6.1 1.6 %prepare.1 = (bf16[8,128,256]{2,1,0:T(8,128)(2,1)S(1)}, f32[4,256,256]{2,1,0:T(8,128)S(1)}, bf16[256,128]{1,0:T(8,128)(2,1)S(1)}, bf16[256,128]{1,0:T(8,128)(2,1)S(1)}) custom-call(s32[1]{0:T(128)} %bitcast.own_ref.refs_0_, s32[3]{0:T(128)} %lengths_hbm.1, s32[1,128]{1,0:T(1,128)} %bitcast.2, bf16[256,1024]{1,0:T(8,128)(2,1)} %q_hbm.1, ...), custom_call_target="tpu_custom_call" | custom-call | tf_op jit(solution)/shard_map/prepare/pallas_call | solution.py:269
  7.7 1.1 %own_shard.2 = (f32[8,256]{1,0:T(8,128)S(1)}, f32[8,144,256]{2,1,0:T(8,128)S(1)}) custom-call(s32[1]{0:T(128)} %bitcast.own_ref.refs_0_, bf16[8,128,256]{2,1,0:T(8,128)(2,1)S(1)} %get-tuple-element.34.refs_1_.refs_0_, f32[4,256,256]{2,1,0:T(8,128)S(1)} %get-tuple-element.35.refs_2_.refs_1_, bf16[256,128]{1,0:T(8,128)(2,1)S(1)} %get-tuple-element.36.refs_3_, ...), custom_call_target="tpu_custom_call" | custom-call | tf_op jit(solution)/shard_map/own_shard/pallas_call | solution.py:257
  8.8 0.0 collective-permute-done.refs_3_
  8.8 1.2 %collective-permute-start.1 = (bf16[256,128]{1,0:T(8,128)(2,1)S(1)}, bf16[256,128]{1,0:T(8,128)(2,1)S(1)}, u32[]{:S(2)}, u32[]{:S(2)}) collective-permute-start(bf16[256,128]{1,0:T(8,128)(2,1)S(1)} %collective-permute-done.refs_3_), channel_id=1, source_target_pairs={{0,4},{4,0},{8,12},{12,8},{1,5},{5,1},{9,13},{13,9},{2,6},{6,2},{1... | collective-permute-start | bytes 196616 | tf_op jit(solution)/shard_map/ppermute | solution.py:238
  10.0 0.5 %shard_weights.4 = (f32[8,256]{1,0:T(8,128)S(1)}, f32[8,144,256]{2,1,0:T(8,128)S(1)}, bf16[8,256,256]{2,1,0:T(8,128)(2,1)S(1)}) custom-call(s32[1]{0:T(128)} %bitcast.own_ref.refs_0_, bf16[8,128,256]{2,1,0:T(8,128)(2,1)S(1)} %get-tuple-element.34.refs_1_.refs_0_, ...), custom_call_target="tpu_custom_call", output_to_operand_aliasing={{0}: (4, {}), {1}: (5, {})} | custom-call | tf_op jit(solution)/shard_map/shard_weights/pallas_call | solution.py:257
  10.5 0.0 collective-permute-done.4.v_ref
  10.5 1.1 %collective-permute-start.5 = (bf16[256,128]{1,0:T(8,128)(2,1)S(1)}, bf16[256,128]{1,0:T(8,128)(2,1)S(1)}, u32[]{:S(2)}, u32[]{:S(2)}) collective-permute-start(bf16[256,128]{1,0:T(8,128)(2,1)S(1)} %collective-permute-done.4.v_ref), channel_id=1, source_target_pairs={{0,4},{4,0},{8,12},{12,8},{1,5},{5,1},{9,13},{13,9},{2,6},{6,2},{1... | collective-permute-start | bytes 196616 | tf_op jit(solution)/shard_map/ppermute | solution.py:238
  11.6 0.5 %shard_weights.5 = (f32[8,256]{1,0:T(8,128)S(1)}, f32[8,144,256]{2,1,0:T(8,128)S(1)}, bf16[8,256,256]{2,1,0:T(8,128)(2,1)S(1)}) custom-call(s32[1]{0:T(128)} %bitcast.own_ref.refs_0_, bf16[8,128,256]{2,1,0:T(8,128)(2,1)S(1)} %get-tuple-element.34.refs_1_.refs_0_, ...), custom_call_target="tpu_custom_call", output_to_operand_aliasing={{0}: (4, {}), {1}: (5, {}), {2}: (6, {})} | custom-call | tf_op jit(solution)/shard_map/shard_weights/pallas_call | solution.py:257
  12.1 0.3 %shard_values.1.refs_5_ = f32[8,144,256]{2,1,0:T(8,128)S(1)} custom-call(bf16[8,256,256]{2,1,0:T(8,128)(2,1)S(1)} %get-tuple-element.56.weight_ref, bf16[256,128]{1,0:T(8,128)(2,1)S(1)} %collective-permute-done.4.v_ref, f32[8,144,256]{2,1,0:T(8,128)S(1)} %get-tuple-element.58.old_sum_ref), custom_call_target="tpu_custom_call", output_to_operand_aliasing={{}: (2, {})} | custom-call | tf_op jit(solution)/shard_map/shard_values/pallas_call | solution.py:257
  12.5 0.0 collective-permute-done.2.refs_2_
  12.5 0.0 collective-permute-done.3.refs_3_
  12.5 1.1 %next_shard.1 = (f32[8,256]{1,0:T(8,128)S(1)}, f32[8,144,256]{2,1,0:T(8,128)S(1)}) custom-call(bf16[8,128,256]{2,1,0:T(8,128)(2,1)S(1)} %get-tuple-element.34.refs_1_.refs_0_, f32[4,256,256]{2,1,0:T(8,128)S(1)} %get-tuple-element.35.refs_2_.refs_1_, ...), custom_call_target="tpu_custom_call", output_to_operand_aliasing={{0}: (4, {}), {1}: (5, {})} | custom-call | tf_op jit(solution)/shard_map/next_shard/pallas_call | solution.py:257
  13.6 0.2 %collective-permute-done.1.refs_3_ = bf16[256,128]{1,0:T(8,128)(2,1)S(1)} collective-permute-done((bf16[256,128]{1,0:T(8,128)(2,1)S(1)}, bf16[256,128]{1,0:T(8,128)(2,1)S(1)}, u32[]{:S(2)}, u32[]{:S(2)}) %collective-permute-start.1) | collective-permute-done | bytes 65568 | tf_op jit(solution)/shard_map/ppermute | solution.py:238
  13.8 0.8 %shard_weights.7 = (f32[8,256]{1,0:T(8,128)S(1)}, f32[8,144,256]{2,1,0:T(8,128)S(1)}, bf16[8,256,256]{2,1,0:T(8,128)(2,1)S(1)}) custom-call(s32[1]{0:T(128)} %bitcast.own_ref.refs_0_, bf16[8,128,256]{2,1,0:T(8,128)(2,1)S(1)} %get-tuple-element.34.refs_1_.refs_0_, ...), custom_call_target="tpu_custom_call", output_to_operand_aliasing={{0}: (4, {}), {1}: (5, {})} | custom-call | tf_op jit(solution)/shard_map/shard_weights/pallas_call | solution.py:257
  14.6 0.2 %collective-permute-done.5.v_ref = bf16[256,128]{1,0:T(8,128)(2,1)S(1)} collective-permute-done((bf16[256,128]{1,0:T(8,128)(2,1)S(1)}, bf16[256,128]{1,0:T(8,128)(2,1)S(1)}, u32[]{:S(2)}, u32[]{:S(2)}) %collective-permute-start.5) | collective-permute-done | bytes 65568 | tf_op jit(solution)/shard_map/ppermute | solution.py:238
  14.8 1.2 %last_values.1 = bf16[256,1024]{1,0:T(8,128)(2,1)} custom-call(bf16[8,256,256]{2,1,0:T(8,128)(2,1)S(1)} %get-tuple-element.61.weight_ref, bf16[256,128]{1,0:T(8,128)(2,1)S(1)} %collective-permute-done.5.v_ref, f32[8,144,256]{2,1,0:T(8,128)S(1)} %get-tuple-element.62.sum_ref), custom_call_target="tpu_custom_call" | custom-call | tf_op jit(solution)/shard_map/last_values/pallas_call | solution.py:320
  (2 shorter events, 0.0 us)
Async XLA Ops:
  0.0 8.8 %collective-permute-start = (bf16[256,128]{1,0:T(8,128)(2,1)}, bf16[256,128]{1,0:T(8,128)(2,1)S(1)}, u32[]{:S(2)}, u32[]{:S(2)}) collective-permute-start(bf16[256,128]{1,0:T(8,128)(2,1)} %k_hbm.1), channel_id=1, source_target_pairs={{0,8},{4,12},{8,0},{12,4},{1,9},{5,13},{9,1},{13,5},{2,10},{6,14},... | collective-permute-start | bytes 196616 | tf_op jit(solution)/shard_map/ppermute | solution.py:238
  4.0 6.5 %collective-permute-start.4 = (bf16[256,128]{1,0:T(8,128)(2,1)}, bf16[256,128]{1,0:T(8,128)(2,1)S(1)}, u32[]{:S(2)}, u32[]{:S(2)}) collective-permute-start(bf16[256,128]{1,0:T(8,128)(2,1)} %v_hbm.1), channel_id=1, source_target_pairs={{0,8},{4,12},{8,0},{12,4},{1,9},{5,13},{9,1},{13,5},{2,10},{6,14},... | collective-permute-start | bytes 196616 | tf_op jit(solution)/shard_map/ppermute | solution.py:238
  4.1 8.4 %collective-permute-start.2 = (bf16[256,128]{1,0:T(8,128)(2,1)}, bf16[256,128]{1,0:T(8,128)(2,1)S(1)}, u32[]{:S(2)}, u32[]{:S(2)}) collective-permute-start(bf16[256,128]{1,0:T(8,128)(2,1)} %k_hbm.1), channel_id=1, source_target_pairs={{0,4},{4,0},{8,12},{12,8},{1,5},{5,1},{9,13},{13,9},{2,6},{6,2},{1... | collective-permute-start | bytes 196616 | tf_op jit(solution)/shard_map/ppermute | solution.py:238
  6.0 6.5 %collective-permute-start.3 = (bf16[256,128]{1,0:T(8,128)(2,1)}, bf16[256,128]{1,0:T(8,128)(2,1)S(1)}, u32[]{:S(2)}, u32[]{:S(2)}) collective-permute-start(bf16[256,128]{1,0:T(8,128)(2,1)} %v_hbm.1), channel_id=1, source_target_pairs={{0,4},{4,0},{8,12},{12,8},{1,5},{5,1},{9,13},{13,9},{2,6},{6,2},{1... | collective-permute-start | bytes 196616 | tf_op jit(solution)/shard_map/ppermute | solution.py:238
  8.8 5.0 %collective-permute-start.1 = (bf16[256,128]{1,0:T(8,128)(2,1)S(1)}, bf16[256,128]{1,0:T(8,128)(2,1)S(1)}, u32[]{:S(2)}, u32[]{:S(2)}) collective-permute-start(bf16[256,128]{1,0:T(8,128)(2,1)S(1)} %collective-permute-done.refs_3_), channel_id=1, source_target_pairs={{0,4},{4,0},{8,12},{12,8},{1,5},{5,1},{9,13},{13,9},{2,6},{6,2},{1... | collective-permute-start | bytes 196616 | tf_op jit(solution)/shard_map/ppermute | solution.py:238
  10.5 4.3 %collective-permute-start.5 = (bf16[256,128]{1,0:T(8,128)(2,1)S(1)}, bf16[256,128]{1,0:T(8,128)(2,1)S(1)}, u32[]{:S(2)}, u32[]{:S(2)}) collective-permute-start(bf16[256,128]{1,0:T(8,128)(2,1)S(1)} %collective-permute-done.4.v_ref), channel_id=1, source_target_pairs={{0,4},{4,0},{8,12},{12,8},{1,5},{5,1},{9,13},{13,9},{2,6},{6,2},{1... | collective-permute-start | bytes 196616 | tf_op jit(solution)/shard_map/ppermute | solution.py:238

commit v22 on v21

--- a/solution.py
+++ b/solution.py
@@ -98,33 +98,35 @@
     return stage
 
 
-def prepare_kernel(
-    own_ref, lengths_hbm, places_hbm, q_hbm, k_hbm, v_hbm,
-    across_ref, bias_ref, k_ref, v_ref, lengths_ref, places_ref, q_ref, sems,
-):
-    moves = (
-        (lengths_hbm, lengths_ref), (places_hbm, places_ref),
-        (q_hbm, q_ref), (k_hbm, k_ref), (v_hbm, v_ref),
-    )
-    copies = [pltpu.make_async_copy(*move, sems.at[n]) for n, move in enumerate(moves)]
-    for copy in copies:
-        copy.start()
-    for copy in copies:
-        copy.wait()
-    heads, _, rows = across_ref.shape
-    own, places = own_ref[0], places_ref[...]
-    query_pos, starts = query_places(own, lengths_ref, places, rows)
-    for mask in range(bias_ref.shape[0]):
-        bias_ref[mask] = mask_table(own ^ mask, query_pos, starts, places)
-    for head in range(heads):
-        across_ref[head] = jnp.transpose(q_ref[:, head * HEAD_WIDTH:(head + 1) * HEAD_WIDTH])
-
-
 def only_for(members, own_ref):
     found = own_ref[0] == members[0]
     for member in members[1:]:
         found = found | (own_ref[0] == member)
     return pl.when(found)
+
+
+def prepare_kernel(members, own_ref, *refs):
+    lengths_hbm, places_hbm, q_hbm, k_hbm, v_hbm = refs[:5]
+    across_ref, bias_ref, k_ref, v_ref, lengths_ref, places_ref, q_ref, sems = refs[-8:]
+
+    @only_for(members, own_ref)
+    def _():
+        moves = (
+            (lengths_hbm, lengths_ref), (places_hbm, places_ref),
+            (q_hbm, q_ref), (k_hbm, k_ref), (v_hbm, v_ref),
+        )
+        copies = [pltpu.make_async_copy(*move, sems.at[n]) for n, move in enumerate(moves)]
+        for copy in copies:
+            copy.start()
+        for copy in copies:
+            copy.wait()
+        heads, _, rows = across_ref.shape
+        own, places = own_ref[0], places_ref[...]
+        query_pos, starts = query_places(own, lengths_ref, places, rows)
+        for mask in range(bias_ref.shape[0]):
+            bias_ref[mask] = mask_table(own ^ mask, query_pos, starts, places)
+        for head in range(heads):
+            across_ref[head] = jnp.transpose(q_ref[:, head * HEAD_WIDTH:(head + 1) * HEAD_WIDTH])
 
 
 def own_kernel(members, own_ref, across_ref, bias_ref, k_ref, v_ref, *refs):
@@ -240,7 +242,6 @@
 
 def staged_attention(queries, keys, values, lengths, old_place):
     far_keys, far_values = moved(keys, 2), moved(values, 2)
-    near_keys, near_values = moved(keys, 1), moved(values, 1)
     rows, cols = queries.shape
     heads = cols // HEAD_WIDTH
     devices = lax.axis_size("seq")
@@ -266,26 +267,33 @@
             name=name,
         )(*scalars, *in_vmem(*ins, *state))
 
-    across, bias, own_keys, own_values = pl.pallas_call(
-        prepare_kernel,
-        in_specs=[scalar] + [HBM_REF] * 5,
-        out_specs=[VMEM_REF] * 4,
-        out_shape=[
-            pltpu.VMEM((heads, HEAD_WIDTH, rows), jnp.bfloat16),
-            pltpu.VMEM((devices, rows, rows), jnp.float32),
-            pltpu.VMEM(keys.shape, jnp.bfloat16),
-            pltpu.VMEM(values.shape, jnp.bfloat16),
-        ],
-        scratch_shapes=[
-            pltpu.SMEM(lengths.shape, jnp.int32),
-            pltpu.VMEM(places.shape, jnp.int32),
-            pltpu.VMEM(queries.shape, jnp.bfloat16),
-            pltpu.SemaphoreType.DMA((5,)),
-        ],
-        compiler_params=PARAMS,
-        cost_estimate=SHORT,
-        name="prepare",
-    )(own, *in_hbm(lengths, places, queries, keys, values))
+    def prepare(members, near=()):
+        return pl.pallas_call(
+            lambda *refs: prepare_kernel(members, *refs),
+            in_specs=[scalar] + [HBM_REF] * 5 + [VMEM_REF] * len(near),
+            out_specs=[VMEM_REF] * 4,
+            out_shape=[
+                pltpu.VMEM((heads, HEAD_WIDTH, rows), jnp.bfloat16),
+                pltpu.VMEM((devices, rows, rows), jnp.float32),
+                pltpu.VMEM(keys.shape, jnp.bfloat16),
+                pltpu.VMEM(values.shape, jnp.bfloat16),
+            ],
+            input_output_aliases={6 + n: n for n in range(len(near))},
+            scratch_shapes=[
+                pltpu.SMEM(lengths.shape, jnp.int32),
+                pltpu.VMEM(places.shape, jnp.int32),
+                pltpu.VMEM(queries.shape, jnp.bfloat16),
+                pltpu.SemaphoreType.DMA((5,)),
+            ],
+            compiler_params=PARAMS,
+            cost_estimate=SHORT,
+            name="prepare",
+        )(own, *in_hbm(lengths, places, queries, keys, values), *in_vmem(*near))
+
+    prepared = prepare((0, 2))
+    keys, values, *prepared = lax.optimization_barrier((keys, values, *prepared))
+    near_keys, near_values = moved(keys, 1), moved(values, 1)
+    across, bias, own_keys, own_values = prepare((1, 3), prepared)
 
     def own_shard(members, state):
         return call(

time: 16.2 us -> 16.4 us (1.012)
  waiting for transfers between devices: 0.42 us -> 0.9 us
  starting transfers between devices: 8.42 us -> 8.08 us
    ppermute x6, waiting for transfers between devices: 0.42 us -> 0.9 us  [moved(): lax.ppermute(value, 'seq', [(i, i ^ mask) for i in range(lax.axis_size('s...]
    ppermute x6, starting transfers between devices: 8.42 us -> 8.08 us  [moved(): lax.ppermute(value, 'seq', [(i, i ^ mask) for i in range(lax.axis_size('s...]
    pallas_call x1 -> x2, Pallas kernels: 1.56 us -> 1.6 us  [prepare(): pl.pallas_call(lambda *refs: prepare_kernel(members, *refs), in_specs=[sc...]
  transfers between devices with their start and end apart: 6 -> 6, of which waited for: 2 -> 3; matrix products, arithmetic and copies ran while one was open for 0% -> 0% of each run, Pallas kernels for 37% -> 37%
where the time goes in v22:
time: 16.4 us; the launch traced here: 16.2 us
  starting transfers between devices  8.08 us (49%)
  Pallas kernels  7.17 us (44%)
  waiting for transfers between devices  0.9 us (5%)
    ppermute x6, starting transfers between devices, moved(): lax.ppermute(value, 'seq', [(i, i ^ mask) for i in range(lax.axis_size('s...  8.08 us
    pallas_call x8, Pallas kernels, call(): pl.pallas_call(kernel, in_specs=[scalar] * len(scalars) + [VMEM_REF] * (l...  4.35 us
    pallas_call x2, Pallas kernels, prepare(): pl.pallas_call(lambda *refs: prepare_kernel(members, *refs), in_specs=[sc...  1.6 us
    pallas_call x1, Pallas kernels, staged_attention(): pl.pallas_call(last_kernel, in_specs=[VMEM_REF] * 3, out_specs=pl.BlockSp...  1.22 us
    ppermute x6, waiting for transfers between devices, moved(): lax.ppermute(value, 'seq', [(i, i ^ mask) for i in range(lax.axis_size('s...  0.9 us
  transfers between devices with their start and end apart: 6, of which 3 were waited for; matrix products, arithmetic and copies ran while one was open for 0% of the time, Pallas kernels for 37%

profile of v22, /device:TPU:0, one launch (start us, length us, event | category | flops | bytes accessed | tf_op | source)
XLA Modules:
  0.0 16.2 jit_solution(13129222284049891164)
XLA Ops:
  0.0 4.0 %collective-permute-start = (bf16[256,128]{1,0:T(8,128)(2,1)}, bf16[256,128]{1,0:T(8,128)(2,1)S(1)}, u32[]{:S(2)}, u32[]{:S(2)}) collective-permute-start(bf16[256,128]{1,0:T(8,128)(2,1)} %refs_4_.2), channel_id=1, source_target_pairs={{0,8},{4,12},{8,0},{12,4},{1,9},{5,13},{9,1},{13,5},{2,10},{6,14},... | collective-permute-start | bytes 196616 | tf_op jit(solution)/shard_map/ppermute | solution.py:240
  4.0 0.0 collective-permute-start.4
  4.1 1.6 %prepare.2 = (bf16[8,128,256]{2,1,0:T(8,128)(2,1)S(1)}, f32[4,256,256]{2,1,0:T(8,128)S(1)}, bf16[256,128]{1,0:T(8,128)(2,1)S(1)}, bf16[256,128]{1,0:T(8,128)(2,1)S(1)}) custom-call(s32[1]{0:T(128)} %bitcast.refs_0_, s32[3]{0:T(128)} %refs_1_.3, s32[1,128]{1,0:T(1,128)} %bitcast.2, bf16[256,1024]{1,0:T(8,128)(2,1)} %refs_3_.3, bf16[256,128]{1,0:T(8,128)(2,1)} %refs_4_.2, ...), custom_call_target="tpu_custom_call" | custom-call | tf_op jit(solution)/shard_map/prepare/pallas_call | solution.py:271
  5.6 0.4 %collective-permute-start.2 = (bf16[256,128]{1,0:T(8,128)(2,1)}, bf16[256,128]{1,0:T(8,128)(2,1)S(1)}, u32[]{:S(2)}, u32[]{:S(2)}) collective-permute-start(bf16[256,128]{1,0:T(8,128)(2,1)} %refs_4_.2), channel_id=1, source_target_pairs={{0,4},{4,0},{8,12},{12,8},{1,5},{5,1},{9,13},{13,9},{2,6},{6,2},{1... | collective-permute-start | bytes 196616 | tf_op jit(solution)/shard_map/ppermute | solution.py:240
  6.1 1.7 %collective-permute-start.3 = (bf16[256,128]{1,0:T(8,128)(2,1)}, bf16[256,128]{1,0:T(8,128)(2,1)S(1)}, u32[]{:S(2)}, u32[]{:S(2)}) collective-permute-start(bf16[256,128]{1,0:T(8,128)(2,1)} %refs_5_.2), channel_id=1, source_target_pairs={{0,4},{4,0},{8,12},{12,8},{1,5},{5,1},{9,13},{13,9},{2,6},{6,2},{1... | collective-permute-start | bytes 196616 | tf_op jit(solution)/shard_map/ppermute | solution.py:240
  7.8 1.1 %own_shard.2 = (f32[8,256]{1,0:T(8,128)S(1)}, f32[8,144,256]{2,1,0:T(8,128)S(1)}) custom-call(s32[1]{0:T(128)} %bitcast.refs_0_, bf16[8,128,256]{2,1,0:T(8,128)(2,1)S(1)} %get-tuple-element.54.refs_1_.refs_0_, f32[4,256,256]{2,1,0:T(8,128)S(1)} %get-tuple-element.55.refs_2_.refs_1_, bf16[256,128]{1,0:T(8,128)(2,1)S(1)} %get-tuple-element.56.refs_3_, ...), custom_call_target="tpu_custom_call" | custom-call | tf_op jit(solution)/shard_map/own_shard/pallas_call | solution.py:258
  8.9 0.0 collective-permute-done.refs_3_
  8.9 1.1 %collective-permute-start.1 = (bf16[256,128]{1,0:T(8,128)(2,1)S(1)}, bf16[256,128]{1,0:T(8,128)(2,1)S(1)}, u32[]{:S(2)}, u32[]{:S(2)}) collective-permute-start(bf16[256,128]{1,0:T(8,128)(2,1)S(1)} %collective-permute-done.refs_3_), channel_id=1, source_target_pairs={{0,4},{4,0},{8,12},{12,8},{1,5},{5,1},{9,13},{13,9},{2,6},{6,2},{1... | collective-permute-start | bytes 196616 | tf_op jit(solution)/shard_map/ppermute | solution.py:240
  10.0 0.5 %shard_weights.4 = (f32[8,256]{1,0:T(8,128)S(1)}, f32[8,144,256]{2,1,0:T(8,128)S(1)}, bf16[8,256,256]{2,1,0:T(8,128)(2,1)S(1)}) custom-call(s32[1]{0:T(128)} %bitcast.refs_0_, bf16[8,128,256]{2,1,0:T(8,128)(2,1)S(1)} %get-tuple-element.54.refs_1_.refs_0_, ...), custom_call_target="tpu_custom_call", output_to_operand_aliasing={{0}: (4, {}), {1}: (5, {})} | custom-call | tf_op jit(solution)/shard_map/shard_weights/pallas_call | solution.py:258
  10.5 0.1 collective-permute-done.4.v_ref
  10.6 0.9 %collective-permute-start.5 = (bf16[256,128]{1,0:T(8,128)(2,1)S(1)}, bf16[256,128]{1,0:T(8,128)(2,1)S(1)}, u32[]{:S(2)}, u32[]{:S(2)}) collective-permute-start(bf16[256,128]{1,0:T(8,128)(2,1)S(1)} %collective-permute-done.4.v_ref), channel_id=1, source_target_pairs={{0,4},{4,0},{8,12},{12,8},{1,5},{5,1},{9,13},{13,9},{2,6},{6,2},{1... | collective-permute-start | bytes 196616 | tf_op jit(solution)/shard_map/ppermute | solution.py:240
  11.4 0.5 %shard_weights.5 = (f32[8,256]{1,0:T(8,128)S(1)}, f32[8,144,256]{2,1,0:T(8,128)S(1)}, bf16[8,256,256]{2,1,0:T(8,128)(2,1)S(1)}) custom-call(s32[1]{0:T(128)} %bitcast.refs_0_, bf16[8,128,256]{2,1,0:T(8,128)(2,1)S(1)} %get-tuple-element.54.refs_1_.refs_0_, ...), custom_call_target="tpu_custom_call", output_to_operand_aliasing={{0}: (4, {}), {1}: (5, {}), {2}: (6, {})} | custom-call | tf_op jit(solution)/shard_map/shard_weights/pallas_call | solution.py:258
  11.9 0.3 %shard_values.1.refs_5_ = f32[8,144,256]{2,1,0:T(8,128)S(1)} custom-call(bf16[8,256,256]{2,1,0:T(8,128)(2,1)S(1)} %get-tuple-element.76.weight_ref, bf16[256,128]{1,0:T(8,128)(2,1)S(1)} %collective-permute-done.4.v_ref, f32[8,144,256]{2,1,0:T(8,128)S(1)} %get-tuple-element.78.old_sum_ref), custom_call_target="tpu_custom_call", output_to_operand_aliasing={{}: (2, {})} | custom-call | tf_op jit(solution)/shard_map/shard_values/pallas_call | solution.py:258
  12.3 0.0 collective-permute-done.2.refs_2_
  12.3 0.7 %collective-permute-done.3.refs_3_ = bf16[256,128]{1,0:T(8,128)(2,1)S(1)} collective-permute-done((bf16[256,128]{1,0:T(8,128)(2,1)}, bf16[256,128]{1,0:T(8,128)(2,1)S(1)}, u32[]{:S(2)}, u32[]{:S(2)}) %collective-permute-start.3) | collective-permute-done | bytes 65568 | tf_op jit(solution)/shard_map/ppermute | solution.py:240
  13.0 1.1 %next_shard.1 = (f32[8,256]{1,0:T(8,128)S(1)}, f32[8,144,256]{2,1,0:T(8,128)S(1)}) custom-call(bf16[8,128,256]{2,1,0:T(8,128)(2,1)S(1)} %get-tuple-element.54.refs_1_.refs_0_, f32[4,256,256]{2,1,0:T(8,128)S(1)} %get-tuple-element.55.refs_2_.refs_1_, ...), custom_call_target="tpu_custom_call", output_to_operand_aliasing={{0}: (4, {}), {1}: (5, {})} | custom-call | tf_op jit(solution)/shard_map/next_shard/pallas_call | solution.py:258
  14.1 0.1 collective-permute-done.1.refs_3_
  14.2 0.8 %shard_weights.7 = (f32[8,256]{1,0:T(8,128)S(1)}, f32[8,144,256]{2,1,0:T(8,128)S(1)}, bf16[8,256,256]{2,1,0:T(8,128)(2,1)S(1)}) custom-call(s32[1]{0:T(128)} %bitcast.refs_0_, bf16[8,128,256]{2,1,0:T(8,128)(2,1)S(1)} %get-tuple-element.54.refs_1_.refs_0_, ...), custom_call_target="tpu_custom_call", output_to_operand_aliasing={{0}: (4, {}), {1}: (5, {})} | custom-call | tf_op jit(solution)/shard_map/shard_weights/pallas_call | solution.py:258
  15.0 0.0 collective-permute-done.5.v_ref
  15.0 1.2 %last_values.1 = bf16[256,1024]{1,0:T(8,128)(2,1)} custom-call(bf16[8,256,256]{2,1,0:T(8,128)(2,1)S(1)} %get-tuple-element.81.weight_ref, bf16[256,128]{1,0:T(8,128)(2,1)S(1)} %collective-permute-done.5.v_ref, f32[8,144,256]{2,1,0:T(8,128)S(1)} %get-tuple-element.82.sum_ref), custom_call_target="tpu_custom_call" | custom-call | tf_op jit(solution)/shard_map/last_values/pallas_call | solution.py:328
  (3 shorter events, 0.1 us)
Async XLA Ops:
  0.0 8.9 %collective-permute-start = (bf16[256,128]{1,0:T(8,128)(2,1)}, bf16[256,128]{1,0:T(8,128)(2,1)S(1)}, u32[]{:S(2)}, u32[]{:S(2)}) collective-permute-start(bf16[256,128]{1,0:T(8,128)(2,1)} %refs_4_.2), channel_id=1, source_target_pairs={{0,8},{4,12},{8,0},{12,4},{1,9},{5,13},{9,1},{13,5},{2,10},{6,14},... | collective-permute-start | bytes 196616 | tf_op jit(solution)/shard_map/ppermute | solution.py:240
  4.0 6.5 %collective-permute-start.4 = (bf16[256,128]{1,0:T(8,128)(2,1)}, bf16[256,128]{1,0:T(8,128)(2,1)S(1)}, u32[]{:S(2)}, u32[]{:S(2)}) collective-permute-start(bf16[256,128]{1,0:T(8,128)(2,1)} %refs_5_.2), channel_id=1, source_target_pairs={{0,8},{4,12},{8,0},{12,4},{1,9},{5,13},{9,1},{13,5},{2,10},{6,14},... | collective-permute-start | bytes 196616 | tf_op jit(solution)/shard_map/ppermute | solution.py:240
  5.6 6.6 %collective-permute-start.2 = (bf16[256,128]{1,0:T(8,128)(2,1)}, bf16[256,128]{1,0:T(8,128)(2,1)S(1)}, u32[]{:S(2)}, u32[]{:S(2)}) collective-permute-start(bf16[256,128]{1,0:T(8,128)(2,1)} %refs_4_.2), channel_id=1, source_target_pairs={{0,4},{4,0},{8,12},{12,8},{1,5},{5,1},{9,13},{13,9},{2,6},{6,2},{1... | collective-permute-start | bytes 196616 | tf_op jit(solution)/shard_map/ppermute | solution.py:240
  6.1 6.9 %collective-permute-start.3 = (bf16[256,128]{1,0:T(8,128)(2,1)}, bf16[256,128]{1,0:T(8,128)(2,1)S(1)}, u32[]{:S(2)}, u32[]{:S(2)}) collective-permute-start(bf16[256,128]{1,0:T(8,128)(2,1)} %refs_5_.2), channel_id=1, source_target_pairs={{0,4},{4,0},{8,12},{12,8},{1,5},{5,1},{9,13},{13,9},{2,6},{6,2},{1... | collective-permute-start | bytes 196616 | tf_op jit(solution)/shard_map/ppermute | solution.py:240
  8.9 5.3 %collective-permute-start.1 = (bf16[256,128]{1,0:T(8,128)(2,1)S(1)}, bf16[256,128]{1,0:T(8,128)(2,1)S(1)}, u32[]{:S(2)}, u32[]{:S(2)}) collective-permute-start(bf16[256,128]{1,0:T(8,128)(2,1)S(1)} %collective-permute-done.refs_3_), channel_id=1, source_target_pairs={{0,4},{4,0},{8,12},{12,8},{1,5},{5,1},{9,13},{13,9},{2,6},{6,2},{1... | collective-permute-start | bytes 196616 | tf_op jit(solution)/shard_map/ppermute | solution.py:240
  10.6 4.4 %collective-permute-start.5 = (bf16[256,128]{1,0:T(8,128)(2,1)S(1)}, bf16[256,128]{1,0:T(8,128)(2,1)S(1)}, u32[]{:S(2)}, u32[]{:S(2)}) collective-permute-start(bf16[256,128]{1,0:T(8,128)(2,1)S(1)} %collective-permute-done.4.v_ref), channel_id=1, source_target_pairs={{0,4},{4,0},{8,12},{12,8},{1,5},{5,1},{9,13},{13,9},{2,6},{6,2},{1... | collective-permute-start | bytes 196616 | tf_op jit(solution)/shard_map/ppermute | solution.py:240

commit v23 on v22

--- a/solution.py
+++ b/solution.py
@@ -241,7 +241,7 @@
 
 
 def staged_attention(queries, keys, values, lengths, old_place):
-    far_keys, far_values = moved(keys, 2), moved(values, 2)
+    far_keys = moved(keys, 2)
     rows, cols = queries.shape
     heads = cols // HEAD_WIDTH
     devices = lax.axis_size("seq")
@@ -292,6 +292,7 @@
 
     prepared = prepare((0, 2))
     keys, values, *prepared = lax.optimization_barrier((keys, values, *prepared))
+    far_values = moved(values, 2)
     near_keys, near_values = moved(keys, 1), moved(values, 1)
     across, bias, own_keys, own_values = prepare((1, 3), prepared)
 

time: 16.4 us -> 17 us (1.037)
  waiting for transfers between devices: 0.9 us -> 1.98 us
  starting transfers between devices: 8.08 us -> 7.63 us
    ppermute x6, waiting for transfers between devices: 0.9 us -> 1.98 us  [moved(): lax.ppermute(value, 'seq', [(i, i ^ mask) for i in range(lax.axis_size('s...]
    ppermute x6, starting transfers between devices: 8.08 us -> 7.63 us  [moved(): lax.ppermute(value, 'seq', [(i, i ^ mask) for i in range(lax.axis_size('s...]
  transfers between devices with their start and end apart: 6 -> 6, of which waited for: 3 -> 3; matrix products, arithmetic and copies ran while one was open for 0% -> 0% of each run, Pallas kernels for 37% -> 35%
where the time goes in v23:
time: 17 us; the launch traced here: 16.9 us
  starting transfers between devices  7.63 us (45%)
  Pallas kernels  7.17 us (42%)
  waiting for transfers between devices  1.98 us (12%)
    ppermute x6, starting transfers between devices, moved(): lax.ppermute(value, 'seq', [(i, i ^ mask) for i in range(lax.axis_size('s...  7.63 us
    pallas_call x8, Pallas kernels, call(): pl.pallas_call(kernel, in_specs=[scalar] * len(scalars) + [VMEM_REF] * (l...  4.36 us
    ppermute x6, waiting for transfers between devices, moved(): lax.ppermute(value, 'seq', [(i, i ^ mask) for i in range(lax.axis_size('s...  1.98 us
    pallas_call x2, Pallas kernels, prepare(): pl.pallas_call(lambda *refs: prepare_kernel(members, *refs), in_specs=[sc...  1.6 us
    pallas_call x1, Pallas kernels, staged_attention(): pl.pallas_call(last_kernel, in_specs=[VMEM_REF] * 3, out_specs=pl.BlockSp...  1.21 us
  transfers between devices with their start and end apart: 6, of which 3 were waited for; matrix products, arithmetic and copies ran while one was open for 0% of the time, Pallas kernels for 35%

profile of v23, /device:TPU:0, one launch (start us, length us, event | category | flops | bytes accessed | tf_op | source)
XLA Modules:
  0.0 16.9 jit_solution(15712380243685826423)
XLA Ops:
  0.0 4.0 %collective-permute-start = (bf16[256,128]{1,0:T(8,128)(2,1)}, bf16[256,128]{1,0:T(8,128)(2,1)S(1)}, u32[]{:S(2)}, u32[]{:S(2)}) collective-permute-start(bf16[256,128]{1,0:T(8,128)(2,1)} %refs_4_.2), channel_id=1, source_target_pairs={{0,8},{4,12},{8,0},{12,4},{1,9},{5,13},{9,1},{13,5},{2,10},{6,14},... | collective-permute-start | bytes 196616 | tf_op jit(solution)/shard_map/ppermute | solution.py:240
  4.0 1.6 %prepare.2 = (bf16[8,128,256]{2,1,0:T(8,128)(2,1)S(1)}, f32[4,256,256]{2,1,0:T(8,128)S(1)}, bf16[256,128]{1,0:T(8,128)(2,1)S(1)}, bf16[256,128]{1,0:T(8,128)(2,1)S(1)}) custom-call(s32[1]{0:T(128)} %bitcast.refs_0_, s32[3]{0:T(128)} %refs_1_.3, s32[1,128]{1,0:T(1,128)} %bitcast.2, bf16[256,1024]{1,0:T(8,128)(2,1)} %refs_3_.3, bf16[256,128]{1,0:T(8,128)(2,1)} %refs_4_.2, ...), custom_call_target="tpu_custom_call" | custom-call | tf_op jit(solution)/shard_map/prepare/pallas_call | solution.py:271
  5.6 0.1 collective-permute-start.4
  5.7 0.4 %collective-permute-start.3 = (bf16[256,128]{1,0:T(8,128)(2,1)}, bf16[256,128]{1,0:T(8,128)(2,1)S(1)}, u32[]{:S(2)}, u32[]{:S(2)}) collective-permute-start(bf16[256,128]{1,0:T(8,128)(2,1)} %refs_5_.2), channel_id=1, source_target_pairs={{0,4},{4,0},{8,12},{12,8},{1,5},{5,1},{9,13},{13,9},{2,6},{6,2},{1... | collective-permute-start | bytes 196616 | tf_op jit(solution)/shard_map/ppermute | solution.py:240
  6.1 1.7 %collective-permute-start.2 = (bf16[256,128]{1,0:T(8,128)(2,1)}, bf16[256,128]{1,0:T(8,128)(2,1)S(1)}, u32[]{:S(2)}, u32[]{:S(2)}) collective-permute-start(bf16[256,128]{1,0:T(8,128)(2,1)} %refs_4_.2), channel_id=1, source_target_pairs={{0,4},{4,0},{8,12},{12,8},{1,5},{5,1},{9,13},{13,9},{2,6},{6,2},{1... | collective-permute-start | bytes 196616 | tf_op jit(solution)/shard_map/ppermute | solution.py:240
  7.8 1.1 %own_shard.2 = (f32[8,256]{1,0:T(8,128)S(1)}, f32[8,144,256]{2,1,0:T(8,128)S(1)}) custom-call(s32[1]{0:T(128)} %bitcast.refs_0_, bf16[8,128,256]{2,1,0:T(8,128)(2,1)S(1)} %get-tuple-element.54.refs_1_.refs_0_, f32[4,256,256]{2,1,0:T(8,128)S(1)} %get-tuple-element.55.refs_2_.refs_1_, bf16[256,128]{1,0:T(8,128)(2,1)S(1)} %get-tuple-element.56.refs_3_, ...), custom_call_target="tpu_custom_call" | custom-call | tf_op jit(solution)/shard_map/own_shard/pallas_call | solution.py:258
  9.0 0.0 collective-permute-done.refs_3_
  9.0 1.3 %collective-permute-start.1 = (bf16[256,128]{1,0:T(8,128)(2,1)S(1)}, bf16[256,128]{1,0:T(8,128)(2,1)S(1)}, u32[]{:S(2)}, u32[]{:S(2)}) collective-permute-start(bf16[256,128]{1,0:T(8,128)(2,1)S(1)} %collective-permute-done.refs_3_), channel_id=1, source_target_pairs={{0,4},{4,0},{8,12},{12,8},{1,5},{5,1},{9,13},{13,9},{2,6},{6,2},{1... | collective-permute-start | bytes 196616 | tf_op jit(solution)/shard_map/ppermute | solution.py:240
  10.3 0.5 %shard_weights.4 = (f32[8,256]{1,0:T(8,128)S(1)}, f32[8,144,256]{2,1,0:T(8,128)S(1)}, bf16[8,256,256]{2,1,0:T(8,128)(2,1)S(1)}) custom-call(s32[1]{0:T(128)} %bitcast.refs_0_, bf16[8,128,256]{2,1,0:T(8,128)(2,1)S(1)} %get-tuple-element.54.refs_1_.refs_0_, ...), custom_call_target="tpu_custom_call", output_to_operand_aliasing={{0}: (4, {}), {1}: (5, {})} | custom-call | tf_op jit(solution)/shard_map/shard_weights/pallas_call | solution.py:258
  10.7 0.7 %collective-permute-done.4.v_ref = bf16[256,128]{1,0:T(8,128)(2,1)S(1)} collective-permute-done((bf16[256,128]{1,0:T(8,128)(2,1)}, bf16[256,128]{1,0:T(8,128)(2,1)S(1)}, u32[]{:S(2)}, u32[]{:S(2)}) %collective-permute-start.4) | collective-permute-done | bytes 65568 | tf_op jit(solution)/shard_map/ppermute | solution.py:240
  11.4 0.1 collective-permute-start.5
  11.5 0.5 %shard_weights.5 = (f32[8,256]{1,0:T(8,128)S(1)}, f32[8,144,256]{2,1,0:T(8,128)S(1)}, bf16[8,256,256]{2,1,0:T(8,128)(2,1)S(1)}) custom-call(s32[1]{0:T(128)} %bitcast.refs_0_, bf16[8,128,256]{2,1,0:T(8,128)(2,1)S(1)} %get-tuple-element.54.refs_1_.refs_0_, ...), custom_call_target="tpu_custom_call", output_to_operand_aliasing={{0}: (4, {}), {1}: (5, {}), {2}: (6, {})} | custom-call | tf_op jit(solution)/shard_map/shard_weights/pallas_call | solution.py:258
  12.0 0.4 %shard_values.1.refs_5_ = f32[8,144,256]{2,1,0:T(8,128)S(1)} custom-call(bf16[8,256,256]{2,1,0:T(8,128)(2,1)S(1)} %get-tuple-element.76.weight_ref, bf16[256,128]{1,0:T(8,128)(2,1)S(1)} %collective-permute-done.4.v_ref, f32[8,144,256]{2,1,0:T(8,128)S(1)} %get-tuple-element.78.old_sum_ref), custom_call_target="tpu_custom_call", output_to_operand_aliasing={{}: (2, {})} | custom-call | tf_op jit(solution)/shard_map/shard_values/pallas_call | solution.py:258
  12.4 0.0 collective-permute-done.3.refs_3_
  12.4 1.0 %collective-permute-done.2.refs_2_ = bf16[256,128]{1,0:T(8,128)(2,1)S(1)} collective-permute-done((bf16[256,128]{1,0:T(8,128)(2,1)}, bf16[256,128]{1,0:T(8,128)(2,1)S(1)}, u32[]{:S(2)}, u32[]{:S(2)}) %collective-permute-start.2) | collective-permute-done | bytes 65568 | tf_op jit(solution)/shard_map/ppermute | solution.py:240
  13.4 1.1 %next_shard.1 = (f32[8,256]{1,0:T(8,128)S(1)}, f32[8,144,256]{2,1,0:T(8,128)S(1)}) custom-call(bf16[8,128,256]{2,1,0:T(8,128)(2,1)S(1)} %get-tuple-element.54.refs_1_.refs_0_, f32[4,256,256]{2,1,0:T(8,128)S(1)} %get-tuple-element.55.refs_2_.refs_1_, ...), custom_call_target="tpu_custom_call", output_to_operand_aliasing={{0}: (4, {}), {1}: (5, {})} | custom-call | tf_op jit(solution)/shard_map/next_shard/pallas_call | solution.py:258
  14.6 0.0 collective-permute-done.1.refs_3_
  14.6 0.8 %shard_weights.7 = (f32[8,256]{1,0:T(8,128)S(1)}, f32[8,144,256]{2,1,0:T(8,128)S(1)}, bf16[8,256,256]{2,1,0:T(8,128)(2,1)S(1)}) custom-call(s32[1]{0:T(128)} %bitcast.refs_0_, bf16[8,128,256]{2,1,0:T(8,128)(2,1)S(1)} %get-tuple-element.54.refs_1_.refs_0_, ...), custom_call_target="tpu_custom_call", output_to_operand_aliasing={{0}: (4, {}), {1}: (5, {})} | custom-call | tf_op jit(solution)/shard_map/shard_weights/pallas_call | solution.py:258
  15.4 0.3 %collective-permute-done.5.v_ref = bf16[256,128]{1,0:T(8,128)(2,1)S(1)} collective-permute-done((bf16[256,128]{1,0:T(8,128)(2,1)S(1)}, bf16[256,128]{1,0:T(8,128)(2,1)S(1)}, u32[]{:S(2)}, u32[]{:S(2)}) %collective-permute-start.5) | collective-permute-done | bytes 65568 | tf_op jit(solution)/shard_map/ppermute | solution.py:240
  15.7 1.2 %last_values.1 = bf16[256,1024]{1,0:T(8,128)(2,1)} custom-call(bf16[8,256,256]{2,1,0:T(8,128)(2,1)S(1)} %get-tuple-element.81.weight_ref, bf16[256,128]{1,0:T(8,128)(2,1)S(1)} %collective-permute-done.5.v_ref, f32[8,144,256]{2,1,0:T(8,128)S(1)} %get-tuple-element.82.sum_ref), custom_call_target="tpu_custom_call" | custom-call | tf_op jit(solution)/shard_map/last_values/pallas_call | solution.py:329
  (3 shorter events, 0.1 us)
Async XLA Ops:
  0.0 9.0 %collective-permute-start = (bf16[256,128]{1,0:T(8,128)(2,1)}, bf16[256,128]{1,0:T(8,128)(2,1)S(1)}, u32[]{:S(2)}, u32[]{:S(2)}) collective-permute-start(bf16[256,128]{1,0:T(8,128)(2,1)} %refs_4_.2), channel_id=1, source_target_pairs={{0,8},{4,12},{8,0},{12,4},{1,9},{5,13},{9,1},{13,5},{2,10},{6,14},... | collective-permute-start | bytes 196616 | tf_op jit(solution)/shard_map/ppermute | solution.py:240
  5.6 5.8 %collective-permute-start.4 = (bf16[256,128]{1,0:T(8,128)(2,1)}, bf16[256,128]{1,0:T(8,128)(2,1)S(1)}, u32[]{:S(2)}, u32[]{:S(2)}) collective-permute-start(bf16[256,128]{1,0:T(8,128)(2,1)} %refs_5_.2), channel_id=1, source_target_pairs={{0,8},{4,12},{8,0},{12,4},{1,9},{5,13},{9,1},{13,5},{2,10},{6,14},... | collective-permute-start | bytes 196616 | tf_op jit(solution)/shard_map/ppermute | solution.py:240
  5.7 6.7 %collective-permute-start.3 = (bf16[256,128]{1,0:T(8,128)(2,1)}, bf16[256,128]{1,0:T(8,128)(2,1)S(1)}, u32[]{:S(2)}, u32[]{:S(2)}) collective-permute-start(bf16[256,128]{1,0:T(8,128)(2,1)} %refs_5_.2), channel_id=1, source_target_pairs={{0,4},{4,0},{8,12},{12,8},{1,5},{5,1},{9,13},{13,9},{2,6},{6,2},{1... | collective-permute-start | bytes 196616 | tf_op jit(solution)/shard_map/ppermute | solution.py:240
  6.1 7.4 %collective-permute-start.2 = (bf16[256,128]{1,0:T(8,128)(2,1)}, bf16[256,128]{1,0:T(8,128)(2,1)S(1)}, u32[]{:S(2)}, u32[]{:S(2)}) collective-permute-start(bf16[256,128]{1,0:T(8,128)(2,1)} %refs_4_.2), channel_id=1, source_target_pairs={{0,4},{4,0},{8,12},{12,8},{1,5},{5,1},{9,13},{13,9},{2,6},{6,2},{1... | collective-permute-start | bytes 196616 | tf_op jit(solution)/shard_map/ppermute | solution.py:240
  9.0 5.6 %collective-permute-start.1 = (bf16[256,128]{1,0:T(8,128)(2,1)S(1)}, bf16[256,128]{1,0:T(8,128)(2,1)S(1)}, u32[]{:S(2)}, u32[]{:S(2)}) collective-permute-start(bf16[256,128]{1,0:T(8,128)(2,1)S(1)} %collective-permute-done.refs_3_), channel_id=1, source_target_pairs={{0,4},{4,0},{8,12},{12,8},{1,5},{5,1},{9,13},{13,9},{2,6},{6,2},{1... | collective-permute-start | bytes 196616 | tf_op jit(solution)/shard_map/ppermute | solution.py:240
  11.4 4.3 %collective-permute-start.5 = (bf16[256,128]{1,0:T(8,128)(2,1)S(1)}, bf16[256,128]{1,0:T(8,128)(2,1)S(1)}, u32[]{:S(2)}, u32[]{:S(2)}) collective-permute-start(bf16[256,128]{1,0:T(8,128)(2,1)S(1)} %collective-permute-done.4.v_ref), channel_id=1, source_target_pairs={{0,4},{4,0},{8,12},{12,8},{1,5},{5,1},{9,13},{13,9},{2,6},{6,2},{1... | collective-permute-start | bytes 196616 | tf_op jit(solution)/shard_map/ppermute | solution.py:240

commit v24 on v12

--- a/solution.py
+++ b/solution.py
@@ -95,7 +95,13 @@
     return stage
 
 
-def own_kernel(
+def own_kernel(odd, own_ref, odd_ref, *refs):
+    @pl.when(odd_ref[0] == odd)
+    def _():
+        own_shard(own_ref, *refs[:5], *refs[-12:])
+
+
+def own_shard(
     own_ref, lengths_hbm, places_hbm, q_hbm, k_hbm, v_hbm,
     across_ref, bias_ref, peak_ref, sum_ref,
     lengths_ref, places_ref, q_ref, k_ref, v_ref, scaled_ref, weight_ref, sems,
@@ -216,8 +222,7 @@
 
 
 def staged_attention(queries, keys, values, lengths, old_place):
-    far_keys, far_values = moved(keys, 2), moved(values, 2)
-    near_keys, near_values = moved(keys, 1), moved(values, 1)
+    far_keys = moved(keys, 2)
     rows, cols = queries.shape
     heads = cols // HEAD_WIDTH
     devices = lax.axis_size("seq")
@@ -231,25 +236,36 @@
         pltpu.VMEM((heads, rows, rows), jnp.float32),
         pltpu.VMEM((heads, rows, rows), jnp.bfloat16),
     ]
-    across, bias, *carried = pl.pallas_call(
-        own_kernel,
-        in_specs=[pl.BlockSpec(memory_space=pltpu.SMEM)] + [HBM_REF] * 5,
-        out_specs=[VMEM_REF] * 4,
-        out_shape=[
-            pltpu.VMEM((heads, HEAD_WIDTH, rows), jnp.bfloat16),
-            pltpu.VMEM((devices, rows, rows), jnp.float32),
-        ] + state,
-        scratch_shapes=[
-            pltpu.SMEM(lengths.shape, jnp.int32),
-            pltpu.VMEM(places.shape, jnp.int32),
-            pltpu.VMEM(queries.shape, jnp.bfloat16),
-            pltpu.VMEM(keys.shape, jnp.bfloat16),
-            pltpu.VMEM(values.shape, jnp.bfloat16),
-        ] + work + [pltpu.SemaphoreType.DMA((5,))],
-        compiler_params=PARAMS,
-        cost_estimate=SHORT,
-        name="own_shard",
-    )(own.reshape(1), *in_hbm(lengths, places, queries, keys, values))
+    odd = (lax.axis_index("mp").astype(jnp.int32) & 1).reshape(1)
+
+    def own_on(parity, before=()):
+        return pl.pallas_call(
+            lambda *refs: own_kernel(parity, *refs),
+            in_specs=[pl.BlockSpec(memory_space=pltpu.SMEM)] * 2
+            + [HBM_REF] * 5 + [VMEM_REF] * len(before),
+            out_specs=[VMEM_REF] * 4,
+            out_shape=[
+                pltpu.VMEM((heads, HEAD_WIDTH, rows), jnp.bfloat16),
+                pltpu.VMEM((devices, rows, rows), jnp.float32),
+            ] + state,
+            input_output_aliases={7 + n: n for n in range(len(before))},
+            scratch_shapes=[
+                pltpu.SMEM(lengths.shape, jnp.int32),
+                pltpu.VMEM(places.shape, jnp.int32),
+                pltpu.VMEM(queries.shape, jnp.bfloat16),
+                pltpu.VMEM(keys.shape, jnp.bfloat16),
+                pltpu.VMEM(values.shape, jnp.bfloat16),
+            ] + work + [pltpu.SemaphoreType.DMA((5,))],
+            compiler_params=PARAMS,
+            cost_estimate=SHORT,
+            name="own_shard",
+        )(own.reshape(1), odd, *in_hbm(lengths, places, queries, keys, values), *in_vmem(*before))
+
+    made = own_on(1)
+    keys, values, *made = lax.optimization_barrier((keys, values, *made))
+    far_values = moved(values, 2)
+    near_keys, near_values = moved(keys, 1), moved(values, 1)
+    across, bias, *carried = own_on(0, made)
 
     def add_shard(at, keys, values, carried):
         return pl.pallas_call(

time: 16.2 us -> 16.8 us (1.037)
  waiting for transfers between devices: 0.03 us -> 0.9 us
  starting transfers between devices: 9.19 us -> 8.91 us
    ppermute x6, waiting for transfers between devices: 0.03 us -> 0.9 us  [moved(): lax.ppermute(value, 'seq', [(i, i ^ mask) for i in range(lax.axis_size('s...]
    ppermute x6, starting transfers between devices: 9.19 us -> 8.91 us  [moved(): lax.ppermute(value, 'seq', [(i, i ^ mask) for i in range(lax.axis_size('s...]
    pallas_call x1 -> x2, Pallas kernels: 2.42 us -> 2.48 us  [own_on(): pl.pallas_call(lambda *refs: own_kernel(parity, *refs), in_specs=[pl.Bloc...]
  transfers between devices with their start and end apart: 6 -> 6, of which waited for: 0 -> 1; matrix products, arithmetic and copies ran while one was open for 0% -> 0% of each run, Pallas kernels for 34% -> 33%
where the time goes in v24:
time: 16.8 us; the launch traced here: 16.7 us
  starting transfers between devices  8.91 us (53%)
  Pallas kernels  6.78 us (40%)
  waiting for transfers between devices  0.9 us (5%)
    ppermute x6, starting transfers between devices, moved(): lax.ppermute(value, 'seq', [(i, i ^ mask) for i in range(lax.axis_size('s...  8.91 us
    pallas_call x2, Pallas kernels, own_on(): pl.pallas_call(lambda *refs: own_kernel(parity, *refs), in_specs=[pl.Bloc...  2.48 us
    pallas_call x2, Pallas kernels, add_shard(): pl.pallas_call(lambda *refs: next_kernel(at, *refs), in_specs=[VMEM_REF]...  2.26 us
    pallas_call x1, Pallas kernels, staged_attention(): pl.pallas_call(last_kernel, in_specs=[VMEM_REF] * 3, out_specs=pl.BlockSp...  1.25 us
    ppermute x6, waiting for transfers between devices, moved(): lax.ppermute(value, 'seq', [(i, i ^ mask) for i in range(lax.axis_size('s...  0.9 us
    pallas_call x1, Pallas kernels, staged_attention(): pl.pallas_call(lambda *refs: weights_kernel(3, *refs), in_specs=[VMEM_REF...  0.79 us
  transfers between devices with their start and end apart: 6, of which 1 were waited for; matrix products, arithmetic and copies ran while one was open for 0% of the time, Pallas kernels for 33%

profile of v24, /device:TPU:0, one launch (start us, length us, event | category | flops | bytes accessed | tf_op | source)
XLA Modules:
  0.0 16.7 jit_solution(1164772017168312296)
XLA Ops:
  0.0 4.0 %collective-permute-start.1 = (bf16[256,128]{1,0:T(8,128)(2,1)}, bf16[256,128]{1,0:T(8,128)(2,1)S(1)}, u32[]{:S(2)}, u32[]{:S(2)}) collective-permute-start(bf16[256,128]{1,0:T(8,128)(2,1)} %refs_5_.2), channel_id=1, source_target_pairs={{0,8},{4,12},{8,0},{12,4},{1,9},{5,13},{9,1},{13,5},{2,10},{6,14},... | collective-permute-start | bytes 196616 | tf_op jit(solution)/shard_map/ppermute | solution.py:221
  4.1 0.1 collective-permute-start
  4.2 1.9 %collective-permute-start.3 = (bf16[256,128]{1,0:T(8,128)(2,1)}, bf16[256,128]{1,0:T(8,128)(2,1)S(1)}, u32[]{:S(2)}, u32[]{:S(2)}) collective-permute-start(bf16[256,128]{1,0:T(8,128)(2,1)} %refs_6_.2), channel_id=1, source_target_pairs={{0,4},{4,0},{8,12},{12,8},{1,5},{5,1},{9,13},{13,9},{2,6},{6,2},{1... | collective-permute-start | bytes 196616 | tf_op jit(solution)/shard_map/ppermute | solution.py:221
  6.1 0.2 %collective-permute-start.2 = (bf16[256,128]{1,0:T(8,128)(2,1)}, bf16[256,128]{1,0:T(8,128)(2,1)S(1)}, u32[]{:S(2)}, u32[]{:S(2)}) collective-permute-start(bf16[256,128]{1,0:T(8,128)(2,1)} %refs_5_.2), channel_id=1, source_target_pairs={{0,4},{4,0},{8,12},{12,8},{1,5},{5,1},{9,13},{13,9},{2,6},{6,2},{1... | collective-permute-start | bytes 196616 | tf_op jit(solution)/shard_map/ppermute | solution.py:221
  6.3 2.4 %own_shard.3 = (bf16[8,128,256]{2,1,0:T(8,128)(2,1)S(1)}, f32[4,256,256]{2,1,0:T(8,128)S(1)}, f32[8,256]{1,0:T(8,128)S(1)}, f32[8,144,256]{2,1,0:T(8,128)S(1)}) custom-call(s32[1]{0:T(128)} %bitcast.refs_0_, s32[1]{0:T(128)} %bitcast.1.refs_1_, s32[3]{0:T(128)} %refs_2_.3, ...), custom_call_target="tpu_custom_call", output_to_operand_aliasing={{0}: (7, {}), {1}: (8, {}), {2}: (9, {}), {3}: (10, {})} | custom-call | tf_op jit(solution)/shard_map/own_shard/pallas_call | solution.py:242
  8.7 0.0 collective-permute-done.1.refs_4_
  8.7 1.9 %collective-permute-start.4 = (bf16[256,128]{1,0:T(8,128)(2,1)S(1)}, bf16[256,128]{1,0:T(8,128)(2,1)S(1)}, u32[]{:S(2)}, u32[]{:S(2)}) collective-permute-start(bf16[256,128]{1,0:T(8,128)(2,1)S(1)} %collective-permute-done.1.refs_4_), channel_id=1, source_target_pairs={{0,4},{4,0},{8,12},{12,8},{1,5},{5,1},{9,13},{13,9},{2,6},{6,2},{1... | collective-permute-start | bytes 196616 | tf_op jit(solution)/shard_map/ppermute | solution.py:221
  10.6 0.0 collective-permute-done.refs_5_
  10.6 0.8 %collective-permute-start.5 = (bf16[256,128]{1,0:T(8,128)(2,1)S(1)}, bf16[256,128]{1,0:T(8,128)(2,1)S(1)}, u32[]{:S(2)}, u32[]{:S(2)}) collective-permute-start(bf16[256,128]{1,0:T(8,128)(2,1)S(1)} %collective-permute-done.refs_5_), channel_id=1, source_target_pairs={{0,4},{4,0},{8,12},{12,8},{1,5},{5,1},{9,13},{13,9},{2,6},{6,2},{1... | collective-permute-start | bytes 196616 | tf_op jit(solution)/shard_map/ppermute | solution.py:221
  11.4 1.1 %next_shard.2 = (f32[8,256]{1,0:T(8,128)S(1)}, f32[8,144,256]{2,1,0:T(8,128)S(1)}) custom-call(bf16[8,128,256]{2,1,0:T(8,128)(2,1)S(1)} %get-tuple-element.41.refs_0_, f32[4,256,256]{2,1,0:T(8,128)S(1)} %get-tuple-element.42.refs_1_, f32[8,256]{1,0:T(8,128)S(1)} %get-tuple-element.47.refs_2_, f32[8,144,256]{2,1,0:T(8,128)S(1)} %get-tuple-element.48.refs_3_, ...), custom_call_target="tpu_custom_call" | custom-call | tf_op jit(solution)/shard_map/next_shard/pallas_call | solution.py:271
  12.6 0.0 collective-permute-done.3.refs_5_
  12.6 0.0 collective-permute-done.2.refs_4_
  12.6 1.1 %next_shard.3 = (f32[8,256]{1,0:T(8,128)S(1)}, f32[8,144,256]{2,1,0:T(8,128)S(1)}) custom-call(bf16[8,128,256]{2,1,0:T(8,128)(2,1)S(1)} %get-tuple-element.41.refs_0_, f32[4,256,256]{2,1,0:T(8,128)S(1)} %get-tuple-element.42.refs_1_, f32[8,256]{1,0:T(8,128)S(1)} %get-tuple-element.51.refs_2_, f32[8,144,256]{2,1,0:T(8,128)S(1)} %get-tuple-element.52.refs_3_, ...), custom_call_target="tpu_custom_call" | custom-call | tf_op jit(solution)/shard_map/next_shard/pallas_call | solution.py:271
  13.7 0.0 collective-permute-done.4.refs_4_
  13.7 0.8 %last_weights.1 = (f32[8,144,256]{2,1,0:T(8,128)S(1)}, bf16[8,256,256]{2,1,0:T(8,128)(2,1)S(1)}) custom-call(bf16[8,128,256]{2,1,0:T(8,128)(2,1)S(1)} %get-tuple-element.41.refs_0_, f32[4,256,256]{2,1,0:T(8,128)S(1)} %get-tuple-element.42.refs_1_, f32[8,256]{1,0:T(8,128)S(1)} %get-tuple-element.53.refs_2_, f32[8,144,256]{2,1,0:T(8,128)S(1)} %get-tuple-element.54.refs_3_, ...), custom_call_target="tpu_custom_call" | custom-call | tf_op jit(solution)/shard_map/last_weights/pallas_call | solution.py:288
  14.5 0.9 %collective-permute-done.5.v_ref = bf16[256,128]{1,0:T(8,128)(2,1)S(1)} collective-permute-done((bf16[256,128]{1,0:T(8,128)(2,1)S(1)}, bf16[256,128]{1,0:T(8,128)(2,1)S(1)}, u32[]{:S(2)}, u32[]{:S(2)}) %collective-permute-start.5) | collective-permute-done | bytes 65568 | tf_op jit(solution)/shard_map/ppermute | solution.py:221
  15.4 1.2 %last_values.1 = bf16[256,1024]{1,0:T(8,128)(2,1)} custom-call(f32[8,144,256]{2,1,0:T(8,128)S(1)} %get-tuple-element.55.sum_ref, bf16[8,256,256]{2,1,0:T(8,128)(2,1)S(1)} %get-tuple-element.56.weight_ref, bf16[256,128]{1,0:T(8,128)(2,1)S(1)} %collective-permute-done.5.v_ref), custom_call_target="tpu_custom_call" | custom-call | tf_op jit(solution)/shard_map/last_values/pallas_call | solution.py:298
  (1 shorter events, 0.0 us)
Async XLA Ops:
  0.0 8.7 %collective-permute-start.1 = (bf16[256,128]{1,0:T(8,128)(2,1)}, bf16[256,128]{1,0:T(8,128)(2,1)S(1)}, u32[]{:S(2)}, u32[]{:S(2)}) collective-permute-start(bf16[256,128]{1,0:T(8,128)(2,1)} %refs_5_.2), channel_id=1, source_target_pairs={{0,8},{4,12},{8,0},{12,4},{1,9},{5,13},{9,1},{13,5},{2,10},{6,14},... | collective-permute-start | bytes 196616 | tf_op jit(solution)/shard_map/ppermute | solution.py:221
  4.1 6.5 %collective-permute-start = (bf16[256,128]{1,0:T(8,128)(2,1)}, bf16[256,128]{1,0:T(8,128)(2,1)S(1)}, u32[]{:S(2)}, u32[]{:S(2)}) collective-permute-start(bf16[256,128]{1,0:T(8,128)(2,1)} %refs_6_.2), channel_id=1, source_target_pairs={{0,8},{4,12},{8,0},{12,4},{1,9},{5,13},{9,1},{13,5},{2,10},{6,14},... | collective-permute-start | bytes 196616 | tf_op jit(solution)/shard_map/ppermute | solution.py:221
  4.2 8.4 %collective-permute-start.3 = (bf16[256,128]{1,0:T(8,128)(2,1)}, bf16[256,128]{1,0:T(8,128)(2,1)S(1)}, u32[]{:S(2)}, u32[]{:S(2)}) collective-permute-start(bf16[256,128]{1,0:T(8,128)(2,1)} %refs_6_.2), channel_id=1, source_target_pairs={{0,4},{4,0},{8,12},{12,8},{1,5},{5,1},{9,13},{13,9},{2,6},{6,2},{1... | collective-permute-start | bytes 196616 | tf_op jit(solution)/shard_map/ppermute | solution.py:221
  6.1 6.5 %collective-permute-start.2 = (bf16[256,128]{1,0:T(8,128)(2,1)}, bf16[256,128]{1,0:T(8,128)(2,1)S(1)}, u32[]{:S(2)}, u32[]{:S(2)}) collective-permute-start(bf16[256,128]{1,0:T(8,128)(2,1)} %refs_5_.2), channel_id=1, source_target_pairs={{0,4},{4,0},{8,12},{12,8},{1,5},{5,1},{9,13},{13,9},{2,6},{6,2},{1... | collective-permute-start | bytes 196616 | tf_op jit(solution)/shard_map/ppermute | solution.py:221
  8.7 5.0 %collective-permute-start.4 = (bf16[256,128]{1,0:T(8,128)(2,1)S(1)}, bf16[256,128]{1,0:T(8,128)(2,1)S(1)}, u32[]{:S(2)}, u32[]{:S(2)}) collective-permute-start(bf16[256,128]{1,0:T(8,128)(2,1)S(1)} %collective-permute-done.1.refs_4_), channel_id=1, source_target_pairs={{0,4},{4,0},{8,12},{12,8},{1,5},{5,1},{9,13},{13,9},{2,6},{6,2},{1... | collective-permute-start | bytes 196616 | tf_op jit(solution)/shard_map/ppermute | solution.py:221
  10.6 4.8 %collective-permute-start.5 = (bf16[256,128]{1,0:T(8,128)(2,1)S(1)}, bf16[256,128]{1,0:T(8,128)(2,1)S(1)}, u32[]{:S(2)}, u32[]{:S(2)}) collective-permute-start(bf16[256,128]{1,0:T(8,128)(2,1)S(1)} %collective-permute-done.refs_5_), channel_id=1, source_target_pairs={{0,4},{4,0},{8,12},{12,8},{1,5},{5,1},{9,13},{13,9},{2,6},{6,2},{1... | collective-permute-start | bytes 196616 | tf_op jit(solution)/shard_map/ppermute | solution.py:221

commit v25 on v12

--- a/solution.py
+++ b/solution.py
@@ -217,7 +217,6 @@
 
 def staged_attention(queries, keys, values, lengths, old_place):
     far_keys, far_values = moved(keys, 2), moved(values, 2)
-    near_keys, near_values = moved(keys, 1), moved(values, 1)
     rows, cols = queries.shape
     heads = cols // HEAD_WIDTH
     devices = lax.axis_size("seq")
@@ -265,12 +264,16 @@
 
     far_keys, *carried = lax.optimization_barrier((far_keys, *carried))
     third_keys = moved(far_keys, 1)
-    far_values, *carried = lax.optimization_barrier((far_values, *carried))
+    far_values, far_keys, *carried = lax.optimization_barrier((far_values, far_keys, *carried))
     third_values = moved(far_values, 1)
+    keys, values, far_keys, far_values, *carried = lax.optimization_barrier(
+        (keys, values, far_keys, far_values, *carried)
+    )
+    near_keys, near_values = moved(keys, 1), moved(values, 1)
     carried = add_shard(2, far_keys, far_values, carried)
-    carried = add_shard(1, near_keys, near_values, carried)
+    carried = add_shard(3, third_keys, third_values, carried)
     summed, weights = pl.pallas_call(
-        lambda *refs: weights_kernel(3, *refs),
+        lambda *refs: weights_kernel(1, *refs),
         in_specs=[VMEM_REF] * 5,
         out_specs=[VMEM_REF] * 2,
         out_shape=state[1:] + work[1:],
@@ -278,7 +281,7 @@
         compiler_params=PARAMS,
         cost_estimate=SHORT,
         name="last_weights",
-    )(*in_vmem(across, bias, *carried), third_keys)
+    )(*in_vmem(across, bias, *carried), near_keys)
     return pl.pallas_call(
         last_kernel,
         in_specs=[VMEM_REF] * 3,
@@ -291,7 +294,7 @@
         compiler_params=PARAMS,
         cost_estimate=SHORT,
         name="last_values",
-    )(*in_vmem(summed, weights), third_values)
+    )(*in_vmem(summed, weights), near_values)
 
 
 def online_kernel(heads, q_ref, k_ref, v_ref, key_pos_ref, query_pos_ref, start_ref, out_ref, peak_ref, acc_ref):

time: 16.2 us -> 19 us (1.17)
  waiting for transfers between devices: 0.03 us -> 3.15 us
  starting transfers between devices: 9.19 us -> 8.95 us
    ppermute x6, waiting for transfers between devices: 0.03 us -> 3.15 us  [moved(): lax.ppermute(value, 'seq', [(i, i ^ mask) for i in range(lax.axis_size('s...]
    ppermute x6, starting transfers between devices: 9.19 us -> 8.95 us  [moved(): lax.ppermute(value, 'seq', [(i, i ^ mask) for i in range(lax.axis_size('s...]
  transfers between devices with their start and end apart: 6 -> 6, of which waited for: 0 -> 3; matrix products, arithmetic and copies ran while one was open for 0% -> 0% of each run, Pallas kernels for 34% -> 29%
where the time goes in v25:
time: 19 us; the launch traced here: 18.9 us
  starting transfers between devices  8.95 us (47%)
  Pallas kernels  6.74 us (35%)
  waiting for transfers between devices  3.15 us (17%)
    ppermute x6, starting transfers between devices, moved(): lax.ppermute(value, 'seq', [(i, i ^ mask) for i in range(lax.axis_size('s...  8.95 us
    ppermute x6, waiting for transfers between devices, moved(): lax.ppermute(value, 'seq', [(i, i ^ mask) for i in range(lax.axis_size('s...  3.15 us
    pallas_call x1, Pallas kernels, staged_attention(): pl.pallas_call(own_kernel, in_specs=[pl.BlockSpec(memory_space=pltpu.SMEM...  2.44 us
    pallas_call x2, Pallas kernels, add_shard(): pl.pallas_call(lambda *refs: next_kernel(at, *refs), in_specs=[VMEM_REF]...  2.25 us
    pallas_call x1, Pallas kernels, staged_attention(): pl.pallas_call(last_kernel, in_specs=[VMEM_REF] * 3, out_specs=pl.BlockSp...  1.26 us
    pallas_call x1, Pallas kernels, staged_attention(): pl.pallas_call(lambda *refs: weights_kernel(1, *refs), in_specs=[VMEM_REF...  0.79 us
  transfers between devices with their start and end apart: 6, of which 3 were waited for; matrix products, arithmetic and copies ran while one was open for 0% of the time, Pallas kernels for 29%

profile of v25, /device:TPU:0, one launch (start us, length us, event | category | flops | bytes accessed | tf_op | source)
XLA Modules:
  0.0 18.9 jit_solution(10769999615471797851)
XLA Ops:
  0.0 4.0 %collective-permute-start.1 = (bf16[256,128]{1,0:T(8,128)(2,1)}, bf16[256,128]{1,0:T(8,128)(2,1)S(1)}, u32[]{:S(2)}, u32[]{:S(2)}) collective-permute-start(bf16[256,128]{1,0:T(8,128)(2,1)} %k_hbm.1), channel_id=1, source_target_pairs={{0,8},{4,12},{8,0},{12,4},{1,9},{5,13},{9,1},{13,5},{2,10},{6,14},... | collective-permute-start | bytes 196616 | tf_op jit(solution)/shard_map/ppermute | solution.py:215
  4.0 0.0 collective-permute-start
  4.1 2.4 %own_shard.1 = (bf16[8,128,256]{2,1,0:T(8,128)(2,1)S(1)}, f32[4,256,256]{2,1,0:T(8,128)S(1)}, f32[8,256]{1,0:T(8,128)S(1)}, f32[8,144,256]{2,1,0:T(8,128)S(1)}) custom-call(s32[1]{0:T(128)} %bitcast.own_ref, s32[3]{0:T(128)} %lengths_hbm.1, s32[1,128]{1,0:T(1,128)} %bitcast.2, bf16[256,1024]{1,0:T(8,128)(2,1)} %q_hbm.1, bf16[256,128]{1,0:T(8,128)(2,1)} %k_hbm.1, ...), custom_call_target="tpu_custom_call" | custom-call | tf_op jit(solution)/shard_map/own_shard/pallas_call | solution.py:233
  6.5 1.4 %collective-permute-done.1.refs_4_ = bf16[256,128]{1,0:T(8,128)(2,1)S(1)} collective-permute-done((bf16[256,128]{1,0:T(8,128)(2,1)}, bf16[256,128]{1,0:T(8,128)(2,1)S(1)}, u32[]{:S(2)}, u32[]{:S(2)}) %collective-permute-start.1) | collective-permute-done | bytes 65568 | tf_op jit(solution)/shard_map/ppermute | solution.py:215
  7.9 2.2 %collective-permute-start.2 = (bf16[256,128]{1,0:T(8,128)(2,1)S(1)}, bf16[256,128]{1,0:T(8,128)(2,1)S(1)}, u32[]{:S(2)}, u32[]{:S(2)}) collective-permute-start(bf16[256,128]{1,0:T(8,128)(2,1)S(1)} %collective-permute-done.1.refs_4_), channel_id=1, source_target_pairs={{0,4},{4,0},{8,12},{12,8},{1,5},{5,1},{9,13},{13,9},{2,6},{6,2},{1... | collective-permute-start | bytes 196616 | tf_op jit(solution)/shard_map/ppermute | solution.py:215
  10.1 0.6 %collective-permute-done.refs_5_ = bf16[256,128]{1,0:T(8,128)(2,1)S(1)} collective-permute-done((bf16[256,128]{1,0:T(8,128)(2,1)}, bf16[256,128]{1,0:T(8,128)(2,1)S(1)}, u32[]{:S(2)}, u32[]{:S(2)}) %collective-permute-start) | collective-permute-done | bytes 65568 | tf_op jit(solution)/shard_map/ppermute | solution.py:215
  10.7 0.7 %collective-permute-start.3 = (bf16[256,128]{1,0:T(8,128)(2,1)S(1)}, bf16[256,128]{1,0:T(8,128)(2,1)S(1)}, u32[]{:S(2)}, u32[]{:S(2)}) collective-permute-start(bf16[256,128]{1,0:T(8,128)(2,1)S(1)} %collective-permute-done.refs_5_), channel_id=1, source_target_pairs={{0,4},{4,0},{8,12},{12,8},{1,5},{5,1},{9,13},{13,9},{2,6},{6,2},{1... | collective-permute-start | bytes 196616 | tf_op jit(solution)/shard_map/ppermute | solution.py:215
  11.4 1.3 %collective-permute-start.4 = (bf16[256,128]{1,0:T(8,128)(2,1)}, bf16[256,128]{1,0:T(8,128)(2,1)S(1)}, u32[]{:S(2)}, u32[]{:S(2)}) collective-permute-start(bf16[256,128]{1,0:T(8,128)(2,1)} %k_hbm.1), channel_id=1, source_target_pairs={{0,4},{4,0},{8,12},{12,8},{1,5},{5,1},{9,13},{13,9},{2,6},{6,2},{1... | collective-permute-start | bytes 196616 | tf_op jit(solution)/shard_map/ppermute | solution.py:215
  12.7 0.7 %collective-permute-start.5 = (bf16[256,128]{1,0:T(8,128)(2,1)}, bf16[256,128]{1,0:T(8,128)(2,1)S(1)}, u32[]{:S(2)}, u32[]{:S(2)}) collective-permute-start(bf16[256,128]{1,0:T(8,128)(2,1)} %v_hbm.1), channel_id=1, source_target_pairs={{0,4},{4,0},{8,12},{12,8},{1,5},{5,1},{9,13},{13,9},{2,6},{6,2},{1... | collective-permute-start | bytes 196616 | tf_op jit(solution)/shard_map/ppermute | solution.py:215
  13.4 1.1 %next_shard.2 = (f32[8,256]{1,0:T(8,128)S(1)}, f32[8,144,256]{2,1,0:T(8,128)S(1)}) custom-call(bf16[8,128,256]{2,1,0:T(8,128)(2,1)S(1)} %get-tuple-element.28.refs_0_, f32[4,256,256]{2,1,0:T(8,128)S(1)} %get-tuple-element.29.refs_1_, f32[8,256]{1,0:T(8,128)S(1)} %get-tuple-element.39.refs_2_, f32[8,144,256]{2,1,0:T(8,128)S(1)} %get-tuple-element.40.refs_3_, ...), custom_call_target="tpu_custom_call" | custom-call | tf_op jit(solution)/shard_map/next_shard/pallas_call | solution.py:254
  14.5 1.1 %collective-permute-done.3.refs_5_ = bf16[256,128]{1,0:T(8,128)(2,1)S(1)} collective-permute-done((bf16[256,128]{1,0:T(8,128)(2,1)S(1)}, bf16[256,128]{1,0:T(8,128)(2,1)S(1)}, u32[]{:S(2)}, u32[]{:S(2)}) %collective-permute-start.3) | collective-permute-done | bytes 65568 | tf_op jit(solution)/shard_map/ppermute | solution.py:215
  15.7 0.0 collective-permute-done.2.refs_4_
  15.7 1.1 %next_shard.3 = (f32[8,256]{1,0:T(8,128)S(1)}, f32[8,144,256]{2,1,0:T(8,128)S(1)}) custom-call(bf16[8,128,256]{2,1,0:T(8,128)(2,1)S(1)} %get-tuple-element.28.refs_0_, f32[4,256,256]{2,1,0:T(8,128)S(1)} %get-tuple-element.29.refs_1_, f32[8,256]{1,0:T(8,128)S(1)} %get-tuple-element.43.refs_2_, f32[8,144,256]{2,1,0:T(8,128)S(1)} %get-tuple-element.44.refs_3_, ...), custom_call_target="tpu_custom_call" | custom-call | tf_op jit(solution)/shard_map/next_shard/pallas_call | solution.py:254
  16.8 0.0 collective-permute-done.4.refs_4_
  16.8 0.8 %last_weights.1 = (f32[8,144,256]{2,1,0:T(8,128)S(1)}, bf16[8,256,256]{2,1,0:T(8,128)(2,1)S(1)}) custom-call(bf16[8,128,256]{2,1,0:T(8,128)(2,1)S(1)} %get-tuple-element.28.refs_0_, f32[4,256,256]{2,1,0:T(8,128)S(1)} %get-tuple-element.29.refs_1_, f32[8,256]{1,0:T(8,128)S(1)} %get-tuple-element.45.refs_2_, f32[8,144,256]{2,1,0:T(8,128)S(1)} %get-tuple-element.46.refs_3_, ...), custom_call_target="tpu_custom_call" | custom-call | tf_op jit(solution)/shard_map/last_weights/pallas_call | solution.py:275
  17.6 0.0 collective-permute-done.5.v_ref
  17.6 1.3 %last_values.1 = bf16[256,1024]{1,0:T(8,128)(2,1)} custom-call(f32[8,144,256]{2,1,0:T(8,128)S(1)} %get-tuple-element.48.sum_ref, bf16[8,256,256]{2,1,0:T(8,128)(2,1)S(1)} %get-tuple-element.49.weight_ref, bf16[256,128]{1,0:T(8,128)(2,1)S(1)} %collective-permute-done.5.v_ref), custom_call_target="tpu_custom_call" | custom-call | tf_op jit(solution)/shard_map/last_values/pallas_call | solution.py:285
Async XLA Ops:
  0.0 7.9 %collective-permute-start.1 = (bf16[256,128]{1,0:T(8,128)(2,1)}, bf16[256,128]{1,0:T(8,128)(2,1)S(1)}, u32[]{:S(2)}, u32[]{:S(2)}) collective-permute-start(bf16[256,128]{1,0:T(8,128)(2,1)} %k_hbm.1), channel_id=1, source_target_pairs={{0,8},{4,12},{8,0},{12,4},{1,9},{5,13},{9,1},{13,5},{2,10},{6,14},... | collective-permute-start | bytes 196616 | tf_op jit(solution)/shard_map/ppermute | solution.py:215
  4.0 6.7 %collective-permute-start = (bf16[256,128]{1,0:T(8,128)(2,1)}, bf16[256,128]{1,0:T(8,128)(2,1)S(1)}, u32[]{:S(2)}, u32[]{:S(2)}) collective-permute-start(bf16[256,128]{1,0:T(8,128)(2,1)} %v_hbm.1), channel_id=1, source_target_pairs={{0,8},{4,12},{8,0},{12,4},{1,9},{5,13},{9,1},{13,5},{2,10},{6,14},... | collective-permute-start | bytes 196616 | tf_op jit(solution)/shard_map/ppermute | solution.py:215
  7.9 7.8 %collective-permute-start.2 = (bf16[256,128]{1,0:T(8,128)(2,1)S(1)}, bf16[256,128]{1,0:T(8,128)(2,1)S(1)}, u32[]{:S(2)}, u32[]{:S(2)}) collective-permute-start(bf16[256,128]{1,0:T(8,128)(2,1)S(1)} %collective-permute-done.1.refs_4_), channel_id=1, source_target_pairs={{0,4},{4,0},{8,12},{12,8},{1,5},{5,1},{9,13},{13,9},{2,6},{6,2},{1... | collective-permute-start | bytes 196616 | tf_op jit(solution)/shard_map/ppermute | solution.py:215
  10.7 5.0 %collective-permute-start.3 = (bf16[256,128]{1,0:T(8,128)(2,1)S(1)}, bf16[256,128]{1,0:T(8,128)(2,1)S(1)}, u32[]{:S(2)}, u32[]{:S(2)}) collective-permute-start(bf16[256,128]{1,0:T(8,128)(2,1)S(1)} %collective-permute-done.refs_5_), channel_id=1, source_target_pairs={{0,4},{4,0},{8,12},{12,8},{1,5},{5,1},{9,13},{13,9},{2,6},{6,2},{1... | collective-permute-start | bytes 196616 | tf_op jit(solution)/shard_map/ppermute | solution.py:215
  11.4 5.4 %collective-permute-start.4 = (bf16[256,128]{1,0:T(8,128)(2,1)}, bf16[256,128]{1,0:T(8,128)(2,1)S(1)}, u32[]{:S(2)}, u32[]{:S(2)}) collective-permute-start(bf16[256,128]{1,0:T(8,128)(2,1)} %k_hbm.1), channel_id=1, source_target_pairs={{0,4},{4,0},{8,12},{12,8},{1,5},{5,1},{9,13},{13,9},{2,6},{6,2},{1... | collective-permute-start | bytes 196616 | tf_op jit(solution)/shard_map/ppermute | solution.py:215
  12.7 4.9 %collective-permute-start.5 = (bf16[256,128]{1,0:T(8,128)(2,1)}, bf16[256,128]{1,0:T(8,128)(2,1)S(1)}, u32[]{:S(2)}, u32[]{:S(2)}) collective-permute-start(bf16[256,128]{1,0:T(8,128)(2,1)} %v_hbm.1), channel_id=1, source_target_pairs={{0,4},{4,0},{8,12},{12,8},{1,5},{5,1},{9,13},{13,9},{2,6},{6,2},{1... | collective-permute-start | bytes 196616 | tf_op jit(solution)/shard_map/ppermute | solution.py:215

commit v26 on v12

--- a/solution.py
+++ b/solution.py
@@ -133,29 +133,38 @@
     ])
 
 
-def joined(head, peak, turned, weight_ref, peak_ref, sum_ref):
-    added = jnp.dot(turned, weight_ref[head], preferred_element_type=jnp.float32)
-    return sum_ref[head] * jnp.exp2(peak_ref[head:head + 1, :] - peak) + added
-
-
-def next_kernel(
-    at, across_ref, bias_ref, peak_ref, sum_ref, k_ref, v_ref, new_peak_ref, new_sum_ref,
-    scaled_ref, weight_ref,
+def join_kernel(
+    shards, across_ref, bias_ref, old_peak_ref, old_sum_ref, *refs,
 ):
-    turned = values_down(v_ref[...])
-
-    def mix(head, peak):
-        new_peak_ref[head:head + 1, :] = peak
-        new_sum_ref[head] = joined(head, peak, turned, weight_ref, peak_ref, sum_ref)
-
-    in_stages(across_ref.shape[0], [
-        score_stage(
-            k_ref[...], across_ref, bias_ref, at, scaled_ref,
-            lambda head: peak_ref[head:head + 1, :],
-        ),
-        weight_stage(scaled_ref, weight_ref),
-        mix,
-    ])
+    peak_ref, sum_ref, scaled_ref, weight_ref = refs[-4:]
+    heads = across_ref.shape[0]
+    keys = [ref[...] for ref in refs[:-4:2]]
+    turned = [values_down(ref[...]) for ref in refs[1:-4:2]]
+
+    def peak_before(step):
+        source = old_peak_ref if step < heads else peak_ref
+        return source[step % heads:step % heads + 1, :]
+
+    def score(step, _):
+        shard, head = divmod(step, heads)
+        scores = jnp.dot(keys[shard], across_ref[head], preferred_element_type=jnp.float32)
+        scaled = scores * (HEAD_WIDTH ** -0.5 * LOG2_E) + bias_ref[shards[shard]]
+        scaled_ref[head] = scaled
+        return jnp.maximum(peak_before(step), jnp.max(scaled, axis=0, keepdims=True))
+
+    def weigh(step, peak):
+        head = step % heads
+        weight_ref[head] = jnp.exp2(scaled_ref[head] - peak).astype(jnp.bfloat16)
+        return peak
+
+    def mix(step, peak):
+        shard, head = divmod(step, heads)
+        before = (sum_ref if shard else old_sum_ref)[head] * jnp.exp2(peak_before(step) - peak)
+        added = jnp.dot(turned[shard], weight_ref[head], preferred_element_type=jnp.float32)
+        sum_ref[head] = before + added
+        peak_ref[head:head + 1, :] = peak
+
+    in_stages(heads * len(shards), [score, weigh, mix])
 
 
 def weights_kernel(
@@ -181,7 +190,7 @@
     def mix(head, _):
         added = jnp.dot(turned, weight_ref[head], preferred_element_type=jnp.float32)
         summed = sum_ref[head] + added
-        return summed[:HEAD_WIDTH] / summed[HEAD_WIDTH:HEAD_WIDTH + 1]
+        return summed[:HEAD_WIDTH] * (1.0 / summed[HEAD_WIDTH:HEAD_WIDTH + 1])
 
     def send(head, out):
         cols = slice(head * HEAD_WIDTH, (head + 1) * HEAD_WIDTH)
@@ -251,24 +260,20 @@
         name="own_shard",
     )(own.reshape(1), *in_hbm(lengths, places, queries, keys, values))
 
-    def add_shard(at, keys, values, carried):
-        return pl.pallas_call(
-            lambda *refs: next_kernel(at, *refs),
-            in_specs=[VMEM_REF] * 6,
-            out_specs=[VMEM_REF] * 2,
-            out_shape=state,
-            scratch_shapes=work,
-            compiler_params=PARAMS,
-            cost_estimate=SHORT,
-            name="next_shard",
-        )(*in_vmem(across, bias, *carried), keys, values)
-
     far_keys, *carried = lax.optimization_barrier((far_keys, *carried))
     third_keys = moved(far_keys, 1)
     far_values, *carried = lax.optimization_barrier((far_values, *carried))
     third_values = moved(far_values, 1)
-    carried = add_shard(2, far_keys, far_values, carried)
-    carried = add_shard(1, near_keys, near_values, carried)
+    carried = pl.pallas_call(
+        lambda *refs: join_kernel((2, 1), *refs),
+        in_specs=[VMEM_REF] * 8,
+        out_specs=[VMEM_REF] * 2,
+        out_shape=state,
+        scratch_shapes=work,
+        compiler_params=PARAMS,
+        cost_estimate=SHORT,
+        name="join_shards",
+    )(*in_vmem(across, bias, *carried), far_keys, far_values, near_keys, near_values)
     summed, weights = pl.pallas_call(
         lambda *refs: weights_kernel(3, *refs),
         in_specs=[VMEM_REF] * 5,

time: 16.2 us -> 16.3 us (level)
  waiting for transfers between devices: 0.03 us -> 0.39 us
  Pallas kernels: 6.73 us -> 6.56 us
    ppermute x6, waiting for transfers between devices: 0.03 us -> 0.39 us  [moved(): lax.ppermute(value, 'seq', [(i, i ^ mask) for i in range(lax.axis_size('s...]
    pallas_call x2 -> x1, Pallas kernels: 2.25 us -> 2.08 us  [staged_attention(): pl.pallas_call(lambda *refs: join_kernel((2, 1), *refs), in_specs=[VMEM_R...]
  transfers between devices with their start and end apart: 6 -> 6, of which waited for: 0 -> 1; matrix products, arithmetic and copies ran while one was open for 0% -> 0% of each run, Pallas kernels for 34% -> 33%
where the time goes in v26:
time: 16.3 us; the launch traced here: 16.2 us
  starting transfers between devices  9.19 us (56%)
  Pallas kernels  6.56 us (40%)
  waiting for transfers between devices  0.39 us (2%)
    ppermute x6, starting transfers between devices, moved(): lax.ppermute(value, 'seq', [(i, i ^ mask) for i in range(lax.axis_size('s...  9.19 us
    pallas_call x1, Pallas kernels, staged_attention(): pl.pallas_call(own_kernel, in_specs=[pl.BlockSpec(memory_space=pltpu.SMEM...  2.42 us
    pallas_call x1, Pallas kernels, staged_attention(): pl.pallas_call(lambda *refs: join_kernel((2, 1), *refs), in_specs=[VMEM_R...  2.08 us
    pallas_call x1, Pallas kernels, staged_attention(): pl.pallas_call(last_kernel, in_specs=[VMEM_REF] * 3, out_specs=pl.BlockSp...  1.26 us
    pallas_call x1, Pallas kernels, staged_attention(): pl.pallas_call(lambda *refs: weights_kernel(3, *refs), in_specs=[VMEM_REF...  0.8 us
    ppermute x6, waiting for transfers between devices, moved(): lax.ppermute(value, 'seq', [(i, i ^ mask) for i in range(lax.axis_size('s...  0.39 us
  transfers between devices with their start and end apart: 6, of which 1 were waited for; matrix products, arithmetic and copies ran while one was open for 0% of the time, Pallas kernels for 33%

profile of v26, /device:TPU:0, one launch (start us, length us, event | category | flops | bytes accessed | tf_op | source)
XLA Modules:
  0.0 16.2 jit_solution(3402681988251830483)
XLA Ops:
  0.0 4.0 %collective-permute-start.1 = (bf16[256,128]{1,0:T(8,128)(2,1)}, bf16[256,128]{1,0:T(8,128)(2,1)S(1)}, u32[]{:S(2)}, u32[]{:S(2)}) collective-permute-start(bf16[256,128]{1,0:T(8,128)(2,1)} %k_hbm.1), channel_id=1, source_target_pairs={{0,8},{4,12},{8,0},{12,4},{1,9},{5,13},{9,1},{13,5},{2,10},{6,14},... | collective-permute-start | bytes 196616 | tf_op jit(solution)/shard_map/ppermute | solution.py:224
  4.0 0.0 collective-permute-start
  4.1 1.9 %collective-permute-start.2 = (bf16[256,128]{1,0:T(8,128)(2,1)}, bf16[256,128]{1,0:T(8,128)(2,1)S(1)}, u32[]{:S(2)}, u32[]{:S(2)}) collective-permute-start(bf16[256,128]{1,0:T(8,128)(2,1)} %k_hbm.1), channel_id=1, source_target_pairs={{0,4},{4,0},{8,12},{12,8},{1,5},{5,1},{9,13},{13,9},{2,6},{6,2},{1... | collective-permute-start | bytes 196616 | tf_op jit(solution)/shard_map/ppermute | solution.py:224
  6.0 0.1 collective-permute-start.3
  6.1 2.4 %own_shard.1 = (bf16[8,128,256]{2,1,0:T(8,128)(2,1)S(1)}, f32[4,256,256]{2,1,0:T(8,128)S(1)}, f32[8,256]{1,0:T(8,128)S(1)}, f32[8,144,256]{2,1,0:T(8,128)S(1)}) custom-call(s32[1]{0:T(128)} %bitcast.own_ref, s32[3]{0:T(128)} %lengths_hbm.1, s32[1,128]{1,0:T(1,128)} %bitcast.2, bf16[256,1024]{1,0:T(8,128)(2,1)} %q_hbm.1, bf16[256,128]{1,0:T(8,128)(2,1)} %k_hbm.1, ...), custom_call_target="tpu_custom_call" | custom-call | tf_op jit(solution)/shard_map/own_shard/pallas_call | solution.py:243
  8.5 0.0 collective-permute-done.1.refs_4_
  8.5 1.9 %collective-permute-start.4 = (bf16[256,128]{1,0:T(8,128)(2,1)S(1)}, bf16[256,128]{1,0:T(8,128)(2,1)S(1)}, u32[]{:S(2)}, u32[]{:S(2)}) collective-permute-start(bf16[256,128]{1,0:T(8,128)(2,1)S(1)} %collective-permute-done.1.refs_4_), channel_id=1, source_target_pairs={{0,4},{4,0},{8,12},{12,8},{1,5},{5,1},{9,13},{13,9},{2,6},{6,2},{1... | collective-permute-start | bytes 196616 | tf_op jit(solution)/shard_map/ppermute | solution.py:224
  10.5 0.0 collective-permute-done.refs_5_
  10.5 1.2 %collective-permute-start.5 = (bf16[256,128]{1,0:T(8,128)(2,1)S(1)}, bf16[256,128]{1,0:T(8,128)(2,1)S(1)}, u32[]{:S(2)}, u32[]{:S(2)}) collective-permute-start(bf16[256,128]{1,0:T(8,128)(2,1)S(1)} %collective-permute-done.refs_5_), channel_id=1, source_target_pairs={{0,4},{4,0},{8,12},{12,8},{1,5},{5,1},{9,13},{13,9},{2,6},{6,2},{1... | collective-permute-start | bytes 196616 | tf_op jit(solution)/shard_map/ppermute | solution.py:224
  11.6 0.0 collective-permute-done.2.refs_6_
  11.6 0.4 %collective-permute-done.3.refs_7_ = bf16[256,128]{1,0:T(8,128)(2,1)S(1)} collective-permute-done((bf16[256,128]{1,0:T(8,128)(2,1)}, bf16[256,128]{1,0:T(8,128)(2,1)S(1)}, u32[]{:S(2)}, u32[]{:S(2)}) %collective-permute-start.3) | collective-permute-done | bytes 65568 | tf_op jit(solution)/shard_map/ppermute | solution.py:224
  12.0 2.1 %join_shards.1 = (f32[8,256]{1,0:T(8,128)S(1)}, f32[8,144,256]{2,1,0:T(8,128)S(1)}) custom-call(bf16[8,128,256]{2,1,0:T(8,128)(2,1)S(1)} %get-tuple-element.19.refs_0_, f32[4,256,256]{2,1,0:T(8,128)S(1)} %get-tuple-element.20.refs_1_, f32[8,256]{1,0:T(8,128)S(1)} %get-tuple-element.25.refs_2_, f32[8,144,256]{2,1,0:T(8,128)S(1)} %get-tuple-element.26.refs_3_, ...), custom_call_target="tpu_custom_call" | custom-call | tf_op jit(solution)/shard_map/join_shards/pallas_call | solution.py:267
  14.1 0.0 collective-permute-done.4.refs_4_
  14.1 0.8 %last_weights.1 = (f32[8,144,256]{2,1,0:T(8,128)S(1)}, bf16[8,256,256]{2,1,0:T(8,128)(2,1)S(1)}) custom-call(bf16[8,128,256]{2,1,0:T(8,128)(2,1)S(1)} %get-tuple-element.19.refs_0_, f32[4,256,256]{2,1,0:T(8,128)S(1)} %get-tuple-element.20.refs_1_, f32[8,256]{1,0:T(8,128)S(1)} %get-tuple-element.29.refs_2_, f32[8,144,256]{2,1,0:T(8,128)S(1)} %get-tuple-element.30.refs_3_, ...), custom_call_target="tpu_custom_call" | custom-call | tf_op jit(solution)/shard_map/last_weights/pallas_call | solution.py:277
  14.9 0.0 collective-permute-done.5.v_ref
  14.9 1.3 %last_values.1 = bf16[256,1024]{1,0:T(8,128)(2,1)} custom-call(f32[8,144,256]{2,1,0:T(8,128)S(1)} %get-tuple-element.31.sum_ref, bf16[8,256,256]{2,1,0:T(8,128)(2,1)S(1)} %get-tuple-element.32.weight_ref, bf16[256,128]{1,0:T(8,128)(2,1)S(1)} %collective-permute-done.5.v_ref), custom_call_target="tpu_custom_call" | custom-call | tf_op jit(solution)/shard_map/last_values/pallas_call | solution.py:287
Async XLA Ops:
  0.0 8.5 %collective-permute-start.1 = (bf16[256,128]{1,0:T(8,128)(2,1)}, bf16[256,128]{1,0:T(8,128)(2,1)S(1)}, u32[]{:S(2)}, u32[]{:S(2)}) collective-permute-start(bf16[256,128]{1,0:T(8,128)(2,1)} %k_hbm.1), channel_id=1, source_target_pairs={{0,8},{4,12},{8,0},{12,4},{1,9},{5,13},{9,1},{13,5},{2,10},{6,14},... | collective-permute-start | bytes 196616 | tf_op jit(solution)/shard_map/ppermute | solution.py:224
  4.0 6.4 %collective-permute-start = (bf16[256,128]{1,0:T(8,128)(2,1)}, bf16[256,128]{1,0:T(8,128)(2,1)S(1)}, u32[]{:S(2)}, u32[]{:S(2)}) collective-permute-start(bf16[256,128]{1,0:T(8,128)(2,1)} %v_hbm.1), channel_id=1, source_target_pairs={{0,8},{4,12},{8,0},{12,4},{1,9},{5,13},{9,1},{13,5},{2,10},{6,14},... | collective-permute-start | bytes 196616 | tf_op jit(solution)/shard_map/ppermute | solution.py:224
  4.1 7.6 %collective-permute-start.2 = (bf16[256,128]{1,0:T(8,128)(2,1)}, bf16[256,128]{1,0:T(8,128)(2,1)S(1)}, u32[]{:S(2)}, u32[]{:S(2)}) collective-permute-start(bf16[256,128]{1,0:T(8,128)(2,1)} %k_hbm.1), channel_id=1, source_target_pairs={{0,4},{4,0},{8,12},{12,8},{1,5},{5,1},{9,13},{13,9},{2,6},{6,2},{1... | collective-permute-start | bytes 196616 | tf_op jit(solution)/shard_map/ppermute | solution.py:224
  6.0 6.1 %collective-permute-start.3 = (bf16[256,128]{1,0:T(8,128)(2,1)}, bf16[256,128]{1,0:T(8,128)(2,1)S(1)}, u32[]{:S(2)}, u32[]{:S(2)}) collective-permute-start(bf16[256,128]{1,0:T(8,128)(2,1)} %v_hbm.1), channel_id=1, source_target_pairs={{0,4},{4,0},{8,12},{12,8},{1,5},{5,1},{9,13},{13,9},{2,6},{6,2},{1... | collective-permute-start | bytes 196616 | tf_op jit(solution)/shard_map/ppermute | solution.py:224
  8.5 5.6 %collective-permute-start.4 = (bf16[256,128]{1,0:T(8,128)(2,1)S(1)}, bf16[256,128]{1,0:T(8,128)(2,1)S(1)}, u32[]{:S(2)}, u32[]{:S(2)}) collective-permute-start(bf16[256,128]{1,0:T(8,128)(2,1)S(1)} %collective-permute-done.1.refs_4_), channel_id=1, source_target_pairs={{0,4},{4,0},{8,12},{12,8},{1,5},{5,1},{9,13},{13,9},{2,6},{6,2},{1... | collective-permute-start | bytes 196616 | tf_op jit(solution)/shard_map/ppermute | solution.py:224
  10.5 4.4 %collective-permute-start.5 = (bf16[256,128]{1,0:T(8,128)(2,1)S(1)}, bf16[256,128]{1,0:T(8,128)(2,1)S(1)}, u32[]{:S(2)}, u32[]{:S(2)}) collective-permute-start(bf16[256,128]{1,0:T(8,128)(2,1)S(1)} %collective-permute-done.refs_5_), channel_id=1, source_target_pairs={{0,4},{4,0},{8,12},{12,8},{1,5},{5,1},{9,13},{13,9},{2,6},{6,2},{1... | collective-permute-start | bytes 196616 | tf_op jit(solution)/shard_map/ppermute | solution.py:224

commit v27 on v12

--- a/solution.py
+++ b/solution.py
@@ -176,16 +176,21 @@
 
 def last_kernel(sum_ref, weight_ref, v_ref, out_ref, block_ref, sems):
     turned = values_down(v_ref[...])
+    square = (sum_ref.shape[2],) * 2
+    unit = (iota(square, 0) == iota(square, 1)).astype(jnp.float32).astype(jnp.bfloat16)
     copies = []
 
     def mix(head, _):
         added = jnp.dot(turned, weight_ref[head], preferred_element_type=jnp.float32)
         summed = sum_ref[head] + added
-        return summed[:HEAD_WIDTH] / summed[HEAD_WIDTH:HEAD_WIDTH + 1]
+        share = 1.0 / summed[HEAD_WIDTH:HEAD_WIDTH + 1]
+        return (summed[:HEAD_WIDTH] * share).astype(jnp.bfloat16)
 
     def send(head, out):
         cols = slice(head * HEAD_WIDTH, (head + 1) * HEAD_WIDTH)
-        block_ref[:, cols] = jnp.transpose(out).astype(jnp.bfloat16)
+        block_ref[:, cols] = lax.dot_general(
+            unit, out, (((1,), (1,)), ((), ())), preferred_element_type=jnp.float32
+        ).astype(jnp.bfloat16)
         copy = pltpu.make_async_copy(block_ref.at[:, cols], out_ref.at[:, cols], sems.at[head])
         copy.start()
         copies.append(copy)

time: 16.2 us -> 16.7 us (1.031)
  Pallas kernels: 6.73 us -> 7.26 us
    pallas_call x1, Pallas kernels: 1.26 us -> 1.8 us  [staged_attention(): pl.pallas_call(last_kernel, in_specs=[VMEM_REF] * 3, out_specs=pl.BlockSp...]
  transfers between devices with their start and end apart: 6 -> 6, of which waited for: 0 -> 0; matrix products, arithmetic and copies ran while one was open for 0% -> 0% of each run, Pallas kernels for 34% -> 33%
where the time goes in v27:
time: 16.7 us; the launch traced here: 16.5 us
  starting transfers between devices  9.19 us (55%)
  Pallas kernels  7.26 us (43%)
    ppermute x6, starting transfers between devices, moved(): lax.ppermute(value, 'seq', [(i, i ^ mask) for i in range(lax.axis_size('s...  9.19 us
    pallas_call x1, Pallas kernels, staged_attention(): pl.pallas_call(own_kernel, in_specs=[pl.BlockSpec(memory_space=pltpu.SMEM...  2.42 us
    pallas_call x2, Pallas kernels, add_shard(): pl.pallas_call(lambda *refs: next_kernel(at, *refs), in_specs=[VMEM_REF]...  2.25 us
    pallas_call x1, Pallas kernels, staged_attention(): pl.pallas_call(last_kernel, in_specs=[VMEM_REF] * 3, out_specs=pl.BlockSp...  1.8 us
    pallas_call x1, Pallas kernels, staged_attention(): pl.pallas_call(lambda *refs: weights_kernel(3, *refs), in_specs=[VMEM_REF...  0.8 us
  transfers between devices with their start and end apart: 6, of which 0 were waited for; matrix products, arithmetic and copies ran while one was open for 0% of the time, Pallas kernels for 33%

profile of v27, /device:TPU:0, one launch (start us, length us, event | category | flops | bytes accessed | tf_op | source)
XLA Modules:
  0.0 16.5 jit_solution(4727363348137563790)
XLA Ops:
  0.0 4.0 %collective-permute-start.1 = (bf16[256,128]{1,0:T(8,128)(2,1)}, bf16[256,128]{1,0:T(8,128)(2,1)S(1)}, u32[]{:S(2)}, u32[]{:S(2)}) collective-permute-start(bf16[256,128]{1,0:T(8,128)(2,1)} %k_hbm.1), channel_id=1, source_target_pairs={{0,8},{4,12},{8,0},{12,4},{1,9},{5,13},{9,1},{13,5},{2,10},{6,14},... | collective-permute-start | bytes 196616 | tf_op jit(solution)/shard_map/ppermute | solution.py:220
  4.0 0.0 collective-permute-start
  4.1 1.9 %collective-permute-start.2 = (bf16[256,128]{1,0:T(8,128)(2,1)}, bf16[256,128]{1,0:T(8,128)(2,1)S(1)}, u32[]{:S(2)}, u32[]{:S(2)}) collective-permute-start(bf16[256,128]{1,0:T(8,128)(2,1)} %k_hbm.1), channel_id=1, source_target_pairs={{0,4},{4,0},{8,12},{12,8},{1,5},{5,1},{9,13},{13,9},{2,6},{6,2},{1... | collective-permute-start | bytes 196616 | tf_op jit(solution)/shard_map/ppermute | solution.py:220
  6.0 0.1 collective-permute-start.3
  6.1 2.4 %own_shard.1 = (bf16[8,128,256]{2,1,0:T(8,128)(2,1)S(1)}, f32[4,256,256]{2,1,0:T(8,128)S(1)}, f32[8,256]{1,0:T(8,128)S(1)}, f32[8,144,256]{2,1,0:T(8,128)S(1)}) custom-call(s32[1]{0:T(128)} %bitcast.own_ref, s32[3]{0:T(128)} %lengths_hbm.1, s32[1,128]{1,0:T(1,128)} %bitcast.2, bf16[256,1024]{1,0:T(8,128)(2,1)} %q_hbm.1, bf16[256,128]{1,0:T(8,128)(2,1)} %k_hbm.1, ...), custom_call_target="tpu_custom_call" | custom-call | tf_op jit(solution)/shard_map/own_shard/pallas_call | solution.py:239
  8.5 0.0 collective-permute-done.1.refs_4_
  8.5 1.9 %collective-permute-start.4 = (bf16[256,128]{1,0:T(8,128)(2,1)S(1)}, bf16[256,128]{1,0:T(8,128)(2,1)S(1)}, u32[]{:S(2)}, u32[]{:S(2)}) collective-permute-start(bf16[256,128]{1,0:T(8,128)(2,1)S(1)} %collective-permute-done.1.refs_4_), channel_id=1, source_target_pairs={{0,4},{4,0},{8,12},{12,8},{1,5},{5,1},{9,13},{13,9},{2,6},{6,2},{1... | collective-permute-start | bytes 196616 | tf_op jit(solution)/shard_map/ppermute | solution.py:220
  10.5 0.0 collective-permute-done.refs_5_
  10.5 1.2 %collective-permute-start.5 = (bf16[256,128]{1,0:T(8,128)(2,1)S(1)}, bf16[256,128]{1,0:T(8,128)(2,1)S(1)}, u32[]{:S(2)}, u32[]{:S(2)}) collective-permute-start(bf16[256,128]{1,0:T(8,128)(2,1)S(1)} %collective-permute-done.refs_5_), channel_id=1, source_target_pairs={{0,4},{4,0},{8,12},{12,8},{1,5},{5,1},{9,13},{13,9},{2,6},{6,2},{1... | collective-permute-start | bytes 196616 | tf_op jit(solution)/shard_map/ppermute | solution.py:220
  11.6 1.1 %next_shard.2 = (f32[8,256]{1,0:T(8,128)S(1)}, f32[8,144,256]{2,1,0:T(8,128)S(1)}) custom-call(bf16[8,128,256]{2,1,0:T(8,128)(2,1)S(1)} %get-tuple-element.21.refs_0_, f32[4,256,256]{2,1,0:T(8,128)S(1)} %get-tuple-element.22.refs_1_, f32[8,256]{1,0:T(8,128)S(1)} %get-tuple-element.27.refs_2_, f32[8,144,256]{2,1,0:T(8,128)S(1)} %get-tuple-element.28.refs_3_, ...), custom_call_target="tpu_custom_call" | custom-call | tf_op jit(solution)/shard_map/next_shard/pallas_call | solution.py:260
  12.8 0.0 collective-permute-done.2.refs_4_
  12.8 0.0 collective-permute-done.3.refs_5_
  12.8 1.1 %next_shard.3 = (f32[8,256]{1,0:T(8,128)S(1)}, f32[8,144,256]{2,1,0:T(8,128)S(1)}) custom-call(bf16[8,128,256]{2,1,0:T(8,128)(2,1)S(1)} %get-tuple-element.21.refs_0_, f32[4,256,256]{2,1,0:T(8,128)S(1)} %get-tuple-element.22.refs_1_, f32[8,256]{1,0:T(8,128)S(1)} %get-tuple-element.31.refs_2_, f32[8,144,256]{2,1,0:T(8,128)S(1)} %get-tuple-element.32.refs_3_, ...), custom_call_target="tpu_custom_call" | custom-call | tf_op jit(solution)/shard_map/next_shard/pallas_call | solution.py:260
  13.9 0.0 collective-permute-done.4.refs_4_
  13.9 0.8 %last_weights.1 = (f32[8,144,256]{2,1,0:T(8,128)S(1)}, bf16[8,256,256]{2,1,0:T(8,128)(2,1)S(1)}) custom-call(bf16[8,128,256]{2,1,0:T(8,128)(2,1)S(1)} %get-tuple-element.21.refs_0_, f32[4,256,256]{2,1,0:T(8,128)S(1)} %get-tuple-element.22.refs_1_, f32[8,256]{1,0:T(8,128)S(1)} %get-tuple-element.33.refs_2_, f32[8,144,256]{2,1,0:T(8,128)S(1)} %get-tuple-element.34.refs_3_, ...), custom_call_target="tpu_custom_call" | custom-call | tf_op jit(solution)/shard_map/last_weights/pallas_call | solution.py:277
  14.7 0.0 collective-permute-done.5.v_ref
  14.8 1.8 %last_values.1 = bf16[256,1024]{1,0:T(8,128)(2,1)} custom-call(f32[8,144,256]{2,1,0:T(8,128)S(1)} %get-tuple-element.35.sum_ref, bf16[8,256,256]{2,1,0:T(8,128)(2,1)S(1)} %get-tuple-element.36.weight_ref, bf16[256,128]{1,0:T(8,128)(2,1)S(1)} %collective-permute-done.5.v_ref), custom_call_target="tpu_custom_call" | custom-call | tf_op jit(solution)/shard_map/last_values/pallas_call | solution.py:287
Async XLA Ops:
  0.0 8.5 %collective-permute-start.1 = (bf16[256,128]{1,0:T(8,128)(2,1)}, bf16[256,128]{1,0:T(8,128)(2,1)S(1)}, u32[]{:S(2)}, u32[]{:S(2)}) collective-permute-start(bf16[256,128]{1,0:T(8,128)(2,1)} %k_hbm.1), channel_id=1, source_target_pairs={{0,8},{4,12},{8,0},{12,4},{1,9},{5,13},{9,1},{13,5},{2,10},{6,14},... | collective-permute-start | bytes 196616 | tf_op jit(solution)/shard_map/ppermute | solution.py:220
  4.0 6.4 %collective-permute-start = (bf16[256,128]{1,0:T(8,128)(2,1)}, bf16[256,128]{1,0:T(8,128)(2,1)S(1)}, u32[]{:S(2)}, u32[]{:S(2)}) collective-permute-start(bf16[256,128]{1,0:T(8,128)(2,1)} %v_hbm.1), channel_id=1, source_target_pairs={{0,8},{4,12},{8,0},{12,4},{1,9},{5,13},{9,1},{13,5},{2,10},{6,14},... | collective-permute-start | bytes 196616 | tf_op jit(solution)/shard_map/ppermute | solution.py:220
  4.1 8.7 %collective-permute-start.2 = (bf16[256,128]{1,0:T(8,128)(2,1)}, bf16[256,128]{1,0:T(8,128)(2,1)S(1)}, u32[]{:S(2)}, u32[]{:S(2)}) collective-permute-start(bf16[256,128]{1,0:T(8,128)(2,1)} %k_hbm.1), channel_id=1, source_target_pairs={{0,4},{4,0},{8,12},{12,8},{1,5},{5,1},{9,13},{13,9},{2,6},{6,2},{1... | collective-permute-start | bytes 196616 | tf_op jit(solution)/shard_map/ppermute | solution.py:220
  6.0 6.8 %collective-permute-start.3 = (bf16[256,128]{1,0:T(8,128)(2,1)}, bf16[256,128]{1,0:T(8,128)(2,1)S(1)}, u32[]{:S(2)}, u32[]{:S(2)}) collective-permute-start(bf16[256,128]{1,0:T(8,128)(2,1)} %v_hbm.1), channel_id=1, source_target_pairs={{0,4},{4,0},{8,12},{12,8},{1,5},{5,1},{9,13},{13,9},{2,6},{6,2},{1... | collective-permute-start | bytes 196616 | tf_op jit(solution)/shard_map/ppermute | solution.py:220
  8.5 5.4 %collective-permute-start.4 = (bf16[256,128]{1,0:T(8,128)(2,1)S(1)}, bf16[256,128]{1,0:T(8,128)(2,1)S(1)}, u32[]{:S(2)}, u32[]{:S(2)}) collective-permute-start(bf16[256,128]{1,0:T(8,128)(2,1)S(1)} %collective-permute-done.1.refs_4_), channel_id=1, source_target_pairs={{0,4},{4,0},{8,12},{12,8},{1,5},{5,1},{9,13},{13,9},{2,6},{6,2},{1... | collective-permute-start | bytes 196616 | tf_op jit(solution)/shard_map/ppermute | solution.py:220
  10.5 4.3 %collective-permute-start.5 = (bf16[256,128]{1,0:T(8,128)(2,1)S(1)}, bf16[256,128]{1,0:T(8,128)(2,1)S(1)}, u32[]{:S(2)}, u32[]{:S(2)}) collective-permute-start(bf16[256,128]{1,0:T(8,128)(2,1)S(1)} %collective-permute-done.refs_5_), channel_id=1, source_target_pairs={{0,4},{4,0},{8,12},{12,8},{1,5},{5,1},{9,13},{13,9},{2,6},{6,2},{1... | collective-permute-start | bytes 196616 | tf_op jit(solution)/shard_map/ppermute | solution.py:220

commit v28 on v16

--- a/solution.py
+++ b/solution.py
@@ -8,7 +8,6 @@
 HEAD_WIDTH = 128
 LOG2_E = 1.4426950408889634
 NEG_FILL = -1e30
-ONES = 16
 
 
 def block_places(lengths, old_place, own_index, row_count, key_count):
@@ -64,11 +63,6 @@
     return jnp.where((key_pos >= starts) & (key_pos <= query_pos), 0.0, NEG_FILL)
 
 
-def values_down(values):
-    turned = jnp.transpose(values)
-    return jnp.concatenate([turned, jnp.ones((ONES, values.shape[0]), jnp.bfloat16)], axis=0)
-
-
 def in_stages(heads, stages):
     results = [{} for _ in stages]
     for step in range(heads + len(stages) - 1):
@@ -92,15 +86,16 @@
 
 def weight_stage(scaled_ref, weight_ref):
     def stage(head, peak):
-        weight_ref[head] = jnp.exp2(scaled_ref[head] - peak).astype(jnp.bfloat16)
-        return peak
+        weights = jnp.exp2(scaled_ref[head] - peak)
+        weight_ref[head] = weights.astype(jnp.bfloat16)
+        return peak, jnp.sum(weights, axis=0, keepdims=True)
 
     return stage
 
 
 def own_kernel(
     own_ref, lengths_hbm, places_hbm, q_hbm, k_hbm, v_hbm,
-    across_ref, bias_ref, peak_ref, sum_ref,
+    across_ref, bias_ref, peak_ref, total_ref, sum_ref,
     lengths_ref, places_ref, q_ref, k_ref, v_ref, scaled_ref, weight_ref, sems,
 ):
     moves = (
@@ -117,7 +112,7 @@
     keys = k_ref[...]
     query_pos, starts = query_places(own, lengths_ref, places, rows)
     bias_ref[0] = mask_table(own, query_pos, starts, places)
-    turned = values_down(v_ref[...])
+    turned = jnp.transpose(v_ref[...])
 
     def turn(head, _):
         q = q_ref[:, head * HEAD_WIDTH:(head + 1) * HEAD_WIDTH]
@@ -125,8 +120,8 @@
         if 0 < head < bias_ref.shape[0]:
             bias_ref[head] = mask_table(own ^ head, query_pos, starts, places)
 
-    def mix(head, peak):
-        peak_ref[head:head + 1, :] = peak
+    def mix(head, reached):
+        peak_ref[head:head + 1, :], total_ref[head:head + 1, :] = reached
         sum_ref[head] = jnp.dot(turned, weight_ref[head], preferred_element_type=jnp.float32)
 
     in_stages(heads, [
@@ -137,20 +132,20 @@
     ])
 
 
-def joined(head, peak, turned, weight_ref, peak_ref, sum_ref):
-    added = jnp.dot(turned, weight_ref[head], preferred_element_type=jnp.float32)
-    return sum_ref[head] * jnp.exp2(peak_ref[head:head + 1, :] - peak) + added
-
-
 def next_kernel(
-    at, across_ref, bias_ref, peak_ref, sum_ref, k_ref, v_ref, new_peak_ref, new_sum_ref,
-    scaled_ref, weight_ref,
+    at, across_ref, bias_ref, peak_ref, total_ref, sum_ref, k_ref, v_ref,
+    new_peak_ref, new_total_ref, new_sum_ref, scaled_ref, weight_ref,
 ):
-    turned = values_down(v_ref[...])
-
-    def mix(head, peak):
-        new_peak_ref[head:head + 1, :] = peak
-        new_sum_ref[head] = joined(head, peak, turned, weight_ref, peak_ref, sum_ref)
+    turned = jnp.transpose(v_ref[...])
+
+    def mix(head, reached):
+        peak, total = reached
+        row = slice(head, head + 1)
+        factor = jnp.exp2(peak_ref[row, :] - peak)
+        new_peak_ref[row, :] = peak
+        new_total_ref[row, :] = total_ref[row, :] * factor + total
+        added = jnp.dot(turned, weight_ref[head], preferred_element_type=jnp.float32)
+        new_sum_ref[head] = sum_ref[head] * factor + added
 
     in_stages(across_ref.shape[0], [
         score_stage(
@@ -163,18 +158,16 @@
 
 
 def weights_kernel(
-    at, across_ref, bias_ref, peak_ref, sum_ref, k_ref,
+    at, across_ref, bias_ref, peak_ref, total_ref, sum_ref, k_ref,
     new_sum_ref, weight_ref, share_ref, scaled_ref,
 ):
-    ones = jnp.ones((ONES, k_ref.shape[0]), jnp.bfloat16)
-
-    def rescale(head, peak):
-        factor = jnp.exp2(peak_ref[head:head + 1, :] - peak)
-        added = jnp.dot(ones, weight_ref[head], preferred_element_type=jnp.float32)
-        total = sum_ref[head, HEAD_WIDTH:HEAD_WIDTH + 1, :] * factor + added[:1]
-        share = 1.0 / total
-        share_ref[head:head + 1, :] = share
-        new_sum_ref[head] = sum_ref[head, :HEAD_WIDTH, :] * (factor * share)
+    def rescale(head, reached):
+        peak, total = reached
+        row = slice(head, head + 1)
+        factor = jnp.exp2(peak_ref[row, :] - peak)
+        share = 1.0 / (total_ref[row, :] * factor + total)
+        share_ref[row, :] = share
+        new_sum_ref[head] = sum_ref[head] * (factor * share)
 
     in_stages(across_ref.shape[0], [
         score_stage(
@@ -236,7 +229,8 @@
     places = old_place.reshape(1, -1)
     state = [
         pltpu.VMEM((heads, rows), jnp.float32),
-        pltpu.VMEM((heads, HEAD_WIDTH + ONES, rows), jnp.float32),
+        pltpu.VMEM((heads, rows), jnp.float32),
+        pltpu.VMEM((heads, HEAD_WIDTH, rows), jnp.float32),
     ]
     work = [
         pltpu.VMEM((heads, rows, rows), jnp.float32),
@@ -245,7 +239,7 @@
     across, bias, *carried = pl.pallas_call(
         own_kernel,
         in_specs=[pl.BlockSpec(memory_space=pltpu.SMEM)] + [HBM_REF] * 5,
-        out_specs=[VMEM_REF] * 4,
+        out_specs=[VMEM_REF] * 5,
         out_shape=[
             pltpu.VMEM((heads, HEAD_WIDTH, rows), jnp.bfloat16),
             pltpu.VMEM((devices, rows, rows), jnp.float32),
@@ -265,8 +259,8 @@
     def add_shard(at, keys, values, carried):
         return pl.pallas_call(
             lambda *refs: next_kernel(at, *refs),
-            in_specs=[VMEM_REF] * 6,
-            out_specs=[VMEM_REF] * 2,
+            in_specs=[VMEM_REF] * 7,
+            out_specs=[VMEM_REF] * 3,
             out_shape=state,
             scratch_shapes=work,
             compiler_params=PARAMS,
@@ -283,7 +277,7 @@
     scaled_sum = pltpu.VMEM((heads, HEAD_WIDTH, rows), jnp.float32)
     last = pl.pallas_call(
         lambda *refs: weights_kernel(3, *refs),
-        in_specs=[VMEM_REF] * 5,
+        in_specs=[VMEM_REF] * 6,
         out_specs=[VMEM_REF] * 3,
         out_shape=[scaled_sum, work[1], state[0]],
         scratch_shapes=work[:1],

time: 16.3 us -> 16.1 us (0.988)
    pallas_call x1, Pallas kernels: 1.06 us -> 0.83 us  [staged_attention(): pl.pallas_call(lambda *refs: weights_kernel(3, *refs), in_specs=[VMEM_REF...]
where the time goes in v28:
time: 16.1 us; the launch traced here: 16 us
  starting transfers between devices  9.18 us (57%)
  Pallas kernels  6.69 us (42%)
    ppermute x6, starting transfers between devices, moved(): lax.ppermute(value, 'seq', [(i, i ^ mask) for i in range(lax.axis_size('s...  9.18 us
    pallas_call x1, Pallas kernels, staged_attention(): pl.pallas_call(own_kernel, in_specs=[pl.BlockSpec(memory_space=pltpu.SMEM...  2.43 us
    pallas_call x2, Pallas kernels, add_shard(): pl.pallas_call(lambda *refs: next_kernel(at, *refs), in_specs=[VMEM_REF]...  2.29 us
    pallas_call x1, Pallas kernels, staged_attention(): pl.pallas_call(last_kernel, in_specs=[VMEM_REF] * 4, out_specs=pl.BlockSp...  1.14 us
    pallas_call x1, Pallas kernels, staged_attention(): pl.pallas_call(lambda *refs: weights_kernel(3, *refs), in_specs=[VMEM_REF...  0.83 us
  transfers between devices with their start and end apart: 6, of which 0 were waited for; matrix products, arithmetic and copies ran while one was open for 0% of the time, Pallas kernels for 35%

profile of v28, /device:TPU:0, one launch (start us, length us, event | category | flops | bytes accessed | tf_op | source)
XLA Modules:
  0.0 16.0 jit_solution(12564418923496247828)
XLA Ops:
  0.0 4.0 %collective-permute-start.1 = (bf16[256,128]{1,0:T(8,128)(2,1)}, bf16[256,128]{1,0:T(8,128)(2,1)S(1)}, u32[]{:S(2)}, u32[]{:S(2)}) collective-permute-start(bf16[256,128]{1,0:T(8,128)(2,1)} %k_hbm.1), channel_id=1, source_target_pairs={{0,8},{4,12},{8,0},{12,4},{1,9},{5,13},{9,1},{13,5},{2,10},{6,14},... | collective-permute-start | bytes 196616 | tf_op jit(solution)/shard_map/ppermute | solution.py:219
  4.0 0.0 collective-permute-start
  4.1 1.9 %collective-permute-start.2 = (bf16[256,128]{1,0:T(8,128)(2,1)}, bf16[256,128]{1,0:T(8,128)(2,1)S(1)}, u32[]{:S(2)}, u32[]{:S(2)}) collective-permute-start(bf16[256,128]{1,0:T(8,128)(2,1)} %k_hbm.1), channel_id=1, source_target_pairs={{0,4},{4,0},{8,12},{12,8},{1,5},{5,1},{9,13},{13,9},{2,6},{6,2},{1... | collective-permute-start | bytes 196616 | tf_op jit(solution)/shard_map/ppermute | solution.py:219
  6.0 0.1 collective-permute-start.3
  6.1 2.4 %own_shard.1 = (bf16[8,128,256]{2,1,0:T(8,128)(2,1)S(1)}, f32[4,256,256]{2,1,0:T(8,128)S(1)}, f32[8,256]{1,0:T(8,128)S(1)}, f32[8,256]{1,0:T(8,128)S(1)}, f32[8,128,256]{2,1,0:T(8,128)S(1)}) custom-call(s32[1]{0:T(128)} %bitcast.own_ref, s32[3]{0:T(128)} %lengths_hbm.1, s32[1,128]{1,0:T(1,128)} %bitcast.2, bf16[256,1024]{1,0:T(8,128)(2,1)} %q_hbm.1, ...), custom_call_target="tpu_custom_call" | custom-call | tf_op jit(solution)/shard_map/own_shard/pallas_call | solution.py:239
  8.5 0.0 collective-permute-done.1.refs_5_
  8.6 1.9 %collective-permute-start.4 = (bf16[256,128]{1,0:T(8,128)(2,1)S(1)}, bf16[256,128]{1,0:T(8,128)(2,1)S(1)}, u32[]{:S(2)}, u32[]{:S(2)}) collective-permute-start(bf16[256,128]{1,0:T(8,128)(2,1)S(1)} %collective-permute-done.1.refs_5_), channel_id=1, source_target_pairs={{0,4},{4,0},{8,12},{12,8},{1,5},{5,1},{9,13},{13,9},{2,6},{6,2},{1... | collective-permute-start | bytes 196616 | tf_op jit(solution)/shard_map/ppermute | solution.py:219
  10.5 0.0 collective-permute-done.refs_6_
  10.5 1.1 %collective-permute-start.5 = (bf16[256,128]{1,0:T(8,128)(2,1)S(1)}, bf16[256,128]{1,0:T(8,128)(2,1)S(1)}, u32[]{:S(2)}, u32[]{:S(2)}) collective-permute-start(bf16[256,128]{1,0:T(8,128)(2,1)S(1)} %collective-permute-done.refs_6_), channel_id=1, source_target_pairs={{0,4},{4,0},{8,12},{12,8},{1,5},{5,1},{9,13},{13,9},{2,6},{6,2},{1... | collective-permute-start | bytes 196616 | tf_op jit(solution)/shard_map/ppermute | solution.py:219
  11.6 1.1 %next_shard.2 = (f32[8,256]{1,0:T(8,128)S(1)}, f32[8,256]{1,0:T(8,128)S(1)}, f32[8,128,256]{2,1,0:T(8,128)S(1)}) custom-call(bf16[8,128,256]{2,1,0:T(8,128)(2,1)S(1)} %get-tuple-element.27.refs_0_, f32[4,256,256]{2,1,0:T(8,128)S(1)} %get-tuple-element.28.refs_1_, f32[8,256]{1,0:T(8,128)S(1)} %get-tuple-element.35.refs_2_, ...), custom_call_target="tpu_custom_call" | custom-call | tf_op jit(solution)/shard_map/next_shard/pallas_call | solution.py:260
  12.8 0.0 collective-permute-done.2.refs_5_
  12.8 0.0 collective-permute-done.3.refs_6_
  12.8 1.1 %next_shard.3 = (f32[8,256]{1,0:T(8,128)S(1)}, f32[8,256]{1,0:T(8,128)S(1)}, f32[8,128,256]{2,1,0:T(8,128)S(1)}) custom-call(bf16[8,128,256]{2,1,0:T(8,128)(2,1)S(1)} %get-tuple-element.27.refs_0_, f32[4,256,256]{2,1,0:T(8,128)S(1)} %get-tuple-element.28.refs_1_, f32[8,256]{1,0:T(8,128)S(1)} %get-tuple-element.40.refs_2_, ...), custom_call_target="tpu_custom_call" | custom-call | tf_op jit(solution)/shard_map/next_shard/pallas_call | solution.py:260
  14.0 0.0 collective-permute-done.4.refs_5_
  14.0 0.8 %last_weights.1 = (f32[8,128,256]{2,1,0:T(8,128)S(1)}, bf16[8,256,256]{2,1,0:T(8,128)(2,1)S(1)}, f32[8,256]{1,0:T(8,128)S(1)}) custom-call(bf16[8,128,256]{2,1,0:T(8,128)(2,1)S(1)} %get-tuple-element.27.refs_0_, f32[4,256,256]{2,1,0:T(8,128)S(1)} %get-tuple-element.28.refs_1_, f32[8,256]{1,0:T(8,128)S(1)} %get-tuple-element.43.refs_2_, ...), custom_call_target="tpu_custom_call" | custom-call | tf_op jit(solution)/shard_map/last_weights/pallas_call | solution.py:278
  14.8 0.0 collective-permute-done.5.v_ref
  14.8 1.1 %last_values.1 = bf16[256,1024]{1,0:T(8,128)(2,1)} custom-call(f32[8,128,256]{2,1,0:T(8,128)S(1)} %get-tuple-element.46.sum_ref, bf16[8,256,256]{2,1,0:T(8,128)(2,1)S(1)} %get-tuple-element.47.weight_ref, f32[8,256]{1,0:T(8,128)S(1)} %get-tuple-element.48.share_ref, bf16[256,128]{1,0:T(8,128)(2,1)S(1)} %collective-permute-done.5.v_ref), custom_call_target="tpu_custom_call" | custom-call | tf_op jit(solution)/shard_map/last_values/pallas_call | solution.py:288
Async XLA Ops:
  0.0 8.5 %collective-permute-start.1 = (bf16[256,128]{1,0:T(8,128)(2,1)}, bf16[256,128]{1,0:T(8,128)(2,1)S(1)}, u32[]{:S(2)}, u32[]{:S(2)}) collective-permute-start(bf16[256,128]{1,0:T(8,128)(2,1)} %k_hbm.1), channel_id=1, source_target_pairs={{0,8},{4,12},{8,0},{12,4},{1,9},{5,13},{9,1},{13,5},{2,10},{6,14},... | collective-permute-start | bytes 196616 | tf_op jit(solution)/shard_map/ppermute | solution.py:219
  4.0 6.5 %collective-permute-start = (bf16[256,128]{1,0:T(8,128)(2,1)}, bf16[256,128]{1,0:T(8,128)(2,1)S(1)}, u32[]{:S(2)}, u32[]{:S(2)}) collective-permute-start(bf16[256,128]{1,0:T(8,128)(2,1)} %v_hbm.1), channel_id=1, source_target_pairs={{0,8},{4,12},{8,0},{12,4},{1,9},{5,13},{9,1},{13,5},{2,10},{6,14},... | collective-permute-start | bytes 196616 | tf_op jit(solution)/shard_map/ppermute | solution.py:219
  4.1 8.7 %collective-permute-start.2 = (bf16[256,128]{1,0:T(8,128)(2,1)}, bf16[256,128]{1,0:T(8,128)(2,1)S(1)}, u32[]{:S(2)}, u32[]{:S(2)}) collective-permute-start(bf16[256,128]{1,0:T(8,128)(2,1)} %k_hbm.1), channel_id=1, source_target_pairs={{0,4},{4,0},{8,12},{12,8},{1,5},{5,1},{9,13},{13,9},{2,6},{6,2},{1... | collective-permute-start | bytes 196616 | tf_op jit(solution)/shard_map/ppermute | solution.py:219
  6.0 6.9 %collective-permute-start.3 = (bf16[256,128]{1,0:T(8,128)(2,1)}, bf16[256,128]{1,0:T(8,128)(2,1)S(1)}, u32[]{:S(2)}, u32[]{:S(2)}) collective-permute-start(bf16[256,128]{1,0:T(8,128)(2,1)} %v_hbm.1), channel_id=1, source_target_pairs={{0,4},{4,0},{8,12},{12,8},{1,5},{5,1},{9,13},{13,9},{2,6},{6,2},{1... | collective-permute-start | bytes 196616 | tf_op jit(solution)/shard_map/ppermute | solution.py:219
  8.6 5.4 %collective-permute-start.4 = (bf16[256,128]{1,0:T(8,128)(2,1)S(1)}, bf16[256,128]{1,0:T(8,128)(2,1)S(1)}, u32[]{:S(2)}, u32[]{:S(2)}) collective-permute-start(bf16[256,128]{1,0:T(8,128)(2,1)S(1)} %collective-permute-done.1.refs_5_), channel_id=1, source_target_pairs={{0,4},{4,0},{8,12},{12,8},{1,5},{5,1},{9,13},{13,9},{2,6},{6,2},{1... | collective-permute-start | bytes 196616 | tf_op jit(solution)/shard_map/ppermute | solution.py:219
  10.5 4.3 %collective-permute-start.5 = (bf16[256,128]{1,0:T(8,128)(2,1)S(1)}, bf16[256,128]{1,0:T(8,128)(2,1)S(1)}, u32[]{:S(2)}, u32[]{:S(2)}) collective-permute-start(bf16[256,128]{1,0:T(8,128)(2,1)S(1)} %collective-permute-done.refs_6_), channel_id=1, source_target_pairs={{0,4},{4,0},{8,12},{12,8},{1,5},{5,1},{9,13},{13,9},{2,6},{6,2},{1... | collective-permute-start | bytes 196616 | tf_op jit(solution)/shard_map/ppermute | solution.py:219

commit v29 on v28

--- a/solution.py
+++ b/solution.py
@@ -73,30 +73,26 @@
                 results[late][head] = stage(head, before)
 
 
-def score_stage(keys, across_ref, bias_ref, at, scaled_ref, old_peak):
+def score_stage(keys, across_ref, bias_ref, at, old_peak):
     def stage(head, _):
         scores = jnp.dot(keys, across_ref[head], preferred_element_type=jnp.float32)
         scaled = scores * (HEAD_WIDTH ** -0.5 * LOG2_E) + bias_ref[at]
-        scaled_ref[head] = scaled
         peak = jnp.max(scaled, axis=0, keepdims=True)
-        return peak if old_peak is None else jnp.maximum(old_peak(head), peak)
+        return scaled, peak if old_peak is None else jnp.maximum(old_peak(head), peak)
 
     return stage
 
 
-def weight_stage(scaled_ref, weight_ref):
-    def stage(head, peak):
-        weights = jnp.exp2(scaled_ref[head] - peak)
-        weight_ref[head] = weights.astype(jnp.bfloat16)
-        return peak, jnp.sum(weights, axis=0, keepdims=True)
-
-    return stage
+def weight_stage(head, before):
+    scaled, peak = before
+    weights = jnp.exp2(scaled - peak)
+    return peak, jnp.sum(weights, axis=0, keepdims=True), weights.astype(jnp.bfloat16)
 
 
 def own_kernel(
     own_ref, lengths_hbm, places_hbm, q_hbm, k_hbm, v_hbm,
     across_ref, bias_ref, peak_ref, total_ref, sum_ref,
-    lengths_ref, places_ref, q_ref, k_ref, v_ref, scaled_ref, weight_ref, sems,
+    lengths_ref, places_ref, q_ref, k_ref, v_ref, sems,
 ):
     moves = (
         (lengths_hbm, lengths_ref), (places_hbm, places_ref),
@@ -121,48 +117,48 @@
             bias_ref[head] = mask_table(own ^ head, query_pos, starts, places)
 
     def mix(head, reached):
-        peak_ref[head:head + 1, :], total_ref[head:head + 1, :] = reached
-        sum_ref[head] = jnp.dot(turned, weight_ref[head], preferred_element_type=jnp.float32)
+        peak_ref[head:head + 1, :], total_ref[head:head + 1, :], weights = reached
+        sum_ref[head] = jnp.dot(turned, weights, preferred_element_type=jnp.float32)
 
     in_stages(heads, [
         turn,
-        score_stage(keys, across_ref, bias_ref, 0, scaled_ref, None),
-        weight_stage(scaled_ref, weight_ref),
+        score_stage(keys, across_ref, bias_ref, 0, None),
+        weight_stage,
         mix,
     ])
 
 
 def next_kernel(
     at, across_ref, bias_ref, peak_ref, total_ref, sum_ref, k_ref, v_ref,
-    new_peak_ref, new_total_ref, new_sum_ref, scaled_ref, weight_ref,
+    new_peak_ref, new_total_ref, new_sum_ref,
 ):
     turned = jnp.transpose(v_ref[...])
 
     def mix(head, reached):
-        peak, total = reached
+        peak, total, weights = reached
         row = slice(head, head + 1)
         factor = jnp.exp2(peak_ref[row, :] - peak)
         new_peak_ref[row, :] = peak
         new_total_ref[row, :] = total_ref[row, :] * factor + total
-        added = jnp.dot(turned, weight_ref[head], preferred_element_type=jnp.float32)
+        added = jnp.dot(turned, weights, preferred_element_type=jnp.float32)
         new_sum_ref[head] = sum_ref[head] * factor + added
 
     in_stages(across_ref.shape[0], [
         score_stage(
-            k_ref[...], across_ref, bias_ref, at, scaled_ref,
+            k_ref[...], across_ref, bias_ref, at,
             lambda head: peak_ref[head:head + 1, :],
         ),
-        weight_stage(scaled_ref, weight_ref),
+        weight_stage,
         mix,
     ])
 
 
 def weights_kernel(
     at, across_ref, bias_ref, peak_ref, total_ref, sum_ref, k_ref,
-    new_sum_ref, weight_ref, share_ref, scaled_ref,
+    new_sum_ref, weight_ref, share_ref,
 ):
     def rescale(head, reached):
-        peak, total = reached
+        peak, total, weight_ref[head] = reached
         row = slice(head, head + 1)
         factor = jnp.exp2(peak_ref[row, :] - peak)
         share = 1.0 / (total_ref[row, :] * factor + total)
@@ -171,10 +167,10 @@
 
     in_stages(across_ref.shape[0], [
         score_stage(
-            k_ref[...], across_ref, bias_ref, at, scaled_ref,
+            k_ref[...], across_ref, bias_ref, at,
             lambda head: peak_ref[head:head + 1, :],
         ),
-        weight_stage(scaled_ref, weight_ref),
+        weight_stage,
         rescale,
     ])
 
@@ -232,10 +228,7 @@
         pltpu.VMEM((heads, rows), jnp.float32),
         pltpu.VMEM((heads, HEAD_WIDTH, rows), jnp.float32),
     ]
-    work = [
-        pltpu.VMEM((heads, rows, rows), jnp.float32),
-        pltpu.VMEM((heads, rows, rows), jnp.bfloat16),
-    ]
+    weight_type = pltpu.VMEM((heads, rows, rows), jnp.bfloat16)
     across, bias, *carried = pl.pallas_call(
         own_kernel,
         in_specs=[pl.BlockSpec(memory_space=pltpu.SMEM)] + [HBM_REF] * 5,
@@ -250,7 +243,8 @@
             pltpu.VMEM(queries.shape, jnp.bfloat16),
             pltpu.VMEM(keys.shape, jnp.bfloat16),
             pltpu.VMEM(values.shape, jnp.bfloat16),
-        ] + work + [pltpu.SemaphoreType.DMA((5,))],
+            pltpu.SemaphoreType.DMA((5,)),
+        ],
         compiler_params=PARAMS,
         cost_estimate=SHORT,
         name="own_shard",
@@ -262,7 +256,6 @@
             in_specs=[VMEM_REF] * 7,
             out_specs=[VMEM_REF] * 3,
             out_shape=state,
-            scratch_shapes=work,
             compiler_params=PARAMS,
             cost_estimate=SHORT,
             name="next_shard",
@@ -279,8 +272,7 @@
         lambda *refs: weights_kernel(3, *refs),
         in_specs=[VMEM_REF] * 6,
         out_specs=[VMEM_REF] * 3,
-        out_shape=[scaled_sum, work[1], state[0]],
-        scratch_shapes=work[:1],
+        out_shape=[scaled_sum, weight_type, state[0]],
         compiler_params=PARAMS,
         cost_estimate=SHORT,
         name="last_weights",

time: 16.1 us -> 16.1 us (level)
  no operation moved by 1% of the time
where the time goes in v29:
time: 16.1 us; the launch traced here: 16 us
  starting transfers between devices  9.18 us (57%)
  Pallas kernels  6.72 us (42%)
    ppermute x6, starting transfers between devices, moved(): lax.ppermute(value, 'seq', [(i, i ^ mask) for i in range(lax.axis_size('s...  9.18 us
    pallas_call x1, Pallas kernels, staged_attention(): pl.pallas_call(own_kernel, in_specs=[pl.BlockSpec(memory_space=pltpu.SMEM...  2.43 us
    pallas_call x2, Pallas kernels, add_shard(): pl.pallas_call(lambda *refs: next_kernel(at, *refs), in_specs=[VMEM_REF]...  2.3 us
    pallas_call x1, Pallas kernels, staged_attention(): pl.pallas_call(last_kernel, in_specs=[VMEM_REF] * 4, out_specs=pl.BlockSp...  1.14 us
    pallas_call x1, Pallas kernels, staged_attention(): pl.pallas_call(lambda *refs: weights_kernel(3, *refs), in_specs=[VMEM_REF...  0.84 us
  transfers between devices with their start and end apart: 6, of which 0 were waited for; matrix products, arithmetic and copies ran while one was open for 0% of the time, Pallas kernels for 35%

profile of v29, /device:TPU:0, one launch (start us, length us, event | category | flops | bytes accessed | tf_op | source)
XLA Modules:
  0.0 16.0 jit_solution(649618783524841528)
XLA Ops:
  0.0 4.0 %collective-permute-start.1 = (bf16[256,128]{1,0:T(8,128)(2,1)}, bf16[256,128]{1,0:T(8,128)(2,1)S(1)}, u32[]{:S(2)}, u32[]{:S(2)}) collective-permute-start(bf16[256,128]{1,0:T(8,128)(2,1)} %k_hbm.1), channel_id=1, source_target_pairs={{0,8},{4,12},{8,0},{12,4},{1,9},{5,13},{9,1},{13,5},{2,10},{6,14},... | collective-permute-start | bytes 196616 | tf_op jit(solution)/shard_map/ppermute | solution.py:215
  4.0 0.0 collective-permute-start
  4.1 1.9 %collective-permute-start.2 = (bf16[256,128]{1,0:T(8,128)(2,1)}, bf16[256,128]{1,0:T(8,128)(2,1)S(1)}, u32[]{:S(2)}, u32[]{:S(2)}) collective-permute-start(bf16[256,128]{1,0:T(8,128)(2,1)} %k_hbm.1), channel_id=1, source_target_pairs={{0,4},{4,0},{8,12},{12,8},{1,5},{5,1},{9,13},{13,9},{2,6},{6,2},{1... | collective-permute-start | bytes 196616 | tf_op jit(solution)/shard_map/ppermute | solution.py:215
  6.0 0.1 collective-permute-start.3
  6.1 2.4 %own_shard.1 = (bf16[8,128,256]{2,1,0:T(8,128)(2,1)S(1)}, f32[4,256,256]{2,1,0:T(8,128)S(1)}, f32[8,256]{1,0:T(8,128)S(1)}, f32[8,256]{1,0:T(8,128)S(1)}, f32[8,128,256]{2,1,0:T(8,128)S(1)}) custom-call(s32[1]{0:T(128)} %bitcast.own_ref, s32[3]{0:T(128)} %lengths_hbm.1, s32[1,128]{1,0:T(1,128)} %bitcast.2, bf16[256,1024]{1,0:T(8,128)(2,1)} %q_hbm.1, ...), custom_call_target="tpu_custom_call" | custom-call | tf_op jit(solution)/shard_map/own_shard/pallas_call | solution.py:232
  8.5 0.0 collective-permute-done.1.refs_5_
  8.6 1.9 %collective-permute-start.4 = (bf16[256,128]{1,0:T(8,128)(2,1)S(1)}, bf16[256,128]{1,0:T(8,128)(2,1)S(1)}, u32[]{:S(2)}, u32[]{:S(2)}) collective-permute-start(bf16[256,128]{1,0:T(8,128)(2,1)S(1)} %collective-permute-done.1.refs_5_), channel_id=1, source_target_pairs={{0,4},{4,0},{8,12},{12,8},{1,5},{5,1},{9,13},{13,9},{2,6},{6,2},{1... | collective-permute-start | bytes 196616 | tf_op jit(solution)/shard_map/ppermute | solution.py:215
  10.5 0.0 collective-permute-done.refs_6_
  10.5 1.1 %collective-permute-start.5 = (bf16[256,128]{1,0:T(8,128)(2,1)S(1)}, bf16[256,128]{1,0:T(8,128)(2,1)S(1)}, u32[]{:S(2)}, u32[]{:S(2)}) collective-permute-start(bf16[256,128]{1,0:T(8,128)(2,1)S(1)} %collective-permute-done.refs_6_), channel_id=1, source_target_pairs={{0,4},{4,0},{8,12},{12,8},{1,5},{5,1},{9,13},{13,9},{2,6},{6,2},{1... | collective-permute-start | bytes 196616 | tf_op jit(solution)/shard_map/ppermute | solution.py:215
  11.6 1.1 %next_shard.2 = (f32[8,256]{1,0:T(8,128)S(1)}, f32[8,256]{1,0:T(8,128)S(1)}, f32[8,128,256]{2,1,0:T(8,128)S(1)}) custom-call(bf16[8,128,256]{2,1,0:T(8,128)(2,1)S(1)} %get-tuple-element.27.refs_0_, f32[4,256,256]{2,1,0:T(8,128)S(1)} %get-tuple-element.28.refs_1_, f32[8,256]{1,0:T(8,128)S(1)} %get-tuple-element.35.refs_2_, ...), custom_call_target="tpu_custom_call" | custom-call | tf_op jit(solution)/shard_map/next_shard/pallas_call | solution.py:254
  12.8 0.0 collective-permute-done.2.refs_5_
  12.8 0.0 collective-permute-done.3.refs_6_
  12.8 1.1 %next_shard.3 = (f32[8,256]{1,0:T(8,128)S(1)}, f32[8,256]{1,0:T(8,128)S(1)}, f32[8,128,256]{2,1,0:T(8,128)S(1)}) custom-call(bf16[8,128,256]{2,1,0:T(8,128)(2,1)S(1)} %get-tuple-element.27.refs_0_, f32[4,256,256]{2,1,0:T(8,128)S(1)} %get-tuple-element.28.refs_1_, f32[8,256]{1,0:T(8,128)S(1)} %get-tuple-element.40.refs_2_, ...), custom_call_target="tpu_custom_call" | custom-call | tf_op jit(solution)/shard_map/next_shard/pallas_call | solution.py:254
  14.0 0.0 collective-permute-done.4.refs_5_
  14.0 0.8 %last_weights.1 = (f32[8,128,256]{2,1,0:T(8,128)S(1)}, bf16[8,256,256]{2,1,0:T(8,128)(2,1)S(1)}, f32[8,256]{1,0:T(8,128)S(1)}) custom-call(bf16[8,128,256]{2,1,0:T(8,128)(2,1)S(1)} %get-tuple-element.27.refs_0_, f32[4,256,256]{2,1,0:T(8,128)S(1)} %get-tuple-element.28.refs_1_, f32[8,256]{1,0:T(8,128)S(1)} %get-tuple-element.43.refs_2_, ...), custom_call_target="tpu_custom_call" | custom-call | tf_op jit(solution)/shard_map/last_weights/pallas_call | solution.py:271
  14.8 0.0 collective-permute-done.5.v_ref
  14.8 1.1 %last_values.1 = bf16[256,1024]{1,0:T(8,128)(2,1)} custom-call(f32[8,128,256]{2,1,0:T(8,128)S(1)} %get-tuple-element.46.sum_ref, bf16[8,256,256]{2,1,0:T(8,128)(2,1)S(1)} %get-tuple-element.47.weight_ref, f32[8,256]{1,0:T(8,128)S(1)} %get-tuple-element.48.share_ref, bf16[256,128]{1,0:T(8,128)(2,1)S(1)} %collective-permute-done.5.v_ref), custom_call_target="tpu_custom_call" | custom-call | tf_op jit(solution)/shard_map/last_values/pallas_call | solution.py:280
Async XLA Ops:
  0.0 8.5 %collective-permute-start.1 = (bf16[256,128]{1,0:T(8,128)(2,1)}, bf16[256,128]{1,0:T(8,128)(2,1)S(1)}, u32[]{:S(2)}, u32[]{:S(2)}) collective-permute-start(bf16[256,128]{1,0:T(8,128)(2,1)} %k_hbm.1), channel_id=1, source_target_pairs={{0,8},{4,12},{8,0},{12,4},{1,9},{5,13},{9,1},{13,5},{2,10},{6,14},... | collective-permute-start | bytes 196616 | tf_op jit(solution)/shard_map/ppermute | solution.py:215
  4.0 6.5 %collective-permute-start = (bf16[256,128]{1,0:T(8,128)(2,1)}, bf16[256,128]{1,0:T(8,128)(2,1)S(1)}, u32[]{:S(2)}, u32[]{:S(2)}) collective-permute-start(bf16[256,128]{1,0:T(8,128)(2,1)} %v_hbm.1), channel_id=1, source_target_pairs={{0,8},{4,12},{8,0},{12,4},{1,9},{5,13},{9,1},{13,5},{2,10},{6,14},... | collective-permute-start | bytes 196616 | tf_op jit(solution)/shard_map/ppermute | solution.py:215
  4.1 8.7 %collective-permute-start.2 = (bf16[256,128]{1,0:T(8,128)(2,1)}, bf16[256,128]{1,0:T(8,128)(2,1)S(1)}, u32[]{:S(2)}, u32[]{:S(2)}) collective-permute-start(bf16[256,128]{1,0:T(8,128)(2,1)} %k_hbm.1), channel_id=1, source_target_pairs={{0,4},{4,0},{8,12},{12,8},{1,5},{5,1},{9,13},{13,9},{2,6},{6,2},{1... | collective-permute-start | bytes 196616 | tf_op jit(solution)/shard_map/ppermute | solution.py:215
  6.0 6.9 %collective-permute-start.3 = (bf16[256,128]{1,0:T(8,128)(2,1)}, bf16[256,128]{1,0:T(8,128)(2,1)S(1)}, u32[]{:S(2)}, u32[]{:S(2)}) collective-permute-start(bf16[256,128]{1,0:T(8,128)(2,1)} %v_hbm.1), channel_id=1, source_target_pairs={{0,4},{4,0},{8,12},{12,8},{1,5},{5,1},{9,13},{13,9},{2,6},{6,2},{1... | collective-permute-start | bytes 196616 | tf_op jit(solution)/shard_map/ppermute | solution.py:215
  8.6 5.4 %collective-permute-start.4 = (bf16[256,128]{1,0:T(8,128)(2,1)S(1)}, bf16[256,128]{1,0:T(8,128)(2,1)S(1)}, u32[]{:S(2)}, u32[]{:S(2)}) collective-permute-start(bf16[256,128]{1,0:T(8,128)(2,1)S(1)} %collective-permute-done.1.refs_5_), channel_id=1, source_target_pairs={{0,4},{4,0},{8,12},{12,8},{1,5},{5,1},{9,13},{13,9},{2,6},{6,2},{1... | collective-permute-start | bytes 196616 | tf_op jit(solution)/shard_map/ppermute | solution.py:215
  10.5 4.3 %collective-permute-start.5 = (bf16[256,128]{1,0:T(8,128)(2,1)S(1)}, bf16[256,128]{1,0:T(8,128)(2,1)S(1)}, u32[]{:S(2)}, u32[]{:S(2)}) collective-permute-start(bf16[256,128]{1,0:T(8,128)(2,1)S(1)} %collective-permute-done.refs_6_), channel_id=1, source_target_pairs={{0,4},{4,0},{8,12},{12,8},{1,5},{5,1},{9,13},{13,9},{2,6},{6,2},{1... | collective-permute-start | bytes 196616 | tf_op jit(solution)/shard_map/ppermute | solution.py:215

commit v30 on v28

--- a/solution.py
+++ b/solution.py
@@ -190,9 +190,11 @@
     def send(head, out):
         cols = slice(head * HEAD_WIDTH, (head + 1) * HEAD_WIDTH)
         block_ref[:, cols] = jnp.transpose(out)
-        copy = pltpu.make_async_copy(block_ref.at[:, cols], out_ref.at[:, cols], sems.at[head])
-        copy.start()
-        copies.append(copy)
+        if head % 2 or head == sum_ref.shape[0] - 1:
+            cols = slice(head // 2 * 2 * HEAD_WIDTH, (head + 1) * HEAD_WIDTH)
+            copy = pltpu.make_async_copy(block_ref.at[:, cols], out_ref.at[:, cols], sems.at[head])
+            copy.start()
+            copies.append(copy)
 
     in_stages(sum_ref.shape[0], [mix, send])
     for copy in copies:

time: 16.1 us -> 16.1 us (level)
  no operation moved by 1% of the time
where the time goes in v30:
time: 16.1 us; the launch traced here: 16 us
  starting transfers between devices  9.18 us (57%)
  Pallas kernels  6.72 us (42%)
    ppermute x6, starting transfers between devices, moved(): lax.ppermute(value, 'seq', [(i, i ^ mask) for i in range(lax.axis_size('s...  9.18 us
    pallas_call x1, Pallas kernels, staged_attention(): pl.pallas_call(own_kernel, in_specs=[pl.BlockSpec(memory_space=pltpu.SMEM...  2.43 us
    pallas_call x2, Pallas kernels, add_shard(): pl.pallas_call(lambda *refs: next_kernel(at, *refs), in_specs=[VMEM_REF]...  2.29 us
    pallas_call x1, Pallas kernels, staged_attention(): pl.pallas_call(last_kernel, in_specs=[VMEM_REF] * 4, out_specs=pl.BlockSp...  1.17 us
    pallas_call x1, Pallas kernels, staged_attention(): pl.pallas_call(lambda *refs: weights_kernel(3, *refs), in_specs=[VMEM_REF...  0.83 us
  transfers between devices with their start and end apart: 6, of which 0 were waited for; matrix products, arithmetic and copies ran while one was open for 0% of the time, Pallas kernels for 35%

profile of v30, /device:TPU:0, one launch (start us, length us, event | category | flops | bytes accessed | tf_op | source)
XLA Modules:
  0.0 16.0 jit_solution(15410567143053767285)
XLA Ops:
  0.0 4.0 %collective-permute-start.1 = (bf16[256,128]{1,0:T(8,128)(2,1)}, bf16[256,128]{1,0:T(8,128)(2,1)S(1)}, u32[]{:S(2)}, u32[]{:S(2)}) collective-permute-start(bf16[256,128]{1,0:T(8,128)(2,1)} %k_hbm.1), channel_id=1, source_target_pairs={{0,8},{4,12},{8,0},{12,4},{1,9},{5,13},{9,1},{13,5},{2,10},{6,14},... | collective-permute-start | bytes 196616 | tf_op jit(solution)/shard_map/ppermute | solution.py:221
  4.0 0.0 collective-permute-start
  4.1 1.9 %collective-permute-start.2 = (bf16[256,128]{1,0:T(8,128)(2,1)}, bf16[256,128]{1,0:T(8,128)(2,1)S(1)}, u32[]{:S(2)}, u32[]{:S(2)}) collective-permute-start(bf16[256,128]{1,0:T(8,128)(2,1)} %k_hbm.1), channel_id=1, source_target_pairs={{0,4},{4,0},{8,12},{12,8},{1,5},{5,1},{9,13},{13,9},{2,6},{6,2},{1... | collective-permute-start | bytes 196616 | tf_op jit(solution)/shard_map/ppermute | solution.py:221
  6.0 0.1 collective-permute-start.3
  6.1 2.4 %own_shard.1 = (bf16[8,128,256]{2,1,0:T(8,128)(2,1)S(1)}, f32[4,256,256]{2,1,0:T(8,128)S(1)}, f32[8,256]{1,0:T(8,128)S(1)}, f32[8,256]{1,0:T(8,128)S(1)}, f32[8,128,256]{2,1,0:T(8,128)S(1)}) custom-call(s32[1]{0:T(128)} %bitcast.own_ref, s32[3]{0:T(128)} %lengths_hbm.1, s32[1,128]{1,0:T(1,128)} %bitcast.2, bf16[256,1024]{1,0:T(8,128)(2,1)} %q_hbm.1, ...), custom_call_target="tpu_custom_call" | custom-call | tf_op jit(solution)/shard_map/own_shard/pallas_call | solution.py:241
  8.5 0.0 collective-permute-done.1.refs_5_
  8.6 1.9 %collective-permute-start.4 = (bf16[256,128]{1,0:T(8,128)(2,1)S(1)}, bf16[256,128]{1,0:T(8,128)(2,1)S(1)}, u32[]{:S(2)}, u32[]{:S(2)}) collective-permute-start(bf16[256,128]{1,0:T(8,128)(2,1)S(1)} %collective-permute-done.1.refs_5_), channel_id=1, source_target_pairs={{0,4},{4,0},{8,12},{12,8},{1,5},{5,1},{9,13},{13,9},{2,6},{6,2},{1... | collective-permute-start | bytes 196616 | tf_op jit(solution)/shard_map/ppermute | solution.py:221
  10.5 0.0 collective-permute-done.refs_6_
  10.5 1.1 %collective-permute-start.5 = (bf16[256,128]{1,0:T(8,128)(2,1)S(1)}, bf16[256,128]{1,0:T(8,128)(2,1)S(1)}, u32[]{:S(2)}, u32[]{:S(2)}) collective-permute-start(bf16[256,128]{1,0:T(8,128)(2,1)S(1)} %collective-permute-done.refs_6_), channel_id=1, source_target_pairs={{0,4},{4,0},{8,12},{12,8},{1,5},{5,1},{9,13},{13,9},{2,6},{6,2},{1... | collective-permute-start | bytes 196616 | tf_op jit(solution)/shard_map/ppermute | solution.py:221
  11.6 1.1 %next_shard.2 = (f32[8,256]{1,0:T(8,128)S(1)}, f32[8,256]{1,0:T(8,128)S(1)}, f32[8,128,256]{2,1,0:T(8,128)S(1)}) custom-call(bf16[8,128,256]{2,1,0:T(8,128)(2,1)S(1)} %get-tuple-element.27.refs_0_, f32[4,256,256]{2,1,0:T(8,128)S(1)} %get-tuple-element.28.refs_1_, f32[8,256]{1,0:T(8,128)S(1)} %get-tuple-element.35.refs_2_, ...), custom_call_target="tpu_custom_call" | custom-call | tf_op jit(solution)/shard_map/next_shard/pallas_call | solution.py:262
  12.8 0.0 collective-permute-done.2.refs_5_
  12.8 0.0 collective-permute-done.3.refs_6_
  12.8 1.1 %next_shard.3 = (f32[8,256]{1,0:T(8,128)S(1)}, f32[8,256]{1,0:T(8,128)S(1)}, f32[8,128,256]{2,1,0:T(8,128)S(1)}) custom-call(bf16[8,128,256]{2,1,0:T(8,128)(2,1)S(1)} %get-tuple-element.27.refs_0_, f32[4,256,256]{2,1,0:T(8,128)S(1)} %get-tuple-element.28.refs_1_, f32[8,256]{1,0:T(8,128)S(1)} %get-tuple-element.40.refs_2_, ...), custom_call_target="tpu_custom_call" | custom-call | tf_op jit(solution)/shard_map/next_shard/pallas_call | solution.py:262
  14.0 0.0 collective-permute-done.4.refs_5_
  14.0 0.8 %last_weights.1 = (f32[8,128,256]{2,1,0:T(8,128)S(1)}, bf16[8,256,256]{2,1,0:T(8,128)(2,1)S(1)}, f32[8,256]{1,0:T(8,128)S(1)}) custom-call(bf16[8,128,256]{2,1,0:T(8,128)(2,1)S(1)} %get-tuple-element.27.refs_0_, f32[4,256,256]{2,1,0:T(8,128)S(1)} %get-tuple-element.28.refs_1_, f32[8,256]{1,0:T(8,128)S(1)} %get-tuple-element.43.refs_2_, ...), custom_call_target="tpu_custom_call" | custom-call | tf_op jit(solution)/shard_map/last_weights/pallas_call | solution.py:280
  14.8 0.0 collective-permute-done.5.v_ref
  14.8 1.2 %last_values.1 = bf16[256,1024]{1,0:T(8,128)(2,1)} custom-call(f32[8,128,256]{2,1,0:T(8,128)S(1)} %get-tuple-element.46.sum_ref, bf16[8,256,256]{2,1,0:T(8,128)(2,1)S(1)} %get-tuple-element.47.weight_ref, f32[8,256]{1,0:T(8,128)S(1)} %get-tuple-element.48.share_ref, bf16[256,128]{1,0:T(8,128)(2,1)S(1)} %collective-permute-done.5.v_ref), custom_call_target="tpu_custom_call" | custom-call | tf_op jit(solution)/shard_map/last_values/pallas_call | solution.py:290
Async XLA Ops:
  0.0 8.5 %collective-permute-start.1 = (bf16[256,128]{1,0:T(8,128)(2,1)}, bf16[256,128]{1,0:T(8,128)(2,1)S(1)}, u32[]{:S(2)}, u32[]{:S(2)}) collective-permute-start(bf16[256,128]{1,0:T(8,128)(2,1)} %k_hbm.1), channel_id=1, source_target_pairs={{0,8},{4,12},{8,0},{12,4},{1,9},{5,13},{9,1},{13,5},{2,10},{6,14},... | collective-permute-start | bytes 196616 | tf_op jit(solution)/shard_map/ppermute | solution.py:221
  4.0 6.5 %collective-permute-start = (bf16[256,128]{1,0:T(8,128)(2,1)}, bf16[256,128]{1,0:T(8,128)(2,1)S(1)}, u32[]{:S(2)}, u32[]{:S(2)}) collective-permute-start(bf16[256,128]{1,0:T(8,128)(2,1)} %v_hbm.1), channel_id=1, source_target_pairs={{0,8},{4,12},{8,0},{12,4},{1,9},{5,13},{9,1},{13,5},{2,10},{6,14},... | collective-permute-start | bytes 196616 | tf_op jit(solution)/shard_map/ppermute | solution.py:221
  4.1 8.7 %collective-permute-start.2 = (bf16[256,128]{1,0:T(8,128)(2,1)}, bf16[256,128]{1,0:T(8,128)(2,1)S(1)}, u32[]{:S(2)}, u32[]{:S(2)}) collective-permute-start(bf16[256,128]{1,0:T(8,128)(2,1)} %k_hbm.1), channel_id=1, source_target_pairs={{0,4},{4,0},{8,12},{12,8},{1,5},{5,1},{9,13},{13,9},{2,6},{6,2},{1... | collective-permute-start | bytes 196616 | tf_op jit(solution)/shard_map/ppermute | solution.py:221
  6.0 6.9 %collective-permute-start.3 = (bf16[256,128]{1,0:T(8,128)(2,1)}, bf16[256,128]{1,0:T(8,128)(2,1)S(1)}, u32[]{:S(2)}, u32[]{:S(2)}) collective-permute-start(bf16[256,128]{1,0:T(8,128)(2,1)} %v_hbm.1), channel_id=1, source_target_pairs={{0,4},{4,0},{8,12},{12,8},{1,5},{5,1},{9,13},{13,9},{2,6},{6,2},{1... | collective-permute-start | bytes 196616 | tf_op jit(solution)/shard_map/ppermute | solution.py:221
  8.6 5.4 %collective-permute-start.4 = (bf16[256,128]{1,0:T(8,128)(2,1)S(1)}, bf16[256,128]{1,0:T(8,128)(2,1)S(1)}, u32[]{:S(2)}, u32[]{:S(2)}) collective-permute-start(bf16[256,128]{1,0:T(8,128)(2,1)S(1)} %collective-permute-done.1.refs_5_), channel_id=1, source_target_pairs={{0,4},{4,0},{8,12},{12,8},{1,5},{5,1},{9,13},{13,9},{2,6},{6,2},{1... | collective-permute-start | bytes 196616 | tf_op jit(solution)/shard_map/ppermute | solution.py:221
  10.5 4.3 %collective-permute-start.5 = (bf16[256,128]{1,0:T(8,128)(2,1)S(1)}, bf16[256,128]{1,0:T(8,128)(2,1)S(1)}, u32[]{:S(2)}, u32[]{:S(2)}) collective-permute-start(bf16[256,128]{1,0:T(8,128)(2,1)S(1)} %collective-permute-done.refs_6_), channel_id=1, source_target_pairs={{0,4},{4,0},{8,12},{12,8},{1,5},{5,1},{9,13},{13,9},{2,6},{6,2},{1... | collective-permute-start | bytes 196616 | tf_op jit(solution)/shard_map/ppermute | solution.py:221

commit v31 on v28

--- a/solution.py
+++ b/solution.py
@@ -74,8 +74,17 @@
 
 
 def score_stage(keys, across_ref, bias_ref, at, scaled_ref, old_peak):
+    ready = {}
+
     def stage(head, _):
-        scores = jnp.dot(keys, across_ref[head], preferred_element_type=jnp.float32)
+        if head not in ready:
+            pair = range(head, min(head + 2, across_ref.shape[0]))
+            across = jnp.concatenate([across_ref[one] for one in pair], axis=1)
+            both = jnp.dot(keys, across, preferred_element_type=jnp.float32)
+            for at_column, one in enumerate(pair):
+                width = across_ref.shape[2]
+                ready[one] = both[:, at_column * width:(at_column + 1) * width]
+        scores = ready.pop(head)
         scaled = scores * (HEAD_WIDTH ** -0.5 * LOG2_E) + bias_ref[at]
         scaled_ref[head] = scaled
         peak = jnp.max(scaled, axis=0, keepdims=True)
@@ -124,8 +133,9 @@
         peak_ref[head:head + 1, :], total_ref[head:head + 1, :] = reached
         sum_ref[head] = jnp.dot(turned, weight_ref[head], preferred_element_type=jnp.float32)
 
+    for head in range(heads):
+        turn(head, None)
     in_stages(heads, [
-        turn,
         score_stage(keys, across_ref, bias_ref, 0, scaled_ref, None),
         weight_stage(scaled_ref, weight_ref),
         mix,

time: 16.1 us -> 16 us (level)
  Pallas kernels: 6.69 us -> 6.42 us
    pallas_call x2, Pallas kernels: 2.29 us -> 2.07 us  [add_shard(): pl.pallas_call(lambda *refs: next_kernel(at, *refs), in_specs=[VMEM_REF]...]
  transfers between devices with their start and end apart: 6 -> 6, of which waited for: 0 -> 1; matrix products, arithmetic and copies ran while one was open for 0% -> 0% of each run, Pallas kernels for 35% -> 33%
where the time goes in v31:
time: 16 us; the launch traced here: 15.9 us
  starting transfers between devices  9.23 us (58%)
  Pallas kernels  6.42 us (40%)
    ppermute x6, starting transfers between devices, moved(): lax.ppermute(value, 'seq', [(i, i ^ mask) for i in range(lax.axis_size('s...  9.23 us
    pallas_call x1, Pallas kernels, staged_attention(): pl.pallas_call(own_kernel, in_specs=[pl.BlockSpec(memory_space=pltpu.SMEM...  2.38 us
    pallas_call x2, Pallas kernels, add_shard(): pl.pallas_call(lambda *refs: next_kernel(at, *refs), in_specs=[VMEM_REF]...  2.07 us
    pallas_call x1, Pallas kernels, staged_attention(): pl.pallas_call(last_kernel, in_specs=[VMEM_REF] * 4, out_specs=pl.BlockSp...  1.14 us
    pallas_call x1, Pallas kernels, staged_attention(): pl.pallas_call(lambda *refs: weights_kernel(3, *refs), in_specs=[VMEM_REF...  0.83 us
  transfers between devices with their start and end apart: 6, of which 1 were waited for; matrix products, arithmetic and copies ran while one was open for 0% of the time, Pallas kernels for 33%

profile of v31, /device:TPU:0, one launch (start us, length us, event | category | flops | bytes accessed | tf_op | source)
XLA Modules:
  0.0 15.9 jit_solution(6493186244949218659)
XLA Ops:
  0.0 4.0 %collective-permute-start.1 = (bf16[256,128]{1,0:T(8,128)(2,1)}, bf16[256,128]{1,0:T(8,128)(2,1)S(1)}, u32[]{:S(2)}, u32[]{:S(2)}) collective-permute-start(bf16[256,128]{1,0:T(8,128)(2,1)} %k_hbm.1), channel_id=1, source_target_pairs={{0,8},{4,12},{8,0},{12,4},{1,9},{5,13},{9,1},{13,5},{2,10},{6,14},... | collective-permute-start | bytes 196616 | tf_op jit(solution)/shard_map/ppermute | solution.py:229
  4.0 0.0 collective-permute-start
  4.1 1.9 %collective-permute-start.2 = (bf16[256,128]{1,0:T(8,128)(2,1)}, bf16[256,128]{1,0:T(8,128)(2,1)S(1)}, u32[]{:S(2)}, u32[]{:S(2)}) collective-permute-start(bf16[256,128]{1,0:T(8,128)(2,1)} %k_hbm.1), channel_id=1, source_target_pairs={{0,4},{4,0},{8,12},{12,8},{1,5},{5,1},{9,13},{13,9},{2,6},{6,2},{1... | collective-permute-start | bytes 196616 | tf_op jit(solution)/shard_map/ppermute | solution.py:229
  6.0 0.1 collective-permute-start.3
  6.1 2.4 %own_shard.1 = (bf16[8,128,256]{2,1,0:T(8,128)(2,1)S(1)}, f32[4,256,256]{2,1,0:T(8,128)S(1)}, f32[8,256]{1,0:T(8,128)S(1)}, f32[8,256]{1,0:T(8,128)S(1)}, f32[8,128,256]{2,1,0:T(8,128)S(1)}) custom-call(s32[1]{0:T(128)} %bitcast.own_ref, s32[3]{0:T(128)} %lengths_hbm.1, s32[1,128]{1,0:T(1,128)} %bitcast.2, bf16[256,1024]{1,0:T(8,128)(2,1)} %q_hbm.1, ...), custom_call_target="tpu_custom_call" | custom-call | tf_op jit(solution)/shard_map/own_shard/pallas_call | solution.py:249
  8.5 0.0 collective-permute-done.1.refs_5_
  8.5 1.9 %collective-permute-start.4 = (bf16[256,128]{1,0:T(8,128)(2,1)S(1)}, bf16[256,128]{1,0:T(8,128)(2,1)S(1)}, u32[]{:S(2)}, u32[]{:S(2)}) collective-permute-start(bf16[256,128]{1,0:T(8,128)(2,1)S(1)} %collective-permute-done.1.refs_5_), channel_id=1, source_target_pairs={{0,4},{4,0},{8,12},{12,8},{1,5},{5,1},{9,13},{13,9},{2,6},{6,2},{1... | collective-permute-start | bytes 196616 | tf_op jit(solution)/shard_map/ppermute | solution.py:229
  10.4 0.0 collective-permute-done.refs_6_
  10.4 1.2 %collective-permute-start.5 = (bf16[256,128]{1,0:T(8,128)(2,1)S(1)}, bf16[256,128]{1,0:T(8,128)(2,1)S(1)}, u32[]{:S(2)}, u32[]{:S(2)}) collective-permute-start(bf16[256,128]{1,0:T(8,128)(2,1)S(1)} %collective-permute-done.refs_6_), channel_id=1, source_target_pairs={{0,4},{4,0},{8,12},{12,8},{1,5},{5,1},{9,13},{13,9},{2,6},{6,2},{1... | collective-permute-start | bytes 196616 | tf_op jit(solution)/shard_map/ppermute | solution.py:229
  11.6 1.0 %next_shard.2 = (f32[8,256]{1,0:T(8,128)S(1)}, f32[8,256]{1,0:T(8,128)S(1)}, f32[8,128,256]{2,1,0:T(8,128)S(1)}) custom-call(bf16[8,128,256]{2,1,0:T(8,128)(2,1)S(1)} %get-tuple-element.27.refs_0_, f32[4,256,256]{2,1,0:T(8,128)S(1)} %get-tuple-element.28.refs_1_, f32[8,256]{1,0:T(8,128)S(1)} %get-tuple-element.35.refs_2_, ...), custom_call_target="tpu_custom_call" | custom-call | tf_op jit(solution)/shard_map/next_shard/pallas_call | solution.py:270
  12.7 0.0 collective-permute-done.2.refs_5_
  12.7 0.0 collective-permute-done.3.refs_6_
  12.7 1.0 %next_shard.3 = (f32[8,256]{1,0:T(8,128)S(1)}, f32[8,256]{1,0:T(8,128)S(1)}, f32[8,128,256]{2,1,0:T(8,128)S(1)}) custom-call(bf16[8,128,256]{2,1,0:T(8,128)(2,1)S(1)} %get-tuple-element.27.refs_0_, f32[4,256,256]{2,1,0:T(8,128)S(1)} %get-tuple-element.28.refs_1_, f32[8,256]{1,0:T(8,128)S(1)} %get-tuple-element.40.refs_2_, ...), custom_call_target="tpu_custom_call" | custom-call | tf_op jit(solution)/shard_map/next_shard/pallas_call | solution.py:270
  13.7 0.0 collective-permute-done.4.refs_5_
  13.8 0.8 %last_weights.1 = (f32[8,128,256]{2,1,0:T(8,128)S(1)}, bf16[8,256,256]{2,1,0:T(8,128)(2,1)S(1)}, f32[8,256]{1,0:T(8,128)S(1)}) custom-call(bf16[8,128,256]{2,1,0:T(8,128)(2,1)S(1)} %get-tuple-element.27.refs_0_, f32[4,256,256]{2,1,0:T(8,128)S(1)} %get-tuple-element.28.refs_1_, f32[8,256]{1,0:T(8,128)S(1)} %get-tuple-element.43.refs_2_, ...), custom_call_target="tpu_custom_call" | custom-call | tf_op jit(solution)/shard_map/last_weights/pallas_call | solution.py:288
  14.6 0.1 collective-permute-done.5.v_ref
  14.7 1.1 %last_values.1 = bf16[256,1024]{1,0:T(8,128)(2,1)} custom-call(f32[8,128,256]{2,1,0:T(8,128)S(1)} %get-tuple-element.46.sum_ref, bf16[8,256,256]{2,1,0:T(8,128)(2,1)S(1)} %get-tuple-element.47.weight_ref, f32[8,256]{1,0:T(8,128)S(1)} %get-tuple-element.48.share_ref, bf16[256,128]{1,0:T(8,128)(2,1)S(1)} %collective-permute-done.5.v_ref), custom_call_target="tpu_custom_call" | custom-call | tf_op jit(solution)/shard_map/last_values/pallas_call | solution.py:298
Async XLA Ops:
  0.0 8.5 %collective-permute-start.1 = (bf16[256,128]{1,0:T(8,128)(2,1)}, bf16[256,128]{1,0:T(8,128)(2,1)S(1)}, u32[]{:S(2)}, u32[]{:S(2)}) collective-permute-start(bf16[256,128]{1,0:T(8,128)(2,1)} %k_hbm.1), channel_id=1, source_target_pairs={{0,8},{4,12},{8,0},{12,4},{1,9},{5,13},{9,1},{13,5},{2,10},{6,14},... | collective-permute-start | bytes 196616 | tf_op jit(solution)/shard_map/ppermute | solution.py:229
  4.0 6.4 %collective-permute-start = (bf16[256,128]{1,0:T(8,128)(2,1)}, bf16[256,128]{1,0:T(8,128)(2,1)S(1)}, u32[]{:S(2)}, u32[]{:S(2)}) collective-permute-start(bf16[256,128]{1,0:T(8,128)(2,1)} %v_hbm.1), channel_id=1, source_target_pairs={{0,8},{4,12},{8,0},{12,4},{1,9},{5,13},{9,1},{13,5},{2,10},{6,14},... | collective-permute-start | bytes 196616 | tf_op jit(solution)/shard_map/ppermute | solution.py:229
  4.1 8.6 %collective-permute-start.2 = (bf16[256,128]{1,0:T(8,128)(2,1)}, bf16[256,128]{1,0:T(8,128)(2,1)S(1)}, u32[]{:S(2)}, u32[]{:S(2)}) collective-permute-start(bf16[256,128]{1,0:T(8,128)(2,1)} %k_hbm.1), channel_id=1, source_target_pairs={{0,4},{4,0},{8,12},{12,8},{1,5},{5,1},{9,13},{13,9},{2,6},{6,2},{1... | collective-permute-start | bytes 196616 | tf_op jit(solution)/shard_map/ppermute | solution.py:229
  6.0 6.7 %collective-permute-start.3 = (bf16[256,128]{1,0:T(8,128)(2,1)}, bf16[256,128]{1,0:T(8,128)(2,1)S(1)}, u32[]{:S(2)}, u32[]{:S(2)}) collective-permute-start(bf16[256,128]{1,0:T(8,128)(2,1)} %v_hbm.1), channel_id=1, source_target_pairs={{0,4},{4,0},{8,12},{12,8},{1,5},{5,1},{9,13},{13,9},{2,6},{6,2},{1... | collective-permute-start | bytes 196616 | tf_op jit(solution)/shard_map/ppermute | solution.py:229
  8.5 5.3 %collective-permute-start.4 = (bf16[256,128]{1,0:T(8,128)(2,1)S(1)}, bf16[256,128]{1,0:T(8,128)(2,1)S(1)}, u32[]{:S(2)}, u32[]{:S(2)}) collective-permute-start(bf16[256,128]{1,0:T(8,128)(2,1)S(1)} %collective-permute-done.1.refs_5_), channel_id=1, source_target_pairs={{0,4},{4,0},{8,12},{12,8},{1,5},{5,1},{9,13},{13,9},{2,6},{6,2},{1... | collective-permute-start | bytes 196616 | tf_op jit(solution)/shard_map/ppermute | solution.py:229
  10.4 4.3 %collective-permute-start.5 = (bf16[256,128]{1,0:T(8,128)(2,1)S(1)}, bf16[256,128]{1,0:T(8,128)(2,1)S(1)}, u32[]{:S(2)}, u32[]{:S(2)}) collective-permute-start(bf16[256,128]{1,0:T(8,128)(2,1)S(1)} %collective-permute-done.refs_6_), channel_id=1, source_target_pairs={{0,4},{4,0},{8,12},{12,8},{1,5},{5,1},{9,13},{13,9},{2,6},{6,2},{1... | collective-permute-start | bytes 196616 | tf_op jit(solution)/shard_map/ppermute | solution.py:229

commit v32 on v31

--- a/solution.py
+++ b/solution.py
@@ -193,8 +193,17 @@
     turned = jnp.transpose(v_ref[...])
     copies = []
 
+    ready = {}
+
     def mix(head, _):
-        added = jnp.dot(turned, weight_ref[head], preferred_element_type=jnp.float32)
+        if head not in ready:
+            pair = range(head, min(head + 2, sum_ref.shape[0]))
+            weights = jnp.concatenate([weight_ref[one] for one in pair], axis=1)
+            both = jnp.dot(turned, weights, preferred_element_type=jnp.float32)
+            width = sum_ref.shape[2]
+            for at_column, one in enumerate(pair):
+                ready[one] = both[:, at_column * width:(at_column + 1) * width]
+        added = ready.pop(head)
         return (sum_ref[head] + added * share_ref[head:head + 1, :]).astype(jnp.bfloat16)
 
     def send(head, out):

time: 16 us -> 16 us (level)
  no operation moved by 1% of the time
where the time goes in v32:
time: 16 us; the launch traced here: 15.9 us
  starting transfers between devices  9.23 us (58%)
  Pallas kernels  6.42 us (40%)
    ppermute x6, starting transfers between devices, moved(): lax.ppermute(value, 'seq', [(i, i ^ mask) for i in range(lax.axis_size('s...  9.23 us
    pallas_call x1, Pallas kernels, staged_attention(): pl.pallas_call(own_kernel, in_specs=[pl.BlockSpec(memory_space=pltpu.SMEM...  2.38 us
    pallas_call x2, Pallas kernels, add_shard(): pl.pallas_call(lambda *refs: next_kernel(at, *refs), in_specs=[VMEM_REF]...  2.07 us
    pallas_call x1, Pallas kernels, staged_attention(): pl.pallas_call(last_kernel, in_specs=[VMEM_REF] * 4, out_specs=pl.BlockSp...  1.14 us
    pallas_call x1, Pallas kernels, staged_attention(): pl.pallas_call(lambda *refs: weights_kernel(3, *refs), in_specs=[VMEM_REF...  0.83 us
  transfers between devices with their start and end apart: 6, of which 1 were waited for; matrix products, arithmetic and copies ran while one was open for 0% of the time, Pallas kernels for 33%

profile of v32, /device:TPU:0, one launch (start us, length us, event | category | flops | bytes accessed | tf_op | source)
XLA Modules:
  0.0 15.9 jit_solution(6493186244949218659)
XLA Ops:
  0.0 4.0 %collective-permute-start.1 = (bf16[256,128]{1,0:T(8,128)(2,1)}, bf16[256,128]{1,0:T(8,128)(2,1)S(1)}, u32[]{:S(2)}, u32[]{:S(2)}) collective-permute-start(bf16[256,128]{1,0:T(8,128)(2,1)} %k_hbm.1), channel_id=1, source_target_pairs={{0,8},{4,12},{8,0},{12,4},{1,9},{5,13},{9,1},{13,5},{2,10},{6,14},... | collective-permute-start | bytes 196616 | tf_op jit(solution)/shard_map/ppermute | solution.py:238
  4.0 0.0 collective-permute-start
  4.1 1.9 %collective-permute-start.2 = (bf16[256,128]{1,0:T(8,128)(2,1)}, bf16[256,128]{1,0:T(8,128)(2,1)S(1)}, u32[]{:S(2)}, u32[]{:S(2)}) collective-permute-start(bf16[256,128]{1,0:T(8,128)(2,1)} %k_hbm.1), channel_id=1, source_target_pairs={{0,4},{4,0},{8,12},{12,8},{1,5},{5,1},{9,13},{13,9},{2,6},{6,2},{1... | collective-permute-start | bytes 196616 | tf_op jit(solution)/shard_map/ppermute | solution.py:238
  6.0 0.1 collective-permute-start.3
  6.1 2.4 %own_shard.1 = (bf16[8,128,256]{2,1,0:T(8,128)(2,1)S(1)}, f32[4,256,256]{2,1,0:T(8,128)S(1)}, f32[8,256]{1,0:T(8,128)S(1)}, f32[8,256]{1,0:T(8,128)S(1)}, f32[8,128,256]{2,1,0:T(8,128)S(1)}) custom-call(s32[1]{0:T(128)} %bitcast.own_ref, s32[3]{0:T(128)} %lengths_hbm.1, s32[1,128]{1,0:T(1,128)} %bitcast.2, bf16[256,1024]{1,0:T(8,128)(2,1)} %q_hbm.1, ...), custom_call_target="tpu_custom_call" | custom-call | tf_op jit(solution)/shard_map/own_shard/pallas_call | solution.py:258
  8.5 0.0 collective-permute-done.1.refs_5_
  8.5 1.9 %collective-permute-start.4 = (bf16[256,128]{1,0:T(8,128)(2,1)S(1)}, bf16[256,128]{1,0:T(8,128)(2,1)S(1)}, u32[]{:S(2)}, u32[]{:S(2)}) collective-permute-start(bf16[256,128]{1,0:T(8,128)(2,1)S(1)} %collective-permute-done.1.refs_5_), channel_id=1, source_target_pairs={{0,4},{4,0},{8,12},{12,8},{1,5},{5,1},{9,13},{13,9},{2,6},{6,2},{1... | collective-permute-start | bytes 196616 | tf_op jit(solution)/shard_map/ppermute | solution.py:238
  10.4 0.0 collective-permute-done.refs_6_
  10.4 1.2 %collective-permute-start.5 = (bf16[256,128]{1,0:T(8,128)(2,1)S(1)}, bf16[256,128]{1,0:T(8,128)(2,1)S(1)}, u32[]{:S(2)}, u32[]{:S(2)}) collective-permute-start(bf16[256,128]{1,0:T(8,128)(2,1)S(1)} %collective-permute-done.refs_6_), channel_id=1, source_target_pairs={{0,4},{4,0},{8,12},{12,8},{1,5},{5,1},{9,13},{13,9},{2,6},{6,2},{1... | collective-permute-start | bytes 196616 | tf_op jit(solution)/shard_map/ppermute | solution.py:238
  11.6 1.0 %next_shard.2 = (f32[8,256]{1,0:T(8,128)S(1)}, f32[8,256]{1,0:T(8,128)S(1)}, f32[8,128,256]{2,1,0:T(8,128)S(1)}) custom-call(bf16[8,128,256]{2,1,0:T(8,128)(2,1)S(1)} %get-tuple-element.27.refs_0_, f32[4,256,256]{2,1,0:T(8,128)S(1)} %get-tuple-element.28.refs_1_, f32[8,256]{1,0:T(8,128)S(1)} %get-tuple-element.35.refs_2_, ...), custom_call_target="tpu_custom_call" | custom-call | tf_op jit(solution)/shard_map/next_shard/pallas_call | solution.py:279
  12.7 0.0 collective-permute-done.2.refs_5_
  12.7 0.0 collective-permute-done.3.refs_6_
  12.7 1.0 %next_shard.3 = (f32[8,256]{1,0:T(8,128)S(1)}, f32[8,256]{1,0:T(8,128)S(1)}, f32[8,128,256]{2,1,0:T(8,128)S(1)}) custom-call(bf16[8,128,256]{2,1,0:T(8,128)(2,1)S(1)} %get-tuple-element.27.refs_0_, f32[4,256,256]{2,1,0:T(8,128)S(1)} %get-tuple-element.28.refs_1_, f32[8,256]{1,0:T(8,128)S(1)} %get-tuple-element.40.refs_2_, ...), custom_call_target="tpu_custom_call" | custom-call | tf_op jit(solution)/shard_map/next_shard/pallas_call | solution.py:279
  13.7 0.0 collective-permute-done.4.refs_5_
  13.8 0.8 %last_weights.1 = (f32[8,128,256]{2,1,0:T(8,128)S(1)}, bf16[8,256,256]{2,1,0:T(8,128)(2,1)S(1)}, f32[8,256]{1,0:T(8,128)S(1)}) custom-call(bf16[8,128,256]{2,1,0:T(8,128)(2,1)S(1)} %get-tuple-element.27.refs_0_, f32[4,256,256]{2,1,0:T(8,128)S(1)} %get-tuple-element.28.refs_1_, f32[8,256]{1,0:T(8,128)S(1)} %get-tuple-element.43.refs_2_, ...), custom_call_target="tpu_custom_call" | custom-call | tf_op jit(solution)/shard_map/last_weights/pallas_call | solution.py:297
  14.6 0.1 collective-permute-done.5.v_ref
  14.7 1.1 %last_values.1 = bf16[256,1024]{1,0:T(8,128)(2,1)} custom-call(f32[8,128,256]{2,1,0:T(8,128)S(1)} %get-tuple-element.46.sum_ref, bf16[8,256,256]{2,1,0:T(8,128)(2,1)S(1)} %get-tuple-element.47.weight_ref, f32[8,256]{1,0:T(8,128)S(1)} %get-tuple-element.48.share_ref, bf16[256,128]{1,0:T(8,128)(2,1)S(1)} %collective-permute-done.5.v_ref), custom_call_target="tpu_custom_call" | custom-call | tf_op jit(solution)/shard_map/last_values/pallas_call | solution.py:307
Async XLA Ops:
  0.0 8.5 %collective-permute-start.1 = (bf16[256,128]{1,0:T(8,128)(2,1)}, bf16[256,128]{1,0:T(8,128)(2,1)S(1)}, u32[]{:S(2)}, u32[]{:S(2)}) collective-permute-start(bf16[256,128]{1,0:T(8,128)(2,1)} %k_hbm.1), channel_id=1, source_target_pairs={{0,8},{4,12},{8,0},{12,4},{1,9},{5,13},{9,1},{13,5},{2,10},{6,14},... | collective-permute-start | bytes 196616 | tf_op jit(solution)/shard_map/ppermute | solution.py:238
  4.0 6.4 %collective-permute-start = (bf16[256,128]{1,0:T(8,128)(2,1)}, bf16[256,128]{1,0:T(8,128)(2,1)S(1)}, u32[]{:S(2)}, u32[]{:S(2)}) collective-permute-start(bf16[256,128]{1,0:T(8,128)(2,1)} %v_hbm.1), channel_id=1, source_target_pairs={{0,8},{4,12},{8,0},{12,4},{1,9},{5,13},{9,1},{13,5},{2,10},{6,14},... | collective-permute-start | bytes 196616 | tf_op jit(solution)/shard_map/ppermute | solution.py:238
  4.1 8.6 %collective-permute-start.2 = (bf16[256,128]{1,0:T(8,128)(2,1)}, bf16[256,128]{1,0:T(8,128)(2,1)S(1)}, u32[]{:S(2)}, u32[]{:S(2)}) collective-permute-start(bf16[256,128]{1,0:T(8,128)(2,1)} %k_hbm.1), channel_id=1, source_target_pairs={{0,4},{4,0},{8,12},{12,8},{1,5},{5,1},{9,13},{13,9},{2,6},{6,2},{1... | collective-permute-start | bytes 196616 | tf_op jit(solution)/shard_map/ppermute | solution.py:238
  6.0 6.7 %collective-permute-start.3 = (bf16[256,128]{1,0:T(8,128)(2,1)}, bf16[256,128]{1,0:T(8,128)(2,1)S(1)}, u32[]{:S(2)}, u32[]{:S(2)}) collective-permute-start(bf16[256,128]{1,0:T(8,128)(2,1)} %v_hbm.1), channel_id=1, source_target_pairs={{0,4},{4,0},{8,12},{12,8},{1,5},{5,1},{9,13},{13,9},{2,6},{6,2},{1... | collective-permute-start | bytes 196616 | tf_op jit(solution)/shard_map/ppermute | solution.py:238
  8.5 5.3 %collective-permute-start.4 = (bf16[256,128]{1,0:T(8,128)(2,1)S(1)}, bf16[256,128]{1,0:T(8,128)(2,1)S(1)}, u32[]{:S(2)}, u32[]{:S(2)}) collective-permute-start(bf16[256,128]{1,0:T(8,128)(2,1)S(1)} %collective-permute-done.1.refs_5_), channel_id=1, source_target_pairs={{0,4},{4,0},{8,12},{12,8},{1,5},{5,1},{9,13},{13,9},{2,6},{6,2},{1... | collective-permute-start | bytes 196616 | tf_op jit(solution)/shard_map/ppermute | solution.py:238
  10.4 4.3 %collective-permute-start.5 = (bf16[256,128]{1,0:T(8,128)(2,1)S(1)}, bf16[256,128]{1,0:T(8,128)(2,1)S(1)}, u32[]{:S(2)}, u32[]{:S(2)}) collective-permute-start(bf16[256,128]{1,0:T(8,128)(2,1)S(1)} %collective-permute-done.refs_6_), channel_id=1, source_target_pairs={{0,4},{4,0},{8,12},{12,8},{1,5},{5,1},{9,13},{13,9},{2,6},{6,2},{1... | collective-permute-start | bytes 196616 | tf_op jit(solution)/shard_map/ppermute | solution.py:238

commit v33 on v32

--- a/solution.py
+++ b/solution.py
@@ -78,10 +78,10 @@
 
     def stage(head, _):
         if head not in ready:
-            pair = range(head, min(head + 2, across_ref.shape[0]))
-            across = jnp.concatenate([across_ref[one] for one in pair], axis=1)
+            group = range(head, min(head + 4, across_ref.shape[0]))
+            across = jnp.concatenate([across_ref[one] for one in group], axis=1)
             both = jnp.dot(keys, across, preferred_element_type=jnp.float32)
-            for at_column, one in enumerate(pair):
+            for at_column, one in enumerate(group):
                 width = across_ref.shape[2]
                 ready[one] = both[:, at_column * width:(at_column + 1) * width]
         scores = ready.pop(head)
@@ -197,11 +197,11 @@
 
     def mix(head, _):
         if head not in ready:
-            pair = range(head, min(head + 2, sum_ref.shape[0]))
-            weights = jnp.concatenate([weight_ref[one] for one in pair], axis=1)
+            group = range(head, min(head + 4, sum_ref.shape[0]))
+            weights = jnp.concatenate([weight_ref[one] for one in group], axis=1)
             both = jnp.dot(turned, weights, preferred_element_type=jnp.float32)
             width = sum_ref.shape[2]
-            for at_column, one in enumerate(pair):
+            for at_column, one in enumerate(group):
                 ready[one] = both[:, at_column * width:(at_column + 1) * width]
         added = ready.pop(head)
         return (sum_ref[head] + added * share_ref[head:head + 1, :]).astype(jnp.bfloat16)

time: 16 us -> 16.1 us (level)
  no operation moved by 1% of the time
where the time goes in v33:
time: 16.1 us; the launch traced here: 15.9 us
  starting transfers between devices  9.17 us (57%)
  Pallas kernels  6.4 us (40%)
  waiting for transfers between devices  0.27 us (2%)
    ppermute x6, starting transfers between devices, moved(): lax.ppermute(value, 'seq', [(i, i ^ mask) for i in range(lax.axis_size('s...  9.17 us
    pallas_call x1, Pallas kernels, staged_attention(): pl.pallas_call(own_kernel, in_specs=[pl.BlockSpec(memory_space=pltpu.SMEM...  2.44 us
    pallas_call x2, Pallas kernels, add_shard(): pl.pallas_call(lambda *refs: next_kernel(at, *refs), in_specs=[VMEM_REF]...  2 us
    pallas_call x1, Pallas kernels, staged_attention(): pl.pallas_call(last_kernel, in_specs=[VMEM_REF] * 4, out_specs=pl.BlockSp...  1.14 us
    pallas_call x1, Pallas kernels, staged_attention(): pl.pallas_call(lambda *refs: weights_kernel(3, *refs), in_specs=[VMEM_REF...  0.82 us
  transfers between devices with their start and end apart: 6, of which 1 were waited for; matrix products, arithmetic and copies ran while one was open for 0% of the time, Pallas kernels for 33%

profile of v33, /device:TPU:0, one launch (start us, length us, event | category | flops | bytes accessed | tf_op | source)
XLA Modules:
  0.0 15.9 jit_solution(6913413312591294033)
XLA Ops:
  0.0 4.0 %collective-permute-start.1 = (bf16[256,128]{1,0:T(8,128)(2,1)}, bf16[256,128]{1,0:T(8,128)(2,1)S(1)}, u32[]{:S(2)}, u32[]{:S(2)}) collective-permute-start(bf16[256,128]{1,0:T(8,128)(2,1)} %k_hbm.1), channel_id=1, source_target_pairs={{0,8},{4,12},{8,0},{12,4},{1,9},{5,13},{9,1},{13,5},{2,10},{6,14},... | collective-permute-start | bytes 196616 | tf_op jit(solution)/shard_map/ppermute | solution.py:238
  4.0 0.0 collective-permute-start
  4.1 1.9 %collective-permute-start.2 = (bf16[256,128]{1,0:T(8,128)(2,1)}, bf16[256,128]{1,0:T(8,128)(2,1)S(1)}, u32[]{:S(2)}, u32[]{:S(2)}) collective-permute-start(bf16[256,128]{1,0:T(8,128)(2,1)} %k_hbm.1), channel_id=1, source_target_pairs={{0,4},{4,0},{8,12},{12,8},{1,5},{5,1},{9,13},{13,9},{2,6},{6,2},{1... | collective-permute-start | bytes 196616 | tf_op jit(solution)/shard_map/ppermute | solution.py:238
  6.0 0.1 collective-permute-start.3
  6.1 2.4 %own_shard.1 = (bf16[8,128,256]{2,1,0:T(8,128)(2,1)S(1)}, f32[4,256,256]{2,1,0:T(8,128)S(1)}, f32[8,256]{1,0:T(8,128)S(1)}, f32[8,256]{1,0:T(8,128)S(1)}, f32[8,128,256]{2,1,0:T(8,128)S(1)}) custom-call(s32[1]{0:T(128)} %bitcast.own_ref, s32[3]{0:T(128)} %lengths_hbm.1, s32[1,128]{1,0:T(1,128)} %bitcast.2, bf16[256,1024]{1,0:T(8,128)(2,1)} %q_hbm.1, ...), custom_call_target="tpu_custom_call" | custom-call | tf_op jit(solution)/shard_map/own_shard/pallas_call | solution.py:258
  8.5 0.0 collective-permute-done.1.refs_5_
  8.6 1.9 %collective-permute-start.4 = (bf16[256,128]{1,0:T(8,128)(2,1)S(1)}, bf16[256,128]{1,0:T(8,128)(2,1)S(1)}, u32[]{:S(2)}, u32[]{:S(2)}) collective-permute-start(bf16[256,128]{1,0:T(8,128)(2,1)S(1)} %collective-permute-done.1.refs_5_), channel_id=1, source_target_pairs={{0,4},{4,0},{8,12},{12,8},{1,5},{5,1},{9,13},{13,9},{2,6},{6,2},{1... | collective-permute-start | bytes 196616 | tf_op jit(solution)/shard_map/ppermute | solution.py:238
  10.5 0.0 collective-permute-done.refs_6_
  10.5 1.1 %collective-permute-start.5 = (bf16[256,128]{1,0:T(8,128)(2,1)S(1)}, bf16[256,128]{1,0:T(8,128)(2,1)S(1)}, u32[]{:S(2)}, u32[]{:S(2)}) collective-permute-start(bf16[256,128]{1,0:T(8,128)(2,1)S(1)} %collective-permute-done.refs_6_), channel_id=1, source_target_pairs={{0,4},{4,0},{8,12},{12,8},{1,5},{5,1},{9,13},{13,9},{2,6},{6,2},{1... | collective-permute-start | bytes 196616 | tf_op jit(solution)/shard_map/ppermute | solution.py:238
  11.6 1.0 %next_shard.2 = (f32[8,256]{1,0:T(8,128)S(1)}, f32[8,256]{1,0:T(8,128)S(1)}, f32[8,128,256]{2,1,0:T(8,128)S(1)}) custom-call(bf16[8,128,256]{2,1,0:T(8,128)(2,1)S(1)} %get-tuple-element.27.refs_0_, f32[4,256,256]{2,1,0:T(8,128)S(1)} %get-tuple-element.28.refs_1_, f32[8,256]{1,0:T(8,128)S(1)} %get-tuple-element.35.refs_2_, ...), custom_call_target="tpu_custom_call" | custom-call | tf_op jit(solution)/shard_map/next_shard/pallas_call | solution.py:279
  12.6 0.0 collective-permute-done.2.refs_5_
  12.7 0.0 collective-permute-done.3.refs_6_
  12.7 1.0 %next_shard.3 = (f32[8,256]{1,0:T(8,128)S(1)}, f32[8,256]{1,0:T(8,128)S(1)}, f32[8,128,256]{2,1,0:T(8,128)S(1)}) custom-call(bf16[8,128,256]{2,1,0:T(8,128)(2,1)S(1)} %get-tuple-element.27.refs_0_, f32[4,256,256]{2,1,0:T(8,128)S(1)} %get-tuple-element.28.refs_1_, f32[8,256]{1,0:T(8,128)S(1)} %get-tuple-element.40.refs_2_, ...), custom_call_target="tpu_custom_call" | custom-call | tf_op jit(solution)/shard_map/next_shard/pallas_call | solution.py:279
  13.7 0.0 collective-permute-done.4.refs_5_
  13.7 0.8 %last_weights.1 = (f32[8,128,256]{2,1,0:T(8,128)S(1)}, bf16[8,256,256]{2,1,0:T(8,128)(2,1)S(1)}, f32[8,256]{1,0:T(8,128)S(1)}) custom-call(bf16[8,128,256]{2,1,0:T(8,128)(2,1)S(1)} %get-tuple-element.27.refs_0_, f32[4,256,256]{2,1,0:T(8,128)S(1)} %get-tuple-element.28.refs_1_, f32[8,256]{1,0:T(8,128)S(1)} %get-tuple-element.43.refs_2_, ...), custom_call_target="tpu_custom_call" | custom-call | tf_op jit(solution)/shard_map/last_weights/pallas_call | solution.py:297
  14.5 0.3 %collective-permute-done.5.v_ref = bf16[256,128]{1,0:T(8,128)(2,1)S(1)} collective-permute-done((bf16[256,128]{1,0:T(8,128)(2,1)S(1)}, bf16[256,128]{1,0:T(8,128)(2,1)S(1)}, u32[]{:S(2)}, u32[]{:S(2)}) %collective-permute-start.5) | collective-permute-done | bytes 65568 | tf_op jit(solution)/shard_map/ppermute | solution.py:238
  14.8 1.1 %last_values.1 = bf16[256,1024]{1,0:T(8,128)(2,1)} custom-call(f32[8,128,256]{2,1,0:T(8,128)S(1)} %get-tuple-element.46.sum_ref, bf16[8,256,256]{2,1,0:T(8,128)(2,1)S(1)} %get-tuple-element.47.weight_ref, f32[8,256]{1,0:T(8,128)S(1)} %get-tuple-element.48.share_ref, bf16[256,128]{1,0:T(8,128)(2,1)S(1)} %collective-permute-done.5.v_ref), custom_call_target="tpu_custom_call" | custom-call | tf_op jit(solution)/shard_map/last_values/pallas_call | solution.py:307
Async XLA Ops:
  0.0 8.5 %collective-permute-start.1 = (bf16[256,128]{1,0:T(8,128)(2,1)}, bf16[256,128]{1,0:T(8,128)(2,1)S(1)}, u32[]{:S(2)}, u32[]{:S(2)}) collective-permute-start(bf16[256,128]{1,0:T(8,128)(2,1)} %k_hbm.1), channel_id=1, source_target_pairs={{0,8},{4,12},{8,0},{12,4},{1,9},{5,13},{9,1},{13,5},{2,10},{6,14},... | collective-permute-start | bytes 196616 | tf_op jit(solution)/shard_map/ppermute | solution.py:238
  4.0 6.5 %collective-permute-start = (bf16[256,128]{1,0:T(8,128)(2,1)}, bf16[256,128]{1,0:T(8,128)(2,1)S(1)}, u32[]{:S(2)}, u32[]{:S(2)}) collective-permute-start(bf16[256,128]{1,0:T(8,128)(2,1)} %v_hbm.1), channel_id=1, source_target_pairs={{0,8},{4,12},{8,0},{12,4},{1,9},{5,13},{9,1},{13,5},{2,10},{6,14},... | collective-permute-start | bytes 196616 | tf_op jit(solution)/shard_map/ppermute | solution.py:238
  4.1 8.6 %collective-permute-start.2 = (bf16[256,128]{1,0:T(8,128)(2,1)}, bf16[256,128]{1,0:T(8,128)(2,1)S(1)}, u32[]{:S(2)}, u32[]{:S(2)}) collective-permute-start(bf16[256,128]{1,0:T(8,128)(2,1)} %k_hbm.1), channel_id=1, source_target_pairs={{0,4},{4,0},{8,12},{12,8},{1,5},{5,1},{9,13},{13,9},{2,6},{6,2},{1... | collective-permute-start | bytes 196616 | tf_op jit(solution)/shard_map/ppermute | solution.py:238
  6.0 6.7 %collective-permute-start.3 = (bf16[256,128]{1,0:T(8,128)(2,1)}, bf16[256,128]{1,0:T(8,128)(2,1)S(1)}, u32[]{:S(2)}, u32[]{:S(2)}) collective-permute-start(bf16[256,128]{1,0:T(8,128)(2,1)} %v_hbm.1), channel_id=1, source_target_pairs={{0,4},{4,0},{8,12},{12,8},{1,5},{5,1},{9,13},{13,9},{2,6},{6,2},{1... | collective-permute-start | bytes 196616 | tf_op jit(solution)/shard_map/ppermute | solution.py:238
  8.6 5.1 %collective-permute-start.4 = (bf16[256,128]{1,0:T(8,128)(2,1)S(1)}, bf16[256,128]{1,0:T(8,128)(2,1)S(1)}, u32[]{:S(2)}, u32[]{:S(2)}) collective-permute-start(bf16[256,128]{1,0:T(8,128)(2,1)S(1)} %collective-permute-done.1.refs_5_), channel_id=1, source_target_pairs={{0,4},{4,0},{8,12},{12,8},{1,5},{5,1},{9,13},{13,9},{2,6},{6,2},{1... | collective-permute-start | bytes 196616 | tf_op jit(solution)/shard_map/ppermute | solution.py:238
  10.5 4.3 %collective-permute-start.5 = (bf16[256,128]{1,0:T(8,128)(2,1)S(1)}, bf16[256,128]{1,0:T(8,128)(2,1)S(1)}, u32[]{:S(2)}, u32[]{:S(2)}) collective-permute-start(bf16[256,128]{1,0:T(8,128)(2,1)S(1)} %collective-permute-done.refs_6_), channel_id=1, source_target_pairs={{0,4},{4,0},{8,12},{12,8},{1,5},{5,1},{9,13},{13,9},{2,6},{6,2},{1... | collective-permute-start | bytes 196616 | tf_op jit(solution)/shard_map/ppermute | solution.py:238

commit v34 on v33

--- a/solution.py
+++ b/solution.py
@@ -197,7 +197,7 @@
 
     def mix(head, _):
         if head not in ready:
-            group = range(head, min(head + 4, sum_ref.shape[0]))
+            group = range(head, min(head + 8, sum_ref.shape[0]))
             weights = jnp.concatenate([weight_ref[one] for one in group], axis=1)
             both = jnp.dot(turned, weights, preferred_element_type=jnp.float32)
             width = sum_ref.shape[2]

time: 16.1 us -> 16.1 us (level)
  no operation moved by 1% of the time
where the time goes in v34:
time: 16.1 us; the launch traced here: 15.9 us
  starting transfers between devices  9.17 us (57%)
  Pallas kernels  6.4 us (40%)
  waiting for transfers between devices  0.27 us (2%)
    ppermute x6, starting transfers between devices, moved(): lax.ppermute(value, 'seq', [(i, i ^ mask) for i in range(lax.axis_size('s...  9.17 us
    pallas_call x1, Pallas kernels, staged_attention(): pl.pallas_call(own_kernel, in_specs=[pl.BlockSpec(memory_space=pltpu.SMEM...  2.44 us
    pallas_call x2, Pallas kernels, add_shard(): pl.pallas_call(lambda *refs: next_kernel(at, *refs), in_specs=[VMEM_REF]...  2 us
    pallas_call x1, Pallas kernels, staged_attention(): pl.pallas_call(last_kernel, in_specs=[VMEM_REF] * 4, out_specs=pl.BlockSp...  1.14 us
    pallas_call x1, Pallas kernels, staged_attention(): pl.pallas_call(lambda *refs: weights_kernel(3, *refs), in_specs=[VMEM_REF...  0.82 us
  transfers between devices with their start and end apart: 6, of which 1 were waited for; matrix products, arithmetic and copies ran while one was open for 0% of the time, Pallas kernels for 33%

profile of v34, /device:TPU:0, one launch (start us, length us, event | category | flops | bytes accessed | tf_op | source)
XLA Modules:
  0.0 15.9 jit_solution(6913413312591294033)
XLA Ops:
  0.0 4.0 %collective-permute-start.1 = (bf16[256,128]{1,0:T(8,128)(2,1)}, bf16[256,128]{1,0:T(8,128)(2,1)S(1)}, u32[]{:S(2)}, u32[]{:S(2)}) collective-permute-start(bf16[256,128]{1,0:T(8,128)(2,1)} %k_hbm.1), channel_id=1, source_target_pairs={{0,8},{4,12},{8,0},{12,4},{1,9},{5,13},{9,1},{13,5},{2,10},{6,14},... | collective-permute-start | bytes 196616 | tf_op jit(solution)/shard_map/ppermute | solution.py:238
  4.0 0.0 collective-permute-start
  4.1 1.9 %collective-permute-start.2 = (bf16[256,128]{1,0:T(8,128)(2,1)}, bf16[256,128]{1,0:T(8,128)(2,1)S(1)}, u32[]{:S(2)}, u32[]{:S(2)}) collective-permute-start(bf16[256,128]{1,0:T(8,128)(2,1)} %k_hbm.1), channel_id=1, source_target_pairs={{0,4},{4,0},{8,12},{12,8},{1,5},{5,1},{9,13},{13,9},{2,6},{6,2},{1... | collective-permute-start | bytes 196616 | tf_op jit(solution)/shard_map/ppermute | solution.py:238
  6.0 0.1 collective-permute-start.3
  6.1 2.4 %own_shard.1 = (bf16[8,128,256]{2,1,0:T(8,128)(2,1)S(1)}, f32[4,256,256]{2,1,0:T(8,128)S(1)}, f32[8,256]{1,0:T(8,128)S(1)}, f32[8,256]{1,0:T(8,128)S(1)}, f32[8,128,256]{2,1,0:T(8,128)S(1)}) custom-call(s32[1]{0:T(128)} %bitcast.own_ref, s32[3]{0:T(128)} %lengths_hbm.1, s32[1,128]{1,0:T(1,128)} %bitcast.2, bf16[256,1024]{1,0:T(8,128)(2,1)} %q_hbm.1, ...), custom_call_target="tpu_custom_call" | custom-call | tf_op jit(solution)/shard_map/own_shard/pallas_call | solution.py:258
  8.5 0.0 collective-permute-done.1.refs_5_
  8.6 1.9 %collective-permute-start.4 = (bf16[256,128]{1,0:T(8,128)(2,1)S(1)}, bf16[256,128]{1,0:T(8,128)(2,1)S(1)}, u32[]{:S(2)}, u32[]{:S(2)}) collective-permute-start(bf16[256,128]{1,0:T(8,128)(2,1)S(1)} %collective-permute-done.1.refs_5_), channel_id=1, source_target_pairs={{0,4},{4,0},{8,12},{12,8},{1,5},{5,1},{9,13},{13,9},{2,6},{6,2},{1... | collective-permute-start | bytes 196616 | tf_op jit(solution)/shard_map/ppermute | solution.py:238
  10.5 0.0 collective-permute-done.refs_6_
  10.5 1.1 %collective-permute-start.5 = (bf16[256,128]{1,0:T(8,128)(2,1)S(1)}, bf16[256,128]{1,0:T(8,128)(2,1)S(1)}, u32[]{:S(2)}, u32[]{:S(2)}) collective-permute-start(bf16[256,128]{1,0:T(8,128)(2,1)S(1)} %collective-permute-done.refs_6_), channel_id=1, source_target_pairs={{0,4},{4,0},{8,12},{12,8},{1,5},{5,1},{9,13},{13,9},{2,6},{6,2},{1... | collective-permute-start | bytes 196616 | tf_op jit(solution)/shard_map/ppermute | solution.py:238
  11.6 1.0 %next_shard.2 = (f32[8,256]{1,0:T(8,128)S(1)}, f32[8,256]{1,0:T(8,128)S(1)}, f32[8,128,256]{2,1,0:T(8,128)S(1)}) custom-call(bf16[8,128,256]{2,1,0:T(8,128)(2,1)S(1)} %get-tuple-element.27.refs_0_, f32[4,256,256]{2,1,0:T(8,128)S(1)} %get-tuple-element.28.refs_1_, f32[8,256]{1,0:T(8,128)S(1)} %get-tuple-element.35.refs_2_, ...), custom_call_target="tpu_custom_call" | custom-call | tf_op jit(solution)/shard_map/next_shard/pallas_call | solution.py:279
  12.6 0.0 collective-permute-done.2.refs_5_
  12.7 0.0 collective-permute-done.3.refs_6_
  12.7 1.0 %next_shard.3 = (f32[8,256]{1,0:T(8,128)S(1)}, f32[8,256]{1,0:T(8,128)S(1)}, f32[8,128,256]{2,1,0:T(8,128)S(1)}) custom-call(bf16[8,128,256]{2,1,0:T(8,128)(2,1)S(1)} %get-tuple-element.27.refs_0_, f32[4,256,256]{2,1,0:T(8,128)S(1)} %get-tuple-element.28.refs_1_, f32[8,256]{1,0:T(8,128)S(1)} %get-tuple-element.40.refs_2_, ...), custom_call_target="tpu_custom_call" | custom-call | tf_op jit(solution)/shard_map/next_shard/pallas_call | solution.py:279
  13.7 0.0 collective-permute-done.4.refs_5_
  13.7 0.8 %last_weights.1 = (f32[8,128,256]{2,1,0:T(8,128)S(1)}, bf16[8,256,256]{2,1,0:T(8,128)(2,1)S(1)}, f32[8,256]{1,0:T(8,128)S(1)}) custom-call(bf16[8,128,256]{2,1,0:T(8,128)(2,1)S(1)} %get-tuple-element.27.refs_0_, f32[4,256,256]{2,1,0:T(8,128)S(1)} %get-tuple-element.28.refs_1_, f32[8,256]{1,0:T(8,128)S(1)} %get-tuple-element.43.refs_2_, ...), custom_call_target="tpu_custom_call" | custom-call | tf_op jit(solution)/shard_map/last_weights/pallas_call | solution.py:297
  14.5 0.3 %collective-permute-done.5.v_ref = bf16[256,128]{1,0:T(8,128)(2,1)S(1)} collective-permute-done((bf16[256,128]{1,0:T(8,128)(2,1)S(1)}, bf16[256,128]{1,0:T(8,128)(2,1)S(1)}, u32[]{:S(2)}, u32[]{:S(2)}) %collective-permute-start.5) | collective-permute-done | bytes 65568 | tf_op jit(solution)/shard_map/ppermute | solution.py:238
  14.8 1.1 %last_values.1 = bf16[256,1024]{1,0:T(8,128)(2,1)} custom-call(f32[8,128,256]{2,1,0:T(8,128)S(1)} %get-tuple-element.46.sum_ref, bf16[8,256,256]{2,1,0:T(8,128)(2,1)S(1)} %get-tuple-element.47.weight_ref, f32[8,256]{1,0:T(8,128)S(1)} %get-tuple-element.48.share_ref, bf16[256,128]{1,0:T(8,128)(2,1)S(1)} %collective-permute-done.5.v_ref), custom_call_target="tpu_custom_call" | custom-call | tf_op jit(solution)/shard_map/last_values/pallas_call | solution.py:307
Async XLA Ops:
  0.0 8.5 %collective-permute-start.1 = (bf16[256,128]{1,0:T(8,128)(2,1)}, bf16[256,128]{1,0:T(8,128)(2,1)S(1)}, u32[]{:S(2)}, u32[]{:S(2)}) collective-permute-start(bf16[256,128]{1,0:T(8,128)(2,1)} %k_hbm.1), channel_id=1, source_target_pairs={{0,8},{4,12},{8,0},{12,4},{1,9},{5,13},{9,1},{13,5},{2,10},{6,14},... | collective-permute-start | bytes 196616 | tf_op jit(solution)/shard_map/ppermute | solution.py:238
  4.0 6.5 %collective-permute-start = (bf16[256,128]{1,0:T(8,128)(2,1)}, bf16[256,128]{1,0:T(8,128)(2,1)S(1)}, u32[]{:S(2)}, u32[]{:S(2)}) collective-permute-start(bf16[256,128]{1,0:T(8,128)(2,1)} %v_hbm.1), channel_id=1, source_target_pairs={{0,8},{4,12},{8,0},{12,4},{1,9},{5,13},{9,1},{13,5},{2,10},{6,14},... | collective-permute-start | bytes 196616 | tf_op jit(solution)/shard_map/ppermute | solution.py:238
  4.1 8.6 %collective-permute-start.2 = (bf16[256,128]{1,0:T(8,128)(2,1)}, bf16[256,128]{1,0:T(8,128)(2,1)S(1)}, u32[]{:S(2)}, u32[]{:S(2)}) collective-permute-start(bf16[256,128]{1,0:T(8,128)(2,1)} %k_hbm.1), channel_id=1, source_target_pairs={{0,4},{4,0},{8,12},{12,8},{1,5},{5,1},{9,13},{13,9},{2,6},{6,2},{1... | collective-permute-start | bytes 196616 | tf_op jit(solution)/shard_map/ppermute | solution.py:238
  6.0 6.7 %collective-permute-start.3 = (bf16[256,128]{1,0:T(8,128)(2,1)}, bf16[256,128]{1,0:T(8,128)(2,1)S(1)}, u32[]{:S(2)}, u32[]{:S(2)}) collective-permute-start(bf16[256,128]{1,0:T(8,128)(2,1)} %v_hbm.1), channel_id=1, source_target_pairs={{0,4},{4,0},{8,12},{12,8},{1,5},{5,1},{9,13},{13,9},{2,6},{6,2},{1... | collective-permute-start | bytes 196616 | tf_op jit(solution)/shard_map/ppermute | solution.py:238
  8.6 5.1 %collective-permute-start.4 = (bf16[256,128]{1,0:T(8,128)(2,1)S(1)}, bf16[256,128]{1,0:T(8,128)(2,1)S(1)}, u32[]{:S(2)}, u32[]{:S(2)}) collective-permute-start(bf16[256,128]{1,0:T(8,128)(2,1)S(1)} %collective-permute-done.1.refs_5_), channel_id=1, source_target_pairs={{0,4},{4,0},{8,12},{12,8},{1,5},{5,1},{9,13},{13,9},{2,6},{6,2},{1... | collective-permute-start | bytes 196616 | tf_op jit(solution)/shard_map/ppermute | solution.py:238
  10.5 4.3 %collective-permute-start.5 = (bf16[256,128]{1,0:T(8,128)(2,1)S(1)}, bf16[256,128]{1,0:T(8,128)(2,1)S(1)}, u32[]{:S(2)}, u32[]{:S(2)}) collective-permute-start(bf16[256,128]{1,0:T(8,128)(2,1)S(1)} %collective-permute-done.refs_6_), channel_id=1, source_target_pairs={{0,4},{4,0},{8,12},{12,8},{1,5},{5,1},{9,13},{13,9},{2,6},{6,2},{1... | collective-permute-start | bytes 196616 | tf_op jit(solution)/shard_map/ppermute | solution.py:238
